TPU v7x, 32 devices: a whole 2x2x4 slice. The times are simulated.
32 devices in a mesh: vir: 4 (over z), occ: 2 (over x), ka: 4 (over y, core).
Axes of the slice: x: 2, y: 2, z: 4, core: 2. Of those that a mesh axis runs over, the one named last changes fastest.
Arguments:
- ladder_amplitudes: bfloat16 [512, 53248], P('vir', ('occ', 'ka')), may hold values from -6 to 6
- ladder_integrals: bfloat16 [53248, 8192], P(('occ', 'ka'), 'vir'), may hold values from -0.02734375 to 0.02734375
- cycle_amplitudes: bfloat16 [8, 8, 640, 5120], P('occ', 'vir', None, 'ka'), may hold values from -6 to 6
- cycle_integrals: bfloat16 [8, 5120, 8, 640], P('occ', 'ka', 'vir'), may hold values from -0.078125 to 0.078125
Outputs:
- ladder_residual: bfloat16 [512, 8192], P(('occ', 'ka'), 'vir')
- cycle_residual: bfloat16 [8, 8, 640, 8, 640], P('occ', 'vir', 'ka')
All inputs are finite; a program needn't handle non-finite values.
Results may differ from a plain program's by a relative error of at most 0.02.
Values may be sent and summed in bfloat16 or wider, within the bound.
No kernel may reach another device: no remote copies, remote signals or barrier semaphores. Data moves between devices by JAX's collectives and lax.ppermute only.
A program may use at most 256 MiB of HBM per device.

v0:
```python
import jax
import jax.numpy as jnp
from jax import lax
from jax.sharding import PartitionSpec as P


def regroup(blocks):
    local_rows = blocks.shape[1]
    first_irrep = lax.axis_index("vir") * local_rows
    pieces = []
    for local_index in range(local_rows):
        permuted = jnp.bitwise_xor(first_irrep + local_index, jnp.arange(8, dtype=jnp.int32))
        pieces.append(jnp.take(blocks[:, local_index], permuted, axis=2))
    stacked = jnp.stack(pieces, axis=1)
    return jnp.transpose(stacked, (3, 1, 2, 0, 4))


def local(ladder_amplitudes, ladder_integrals, cycle_amplitudes, cycle_integrals):
    partial_ladder = jnp.dot(
        lax.all_gather(ladder_amplitudes, "vir", axis=0, tiled=True),
        ladder_integrals,
        preferred_element_type=jnp.float32,
    )
    summed_ladder = lax.psum_scatter(
        partial_ladder.astype(jnp.bfloat16), ("occ", "ka"), scatter_dimension=0, tiled=True
    )
    partial_cycle = jnp.einsum(
        "gaxk,gkny->gaxny",
        cycle_amplitudes,
        lax.all_gather(cycle_integrals, "vir", axis=2, tiled=True),
        preferred_element_type=jnp.float32,
    )
    summed_cycle = lax.psum_scatter(
        partial_cycle.astype(jnp.bfloat16), "ka", scatter_dimension=2, tiled=True
    )
    arranged = regroup(summed_cycle)
    cycle_residual = lax.all_to_all(arranged, "occ", split_axis=0, concat_axis=3, tiled=True)
    return (summed_ladder, cycle_residual)


def solution(mesh):
    placed = (
        P("vir", ("occ", "ka")),
        P(("occ", "ka"), "vir"),
        P("occ", "vir", None, "ka"),
        P("occ", "ka", "vir", None),
    )
    return jax.shard_map(
        local,
        mesh=mesh,
        in_specs=placed,
        out_specs=(P(("occ", "ka"), "vir"), P("occ", "vir", "ka", None, None)),
        check_vma=False,
    )
```

profile of v0, /device:TPU:10, one launch (start us, length us, event | category | flops | bytes accessed | tf_op | source)
XLA Modules:
  0.0 1583.7 jit_solution(11188026872316991538)
XLA Ops:
  7.2 0.0 all-gather.5.cloned.1.call-start
  7.2 12.3 copy.8
  19.5 0.0 all-gather.5.cloned.1.call-update
  19.5 0.0 reduce-scatter.5.cloned.1.call-start
  19.6 868.9 %all-gather.5.cloned.1.call-done = bf16[4,1280,8,640]{3,1,2,0:T(8,128)(2,1)} async-done(((bf16[4,1280,2,640]{3,1,2,0:T(8,128)(2,1)}), bf16[4,1280,8,640]{3,1,2,0:T(8,128)(2,1)}) %all-gather.5.cloned.1.call-update) | async-done | bytes 52428816 | tf_op jit(solution)/shard_map/all_gather | solution.py:30
  888.5 77.0 %fusion.2 = bf16[4,2,640,8,640]{4,2,3,1,0:T(8,128)(2,1)} fusion(bf16[4,1280,8,640]{3,1,2,0:T(8,128)(2,1)} %all-gather.5.cloned.1.call-done, bf16[4,2,640,1280]{3,2,1,0:T(8,128)(2,1)} %param.8), kind=kOutput, calls=%fused_computation.4 | convolution fusion | flops 67135078400 | bytes 117964800 | tf_op jit(solution)/shard_map/gaxk,gkny->gaxny/dot_general | solution.py:27
  965.5 0.0 reduce-scatter.5.cloned.1.call-update
  965.5 0.0 all-gather.3.cloned.1.call-start
  965.5 0.7 all-gather.3.cloned.1.call-update
  966.3 357.1 %reduce-scatter.5.cloned.1.call-done = bf16[4,2,160,8,640]{4,2,3,1,0:T(8,128)(2,1)} async-done(((bf16[4,2,640,8,640]{4,2,3,1,0:T(8,128)(2,1)}), bf16[4,2,160,8,640]{4,2,3,1,0:T(8,128)(2,1)}) %reduce-scatter.5.cloned.1.call-update) | async-done | bytes 13107216 | tf_op jit(solution)/shard_map/reduce_scatter | solution.py:33
  1323.4 9.8 slice_bitcast_fusion.1
  1333.2 7.6 gather_fusion.1
  1340.7 6.9 gather_fusion
  1347.7 5.9 select_bitcast_fusion
  1353.6 2.4 maximum_bitcast_fusion
  1356.0 5.9 copy.9
  1361.9 9.2 all-to-all-start
  1371.0 0.0 reduce-scatter.3.cloned.1.call-start
  1371.0 75.2 %all-gather.3.cloned.1.call-done = bf16[512,6656]{1,0:T(8,128)(2,1)} async-done(((bf16[128,6656]{1,0:T(8,128)(2,1)}), bf16[512,6656]{1,0:T(8,128)(2,1)}) %all-gather.3.cloned.1.call-update) | async-done | bytes 6815760 | tf_op jit(solution)/shard_map/all_gather | solution.py:20
  1446.3 22.2 %convolution_convert_fusion = bf16[512,2048]{1,0:T(8,128)(2,1)} fusion(bf16[512,6656]{1,0:T(8,128)(2,1)} %all-gather.3.cloned.1.call-done, bf16[6656,2048]{1,0:T(8,128)(2,1)} %param.7), kind=kOutput, calls=%fused_computation.11 | convolution fusion | flops 13959692288 | bytes 36175872 | tf_op jit(solution)/shard_map/dot_general | solution.py:19
  1468.5 0.0 reduce-scatter.3.cloned.1.call-update
  1468.5 52.5 %all-to-all-done = bf16[8,2,160,4,640]{4,2,3,1,0:T(8,128)(2,1)} async-done(((bf16[8,2,160,4,640]{4,2,3,1,0:T(8,128)(2,1)}), bf16[8,2,160,4,640]{4,2,3,1,0:T(8,128)(2,1)}, u32[]{:S(2)}, u32[]{:S(2)}) %all-to-all-start) | async-done | bytes 13107232 | tf_op jit(solution)/shard_map/all_to_all | solution.py:37
  1521.0 34.9 %copy.10 = bf16[4,2,160,2,4,640]{5,4,3,2,1,0:T(4,128)(2,1)} copy(bf16[4,2,160,2,4,640]{5,2,4,1,0,3:T(8,128)(2,1)} %bitcast.12) | data formatting | bytes 26214400 | tf_op jit(solution)/shard_map/all_to_all | solution.py:37
  1555.8 21.3 %all_to_all.16 = bf16[4,2,160,8,640]{4,3,2,1,0:T(8,128)(2,1)} reshape(bf16[4,2,160,2,4,640]{5,4,3,2,1,0:T(4,128)(2,1)} %copy.10) | data formatting | bytes 26214400 | tf_op jit(solution)/shard_map/all_to_all | solution.py:37
  1577.1 0.0 reduce-scatter.3.cloned.1.call-done
  (6 shorter events, 0.0 us)
Async XLA Ops:
  7.2 881.3 %all-gather.5.cloned.1.call-start = ((), (), s32[]{:S(2)}) async-start(), calls=%async_computation.5 | async-start | bytes 65536000 | tf_op jit(solution)/shard_map/all_gather | solution.py:30
  19.5 1303.9 %reduce-scatter.5.cloned.1.call-start = ((), (), s32[]{:S(2)}) async-start(), calls=%async_computation.6 | async-start | bytes 65536000 | tf_op jit(solution)/shard_map/reduce_scatter | solution.py:33
  965.5 480.8 %all-gather.3.cloned.1.call-start = ((), (), s32[]{:S(2)}) async-start(), calls=%async_computation.3 | async-start | bytes 8519680 | tf_op jit(solution)/shard_map/all_gather | solution.py:20
  1361.9 159.1 %all-to-all-start = ((bf16[8,2,160,4,640]{4,2,3,1,0:T(8,128)(2,1)}), bf16[8,2,160,4,640]{4,2,3,1,0:T(8,128)(2,1)}, u32[]{:S(2)}, u32[]{:S(2)}) async-start(bf16[8,2,160,4,640]{4,2,3,1,0:T(8,128)(2,1)} %copy.9), calls=%async_computation.2 | async-start | bytes 26214400 | tf_op jit(solution)/shard_map/all_to_all | solution.py:37
  1371.0 206.1 %reduce-scatter.3.cloned.1.call-start = ((), (), s32[]{:S(2)}) async-start(), calls=%async_computation.4 | async-start | bytes 2359296 | tf_op jit(solution)/shard_map/reduce_scatter | solution.py:24
Sparse Core Ops, SparseCore 0:
  19.6 868.7 all-gather.4
  965.6 357.7 reduce-scatter.4
  1325.1 121.1 all-gather.2
  1468.6 49.8 reduce-scatter.2
where the time goes:
time: 1590 us; the launch traced here: 1580 us
  waiting for transfers between devices  1350 us (85%)
  matrix products  99.2 us (6%)
  local copies, waits for them, and re-layouts  98.6 us (6%)
    all_gather x1, waiting for transfers between devices, local(): lax.all_gather(cycle_integrals, 'vir', axis=2, tiled=True)  869 us
    reduce_scatter x1, waiting for transfers between devices, local(): lax.psum_scatter(partial_cycle.astype(jnp.bfloat16), 'ka', scatter_dimens...  357 us
    dot_general x1, matrix products, local(): jnp.einsum('gaxk,gkny->gaxny', cycle_amplitudes, lax.all_gather(cycle_int...  77 us
    all_gather x1, waiting for transfers between devices, local(): lax.all_gather(ladder_amplitudes, 'vir', axis=0, tiled=True)  75.2 us
    all_to_all x2, local copies, waits for them, and re-layouts, local(): lax.all_to_all(arranged, 'occ', split_axis=0, concat_axis=3, tiled=True)  56.2 us
    all_to_all x1, waiting for transfers between devices, local(): lax.all_to_all(arranged, 'occ', split_axis=0, concat_axis=3, tiled=True)  52.5 us
  transfers between devices with their start and end apart: 5, of which 4 were waited for; matrix products, arithmetic and copies ran while one was open for 6% of the time, Pallas kernels for 0%

commit v1 on v0

v1 whole, which is shorter than its diff:
```python
import jax
import jax.numpy as jnp
from jax import lax
from jax.experimental import pallas as pl
from jax.experimental.pallas import tpu as pltpu
from jax.sharding import PartitionSpec as P

F32, BF16 = jnp.float32, jnp.bfloat16

END_TO_MID = [(0, 1), (3, 2)]
MID_TO_MID = [(1, 2), (2, 1)]
MID_TO_END = [(1, 0), (2, 3)]
RELATIVE = (0, 2, 1, 3)
OTHER_CORE = [(0, 1), (1, 0), (2, 3), (3, 2)]
OTHER_Y = [(0, 2), (2, 0), (1, 3), (3, 1)]
OTHER_OCC = [(0, 1), (1, 0)]
ROOM = 60 << 20
CHEAP = pl.CostEstimate(flops=1 << 20, bytes_accessed=1 << 16, transcendentals=0)


def after(value, *earlier):
    return lax.optimization_barrier((value, *earlier))[0]


def dot_rows(lhs, rhs):
    return jnp.dot(lhs.reshape(-1, lhs.shape[-1]), rhs, preferred_element_type=F32)


def lhs_specs(irrep, sources, rows, depth, first):
    specs = []
    for place in range(sources):
        def quarter(s, r, where, place=place):
            moment = r if sources == 1 else jnp.where(s == place, r, 1 if place == 0 else 0)
            return where[first + moment]
        if place == 0:
            specs.append(pl.BlockSpec((1, 2, rows, depth), lambda s, r, where, q=quarter: (irrep, 0, q(s, r, where), 0)))
        else:
            specs.append(pl.BlockSpec((2, rows, depth), lambda s, r, where, q=quarter: (0, q(s, r, where), 0)))
    return specs


def product(lhs_refs, rhs_ref, use):
    source = pl.program_id(0)
    for place, lhs in enumerate(lhs_refs):
        @pl.when(source == place)
        def _():
            use(dot_rows(lhs[...], rhs_ref[...]))


def send_product(where, irrep, lhs, rhs):
    sources, depth, columns = len(lhs), rhs.shape[0], rhs.shape[1]
    rows = lhs[0].shape[2] // 4

    def kernel(where_ref, *refs):
        out = refs[-1]

        def use(value):
            out[0, 0] = value.astype(BF16)
        product(refs[:sources], refs[sources], use)

    return pl.pallas_call(
        kernel,
        out_shape=jax.ShapeDtypeStruct((sources, 2, 2 * rows, columns), BF16),
        grid_spec=pltpu.PrefetchScalarGridSpec(
            num_scalar_prefetch=1,
            grid=(sources, 2),
            in_specs=lhs_specs(irrep, sources, rows, depth, 2)
            + [pl.BlockSpec((depth, columns), lambda s, r, where: (0, 0))],
            out_specs=pl.BlockSpec((1, 1, 2 * rows, columns), lambda s, r, where: (s, r, 0, 0)),
        ),
        compiler_params=pltpu.CompilerParams(vmem_limit_bytes=ROOM),
        cost_estimate=CHEAP,
        name="send_product",
    )(where, *lhs, rhs)


def keep_product(where, irrep, lhs, rhs, arrived):
    sources, depth, columns = len(lhs), rhs.shape[0], rhs.shape[1]
    rows = lhs[0].shape[2] // 4

    def kernel(where_ref, *refs):
        arrived_ref, away, own = refs[sources + 1:]
        quarter = pl.program_id(1)

        def use(value):
            total = value + arrived_ref[0, 0].astype(F32)

            @pl.when(quarter == 0)
            def _():
                own[0] = total.astype(BF16)

            @pl.when(quarter == 1)
            def _():
                away[0] = total.astype(BF16)
        product(refs[:sources], refs[sources], use)

    return pl.pallas_call(
        kernel,
        out_shape=(
            jax.ShapeDtypeStruct((sources, 2 * rows, columns), BF16),
            jax.ShapeDtypeStruct((sources, 2 * rows, columns), BF16),
        ),
        grid_spec=pltpu.PrefetchScalarGridSpec(
            num_scalar_prefetch=1,
            grid=(sources, 2),
            in_specs=lhs_specs(irrep, sources, rows, depth, 0)
            + [pl.BlockSpec((depth, columns), lambda s, r, where: (0, 0)),
               pl.BlockSpec((1, 1, 2 * rows, columns), lambda s, r, where: (s, r, 0, 0))],
            out_specs=(pl.BlockSpec((1, 2 * rows, columns), lambda s, r, where: (s, 0, 0)),) * 2,
        ),
        compiler_params=pltpu.CompilerParams(vmem_limit_bytes=ROOM),
        cost_estimate=CHEAP,
        name="keep_product",
    )(where, *lhs, rhs, arrived)


def whole_product(irrep, products):
    count = len(products)
    lhs, rhs = zip(*products)
    depth, columns = lhs[0].shape[-1], rhs[0][0].shape[-1]
    rows = lhs[0].shape[-2] // 4

    def kernel(*refs):
        out = refs[-1]
        for index in range(count):
            @pl.when(pl.program_id(0) == index)
            def _():
                out[0, 0] = dot_rows(refs[index][...], refs[count + index][...]).astype(BF16)

    specs = []
    for index, array in enumerate(lhs):
        def quarter(p, r, index=index):
            return jnp.where(p == index, r, jnp.where(p < index, 0, 3))
        if array.ndim == 4:
            specs.append(pl.BlockSpec((1, 2, rows, depth), lambda p, r, q=quarter: (irrep, 0, q(p, r), 0)))
        else:
            specs.append(pl.BlockSpec((2, rows, depth), lambda p, r, q=quarter: (0, q(p, r), 0)))
    for array, index in rhs:
        specs.append(pl.BlockSpec((depth, columns), lambda p, r, index=index: (index, 0)))
    return pl.pallas_call(
        kernel,
        out_shape=jax.ShapeDtypeStruct((4, count, 2 * rows, columns), BF16),
        grid=(count, 4),
        in_specs=specs,
        out_specs=pl.BlockSpec((1, 1, 2 * rows, columns), lambda p, r: (r, p, 0, 0)),
        compiler_params=pltpu.CompilerParams(vmem_limit_bytes=ROOM),
        cost_estimate=CHEAP,
        name="whole_product",
    )(*lhs, *[array for array, _ in rhs])


def place(base, parity, kept, arrived, out, shape):
    count = len(kept)
    rows, columns = shape[2], shape[4]
    block = rows // 2

    def kernel(base_ref, *refs):
        out_ref, wide = refs[-2:]
        first = base_ref[1] == 0
        for index in range(count):
            mine, theirs = refs[index][0].astype(F32), refs[count + index][0].astype(F32)
            wide[:, index, :] = jnp.where(first, mine, theirs)
            wide[:, count + index, :] = jnp.where(first, theirs, mine)
        out_ref[0, 0] = wide[...].astype(BF16)

    pieces = kept + arrived
    specs = [
        pl.BlockSpec((1, block, columns), lambda a, i, base, j=j, step=array.shape[0] - 2: (
            a + step * (1 - base[1]), i, j))
        for array, j in pieces]
    extra = [] if out is None else [out]
    return pl.pallas_call(
        kernel,
        out_shape=jax.ShapeDtypeStruct(shape, BF16),
        grid_spec=pltpu.PrefetchScalarGridSpec(
            num_scalar_prefetch=1,
            grid=(2, rows // block),
            in_specs=specs + [pl.BlockSpec(memory_space=pl.ANY)] * len(extra),
            out_specs=pl.BlockSpec(
                (1, 1, block, 2 * count, columns),
                lambda a, i, base: (base[0] + (a + parity) % 2, a, i, 0, 0)),
            scratch_shapes=[pltpu.VMEM((block, 2 * count, columns), F32)],
        ),
        input_output_aliases={1 + 2 * count: 0} if extra else {},
        compiler_params=pltpu.CompilerParams(vmem_limit_bytes=ROOM),
        cost_estimate=CHEAP,
        name="place",
    )(base, *[array for array, _ in pieces], *extra)


class Order:
    def __init__(self):
        self.before, self.edge = [], []

    def follow(self, value):
        return after(value, *self.before) if self.before else value

    def step(self, value):
        self.before = [value]
        return value

    def phase(self, *values):
        self.before = self.before + list(values)
        self.edge = self.before

    def open(self, value):
        return after(value, *self.edge) if self.edge else value


class Task:
    def __init__(self, order, where, irrep, lhs, rhs):
        self.order, self.where, self.irrep, self.lhs, self.rhs = order, where, irrep, lhs, rhs

    def send(self):
        self.rhs = self.order.follow(self.rhs)
        part = self.order.step(send_product(self.where, self.irrep, self.lhs, self.rhs))
        self.arrived = lax.ppermute(part, "ka", OTHER_CORE)

    def keep(self):
        arrived = self.order.follow(self.arrived)
        away, self.own = keep_product(self.where, self.irrep, self.lhs, self.rhs, arrived)
        self.order.step(away)
        self.other = lax.ppermute(away, "ka", OTHER_Y)

    def finish(self):
        other = self.order.follow(self.other)
        total = (self.own.astype(F32) + other.astype(F32)).astype(BF16)
        self.order.step(total)
        sources, rows, columns = total.shape
        self.parts = [total[s].reshape(2, rows // 2, columns) for s in range(sources)]


def line_local(ladder_amplitudes, ladder_integrals, cycle_amplitudes, cycle_integrals):
    vir, occ, ka = (lax.axis_index(name) for name in ("vir", "occ", "ka"))
    irreps, rows_here, group, depth = cycle_amplitudes.shape
    quarter = group // 4
    columns = cycle_integrals.shape[3]
    at_end = (vir == 0) | (vir == 3)
    where = jnp.bitwise_xor(ka, jnp.array(RELATIVE, jnp.int32))
    order = Order()

    def columns_of(g):
        return order.open(cycle_integrals[g]).reshape(depth, 2 * columns)

    def task(g, rhs, foreign=None):
        lhs = (cycle_amplitudes,) if foreign is None else (cycle_amplitudes, foreign)
        return Task(order, where, g, lhs, rhs)

    def move(value, route):
        return lax.ppermute(order.open(value), "vir", route)

    def scatter(products, g):
        part = order.step(whole_product(g, [(lhs, (order.follow(rhs), index)) for lhs, (rhs, index) in products]))
        total = lax.psum_scatter(part, "ka", scatter_dimension=0, tiled=True)
        return total.reshape(len(products), 2, quarter, 2 * columns)

    def cross(near, far, by_gather=False):
        away = order.open(jnp.where(occ == 0, far, near))
        if by_gather:
            arrived = lax.all_gather(away, "occ", axis=0, tiled=True)
        else:
            arrived = lax.ppermute(away, "occ", OTHER_OCC)
        return jnp.where(occ == 0, near, far), arrived

    def home(mine, back):
        return jnp.where(at_end, back, mine)

    low = jnp.where((occ == 0) | at_end, 0, 2).astype(jnp.int32)
    shape = (8 // 2, rows_here, quarter, 2 * irreps, columns)

    def put(half, j, crossed, out):
        base = jnp.stack([low if half == 0 else 2 - low, occ.astype(jnp.int32)])
        kept = [(pair[0], jj) for pair, jj in crossed]
        arrived = [(pair[1], jj) for pair, jj in crossed]
        return order.step(place(base, j, kept, arrived, out, shape))

    ca = cycle_amplitudes
    b0 = columns_of(0)
    own0 = move(b0, MID_TO_MID)
    a0 = move(ca[0], END_TO_MID)
    b3 = columns_of(3)
    all3 = lax.all_gather(b3, "vir", axis=0, tiled=True)
    b0_in = move(b0, END_TO_MID)
    b1, b2 = columns_of(1), columns_of(2)

    order.phase(own0, a0, b0_in, b1, b2)
    own1 = move(b1, MID_TO_MID)
    a1 = move(ca[1], END_TO_MID)
    f0 = task(0, own0, a0)
    f0.send()
    s0 = scatter([(ca, (b0, 0)), (a0, (b0, 0))], 0)
    f0.keep()
    n0 = scatter([(ca, (b0_in, 0))], 0)
    f0.finish()

    order.phase(own1, a1, all3)
    relay0 = move(b0_in, MID_TO_MID)
    b1_in = move(b1, END_TO_MID)
    f0_back = move(f0.parts[1], MID_TO_END)
    gathered = lax.all_gather(order.open(ladder_amplitudes), "vir", axis=0, tiled=True)
    f1 = task(1, own1, a1)
    f1.send()
    s1 = scatter([(ca, (b1, 0)), (a1, (b1, 0))], 1)
    f1.keep()
    t3 = scatter([(ca, (all3, w)) for w in range(4)], 3)
    f1.finish()

    order.phase(relay0, b1_in, f0_back, s0, n0)
    own2 = move(b2, MID_TO_MID)
    a2 = move(ca[2], END_TO_MID)
    f1_back = move(f1.parts[1], MID_TO_END)
    s0_back = move(s0[1], MID_TO_END)
    g0 = task(0, relay0, a0)
    g0.send()
    n1 = scatter([(ca, (b1_in, 0))], 1)
    g0.keep()
    g0.finish()

    order.phase(own2, a2, f1_back, s0_back, s1, gathered)
    relay1 = move(b1_in, MID_TO_MID)
    b2_in = move(b2, END_TO_MID)
    g0_back = move(g0.parts[1], MID_TO_END)
    s1_back = move(s1[1], MID_TO_END)
    x0a = cross(s0[0], home(f0.parts[0], f0_back), True)
    x1a = cross(s1[0], home(f1.parts[0], f1_back), True)
    f2 = task(2, own2, a2)
    f2.send()
    s2 = scatter([(ca, (b2, 0)), (a2, (b2, 0))], 2)
    f2.keep()
    partial_ladder = order.step(jnp.dot(
        order.follow(gathered), ladder_integrals, preferred_element_type=F32,
    ).astype(BF16))
    ladder_residual = lax.psum_scatter(partial_ladder, ("occ", "ka"), scatter_dimension=0, tiled=True)
    f2.finish()

    order.phase(relay1, b2_in, g0_back, s1_back, n1, t3, x0a[1], x1a[1])
    relay2 = [move(b2_in[:, j * columns:(j + 1) * columns], MID_TO_MID) for j in range(2)]
    f2_back = move(f2.parts[1], MID_TO_END)
    middle = vir // 2
    near3, next3, far3, last3 = (
        lax.dynamic_index_in_dim(t3, w, 0, keepdims=False)
        for w in (vir, vir + 1 - 2 * (vir % 2), 2 - middle, 3 - 3 * middle))
    x3a = cross(near3, far3, True)
    x0b = cross(home(n0[0], s0_back), home(g0.parts[0], g0_back), True)
    g1 = task(1, relay1, a1)
    g1.send()
    n2 = scatter([(ca, (b2_in, 0))], 2)
    g1.keep()
    x3b = cross(next3, last3)
    g1.finish()

    order.phase(relay2[0], f2_back, x3a[1], x0b[1], x3b[1], s2)
    g1_back = move(g1.parts[1], MID_TO_END)
    s2_back = move(s2[1], MID_TO_END)
    x2a = cross(s2[0], home(f2.parts[0], f2_back))
    g2 = [task(2, value, a2) for value in relay2]
    g2[0].send()
    g2[0].keep()
    g2[1].send()
    g2[1].keep()
    order.phase(g1_back, s2_back, x2a[1], n2, ladder_residual)
    x1b = cross(home(n1[0], s1_back), home(g1.parts[0], g1_back))
    out = put(0, 0, [(x0a, 0), (x1a, 0), (x2a, 0), (x3a, 0)], None)
    g2[0].finish()
    back = [move(g2[0].parts[1], MID_TO_END)]
    out = put(0, 1, [(x0a, 1), (x1a, 1), (x2a, 1), (x3a, 1)], out)
    g2[1].finish()
    back.append(move(g2[1].parts[1], MID_TO_END))
    near = home(n2[0], s2_back)
    x2b = [
        cross(near[..., j * columns:(j + 1) * columns], home(g2[j].parts[0], back[j])) for j in range(2)]
    for j in range(2):
        out = put(1, j, [(x0b, j), (x1b, j), (x2b[j], 0), (x3b, j)], out)
    return ladder_residual, out


def regroup(blocks):
    local_rows = blocks.shape[1]
    first_irrep = lax.axis_index("vir") * local_rows
    pieces = []
    for local_index in range(local_rows):
        permuted = jnp.bitwise_xor(first_irrep + local_index, jnp.arange(8, dtype=jnp.int32))
        pieces.append(jnp.take(blocks[:, local_index], permuted, axis=2))
    stacked = jnp.stack(pieces, axis=1)
    return jnp.transpose(stacked, (3, 1, 2, 0, 4))


def any_local(ladder_amplitudes, ladder_integrals, cycle_amplitudes, cycle_integrals):
    partial_ladder = jnp.dot(
        lax.all_gather(ladder_amplitudes, "vir", axis=0, tiled=True),
        ladder_integrals,
        preferred_element_type=F32,
    )
    summed_ladder = lax.psum_scatter(
        partial_ladder.astype(BF16), ("occ", "ka"), scatter_dimension=0, tiled=True
    )
    partial_cycle = jnp.einsum(
        "gaxk,gkny->gaxny",
        cycle_amplitudes,
        lax.all_gather(cycle_integrals, "vir", axis=2, tiled=True),
        preferred_element_type=F32,
    )
    summed_cycle = lax.psum_scatter(
        partial_cycle.astype(BF16), "ka", scatter_dimension=2, tiled=True
    )
    arranged = regroup(summed_cycle)
    cycle_residual = lax.all_to_all(arranged, "occ", split_axis=0, concat_axis=3, tiled=True)
    return (summed_ladder, cycle_residual)


def solution(mesh):
    line = (mesh.shape["vir"], mesh.shape["occ"], mesh.shape["ka"]) == (4, 2, 4)
    placed = (
        P("vir", ("occ", "ka")),
        P(("occ", "ka"), "vir"),
        P("occ", "vir", None, "ka"),
        P("occ", "ka", "vir", None),
    )
    return jax.shard_map(
        line_local if line else any_local,
        mesh=mesh,
        in_specs=placed,
        out_specs=(P(("occ", "ka"), "vir"), P("occ", "vir", "ka", None, None)),
        check_vma=False,
    )
```

time: 1590 us -> 1160 us (0.73)
  waiting for transfers between devices: 1350 us -> 686 us
  Pallas kernels: 0 us -> 263 us
  matrix products: 99.2 us -> 22.3 us
  starting transfers between devices: 9.29 us -> 67.7 us
  local copies, waits for them, and re-layouts: 98.6 us -> 62.9 us
  other arithmetic: 8.37 us -> 33.1 us
    all_gather x2 -> x6, waiting for transfers between devices: 944 us -> 0.06 us  [the longest x4 0.06 us: cross(): arrived = lax.all_gather(away, 'occ', axis=0, tiled=True)]
    ppermute x0 -> x42, waiting for transfers between devices: none -> 684 us  [the longest x23 430 us: move(): return lax.ppermute(order.open(value), 'vir', route)]
    reduce_scatter x2 -> x8, waiting for transfers between devices: 357 us -> 0.51 us  [the longest x7 0.51 us: scatter(): total = lax.psum_scatter(part, 'ka', scatter_dimension=0, tiled=True)]
    pallas_call x0 -> x25, Pallas kernels: none -> 263 us  [the longest x7 102 us: whole_product(): pl.pallas_call(kernel, out_shape=jax.ShapeDtypeStruct((4, count, 2 * rows...]
    dot_general x2 -> x1, matrix products: 99.2 us -> 22.3 us  [line_local(): jnp.dot(order.follow(gathered), ladder_integrals, preferred_element_type=...]
    ppermute x0 -> x42, starting transfers between devices: none -> 66.5 us  [the longest x23 53.1 us: move(): return lax.ppermute(order.open(value), 'vir', route)]
    all_to_all x2 -> x0, local copies, waits for them, and re-layouts: 56.2 us -> none  [local(): lax.all_to_all(arranged, 'occ', split_axis=0, concat_axis=3, tiled=True)]
    all_to_all x1 -> x0, waiting for transfers between devices: 52.5 us -> none  [local(): lax.all_to_all(arranged, 'occ', split_axis=0, concat_axis=3, tiled=True)]
  transfers between devices with their start and end apart: 5 -> 56, of which waited for: 4 -> 25; matrix products, arithmetic and copies ran while one was open for 6% -> 8% of each run, Pallas kernels for 0% -> 22%
where the time goes in v1:
time: 1160 us; the launch traced here: 1150 us
  waiting for transfers between devices  686 us (59%)
  Pallas kernels  263 us (23%)
  starting transfers between devices  67.7 us (6%)
  local copies, waits for them, and re-layouts  62.9 us (5%)
  other arithmetic  33.1 us (3%)
  matrix products  22.3 us (2%)
  between operations  16.5 us (1%)
    ppermute x23, waiting for transfers between devices, move(): return lax.ppermute(order.open(value), 'vir', route)  430 us
    ppermute x7, waiting for transfers between devices, keep(): self.other = lax.ppermute(away, 'ka', OTHER_Y)  238 us
    pallas_call x7, Pallas kernels, whole_product(): pl.pallas_call(kernel, out_shape=jax.ShapeDtypeStruct((4, count, 2 * rows...  102 us
    pallas_call x7, Pallas kernels, keep_product(): pl.pallas_call(kernel, out_shape=(jax.ShapeDtypeStruct((sources, 2 * rows...  71.4 us
    pallas_call x7, Pallas kernels, send_product(): pl.pallas_call(kernel, out_shape=jax.ShapeDtypeStruct((sources, 2, 2 * ro...  62.4 us
    ppermute x23, starting transfers between devices, move(): return lax.ppermute(order.open(value), 'vir', route)  53.1 us
    pallas_call x4, Pallas kernels, place(): pl.pallas_call(kernel, out_shape=jax.ShapeDtypeStruct(shape, BF16), grid_...  27.4 us
    unnamed x74, local copies, waits for them, and re-layouts  25.2 us
  transfers between devices with their start and end apart: 56, of which 25 were waited for; matrix products, arithmetic and copies ran while one was open for 8% of the time, Pallas kernels for 22%

profile of v1, /device:TPU:10, one launch (start us, length us, event | category | flops | bytes accessed | tf_op | source)
XLA Modules:
  0.0 1151.7 jit_solution(10229394691932277734)
XLA Ops:
  8.0 13.3 %fusion = (bf16[1,1280,2,640]{3,2,1,0:T(2,128)(2,1)S(1)}, bf16[1,1280,2,640]{3,2,1,0:T(2,128)(2,1)}, bf16[1,1280,2,640]{3,2,1,0:T(2,128)(2,1)}, bf16[1,1280,2,640]{3,2,1,0:T(2,128)(2,1)}) fusion(bf16[4,1280,2,640]{3,2,1,0:T(2,128)(2,1)} %param.8), kind=kLoop, calls=%fused_computation.42 | loop fusion | bytes 26214400 | tf_op jit(solution)/shard_map/slice | solution.py:243
  23.8 7.3 slice_bitcast_fusion
  36.1 3.7 collective-permute-start.1
  39.8 4.7 copy.11
  47.3 129.3 %collective-permute-done.refs_1_ = bf16[2,640,1280]{2,1,0:T(8,128)(2,1)S(1)} collective-permute-done((bf16[2,640,1280]{2,1,0:T(8,128)(2,1)}, bf16[2,640,1280]{2,1,0:T(8,128)(2,1)S(1)}, u32[]{:S(2)}, u32[]{:S(2)}) %collective-permute-start) | collective-permute-done | bytes 3276832 | tf_op jit(solution)/shard_map/ppermute | solution.py:250
  176.6 139.3 %collective-permute-done.2.refs_1_ = bf16[1280,1280]{1,0:T(8,128)(2,1)} collective-permute-done((bf16[1280,1280]{1,0:T(8,128)(2,1)}, bf16[1280,1280]{1,0:T(8,128)(2,1)}, u32[]{:S(2)}, u32[]{:S(2)}) %collective-permute-start.2) | collective-permute-done | bytes 3276832 | tf_op jit(solution)/shard_map/ppermute | solution.py:250
  315.9 9.3 send_product.7
  325.3 15.1 %whole_product.7 = bf16[4,2,320,1280]{3,2,1,0:T(8,128)(2,1)} custom-call(bf16[4,2,640,1280]{3,2,1,0:T(8,128)(2,1)} %refs_0_.41, bf16[2,640,1280]{2,1,0:T(8,128)(2,1)} %copy-done.2, bf16[1280,1280]{1,0:T(8,128)(2,1)} %bitcast.42.refs_2_.refs_3_, bf16[1280,1280]{1,0:T(8,128)(2,1)} %bitcast.42.refs_2_.refs_3_), custom_call_target="tpu_custom_call" | custom-call | flops 1048576 | bytes 65536 | tf_op jit(solution)/shard_map/whole_product/pallas_call | solution.py:140
  342.1 10.6 keep_product.7
  352.7 8.3 whole_product.8
  361.7 2.5 collective-permute-start.5
  367.1 54.1 %collective-permute-done.4 = bf16[2,320,1280]{2,1,0:T(8,128)(2,1)S(1)} collective-permute-done((bf16[2,320,1280]{2,1,0:T(8,128)(2,1)}, bf16[2,320,1280]{2,1,0:T(8,128)(2,1)S(1)}, u32[]{:S(2)}, u32[]{:S(2)}) %collective-permute-start.4) | collective-permute-done | bytes 1638432 | tf_op jit(solution)/shard_map/ppermute | solution.py:223
  421.2 3.1 add_convert_fusion.4
  424.3 21.7 %collective-permute-done.5.refs_2_ = bf16[1280,1280]{1,0:T(8,128)(2,1)} collective-permute-done((bf16[1280,1280]{1,0:T(8,128)(2,1)}, bf16[1280,1280]{1,0:T(8,128)(2,1)}, u32[]{:S(2)}, u32[]{:S(2)}) %collective-permute-start.5) | collective-permute-done | bytes 3276832 | tf_op jit(solution)/shard_map/ppermute | solution.py:250
  446.0 10.9 collective-permute-done.6.refs_1_
  458.7 9.4 send_product.8
  468.0 15.6 %whole_product.9 = bf16[4,2,320,1280]{3,2,1,0:T(8,128)(2,1)} custom-call(bf16[4,2,640,1280]{3,2,1,0:T(8,128)(2,1)} %refs_0_.41, bf16[2,640,1280]{2,1,0:T(8,128)(2,1)} %copy-done.1, bf16[1280,1280]{1,0:T(8,128)(2,1)} %bitcast.45.refs_2_.refs_3_, bf16[1280,1280]{1,0:T(8,128)(2,1)} %bitcast.45.refs_2_.refs_3_), custom_call_target="tpu_custom_call" | custom-call | flops 1048576 | bytes 65536 | tf_op jit(solution)/shard_map/whole_product/pallas_call | solution.py:140
  483.8 3.5 collective-permute-start.9
  489.9 11.6 %keep_product.8 = (bf16[2,320,1280]{2,1,0:T(8,128)(2,1)}, bf16[2,320,1280]{2,1,0:T(8,128)(2,1)}) custom-call(s32[4]{0:T(128)} %broadcast_xor_fusion.where_ref, bf16[4,2,640,1280]{3,2,1,0:T(8,128)(2,1)} %refs_0_.41, bf16[2,640,1280]{2,1,0:T(8,128)(2,1)} %copy-done.1, bf16[1280,1280]{1,0:T(8,128)(2,1)} %collective-permute-done.5.refs_2_, ...), custom_call_target="tpu_custom_call" | custom-call | flops 1048576 | bytes 65536 | tf_op jit(solution)/shard_map/keep_product/pallas_call | solution.py:97
  503.2 2.7 fusion.7
  505.9 6.4 collective-permute-start.11
  512.4 28.8 %whole_product.10 = bf16[4,4,320,1280]{3,2,1,0:T(8,128)(2,1)} custom-call(bf16[4,2,640,1280]{3,2,1,0:T(8,128)(2,1)} %refs_0_.41, bf16[4,2,640,1280]{3,2,1,0:T(8,128)(2,1)} %refs_0_.41, bf16[4,2,640,1280]{3,2,1,0:T(8,128)(2,1)} %refs_0_.41, bf16[4,2,640,1280]{3,2,1,0:T(8,128)(2,1)} %refs_0_.41, ...), custom_call_target="tpu_custom_call" | custom-call | flops 1048576 | bytes 65536 | tf_op jit(solution)/shard_map/whole_product/pallas_call | solution.py:140
  541.1 32.1 %collective-permute-done.8 = bf16[2,320,1280]{2,1,0:T(8,128)(2,1)} collective-permute-done((bf16[2,320,1280]{2,1,0:T(8,128)(2,1)}, bf16[2,320,1280]{2,1,0:T(8,128)(2,1)}, u32[]{:S(2)}, u32[]{:S(2)}) %collective-permute-start.8) | collective-permute-done | bytes 1638432 | tf_op jit(solution)/shard_map/ppermute | solution.py:223
  573.2 3.6 add_convert_fusion.3
  576.8 72.9 %collective-permute-done.9.refs_2_ = bf16[1280,1280]{1,0:T(8,128)(2,1)S(1)} collective-permute-done((bf16[1280,1280]{1,0:T(8,128)(2,1)}, bf16[1280,1280]{1,0:T(8,128)(2,1)S(1)}, u32[]{:S(2)}, u32[]{:S(2)}) %collective-permute-start.9) | collective-permute-done | bytes 3276832 | tf_op jit(solution)/shard_map/ppermute | solution.py:250
  651.4 9.3 send_product.9
  660.7 8.3 whole_product.11
  672.6 2.8 collective-permute-done.14.refs_3_
  675.4 11.6 %keep_product.9 = (bf16[2,320,1280]{2,1,0:T(8,128)(2,1)}, bf16[2,320,1280]{2,1,0:T(8,128)(2,1)}) custom-call(s32[4]{0:T(128)} %broadcast_xor_fusion.where_ref, bf16[4,2,640,1280]{3,2,1,0:T(8,128)(2,1)} %refs_0_.41, bf16[2,640,1280]{2,1,0:T(8,128)(2,1)} %copy-done.2, bf16[1280,1280]{1,0:T(8,128)(2,1)} %copy-done.4, ...), custom_call_target="tpu_custom_call" | custom-call | flops 1048576 | bytes 65536 | tf_op jit(solution)/shard_map/keep_product/pallas_call | solution.py:97
  696.0 44.9 %collective-permute-done.15 = bf16[2,320,1280]{2,1,0:T(8,128)(2,1)S(1)} collective-permute-done((bf16[2,320,1280]{2,1,0:T(8,128)(2,1)}, bf16[2,320,1280]{2,1,0:T(8,128)(2,1)S(1)}, u32[]{:S(2)}, u32[]{:S(2)}) %collective-permute-start.15) | collective-permute-done | bytes 1638432 | tf_op jit(solution)/shard_map/ppermute | solution.py:223
  746.1 2.5 fusion.6
  750.9 9.6 send_product.10
  760.6 17.4 %whole_product.12 = bf16[4,2,320,1280]{3,2,1,0:T(8,128)(2,1)} custom-call(bf16[4,2,640,1280]{3,2,1,0:T(8,128)(2,1)} %refs_0_.41, bf16[2,640,1280]{2,1,0:T(8,128)(2,1)} %copy-done, bf16[1280,1280]{1,0:T(8,128)(2,1)} %bitcast.62, bf16[1280,1280]{1,0:T(8,128)(2,1)} %bitcast.63), custom_call_target="tpu_custom_call" | custom-call | flops 1048576 | bytes 65536 | tf_op jit(solution)/shard_map/whole_product/pallas_call | solution.py:140
  786.8 12.9 %collective-permute-done.19 = bf16[2,160,1280]{2,1,0:T(8,128)(2,1)S(1)} collective-permute-done((bf16[2,160,1280]{2,1,0:T(8,128)(2,1)S(1)}, bf16[2,160,1280]{2,1,0:T(8,128)(2,1)S(1)}, u32[]{:S(2)}, u32[]{:S(2)}) %collective-permute-start.19) | collective-permute-done | bytes 819232 | tf_op jit(solution)/shard_map/ppermute | solution.py:250
  799.6 2.6 broadcast_select_fusion.14
  802.2 10.7 keep_product.10
  814.3 22.3 %convolution_convert_fusion = bf16[512,2048]{1,0:T(8,128)(2,1)} fusion(bf16[512,6656]{1,0:T(8,128)(2,1)} %all-gather.9.cloned.1.call-done, bf16[6656,2048]{1,0:T(8,128)(2,1)} %param.6), kind=kOutput, calls=%fused_computation.8 | convolution fusion | flops 13959692288 | bytes 36175872 | tf_op jit(solution)/shard_map/dot_general | solution.py:330
  836.6 49.9 %collective-permute-done.22 = bf16[2,320,1280]{2,1,0:T(8,128)(2,1)} collective-permute-done((bf16[2,320,1280]{2,1,0:T(8,128)(2,1)}, bf16[2,320,1280]{2,1,0:T(8,128)(2,1)}, u32[]{:S(2)}, u32[]{:S(2)}) %collective-permute-start.22) | collective-permute-done | bytes 1638432 | tf_op jit(solution)/shard_map/ppermute | solution.py:223
  886.5 3.5 add_convert_fusion.1
  890.6 3.7 select_bitcast_fusion
  894.6 9.8 send_product.11
  904.5 8.6 whole_product.13
  914.8 10.7 keep_product.11
  926.3 4.4 fusion.1
  930.6 3.2 collective-permute-start.26
  935.7 4.2 collective-permute-start.27
  939.9 50.3 %collective-permute-done.25 = bf16[2,320,1280]{2,1,0:T(8,128)(2,1)} collective-permute-done((bf16[2,320,1280]{2,1,0:T(8,128)(2,1)}, bf16[2,320,1280]{2,1,0:T(8,128)(2,1)}, u32[]{:S(2)}, u32[]{:S(2)}) %collective-permute-start.25) | collective-permute-done | bytes 1638432 | tf_op jit(solution)/shard_map/ppermute | solution.py:223
  990.2 3.0 add_convert_fusion
  994.5 7.4 send_product.12
  1002.0 3.4 collective-permute-start.31
  1006.8 8.2 keep_product.12
  1015.0 27.2 %collective-permute-done.31.refs_2_ = bf16[1280,640]{1,0:T(8,128)(2,1)S(1)} collective-permute-done((bf16[1280,640]{1,0:T(8,128)(2,1)}, bf16[1280,640]{1,0:T(8,128)(2,1)S(1)}, u32[]{:S(2)}, u32[]{:S(2)}) %collective-permute-start.31) | collective-permute-done | bytes 1638432 | tf_op jit(solution)/shard_map/ppermute | solution.py:250
  1043.4 7.5 send_product.13
  1057.4 2.5 collective-permute-start.30
  1059.9 8.0 keep_product.13
  1069.4 2.9 collective-permute-done.29
  1072.3 2.5 broadcast_select_fusion.8
  1077.4 6.9 place.4.refs_8_
  1086.9 6.9 place.5.refs_8_
  1098.0 5.4 collective-permute-done.34
  1106.9 8.5 collective-permute-done.36
  1119.1 9.8 collective-permute-done.41.refs_6_
  1129.6 6.8 place.6.refs_8_
  1137.2 6.8 place.7
  (193 shorter events, 88.9 us)
Async XLA Ops:
  8.0 448.9 %all-gather.7.cloned.1.call-start = ((), (), s32[]{:S(2)}) async-start(), calls=%async_computation.8 | async-start | bytes 16384000 | tf_op jit(solution)/shard_map/all_gather | solution.py:282
  23.8 553.0 %reduce-scatter.11.cloned.1.call-start = ((), (), s32[]{:S(2)}) async-start(), calls=%async_computation.11 | async-start | bytes 4096000 | tf_op jit(solution)/shard_map/reduce_scatter | solution.py:254
  31.1 145.5 %collective-permute-start = (bf16[2,640,1280]{2,1,0:T(8,128)(2,1)}, bf16[2,640,1280]{2,1,0:T(8,128)(2,1)S(1)}, u32[]{:S(2)}, u32[]{:S(2)}) collective-permute-start(bf16[2,640,1280]{2,1,0:T(8,128)(2,1)} %get-tuple-element.150), channel_id=1, source_target_pairs={{0,8},{24,16},{1,9},{25,17},{2,10},{26,18},{3,11},{27,19},{4,12},{... | collective-permute-start | bytes 9830408 | tf_op jit(solution)/shard_map/ppermute | solution.py:250
  34.8 281.1 %collective-permute-start.2 = (bf16[1280,1280]{1,0:T(8,128)(2,1)}, bf16[1280,1280]{1,0:T(8,128)(2,1)}, u32[]{:S(2)}, u32[]{:S(2)}) collective-permute-start(bf16[1280,1280]{1,0:T(8,128)(2,1)} %bitcast.42.refs_2_.refs_3_), channel_id=1, source_target_pairs={{0,8},{24,16},{1,9},{25,17},{2,10},{26,18},{3,11},{27,19},{4,12},{... | collective-permute-start | bytes 9830408 | tf_op jit(solution)/shard_map/ppermute | solution.py:250
  36.1 279.8 %collective-permute-start.1 = (bf16[1280,1280]{1,0:T(8,128)(2,1)}, bf16[1280,1280]{1,0:T(8,128)(2,1)}, u32[]{:S(2)}, u32[]{:S(2)}) collective-permute-start(bf16[1280,1280]{1,0:T(8,128)(2,1)} %bitcast.42.refs_2_.refs_3_), channel_id=1, source_target_pairs={{8,16},{16,8},{9,17},{17,9},{10,18},{18,10},{11,19},{19,11},{12,20... | collective-permute-start | bytes 9830408 | tf_op jit(solution)/shard_map/ppermute | solution.py:250
  176.6 139.3 %copy-start.2 = (bf16[2,640,1280]{2,1,0:T(8,128)(2,1)}, bf16[2,640,1280]{2,1,0:T(8,128)(2,1)S(1)}, u32[]{:S(2)}) copy-start(bf16[2,640,1280]{2,1,0:T(8,128)(2,1)S(1)} %collective-permute-done.refs_1_) | copy-start | bytes 9830404
  325.2 15.1 %collective-permute-start.3 = (bf16[2,2,320,1280]{3,2,1,0:T(8,128)(2,1)}, bf16[2,2,320,1280]{3,2,1,0:T(8,128)(2,1)S(1)}, u32[]{:S(2)}, u32[]{:S(2)}) collective-permute-start(bf16[2,2,320,1280]{3,2,1,0:T(8,128)(2,1)} %send_product.7), channel_id=1, source_target_pairs={{0,1},{1,0},{2,3},{3,2},{4,5},{5,4},{6,7},{7,6},{8,9},{9,8},{10,11... | collective-permute-start | bytes 9830408 | tf_op jit(solution)/shard_map/ppermute | solution.py:217
  361.1 215.7 %reduce-scatter.9.cloned.1.call-start = ((), (), s32[]{:S(2)}) async-start(), calls=%async_computation.10 | async-start | bytes 8192000 | tf_op jit(solution)/shard_map/reduce_scatter | solution.py:254
  361.7 384.4 %all-gather.9.cloned.1.call-start = ((), (), s32[]{:S(2)}) async-start(), calls=%async_computation.9 | async-start | bytes 8519680 | tf_op jit(solution)/shard_map/all_gather | solution.py:300
  361.7 84.3 %collective-permute-start.5 = (bf16[1280,1280]{1,0:T(8,128)(2,1)}, bf16[1280,1280]{1,0:T(8,128)(2,1)}, u32[]{:S(2)}, u32[]{:S(2)}) collective-permute-start(bf16[1280,1280]{1,0:T(8,128)(2,1)} %bitcast.45.refs_2_.refs_3_), channel_id=1, source_target_pairs={{8,16},{16,8},{9,17},{17,9},{10,18},{18,10},{11,19},{19,11},{12,20... | collective-permute-start | bytes 9830408 | tf_op jit(solution)/shard_map/ppermute | solution.py:250
  364.2 92.8 %collective-permute-start.6 = (bf16[2,640,1280]{2,1,0:T(8,128)(2,1)}, bf16[2,640,1280]{2,1,0:T(8,128)(2,1)S(1)}, u32[]{:S(2)}, u32[]{:S(2)}) collective-permute-start(bf16[2,640,1280]{2,1,0:T(8,128)(2,1)} %get-tuple-element.83), channel_id=1, source_target_pairs={{0,8},{24,16},{1,9},{25,17},{2,10},{26,18},{3,11},{27,19},{4,12},{... | collective-permute-start | bytes 9830408 | tf_op jit(solution)/shard_map/ppermute | solution.py:250
  365.5 55.7 %collective-permute-start.4 = (bf16[2,320,1280]{2,1,0:T(8,128)(2,1)}, bf16[2,320,1280]{2,1,0:T(8,128)(2,1)S(1)}, u32[]{:S(2)}, u32[]{:S(2)}) collective-permute-start(bf16[2,320,1280]{2,1,0:T(8,128)(2,1)} %get-tuple-element.79), channel_id=1, source_target_pairs={{0,2},{2,0},{1,3},{3,1},{4,6},{6,4},{5,7},{7,5},{8,10},{10,8},{9,1... | collective-permute-start | bytes 4915208 | tf_op jit(solution)/shard_map/ppermute | solution.py:223
  457.0 289.1 %reduce-scatter.13.cloned.1.call-start = ((), (), s32[]{:S(2)}) async-start(), calls=%async_computation.12 | async-start | bytes 8192000 | tf_op jit(solution)/shard_map/reduce_scatter | solution.py:254
  483.6 406.4 %reduce-scatter.17.cloned.1.call-start = ((), (), s32[]{:S(2)}) async-start(), calls=%async_computation.14 | async-start | bytes 4096000 | tf_op jit(solution)/shard_map/reduce_scatter | solution.py:254
  483.7 6.3 collective-permute-start.7
  483.8 165.9 %collective-permute-start.9 = (bf16[1280,1280]{1,0:T(8,128)(2,1)}, bf16[1280,1280]{1,0:T(8,128)(2,1)S(1)}, u32[]{:S(2)}, u32[]{:S(2)}) collective-permute-start(bf16[1280,1280]{1,0:T(8,128)(2,1)} %collective-permute-done.2.refs_1_), channel_id=1, source_target_pairs={{8,16},{16,8},{9,17},{17,9},{10,18},{18,10},{11,19},{19,11},{12,20... | collective-permute-start | bytes 9830408 | tf_op jit(solution)/shard_map/ppermute | solution.py:250
  487.3 162.5 %collective-permute-start.10 = (bf16[1280,1280]{1,0:T(8,128)(2,1)}, bf16[1280,1280]{1,0:T(8,128)(2,1)}, u32[]{:S(2)}, u32[]{:S(2)}) collective-permute-start(bf16[1280,1280]{1,0:T(8,128)(2,1)} %bitcast.45.refs_2_.refs_3_), channel_id=1, source_target_pairs={{0,8},{24,16},{1,9},{25,17},{2,10},{26,18},{3,11},{27,19},{4,12},{... | collective-permute-start | bytes 9830408 | tf_op jit(solution)/shard_map/ppermute | solution.py:250
  501.5 71.7 %collective-permute-start.8 = (bf16[2,320,1280]{2,1,0:T(8,128)(2,1)}, bf16[2,320,1280]{2,1,0:T(8,128)(2,1)}, u32[]{:S(2)}, u32[]{:S(2)}) collective-permute-start(bf16[2,320,1280]{2,1,0:T(8,128)(2,1)} %get-tuple-element.89), channel_id=1, source_target_pairs={{0,2},{2,0},{1,3},{3,1},{4,6},{6,4},{5,7},{7,5},{8,10},{10,8},{9,1... | collective-permute-start | bytes 4915208 | tf_op jit(solution)/shard_map/ppermute | solution.py:223
  505.9 70.9 %collective-permute-start.11 = (bf16[2,160,1280]{2,1,0:T(8,128)(2,1)}, bf16[2,160,1280]{2,1,0:T(8,128)(2,1)}, u32[]{:S(2)}, u32[]{:S(2)}) collective-permute-start(bf16[2,160,1280]{2,1,0:T(8,128)(2,1)} %bitcast.3), channel_id=1, source_target_pairs={{8,0},{16,24},{9,1},{17,25},{10,2},{18,26},{11,3},{19,27},{12,4},{... | collective-permute-start | bytes 2457608 | tf_op jit(solution)/shard_map/ppermute | solution.py:250
  669.1 220.9 %all-gather.11.cloned.1.call-start = ((), (), s32[]{:S(2)}) async-start(), calls=%async_computation.16 | async-start | bytes 2457600 | tf_op jit(solution)/shard_map/all_gather | solution.py:260
  669.1 6.3 collective-permute-start.14
  669.3 75.3 %collective-permute-start.12 = (bf16[2,640,1280]{2,1,0:T(8,128)(2,1)}, bf16[2,640,1280]{2,1,0:T(8,128)(2,1)S(1)}, u32[]{:S(2)}, u32[]{:S(2)}) collective-permute-start(bf16[2,640,1280]{2,1,0:T(8,128)(2,1)} %get-tuple-element.95), channel_id=1, source_target_pairs={{0,8},{24,16},{1,9},{25,17},{2,10},{26,18},{3,11},{27,19},{4,12},{... | collective-permute-start | bytes 9830408 | tf_op jit(solution)/shard_map/ppermute | solution.py:250
  670.6 75.4 %collective-permute-start.13 = (bf16[1280,1280]{1,0:T(8,128)(2,1)}, bf16[1280,1280]{1,0:T(8,128)(2,1)}, u32[]{:S(2)}, u32[]{:S(2)}) collective-permute-start(bf16[1280,1280]{1,0:T(8,128)(2,1)} %bitcast.61), channel_id=1, source_target_pairs={{8,16},{16,8},{9,17},{17,9},{10,18},{18,10},{11,19},{19,11},{12,20... | collective-permute-start | bytes 9830408 | tf_op jit(solution)/shard_map/ppermute | solution.py:250
  687.0 53.9 %collective-permute-start.15 = (bf16[2,320,1280]{2,1,0:T(8,128)(2,1)}, bf16[2,320,1280]{2,1,0:T(8,128)(2,1)S(1)}, u32[]{:S(2)}, u32[]{:S(2)}) collective-permute-start(bf16[2,320,1280]{2,1,0:T(8,128)(2,1)} %get-tuple-element.101), channel_id=1, source_target_pairs={{0,2},{2,0},{1,3},{3,1},{4,6},{6,4},{5,7},{7,5},{8,10},{10,8},{9,1... | collective-permute-start | bytes 4915208 | tf_op jit(solution)/shard_map/ppermute | solution.py:223
  690.0 50.9 %copy-start.23 = (bf16[2,320,1280]{2,1,0:T(8,128)(2,1)S(1)}, bf16[2,320,1280]{2,1,0:T(8,128)(2,1)}, u32[]{:S(2)}) copy-start(bf16[2,320,1280]{2,1,0:T(8,128)(2,1)} %get-tuple-element.100) | copy-start | bytes 4915204
  690.0 52.4 %collective-permute-start.17 = (bf16[2,160,1280]{2,1,0:T(8,128)(2,1)S(1)}, bf16[2,160,1280]{2,1,0:T(8,128)(2,1)S(1)}, u32[]{:S(2)}, u32[]{:S(2)}) collective-permute-start(bf16[2,160,1280]{2,1,0:T(8,128)(2,1)S(1)} %bitcast.83), channel_id=1, source_target_pairs={{8,0},{16,24},{9,1},{17,25},{10,2},{18,26},{11,3},{19,27},{12,4},{... | collective-permute-start | bytes 2457608 | tf_op jit(solution)/shard_map/ppermute | solution.py:250
  693.3 49.1 %collective-permute-start.16 = (bf16[2,160,1280]{2,1,0:T(8,128)(2,1)S(1)}, bf16[2,160,1280]{2,1,0:T(8,128)(2,1)S(1)}, u32[]{:S(2)}, u32[]{:S(2)}) collective-permute-start(bf16[2,160,1280]{2,1,0:T(8,128)(2,1)S(1)} %bitcast.84), channel_id=1, source_target_pairs={{8,0},{16,24},{9,1},{17,25},{10,2},{18,26},{11,3},{19,27},{12,4},{... | collective-permute-start | bytes 2457608 | tf_op jit(solution)/shard_map/ppermute | solution.py:250
  746.1 143.9 %all-gather.13.cloned.1.call-start = ((), (), s32[]{:S(2)}) async-start(), calls=%async_computation.17 | async-start | bytes 2457600 | tf_op jit(solution)/shard_map/all_gather | solution.py:260
  750.0 140.6 %reduce-scatter.19.cloned.1.call-start = ((), (), s32[]{:S(2)}) async-start(), calls=%async_computation.15 | async-start | bytes 16384000 | tf_op jit(solution)/shard_map/reduce_scatter | solution.py:254
  750.7 242.5 %reduce-scatter.21.cloned.1.call-start = ((), (), s32[]{:S(2)}) async-start(), calls=%async_computation.20 | async-start | bytes 8192000 | tf_op jit(solution)/shard_map/reduce_scatter | solution.py:254
  778.0 215.2 %all-gather.17.cloned.1.call-start = ((), (), s32[]{:S(2)}) async-start(), calls=%async_computation.19 | async-start | bytes 2457600 | tf_op jit(solution)/shard_map/all_gather | solution.py:260
  778.1 24.1 %collective-permute-start.18 = (bf16[2,2,320,1280]{3,2,1,0:T(8,128)(2,1)}, bf16[2,2,320,1280]{3,2,1,0:T(8,128)(2,1)}, u32[]{:S(2)}, u32[]{:S(2)}) collective-permute-start(bf16[2,2,320,1280]{3,2,1,0:T(8,128)(2,1)} %send_product.10), channel_id=1, source_target_pairs={{0,1},{1,0},{2,3},{3,2},{4,5},{5,4},{6,7},{7,6},{8,9},{9,8},{10,11... | collective-permute-start | bytes 9830408 | tf_op jit(solution)/shard_map/ppermute | solution.py:217
  779.8 19.8 %collective-permute-start.19 = (bf16[2,160,1280]{2,1,0:T(8,128)(2,1)S(1)}, bf16[2,160,1280]{2,1,0:T(8,128)(2,1)S(1)}, u32[]{:S(2)}, u32[]{:S(2)}) collective-permute-start(bf16[2,160,1280]{2,1,0:T(8,128)(2,1)S(1)} %bitcast.85), channel_id=1, source_target_pairs={{8,0},{16,24},{9,1},{17,25},{10,2},{18,26},{11,3},{19,27},{12,4},{... | collective-permute-start | bytes 2457608 | tf_op jit(solution)/shard_map/ppermute | solution.py:250
  781.2 108.8 %collective-permute-start.20 = (bf16[2,160,1280]{2,1,0:T(8,128)(2,1)}, bf16[2,160,1280]{2,1,0:T(8,128)(2,1)}, u32[]{:S(2)}, u32[]{:S(2)}) collective-permute-start(bf16[2,160,1280]{2,1,0:T(8,128)(2,1)} %bitcast.81), channel_id=1, source_target_pairs={{8,0},{16,24},{9,1},{17,25},{10,2},{18,26},{11,3},{19,27},{12,4},{... | collective-permute-start | bytes 2457608 | tf_op jit(solution)/shard_map/ppermute | solution.py:250
  783.4 106.6 %collective-permute-start.21 = (bf16[1280,1280]{1,0:T(8,128)(2,1)}, bf16[1280,1280]{1,0:T(8,128)(2,1)}, u32[]{:S(2)}, u32[]{:S(2)}) collective-permute-start(bf16[1280,1280]{1,0:T(8,128)(2,1)} %collective-permute-done.10.refs_1_), channel_id=1, source_target_pairs={{8,16},{16,8},{9,17},{17,9},{10,18},{18,10},{11,19},{19,11},{12,20... | collective-permute-start | bytes 9830408 | tf_op jit(solution)/shard_map/ppermute | solution.py:250
  785.5 104.6 %collective-permute-start.23 = (bf16[1280,1280]{1,0:T(8,128)(2,1)S(1)}, bf16[1280,1280]{1,0:T(8,128)(2,1)}, u32[]{:S(2)}, u32[]{:S(2)}) collective-permute-start(bf16[1280,1280]{1,0:T(8,128)(2,1)S(1)} %bitcast.64), channel_id=1, source_target_pairs={{0,8},{24,16},{1,9},{25,17},{2,10},{26,18},{3,11},{27,19},{4,12},{... | collective-permute-start | bytes 9830408 | tf_op jit(solution)/shard_map/ppermute | solution.py:250
  812.9 73.6 %collective-permute-start.22 = (bf16[2,320,1280]{2,1,0:T(8,128)(2,1)}, bf16[2,320,1280]{2,1,0:T(8,128)(2,1)}, u32[]{:S(2)}, u32[]{:S(2)}) collective-permute-start(bf16[2,320,1280]{2,1,0:T(8,128)(2,1)} %get-tuple-element.108), channel_id=1, source_target_pairs={{0,2},{2,0},{1,3},{3,1},{4,6},{6,4},{5,7},{7,5},{8,10},{10,8},{9,1... | collective-permute-start | bytes 4915208 | tf_op jit(solution)/shard_map/ppermute | solution.py:223
  890.6 102.7 %all-gather.15.cloned.1.call-start = ((), (), s32[]{:S(2)}) async-start(), calls=%async_computation.18 | async-start | bytes 2457600 | tf_op jit(solution)/shard_map/all_gather | solution.py:260
  894.4 201.6 %reduce-scatter.15.cloned.1.call-start = ((), (), s32[]{:S(2)}) async-start(), calls=%async_computation.13 | async-start | bytes 2359296 | tf_op jit(solution)/shard_map/reduce_scatter | solution.py:333
  904.4 8.6 collective-permute-start.24
  904.5 191.6 %reduce-scatter.23.cloned.1.call-start = ((), (), s32[]{:S(2)}) async-start(), calls=%async_computation.21 | async-start | bytes 4096000 | tf_op jit(solution)/shard_map/reduce_scatter | solution.py:254
  925.4 64.7 %collective-permute-start.25 = (bf16[2,320,1280]{2,1,0:T(8,128)(2,1)}, bf16[2,320,1280]{2,1,0:T(8,128)(2,1)}, u32[]{:S(2)}, u32[]{:S(2)}) collective-permute-start(bf16[2,320,1280]{2,1,0:T(8,128)(2,1)} %get-tuple-element.122), channel_id=1, source_target_pairs={{0,2},{2,0},{1,3},{3,1},{4,6},{6,4},{5,7},{7,5},{8,10},{10,8},{9,1... | collective-permute-start | bytes 4915208 | tf_op jit(solution)/shard_map/ppermute | solution.py:223
  930.6 59.5 %copy-start.22 = (bf16[2,320,1280]{2,1,0:T(8,128)(2,1)S(1)}, bf16[2,320,1280]{2,1,0:T(8,128)(2,1)}, u32[]{:S(2)}) copy-start(bf16[2,320,1280]{2,1,0:T(8,128)(2,1)} %get-tuple-element.121) | copy-start | bytes 4915204
  930.6 62.6 %collective-permute-start.26 = (bf16[1280,640]{1,0:T(8,128)(2,1)}, bf16[1280,640]{1,0:T(8,128)(2,1)S(1)}, u32[]{:S(2)}, u32[]{:S(2)}) collective-permute-start(bf16[1280,640]{1,0:T(8,128)(2,1)} %get-tuple-element.124), channel_id=1, source_target_pairs={{8,16},{16,8},{9,17},{17,9},{10,18},{18,10},{11,19},{19,11},{12,20... | collective-permute-start | bytes 4915208 | tf_op jit(solution)/shard_map/ppermute | solution.py:250
  935.1 58.1 %collective-permute-start.28 = (bf16[2,160,1280]{2,1,0:T(8,128)(2,1)S(1)}, bf16[2,160,1280]{2,1,0:T(8,128)(2,1)S(1)}, u32[]{:S(2)}, u32[]{:S(2)}) collective-permute-start(bf16[2,160,1280]{2,1,0:T(8,128)(2,1)S(1)} %copy-done.24), channel_id=1, source_target_pairs={{0,4},{4,0},{1,5},{5,1},{2,6},{6,2},{3,7},{7,3},{8,12},{12,8},{9,1... | collective-permute-start | bytes 2457608 | tf_op jit(solution)/shard_map/ppermute | solution.py:262
  935.7 57.5 %collective-permute-start.27 = (bf16[2,160,1280]{2,1,0:T(8,128)(2,1)}, bf16[2,160,1280]{2,1,0:T(8,128)(2,1)}, u32[]{:S(2)}, u32[]{:S(2)}) collective-permute-start(bf16[2,160,1280]{2,1,0:T(8,128)(2,1)} %bitcast.23), channel_id=1, source_target_pairs={{8,0},{16,24},{9,1},{17,25},{10,2},{18,26},{11,3},{19,27},{12,4},{... | collective-permute-start | bytes 2457608 | tf_op jit(solution)/shard_map/ppermute | solution.py:250
  993.2 8.7 copy-start.17
  1001.9 3.7 collective-permute-start.32
  1002.0 40.2 %collective-permute-start.31 = (bf16[1280,640]{1,0:T(8,128)(2,1)}, bf16[1280,640]{1,0:T(8,128)(2,1)S(1)}, u32[]{:S(2)}, u32[]{:S(2)}) collective-permute-start(bf16[1280,640]{1,0:T(8,128)(2,1)} %get-tuple-element.131), channel_id=1, source_target_pairs={{8,16},{16,8},{9,17},{17,9},{10,18},{18,10},{11,19},{19,11},{12,20... | collective-permute-start | bytes 4915208 | tf_op jit(solution)/shard_map/ppermute | solution.py:250
  1050.9 8.9 collective-permute-start.33
  1051.9 20.4 %collective-permute-start.29 = (bf16[2,160,1280]{2,1,0:T(8,128)(2,1)}, bf16[2,160,1280]{2,1,0:T(8,128)(2,1)}, u32[]{:S(2)}, u32[]{:S(2)}) collective-permute-start(bf16[2,160,1280]{2,1,0:T(8,128)(2,1)} %bitcast.22), channel_id=1, source_target_pairs={{8,0},{16,24},{9,1},{17,25},{10,2},{18,26},{11,3},{19,27},{12,4},{... | collective-permute-start | bytes 2457608 | tf_op jit(solution)/shard_map/ppermute | solution.py:250
  1055.7 20.7 %collective-permute-start.35 = (bf16[2,160,1280]{2,1,0:T(8,128)(2,1)}, bf16[2,160,1280]{2,1,0:T(8,128)(2,1)S(1)}, u32[]{:S(2)}, u32[]{:S(2)}) collective-permute-start(bf16[2,160,1280]{2,1,0:T(8,128)(2,1)} %get-tuple-element.139), channel_id=1, source_target_pairs={{0,4},{4,0},{1,5},{5,1},{2,6},{6,2},{3,7},{7,3},{8,12},{12,8},{9,1... | collective-permute-start | bytes 2457608 | tf_op jit(solution)/shard_map/ppermute | solution.py:262
  1056.3 29.7 %collective-permute-start.39 = (bf16[2,320,640]{2,1,0:T(8,128)(2,1)}, bf16[2,320,640]{2,1,0:T(8,128)(2,1)S(1)}, u32[]{:S(2)}, u32[]{:S(2)}) collective-permute-start(bf16[2,320,640]{2,1,0:T(8,128)(2,1)} %get-tuple-element.134), channel_id=1, source_target_pairs={{0,2},{2,0},{1,3},{3,1},{4,6},{6,4},{5,7},{7,5},{8,10},{10,8},{9,1... | collective-permute-start | bytes 2457608 | tf_op jit(solution)/shard_map/ppermute | solution.py:223
  1057.4 38.6 %collective-permute-start.30 = (bf16[2,160,1280]{2,1,0:T(8,128)(2,1)S(1)}, bf16[2,160,1280]{2,1,0:T(8,128)(2,1)}, u32[]{:S(2)}, u32[]{:S(2)}) collective-permute-start(bf16[2,160,1280]{2,1,0:T(8,128)(2,1)S(1)} %bitcast.82), channel_id=1, source_target_pairs={{8,0},{16,24},{9,1},{17,25},{10,2},{18,26},{11,3},{19,27},{12,4},{... | collective-permute-start | bytes 2457608 | tf_op jit(solution)/shard_map/ppermute | solution.py:250
  1067.9 35.5 %collective-permute-start.34 = (bf16[2,320,640]{2,1,0:T(8,128)(2,1)}, bf16[2,320,640]{2,1,0:T(8,128)(2,1)}, u32[]{:S(2)}, u32[]{:S(2)}) collective-permute-start(bf16[2,320,640]{2,1,0:T(8,128)(2,1)} %get-tuple-element.138), channel_id=1, source_target_pairs={{0,2},{2,0},{1,3},{3,1},{4,6},{6,4},{5,7},{7,5},{8,10},{10,8},{9,1... | collective-permute-start | bytes 2457608 | tf_op jit(solution)/shard_map/ppermute | solution.py:223
  1084.2 9.5 copy-start.25
  1093.8 9.6 copy-start.26
  1096.0 10.1 copy-start.28
  1096.0 23.0 %collective-permute-start.37 = (bf16[2,160,1280]{2,1,0:T(8,128)(2,1)}, bf16[2,160,1280]{2,1,0:T(8,128)(2,1)S(1)}, u32[]{:S(2)}, u32[]{:S(2)}) collective-permute-start(bf16[2,160,1280]{2,1,0:T(8,128)(2,1)} %get-tuple-element.142), channel_id=1, source_target_pairs={{0,4},{4,0},{1,5},{5,1},{2,6},{6,2},{3,7},{7,3},{8,12},{12,8},{9,1... | collective-permute-start | bytes 2457608 | tf_op jit(solution)/shard_map/ppermute | solution.py:262
  1096.6 10.2 collective-permute-start.40
  1104.8 10.6 collective-permute-start.36
  1116.4 12.4 %collective-permute-start.41 = (bf16[2,160,640]{2,1,0:T(8,128)(2,1)S(1)}, bf16[2,160,640]{2,1,0:T(8,128)(2,1)S(1)}, u32[]{:S(2)}, u32[]{:S(2)}) collective-permute-start(bf16[2,160,640]{2,1,0:T(8,128)(2,1)S(1)} %get-tuple-element.147), channel_id=1, source_target_pairs={{0,4},{4,0},{1,5},{5,1},{2,6},{6,2},{3,7},{7,3},{8,12},{12,8},{9,1... | collective-permute-start | bytes 1228808 | tf_op jit(solution)/shard_map/ppermute | solution.py:262
  1117.9 18.5 %collective-permute-start.38 = (bf16[2,160,640]{2,1,0:T(8,128)(2,1)S(1)}, bf16[2,160,640]{2,1,0:T(8,128)(2,1)S(1)}, u32[]{:S(2)}, u32[]{:S(2)}) collective-permute-start(bf16[2,160,640]{2,1,0:T(8,128)(2,1)S(1)} %get-tuple-element.143), channel_id=1, source_target_pairs={{0,4},{4,0},{1,5},{5,1},{2,6},{6,2},{3,7},{7,3},{8,12},{12,8},{9,1... | collective-permute-start | bytes 1228808 | tf_op jit(solution)/shard_map/ppermute | solution.py:262
  1119.0 9.8 copy-start.18
  (27 other events, 91.0 us)
Sparse Core Ops, SparseCore 0:
  23.9 380.5 all-gather.6
  457.1 191.1 all-gather.8
  746.2 26.1 all-gather.10
  773.8 27.9 all-gather.12
  890.7 27.0 all-gather.16
  919.2 37.1 all-gather.14
Sparse Core Ops, SparseCore 1:
  361.2 55.6 reduce-scatter.10
  419.3 59.9 reduce-scatter.8
  483.7 92.5 reduce-scatter.12
  669.2 53.7 reduce-scatter.16
  753.9 136.5 reduce-scatter.18
  893.1 89.6 reduce-scatter.20
  986.8 41.3 reduce-scatter.14
  1030.5 47.7 reduce-scatter.22

commit v2 on v1

v2 whole, which is shorter than its diff:
```python
import jax
import jax.numpy as jnp
from jax import lax
from jax.experimental import pallas as pl
from jax.experimental.pallas import tpu as pltpu
from jax.sharding import PartitionSpec as P

F32, BF16 = jnp.float32, jnp.bfloat16

END_TO_MID = [(0, 1), (3, 2)]
MID_TO_MID = [(1, 2), (2, 1)]
MID_TO_END = [(1, 0), (2, 3)]
RELATIVE = (0, 2, 1, 3)
OTHER_CORE = [(0, 1), (1, 0), (2, 3), (3, 2)]
OTHER_Y = [(0, 2), (2, 0), (1, 3), (3, 1)]
OTHER_OCC = [(0, 1), (1, 0)]
NEIGHBOUR = [(0, 1), (1, 0), (2, 3), (3, 2)]
ROOM = 60 << 20
CHEAP = pl.CostEstimate(flops=1 << 20, bytes_accessed=1 << 16, transcendentals=0)


def after(value, *earlier):
    return lax.optimization_barrier((value, *earlier))[0]


def dot_rows(lhs, rhs):
    return jnp.dot(lhs.reshape(-1, lhs.shape[-1]), rhs, preferred_element_type=F32)


def lhs_specs(irrep, sources, rows, depth, first):
    specs = []
    for place in range(sources):
        def quarter(s, r, where, place=place):
            moment = r if sources == 1 else jnp.where(s == place, r, 1 if place == 0 else 0)
            return where[first + moment]
        if place == 0:
            specs.append(pl.BlockSpec((1, 2, rows, depth), lambda s, r, where, q=quarter: (irrep, 0, q(s, r, where), 0)))
        else:
            specs.append(pl.BlockSpec((2, rows, depth), lambda s, r, where, q=quarter: (0, q(s, r, where), 0)))
    return specs


def product(lhs_refs, rhs_ref, use):
    source = pl.program_id(0)
    for place, lhs in enumerate(lhs_refs):
        @pl.when(source == place)
        def _():
            use(place, dot_rows(lhs[...], rhs_ref[...]))


def quarter_specs(sources, rows, columns):
    def at(place):
        return lambda s, r, where: (r if sources == 1 else jnp.where(s == place, r, 1 - place), 0, 0)
    return [pl.BlockSpec((1, rows, columns), at(place)) for place in range(sources)]


def send_product(where, irrep, lhs, rhs):
    sources, depth, columns = len(lhs), rhs.shape[0], rhs.shape[1]
    rows = lhs[0].shape[2] // 4

    def kernel(where_ref, *refs):
        outs = refs[sources + 1:]

        def use(place, value):
            outs[place][0] = value.astype(BF16)
        product(refs[:sources], refs[sources], use)

    return pl.pallas_call(
        kernel,
        out_shape=[jax.ShapeDtypeStruct((2, 2 * rows, columns), BF16)] * sources,
        grid_spec=pltpu.PrefetchScalarGridSpec(
            num_scalar_prefetch=1,
            grid=(sources, 2),
            in_specs=lhs_specs(irrep, sources, rows, depth, 2)
            + [pl.BlockSpec((depth, columns), lambda s, r, where: (0, 0))],
            out_specs=quarter_specs(sources, 2 * rows, columns),
        ),
        compiler_params=pltpu.CompilerParams(vmem_limit_bytes=ROOM),
        cost_estimate=CHEAP,
        name="send_product",
    )(where, *lhs, rhs)


def keep_product(where, irrep, lhs, rhs, arrived):
    sources, depth, columns = len(lhs), rhs.shape[0], rhs.shape[1]
    rows = lhs[0].shape[2] // 4

    def kernel(where_ref, *refs):
        arrived_refs, (away, own) = refs[sources + 1:-2], refs[-2:]
        quarter = pl.program_id(1)

        def use(place, value):
            total = (value + arrived_refs[place][0].astype(F32)).astype(BF16)

            @pl.when(quarter == 0)
            def _():
                own[0] = total

            @pl.when(quarter == 1)
            def _():
                away[0] = total
        product(refs[:sources], refs[sources], use)

    return pl.pallas_call(
        kernel,
        out_shape=(jax.ShapeDtypeStruct((sources, 2 * rows, columns), BF16),) * 2,
        grid_spec=pltpu.PrefetchScalarGridSpec(
            num_scalar_prefetch=1,
            grid=(sources, 2),
            in_specs=lhs_specs(irrep, sources, rows, depth, 0)
            + [pl.BlockSpec((depth, columns), lambda s, r, where: (0, 0))]
            + quarter_specs(sources, 2 * rows, columns),
            out_specs=(pl.BlockSpec((1, 2 * rows, columns), lambda s, r, where: (s, 0, 0)),) * 2,
        ),
        compiler_params=pltpu.CompilerParams(vmem_limit_bytes=ROOM),
        cost_estimate=CHEAP,
        name="keep_product",
    )(where, *lhs, rhs, *arrived)


def place(base, parity, kept, arrived, out, shape):
    count = len(kept)
    rows, columns = shape[2], shape[4]
    block = rows // 2

    def kernel(base_ref, *refs):
        out_ref, wide = refs[-2:]
        first = base_ref[1] == 0
        for index in range(count):
            mine, theirs = refs[index][0].astype(F32), refs[count + index][0].astype(F32)
            wide[:, index, :] = jnp.where(first, mine, theirs)
            wide[:, count + index, :] = jnp.where(first, theirs, mine)
        out_ref[0, 0] = wide[...].astype(BF16)

    pieces = kept + arrived
    specs = [
        pl.BlockSpec((1, block, columns), lambda a, i, base, j=j, step=array.shape[0] - 2: (
            a + step * (1 - base[1]), i, j))
        for array, j in pieces]
    extra = [] if out is None else [out]
    return pl.pallas_call(
        kernel,
        out_shape=jax.ShapeDtypeStruct(shape, BF16),
        grid_spec=pltpu.PrefetchScalarGridSpec(
            num_scalar_prefetch=1,
            grid=(2, rows // block),
            in_specs=specs + [pl.BlockSpec(memory_space=pl.ANY)] * len(extra),
            out_specs=pl.BlockSpec(
                (1, 1, block, 2 * count, columns),
                lambda a, i, base: (base[0] + (a + parity) % 2, a, i, 0, 0)),
            scratch_shapes=[pltpu.VMEM((block, 2 * count, columns), F32)],
        ),
        input_output_aliases={1 + 2 * count: 0} if extra else {},
        compiler_params=pltpu.CompilerParams(vmem_limit_bytes=ROOM),
        cost_estimate=CHEAP,
        name="place",
    )(base, *[array for array, _ in pieces], *extra)


class Order:
    def __init__(self):
        self.before, self.edge = [], []

    def follow(self, value):
        return after(value, *self.before) if self.before else value

    def step(self, value):
        self.before = [value]
        return value

    def phase(self, *values):
        self.before = self.before + list(values)
        self.edge = self.before

    def open(self, value):
        return after(value, *self.edge) if self.edge else value


class Task:
    def __init__(self, order, where, irrep, lhs, rhs):
        self.order, self.where, self.irrep, self.lhs, self.rhs = order, where, irrep, lhs, rhs

    def send(self):
        self.rhs = self.order.follow(self.rhs)
        parts = send_product(self.where, self.irrep, self.lhs, self.rhs)
        self.order.step(parts[-1])
        self.arrived = [lax.ppermute(part, "ka", OTHER_CORE) for part in parts]

    def keep(self):
        arrived = [self.order.follow(part) for part in self.arrived]
        self.away, self.own = keep_product(self.where, self.irrep, self.lhs, self.rhs, arrived)
        self.order.step(self.away)

    def swap(self):
        self.other = lax.ppermute(self.order.open(self.away), "ka", OTHER_Y)

    def finish(self):
        other = self.order.follow(self.other)
        total = (self.own.astype(F32) + other.astype(F32)).astype(BF16)
        self.order.step(total)
        sources, rows, columns = total.shape
        self.parts = [total[s].reshape(2, rows // 2, columns) for s in range(sources)]


def line_local(ladder_amplitudes, ladder_integrals, cycle_amplitudes, cycle_integrals):
    vir, occ, ka = (lax.axis_index(name) for name in ("vir", "occ", "ka"))
    irreps, rows_here, group, depth = cycle_amplitudes.shape
    quarter = group // 4
    columns = cycle_integrals.shape[3]
    at_end = (vir == 0) | (vir == 3)
    where = jnp.bitwise_xor(ka, jnp.array(RELATIVE, jnp.int32))
    order = Order()

    def columns_of(g):
        return order.open(cycle_integrals)[g].reshape(depth, 2 * columns)

    def task(g, rhs, foreign=None):
        lhs = (cycle_amplitudes,) if foreign is None else (cycle_amplitudes, foreign)
        return Task(order, where, g, lhs, rhs)

    def move(value, route):
        return lax.ppermute(order.open(value), "vir", route)

    def cross(near, far):
        away = order.open(jnp.where(occ == 0, far, near))
        return jnp.where(occ == 0, near, far), lax.ppermute(away, "occ", OTHER_OCC)

    def home(mine, back):
        return jnp.where(at_end, back, mine)

    low = jnp.where((occ == 0) | at_end, 0, 2).astype(jnp.int32)
    shape = (8 // 2, rows_here, quarter, 2 * irreps, columns)

    def put(half, j, crossed, out):
        base = jnp.stack([low if half == 0 else 2 - low, occ.astype(jnp.int32)])
        kept = [(pair[0], jj) for pair, jj in crossed]
        arrived = [(pair[1], jj) for pair, jj in crossed]
        return order.step(place(base, j, kept, arrived, out, shape))

    def rows_of(g):
        return order.open(cycle_amplitudes)[g]

    def each(tasks, step):
        for one in tasks:
            getattr(one, step)()

    def straight(near, near_in, done, one=slice(None)):
        own_rows, foreign = (order.open(value) for value in done.parts)
        first = lax.ppermute(jnp.where(occ == 0, own_rows, foreign), ("vir", "occ"), [(2, 3), (4, 5), (3, 1), (5, 7)])
        second = lax.ppermute(foreign, ("vir", "occ"), [(2, 1), (4, 7)])
        kept = jnp.where(occ == 0, near[..., one], jnp.where(at_end, first, own_rows))
        arrived = jnp.where(occ == 0, near_in[..., one], jnp.where(at_end, second, first))
        return kept, arrived

    def over(near):
        return lax.ppermute(order.open(near), "occ", [(1, 0)])

    gathered = lax.all_gather(ladder_amplitudes, "vir", axis=0, tiled=True)
    b0 = columns_of(0)
    order.phase(b0)
    own0 = move(b0, MID_TO_MID)
    a0 = move(rows_of(0), END_TO_MID)
    b3 = columns_of(3)
    s0, s3 = task(0, b0), task(3, b3)
    s0.send()
    s0.keep()
    s3.send()
    s3.keep()

    order.phase(own0, a0)
    own3 = move(b3, MID_TO_MID)
    swap3 = move(b3, NEIGHBOUR)
    each((s0, s3), "swap")
    b1 = columns_of(1)
    f0, s1 = task(0, own0, a0), task(1, b1)
    each((f0, s1), "send")
    each((f0, s1), "keep")
    each((s0, s3), "finish")

    order.phase(own3, swap3, gathered)
    relay3 = move(swap3, MID_TO_MID)
    swap0 = move(b0, NEIGHBOUR)
    each((f0, s1), "swap")
    b2 = columns_of(2)
    n3, s2 = task(3, swap3), task(2, b2)
    each((n3, s2), "send")
    each((n3, s2), "keep")
    each((f0, s1), "finish")

    order.phase(relay3, swap0)
    relay0 = move(swap0, MID_TO_MID)
    a1 = move(rows_of(1), END_TO_MID)
    on3 = move(own3, MID_TO_END)
    f0_back = move(f0.parts[1], MID_TO_END)
    each((n3, s2), "swap")
    n0 = task(0, swap0)
    n0.send()
    n0.keep()
    partial_ladder = order.step(jnp.dot(
        order.follow(gathered), ladder_integrals, preferred_element_type=F32,
    ).astype(BF16))
    ladder_residual = lax.psum_scatter(partial_ladder, ("occ", "ka"), scatter_dimension=0, tiled=True)
    each((n3, s2), "finish")

    order.phase(relay0, a1, on3, f0_back)
    own1 = move(b1, MID_TO_MID)
    a2 = move(rows_of(2), END_TO_MID)
    on_relay3 = move(relay3, MID_TO_END)
    n0.swap()
    x0a = cross(s0.parts[0], home(f0.parts[0], f0_back))
    g0, f3 = task(0, relay0, a0), task(3, jnp.where(at_end, on3, own3))
    each((g0, f3), "send")
    each((g0, f3), "keep")
    n0.finish()

    order.phase(own1, a2, on_relay3, x0a[1])
    own2 = move(b2, MID_TO_MID)
    swap1 = move(b1, NEIGHBOUR)
    each((g0, f3), "swap")
    f1, g3 = task(1, own1, a1), task(3, jnp.where(at_end, on_relay3, relay3))
    each((f1, g3), "send")
    each((f1, g3), "keep")
    each((g0, f3), "finish")

    order.phase(own2, swap1)
    relay1 = move(swap1, MID_TO_MID)
    swap2 = move(b2, NEIGHBOUR)
    g0_back = move(g0.parts[1], MID_TO_END)
    x3a = cross(s3.parts[0], f3.parts[0])
    each((f1, g3), "swap")
    f2, n1 = task(2, own2, a2), task(1, swap1)
    each((f2, n1), "send")
    each((f2, n1), "keep")
    each((f1, g3), "finish")

    order.phase(relay1, swap2, g0_back, x3a[1], ladder_residual)
    relay2 = [move(swap2[:, :columns], MID_TO_MID)]
    f1_back = move(f1.parts[1], MID_TO_END)
    x0b = cross(n0.parts[0], home(g0.parts[0], g0_back))
    each((f2, n1), "swap")
    g1, n2 = task(1, relay1, a1), task(2, swap2)
    each((g1, n2), "send")
    each((g1, n2), "keep")
    each((f2, n1), "finish")

    order.phase(relay2[0], f1_back, x0b[1])
    relay2.append(move(swap2[:, columns:], MID_TO_MID))
    f2_back = move(f2.parts[1], MID_TO_END)
    x1a = cross(s1.parts[0], home(f1.parts[0], f1_back))
    x3b = cross(n3.parts[0], g3.parts[0])
    each((g1, n2), "swap")
    g2 = [task(2, relay2[0], a2)]
    g2[0].send()
    g2[0].keep()
    each((g1, n2), "finish")

    order.phase(relay2[1], f2_back, x1a[1], x3b[1])
    near1_in, near2_in = over(n1.parts[0]), over(n2.parts[0])
    x2a = cross(s2.parts[0], home(f2.parts[0], f2_back))
    g2[0].swap()
    g2.append(task(2, relay2[1], a2))
    g2[1].send()
    g2[1].keep()
    x1b = straight(n1.parts[0], near1_in, g1)
    g2[0].finish()

    order.phase(x2a[1], near2_in, *x1b)
    g2[1].swap()
    out = None
    for j in range(2):
        out = put(0, j, [(x0a, j), (x1a, j), (x2a, j), (x3a, j)], out)
    x2b = [straight(n2.parts[0], near2_in, g2[0], slice(0, columns))]
    g2[1].finish()

    order.phase(*x2b[0])
    x2b.append(straight(n2.parts[0], near2_in, g2[1], slice(columns, 2 * columns)))
    for j in range(2):
        out = put(1, j, [(x0b, j), (x1b, j), (x2b[j], 0), (x3b, j)], out)
    return ladder_residual, out


def regroup(blocks):
    local_rows = blocks.shape[1]
    first_irrep = lax.axis_index("vir") * local_rows
    pieces = []
    for local_index in range(local_rows):
        permuted = jnp.bitwise_xor(first_irrep + local_index, jnp.arange(8, dtype=jnp.int32))
        pieces.append(jnp.take(blocks[:, local_index], permuted, axis=2))
    stacked = jnp.stack(pieces, axis=1)
    return jnp.transpose(stacked, (3, 1, 2, 0, 4))


def any_local(ladder_amplitudes, ladder_integrals, cycle_amplitudes, cycle_integrals):
    partial_ladder = jnp.dot(
        lax.all_gather(ladder_amplitudes, "vir", axis=0, tiled=True),
        ladder_integrals,
        preferred_element_type=F32,
    )
    summed_ladder = lax.psum_scatter(
        partial_ladder.astype(BF16), ("occ", "ka"), scatter_dimension=0, tiled=True
    )
    partial_cycle = jnp.einsum(
        "gaxk,gkny->gaxny",
        cycle_amplitudes,
        lax.all_gather(cycle_integrals, "vir", axis=2, tiled=True),
        preferred_element_type=F32,
    )
    summed_cycle = lax.psum_scatter(
        partial_cycle.astype(BF16), "ka", scatter_dimension=2, tiled=True
    )
    arranged = regroup(summed_cycle)
    cycle_residual = lax.all_to_all(arranged, "occ", split_axis=0, concat_axis=3, tiled=True)
    return (summed_ladder, cycle_residual)


def solution(mesh):
    line = (mesh.shape["vir"], mesh.shape["occ"], mesh.shape["ka"]) == (4, 2, 4)
    placed = (
        P("vir", ("occ", "ka")),
        P(("occ", "ka"), "vir"),
        P("occ", "vir", None, "ka"),
        P("occ", "ka", "vir", None),
    )
    return jax.shard_map(
        line_local if line else any_local,
        mesh=mesh,
        in_specs=placed,
        out_specs=(P(("occ", "ka"), "vir"), P("occ", "vir", "ka", None, None)),
        check_vma=False,
    )
```

time: 1160 us -> 1020 us (0.88)
  waiting for transfers between devices: 686 us -> 459 us
  starting transfers between devices: 67.7 us -> 112 us
  Pallas kernels: 263 us -> 295 us
  other arithmetic: 33.1 us -> 63 us
  local copies, waits for them, and re-layouts: 62.9 us -> 48.7 us
    ppermute x23 -> x22, waiting for transfers between devices: 430 us -> 281 us  [move(): return lax.ppermute(order.open(value), 'vir', route)]
    ppermute x19 -> x55, waiting for transfers between devices: 254 us -> 177 us  [the longest x17 147 us: swap(): self.other = lax.ppermute(self.order.open(self.away), 'ka', OTHER_Y)]
    pallas_call x7 -> x17, Pallas kernels: 71.4 us -> 141 us  [keep_product(): pl.pallas_call(kernel, out_shape=(jax.ShapeDtypeStruct((sources, 2 * rows...]
    ppermute x19 -> x55, starting transfers between devices: 13.3 us -> 52.8 us  [the longest x17 17.1 us: swap(): self.other = lax.ppermute(self.order.open(self.away), 'ka', OTHER_Y)]
    pallas_call x14 -> x17, Pallas kernels: 165 us -> 126 us  [send_product(): pl.pallas_call(kernel, out_shape=[jax.ShapeDtypeStruct((2, 2 * rows, colu...]
    select_n x4 -> x12, other arithmetic: 6.43 us -> 27.1 us  [the longest x5 11 us: cross(): jnp.where(occ == 0, near, far)]
    convert_element_type x7 -> x15, other arithmetic: 17.5 us -> 30.8 us  [finish(): total = (self.own.astype(F32) + other.astype(F32)).astype(BF16)]
    unnamed x74 -> x84, local copies, waits for them, and re-layouts: 25.2 us -> 17.5 us
  transfers between devices with their start and end apart: 56 -> 79, of which waited for: 25 -> 24; matrix products, arithmetic and copies ran while one was open for 8% -> 11% of each run, Pallas kernels for 22% -> 24%
where the time goes in v2:
time: 1020 us; the launch traced here: 1010 us
  waiting for transfers between devices  459 us (45%)
  Pallas kernels  295 us (29%)
  starting transfers between devices  112 us (11%)
  other arithmetic  63 us (6%)
  local copies, waits for them, and re-layouts  48.7 us (5%)
  matrix products  22.2 us (2%)
  between operations  15.1 us (1%)
    ppermute x22, waiting for transfers between devices, move(): return lax.ppermute(order.open(value), 'vir', route)  281 us
    ppermute x17, waiting for transfers between devices, swap(): self.other = lax.ppermute(self.order.open(self.away), 'ka', OTHER_Y)  147 us
    pallas_call x17, Pallas kernels, keep_product(): pl.pallas_call(kernel, out_shape=(jax.ShapeDtypeStruct((sources, 2 * rows...  141 us
    pallas_call x17, Pallas kernels, send_product(): pl.pallas_call(kernel, out_shape=[jax.ShapeDtypeStruct((2, 2 * rows, colu...  126 us
    ppermute x22, starting transfers between devices, move(): return lax.ppermute(order.open(value), 'vir', route)  58.7 us
    convert_element_type x15, other arithmetic, finish(): total = (self.own.astype(F32) + other.astype(F32)).astype(BF16)  30.8 us
    pallas_call x4, Pallas kernels, place(): pl.pallas_call(kernel, out_shape=jax.ShapeDtypeStruct(shape, BF16), grid_...  27.3 us
    dot_general x1, matrix products, line_local(): jnp.dot(order.follow(gathered), ladder_integrals, preferred_element_type=...  22.2 us
  transfers between devices with their start and end apart: 79, of which 24 were waited for; matrix products, arithmetic and copies ran while one was open for 11% of the time, Pallas kernels for 24%

profile of v2, /device:TPU:10, one launch (start us, length us, event | category | flops | bytes accessed | tf_op | source)
XLA Modules:
  0.0 1014.1 jit_solution(12324579629517750866)
XLA Ops:
  16.2 6.7 send_product.17
  32.4 7.0 keep_product.17
  39.4 6.3 send_product.18
  49.6 7.0 keep_product.18
  56.6 135.5 %collective-permute-done.2.refs_2_ = bf16[1280,1280]{1,0:T(8,128)(2,1)} collective-permute-done((bf16[1280,1280]{1,0:T(8,128)(2,1)}, bf16[1280,1280]{1,0:T(8,128)(2,1)}, u32[]{:S(2)}, u32[]{:S(2)}) %collective-permute-start.2) | collective-permute-done | bytes 3276832 | tf_op jit(solution)/shard_map/ppermute | solution.py:222
  193.7 9.5 send_product.19
  211.6 6.3 send_product.20
  220.2 10.9 %keep_product.19 = (bf16[2,320,1280]{2,1,0:T(8,128)(2,1)}, bf16[2,320,1280]{2,1,0:T(8,128)(2,1)}) custom-call(s32[4]{0:T(128)} %broadcast_xor_fusion.where_ref, bf16[4,2,640,1280]{3,2,1,0:T(8,128)(2,1)} %refs_0_.67, bf16[2,640,1280]{2,1,0:T(8,128)(2,1)} %copy-done.2, bf16[1280,1280]{1,0:T(8,128)(2,1)} %collective-permute-done.2.refs_2_, ...), custom_call_target="tpu_custom_call" | custom-call | flops 1048576 | bytes 65536 | tf_op jit(solution)/shard_map/keep_product/pallas_call | solution.py:104
  232.3 7.1 keep_product.20
  240.5 15.8 %collective-permute-done.4 = bf16[1,320,1280]{2,1,0:T(8,128)(2,1)S(1)} collective-permute-done((bf16[1,320,1280]{2,1,0:T(8,128)(2,1)}, bf16[1,320,1280]{2,1,0:T(8,128)(2,1)S(1)}, u32[]{:S(2)}, u32[]{:S(2)}) %collective-permute-start.4) | collective-permute-done | bytes 819232 | tf_op jit(solution)/shard_map/ppermute | solution.py:195
  257.4 21.4 %collective-permute-done.9 = bf16[1280,1280]{1,0:T(8,128)(2,1)} collective-permute-done((bf16[1280,1280]{1,0:T(8,128)(2,1)}, bf16[1280,1280]{1,0:T(8,128)(2,1)}, u32[]{:S(2)}, u32[]{:S(2)}) %collective-permute-start.9) | collective-permute-done | bytes 3276832 | tf_op jit(solution)/shard_map/ppermute | solution.py:222
  283.2 6.3 send_product.21
  293.8 6.3 send_product.22
  303.3 7.0 keep_product.21
  310.3 7.1 keep_product.22
  317.4 22.1 %collective-permute-done.13 = bf16[2,320,1280]{2,1,0:T(8,128)(2,1)S(1)} collective-permute-done((bf16[2,320,1280]{2,1,0:T(8,128)(2,1)}, bf16[2,320,1280]{2,1,0:T(8,128)(2,1)S(1)}, u32[]{:S(2)}, u32[]{:S(2)}) %collective-permute-start.13) | collective-permute-done | bytes 1638432 | tf_op jit(solution)/shard_map/ppermute | solution.py:195
  342.6 13.5 %collective-permute-done.12 = bf16[1,320,1280]{2,1,0:T(8,128)(2,1)S(1)} collective-permute-done((bf16[1,320,1280]{2,1,0:T(8,128)(2,1)}, bf16[1,320,1280]{2,1,0:T(8,128)(2,1)S(1)}, u32[]{:S(2)}, u32[]{:S(2)}) %collective-permute-start.12) | collective-permute-done | bytes 819232 | tf_op jit(solution)/shard_map/ppermute | solution.py:195
  357.2 6.3 send_product.23
  375.5 6.7 collective-permute-start.22
  382.3 7.0 keep_product.23
  389.2 22.2 %convolution_convert_fusion = bf16[512,2048]{1,0:T(8,128)(2,1)} fusion(bf16[512,6656]{1,0:T(8,128)(2,1)} %all-gather.2.cloned.1.call-done, bf16[6656,2048]{1,0:T(8,128)(2,1)} %param.6), kind=kOutput, calls=%fused_computation.10 | convolution fusion | flops 13959692288 | bytes 36175872 | tf_op jit(solution)/shard_map/dot_general | solution.py:299
  417.7 50.2 %collective-permute-done.23 = bf16[2,160,1280]{2,1,0:T(8,128)(2,1)S(1)} collective-permute-done((bf16[2,160,1280]{2,1,0:T(8,128)(2,1)}, bf16[2,160,1280]{2,1,0:T(8,128)(2,1)S(1)}, u32[]{:S(2)}, u32[]{:S(2)}) %collective-permute-start.23) | collective-permute-done | bytes 819232 | tf_op jit(solution)/shard_map/ppermute | solution.py:222
  468.8 6.0 collective-permute-start.30
  474.8 9.5 send_product.24
  492.8 49.3 %collective-permute-done.30 = bf16[1280,1280]{1,0:T(8,128)(2,1)} collective-permute-done((bf16[1280,1280]{1,0:T(8,128)(2,1)}, bf16[1280,1280]{1,0:T(8,128)(2,1)}, u32[]{:S(2)}, u32[]{:S(2)}) %collective-permute-start.30) | collective-permute-done | bytes 3276832 | tf_op jit(solution)/shard_map/ppermute | solution.py:222
  542.1 6.3 broadcast_select_fusion
  548.4 6.3 send_product.25
  559.6 10.9 %keep_product.24 = (bf16[2,320,1280]{2,1,0:T(8,128)(2,1)}, bf16[2,320,1280]{2,1,0:T(8,128)(2,1)}) custom-call(s32[4]{0:T(128)} %broadcast_xor_fusion.where_ref, bf16[4,2,640,1280]{3,2,1,0:T(8,128)(2,1)} %refs_0_.67, bf16[2,640,1280]{2,1,0:T(8,128)(2,1)} %copy-done.2, bf16[1280,1280]{1,0:T(8,128)(2,1)} %collective-permute-done.20.refs_2_, ...), custom_call_target="tpu_custom_call" | custom-call | flops 1048576 | bytes 65536 | tf_op jit(solution)/shard_map/keep_product/pallas_call | solution.py:104
  570.5 6.9 keep_product.25
  580.0 9.9 send_product.26
  593.7 6.3 send_product.27
  602.4 10.9 %keep_product.26 = (bf16[2,320,1280]{2,1,0:T(8,128)(2,1)}, bf16[2,320,1280]{2,1,0:T(8,128)(2,1)}) custom-call(s32[4]{0:T(128)} %broadcast_xor_fusion.where_ref, bf16[4,2,640,1280]{3,2,1,0:T(8,128)(2,1)} %refs_0_.67, bf16[2,640,1280]{2,1,0:T(8,128)(2,1)} %copy-done.1, bf16[1280,1280]{1,0:T(8,128)(2,1)} %collective-permute-done.28.refs_2_, ...), custom_call_target="tpu_custom_call" | custom-call | flops 1048576 | bytes 65536 | tf_op jit(solution)/shard_map/keep_product/pallas_call | solution.py:104
  613.3 7.0 keep_product.27
  620.3 19.0 %collective-permute-done.32 = bf16[2,320,1280]{2,1,0:T(8,128)(2,1)} collective-permute-done((bf16[2,320,1280]{2,1,0:T(8,128)(2,1)}, bf16[2,320,1280]{2,1,0:T(8,128)(2,1)}, u32[]{:S(2)}, u32[]{:S(2)}) %collective-permute-start.32) | collective-permute-done | bytes 1638432 | tf_op jit(solution)/shard_map/ppermute | solution.py:195
  642.9 13.2 %collective-permute-done.36 = bf16[1,320,1280]{2,1,0:T(8,128)(2,1)S(1)} collective-permute-done((bf16[1,320,1280]{2,1,0:T(8,128)(2,1)}, bf16[1,320,1280]{2,1,0:T(8,128)(2,1)S(1)}, u32[]{:S(2)}, u32[]{:S(2)}) %collective-permute-start.36) | collective-permute-done | bytes 819232 | tf_op jit(solution)/shard_map/ppermute | solution.py:195
  657.6 7.8 collective-permute-done.37.refs_2_
  667.1 9.8 send_product.28
  679.8 6.3 send_product.29
  691.9 11.1 %keep_product.28 = (bf16[2,320,1280]{2,1,0:T(8,128)(2,1)}, bf16[2,320,1280]{2,1,0:T(8,128)(2,1)}) custom-call(s32[4]{0:T(128)} %broadcast_xor_fusion.where_ref, bf16[4,2,640,1280]{3,2,1,0:T(8,128)(2,1)} %refs_0_.67, bf16[2,640,1280]{2,1,0:T(8,128)(2,1)} %copy-done, bf16[1280,1280]{1,0:T(8,128)(2,1)} %copy-done.4, ...), custom_call_target="tpu_custom_call" | custom-call | flops 1048576 | bytes 65536 | tf_op jit(solution)/shard_map/keep_product/pallas_call | solution.py:104
  703.1 4.9 collective-permute-start.39
  708.0 7.0 keep_product.29
  715.0 18.5 %collective-permute-done.44 = bf16[2,320,1280]{2,1,0:T(8,128)(2,1)} collective-permute-done((bf16[2,320,1280]{2,1,0:T(8,128)(2,1)}, bf16[2,320,1280]{2,1,0:T(8,128)(2,1)}, u32[]{:S(2)}, u32[]{:S(2)}) %collective-permute-start.44) | collective-permute-done | bytes 1638432 | tf_op jit(solution)/shard_map/ppermute | solution.py:195
  738.6 12.0 %collective-permute-done.43 = bf16[1,320,1280]{2,1,0:T(8,128)(2,1)} collective-permute-done((bf16[1,320,1280]{2,1,0:T(8,128)(2,1)}, bf16[1,320,1280]{2,1,0:T(8,128)(2,1)}, u32[]{:S(2)}, u32[]{:S(2)}) %collective-permute-start.43) | collective-permute-done | bytes 819232 | tf_op jit(solution)/shard_map/ppermute | solution.py:195
  753.4 14.4 %collective-permute-done.39 = bf16[2,160,1280]{2,1,0:T(8,128)(2,1)} collective-permute-done((bf16[2,160,1280]{2,1,0:T(8,128)(2,1)}, bf16[2,160,1280]{2,1,0:T(8,128)(2,1)}, u32[]{:S(2)}, u32[]{:S(2)}) %collective-permute-start.39) | collective-permute-done | bytes 819232 | tf_op jit(solution)/shard_map/ppermute | solution.py:222
  767.8 9.6 send_product.30
  778.1 6.4 send_product.31
  800.1 11.0 %keep_product.30 = (bf16[2,320,1280]{2,1,0:T(8,128)(2,1)}, bf16[2,320,1280]{2,1,0:T(8,128)(2,1)}) custom-call(s32[4]{0:T(128)} %broadcast_xor_fusion.where_ref, bf16[4,2,640,1280]{3,2,1,0:T(8,128)(2,1)} %refs_0_.67, bf16[2,640,1280]{2,1,0:T(8,128)(2,1)} %copy-done.1, bf16[1280,1280]{1,0:T(8,128)(2,1)} %collective-permute-done.45.refs_2_, ...), custom_call_target="tpu_custom_call" | custom-call | flops 1048576 | bytes 65536 | tf_op jit(solution)/shard_map/keep_product/pallas_call | solution.py:104
  812.7 7.0 keep_product.31
  822.1 11.3 %collective-permute-done.48 = bf16[1,320,1280]{2,1,0:T(8,128)(2,1)} collective-permute-done((bf16[1,320,1280]{2,1,0:T(8,128)(2,1)}, bf16[1,320,1280]{2,1,0:T(8,128)(2,1)}, u32[]{:S(2)}, u32[]{:S(2)}) %collective-permute-start.48) | collective-permute-done | bytes 819232 | tf_op jit(solution)/shard_map/ppermute | solution.py:195
  837.4 7.3 send_product.32
  858.5 8.1 keep_product.32
  866.6 8.2 collective-permute-done.56
  878.7 12.4 %collective-permute-done.59 = bf16[1,320,1280]{2,1,0:T(8,128)(2,1)} collective-permute-done((bf16[1,320,1280]{2,1,0:T(8,128)(2,1)}, bf16[1,320,1280]{2,1,0:T(8,128)(2,1)}, u32[]{:S(2)}, u32[]{:S(2)}) %collective-permute-start.59) | collective-permute-done | bytes 819232 | tf_op jit(solution)/shard_map/ppermute | solution.py:195
  895.7 7.3 send_product.33
  904.2 4.4 collective-permute-start.70
  917.5 4.7 collective-permute-start.69
  922.2 8.1 keep_product.33
  939.5 4.3 collective-permute-done.69
  943.8 17.2 %collective-permute-done.68.refs_6_ = bf16[2,160,1280]{2,1,0:T(8,128)(2,1)} collective-permute-done((bf16[2,160,1280]{2,1,0:T(8,128)(2,1)}, bf16[2,160,1280]{2,1,0:T(8,128)(2,1)}, u32[]{:S(2)}, u32[]{:S(2)}) %collective-permute-start.68) | collective-permute-done | bytes 819232 | tf_op jit(solution)/shard_map/ppermute | solution.py:226
  967.5 6.8 place.4.refs_8_
  974.3 6.8 place.5.refs_8_
  987.0 6.8 place.6.refs_8_
  993.8 4.2 collective-permute-done.75
  1000.1 6.8 place.7
  (271 shorter events, 198.9 us)
Async XLA Ops:
  7.2 273.2 %all-gather.2.cloned.1.call-start = ((), (), s32[]{:S(2)}) async-start(), calls=%async_computation.1 | async-start | bytes 8519680 | tf_op jit(solution)/shard_map/all_gather | solution.py:258
  7.9 745.5 %reduce-scatter.2.cloned.1.call-start = ((), (), s32[]{:S(2)}) async-start(), calls=%async_computation.2 | async-start | bytes 2359296 | tf_op jit(solution)/shard_map/reduce_scatter | solution.py:302
  12.2 179.8 %collective-permute-start.2 = (bf16[1280,1280]{1,0:T(8,128)(2,1)}, bf16[1280,1280]{1,0:T(8,128)(2,1)}, u32[]{:S(2)}, u32[]{:S(2)}) collective-permute-start(bf16[1280,1280]{1,0:T(8,128)(2,1)} %bitcast.32.refs_1_), channel_id=1, source_target_pairs={{8,16},{16,8},{9,17},{17,9},{10,18},{18,10},{11,19},{19,11},{12,20... | collective-permute-start | bytes 9830408 | tf_op jit(solution)/shard_map/ppermute | solution.py:222
  26.9 165.2 %collective-permute-start.3 = (bf16[2,640,1280]{2,1,0:T(8,128)(2,1)}, bf16[2,640,1280]{2,1,0:T(8,128)(2,1)S(1)}, u32[]{:S(2)}, u32[]{:S(2)}) collective-permute-start(bf16[2,640,1280]{2,1,0:T(8,128)(2,1)} %slice_bitcast_fusion.2), channel_id=1, source_target_pairs={{0,8},{24,16},{1,9},{25,17},{2,10},{26,18},{3,11},{27,19},{4,12},{... | collective-permute-start | bytes 9830408 | tf_op jit(solution)/shard_map/ppermute | solution.py:222
  203.3 14.9 %collective-permute-start.7 = (bf16[2,320,1280]{2,1,0:T(8,128)(2,1)}, bf16[2,320,1280]{2,1,0:T(8,128)(2,1)}, u32[]{:S(2)}, u32[]{:S(2)}) collective-permute-start(bf16[2,320,1280]{2,1,0:T(8,128)(2,1)} %get-tuple-element.181), channel_id=1, source_target_pairs={{0,1},{1,0},{2,3},{3,2},{4,5},{5,4},{6,7},{7,6},{8,9},{9,8},{10,11... | collective-permute-start | bytes 4915208 | tf_op jit(solution)/shard_map/ppermute | solution.py:187
  203.3 75.5 %collective-permute-start.9 = (bf16[1280,1280]{1,0:T(8,128)(2,1)}, bf16[1280,1280]{1,0:T(8,128)(2,1)}, u32[]{:S(2)}, u32[]{:S(2)}) collective-permute-start(bf16[1280,1280]{1,0:T(8,128)(2,1)} %bitcast.57), channel_id=1, source_target_pairs={{8,16},{16,8},{9,17},{17,9},{10,18},{18,10},{11,19},{19,11},{12,20... | collective-permute-start | bytes 9830408 | tf_op jit(solution)/shard_map/ppermute | solution.py:222
  207.0 73.4 %collective-permute-start.10 = (bf16[1280,1280]{1,0:T(8,128)(2,1)}, bf16[1280,1280]{1,0:T(8,128)(2,1)}, u32[]{:S(2)}, u32[]{:S(2)}) collective-permute-start(bf16[1280,1280]{1,0:T(8,128)(2,1)} %bitcast.58), channel_id=1, source_target_pairs={{0,8},{8,0},{16,24},{24,16},{1,9},{9,1},{17,25},{25,17},{2,10},{10... | collective-permute-start | bytes 9830408 | tf_op jit(solution)/shard_map/ppermute | solution.py:222
  217.9 13.2 %collective-permute-start.6 = (bf16[2,320,1280]{2,1,0:T(8,128)(2,1)}, bf16[2,320,1280]{2,1,0:T(8,128)(2,1)S(1)}, u32[]{:S(2)}, u32[]{:S(2)}) collective-permute-start(bf16[2,320,1280]{2,1,0:T(8,128)(2,1)} %send_product.20), channel_id=1, source_target_pairs={{0,1},{1,0},{2,3},{3,2},{4,5},{5,4},{6,7},{7,6},{8,9},{9,8},{10,11... | collective-permute-start | bytes 4915208 | tf_op jit(solution)/shard_map/ppermute | solution.py:187
  218.1 21.3 %collective-permute-start.5 = (bf16[1,320,1280]{2,1,0:T(8,128)(2,1)}, bf16[1,320,1280]{2,1,0:T(8,128)(2,1)S(1)}, u32[]{:S(2)}, u32[]{:S(2)}) collective-permute-start(bf16[1,320,1280]{2,1,0:T(8,128)(2,1)} %get-tuple-element.176), channel_id=1, source_target_pairs={{0,2},{2,0},{1,3},{3,1},{4,6},{6,4},{5,7},{7,5},{8,10},{10,8},{9,1... | collective-permute-start | bytes 2457608 | tf_op jit(solution)/shard_map/ppermute | solution.py:195
  219.7 36.6 %collective-permute-start.4 = (bf16[1,320,1280]{2,1,0:T(8,128)(2,1)}, bf16[1,320,1280]{2,1,0:T(8,128)(2,1)S(1)}, u32[]{:S(2)}, u32[]{:S(2)}) collective-permute-start(bf16[1,320,1280]{2,1,0:T(8,128)(2,1)} %get-tuple-element.174), channel_id=1, source_target_pairs={{0,2},{2,0},{1,3},{3,1},{4,6},{6,4},{5,7},{7,5},{8,10},{10,8},{9,1... | collective-permute-start | bytes 2457608 | tf_op jit(solution)/shard_map/ppermute | solution.py:195
  280.4 76.8 %collective-permute-start.11 = (bf16[1280,1280]{1,0:T(8,128)(2,1)}, bf16[1280,1280]{1,0:T(8,128)(2,1)}, u32[]{:S(2)}, u32[]{:S(2)}) collective-permute-start(bf16[1280,1280]{1,0:T(8,128)(2,1)} %bitcast.32.refs_1_), channel_id=1, source_target_pairs={{0,8},{8,0},{16,24},{24,16},{1,9},{9,1},{17,25},{25,17},{2,10},{10... | collective-permute-start | bytes 9830408 | tf_op jit(solution)/shard_map/ppermute | solution.py:222
  280.7 76.5 %collective-permute-start.16 = (bf16[1280,1280]{1,0:T(8,128)(2,1)}, bf16[1280,1280]{1,0:T(8,128)(2,1)}, u32[]{:S(2)}, u32[]{:S(2)}) collective-permute-start(bf16[1280,1280]{1,0:T(8,128)(2,1)} %collective-permute-done.10.refs_1_), channel_id=1, source_target_pairs={{8,16},{16,8},{9,17},{17,9},{10,18},{18,10},{11,19},{19,11},{12,20... | collective-permute-start | bytes 9830408 | tf_op jit(solution)/shard_map/ppermute | solution.py:222
  300.6 38.9 %collective-permute-start.13 = (bf16[2,320,1280]{2,1,0:T(8,128)(2,1)}, bf16[2,320,1280]{2,1,0:T(8,128)(2,1)S(1)}, u32[]{:S(2)}, u32[]{:S(2)}) collective-permute-start(bf16[2,320,1280]{2,1,0:T(8,128)(2,1)} %get-tuple-element.194), channel_id=1, source_target_pairs={{0,2},{2,0},{1,3},{3,1},{4,6},{6,4},{5,7},{7,5},{8,10},{10,8},{9,1... | collective-permute-start | bytes 4915208 | tf_op jit(solution)/shard_map/ppermute | solution.py:195
  302.1 53.9 %collective-permute-start.12 = (bf16[1,320,1280]{2,1,0:T(8,128)(2,1)}, bf16[1,320,1280]{2,1,0:T(8,128)(2,1)S(1)}, u32[]{:S(2)}, u32[]{:S(2)}) collective-permute-start(bf16[1,320,1280]{2,1,0:T(8,128)(2,1)} %get-tuple-element.192), channel_id=1, source_target_pairs={{0,2},{2,0},{1,3},{3,1},{4,6},{6,4},{5,7},{7,5},{8,10},{10,8},{9,1... | collective-permute-start | bytes 2457608 | tf_op jit(solution)/shard_map/ppermute | solution.py:195
  364.8 103.1 %collective-permute-start.20 = (bf16[1280,1280]{1,0:T(8,128)(2,1)}, bf16[1280,1280]{1,0:T(8,128)(2,1)}, u32[]{:S(2)}, u32[]{:S(2)}) collective-permute-start(bf16[1280,1280]{1,0:T(8,128)(2,1)} %collective-permute-done.11.refs_1_), channel_id=1, source_target_pairs={{8,16},{16,8},{9,17},{17,9},{10,18},{18,10},{11,19},{19,11},{12,20... | collective-permute-start | bytes 9830408 | tf_op jit(solution)/shard_map/ppermute | solution.py:222
  368.3 47.1 %collective-permute-start.18 = (bf16[1,320,1280]{2,1,0:T(8,128)(2,1)}, bf16[1,320,1280]{2,1,0:T(8,128)(2,1)}, u32[]{:S(2)}, u32[]{:S(2)}) collective-permute-start(bf16[1,320,1280]{2,1,0:T(8,128)(2,1)} %get-tuple-element.210), channel_id=1, source_target_pairs={{0,2},{2,0},{1,3},{3,1},{4,6},{6,4},{5,7},{7,5},{8,10},{10,8},{9,1... | collective-permute-start | bytes 2457608 | tf_op jit(solution)/shard_map/ppermute | solution.py:195
  369.9 41.6 %collective-permute-start.19 = (bf16[1,320,1280]{2,1,0:T(8,128)(2,1)}, bf16[1,320,1280]{2,1,0:T(8,128)(2,1)}, u32[]{:S(2)}, u32[]{:S(2)}) collective-permute-start(bf16[1,320,1280]{2,1,0:T(8,128)(2,1)} %get-tuple-element.212), channel_id=1, source_target_pairs={{0,2},{2,0},{1,3},{3,1},{4,6},{6,4},{5,7},{7,5},{8,10},{10,8},{9,1... | collective-permute-start | bytes 2457608 | tf_op jit(solution)/shard_map/ppermute | solution.py:195
  374.2 93.6 %collective-permute-start.21 = (bf16[2,640,1280]{2,1,0:T(8,128)(2,1)}, bf16[2,640,1280]{2,1,0:T(8,128)(2,1)S(1)}, u32[]{:S(2)}, u32[]{:S(2)}) collective-permute-start(bf16[2,640,1280]{2,1,0:T(8,128)(2,1)} %slice_bitcast_fusion.1), channel_id=1, source_target_pairs={{0,8},{24,16},{1,9},{25,17},{2,10},{26,18},{3,11},{27,19},{4,12},{... | collective-permute-start | bytes 9830408 | tf_op jit(solution)/shard_map/ppermute | solution.py:222
  375.5 93.2 %collective-permute-start.22 = (bf16[1280,1280]{1,0:T(8,128)(2,1)}, bf16[1280,1280]{1,0:T(8,128)(2,1)}, u32[]{:S(2)}, u32[]{:S(2)}) collective-permute-start(bf16[1280,1280]{1,0:T(8,128)(2,1)} %collective-permute-done.9), channel_id=1, source_target_pairs={{8,0},{16,24},{9,1},{17,25},{10,2},{18,26},{11,3},{19,27},{12,4},{... | collective-permute-start | bytes 9830408 | tf_op jit(solution)/shard_map/ppermute | solution.py:222
  411.4 56.4 %collective-permute-start.23 = (bf16[2,160,1280]{2,1,0:T(8,128)(2,1)}, bf16[2,160,1280]{2,1,0:T(8,128)(2,1)S(1)}, u32[]{:S(2)}, u32[]{:S(2)}) collective-permute-start(bf16[2,160,1280]{2,1,0:T(8,128)(2,1)} %bitcast.91), channel_id=1, source_target_pairs={{8,0},{16,24},{9,1},{17,25},{10,2},{18,26},{11,3},{19,27},{12,4},{... | collective-permute-start | bytes 2457608 | tf_op jit(solution)/shard_map/ppermute | solution.py:222
  468.8 73.4 %collective-permute-start.30 = (bf16[1280,1280]{1,0:T(8,128)(2,1)}, bf16[1280,1280]{1,0:T(8,128)(2,1)}, u32[]{:S(2)}, u32[]{:S(2)}) collective-permute-start(bf16[1280,1280]{1,0:T(8,128)(2,1)} %collective-permute-done.16), channel_id=1, source_target_pairs={{8,0},{16,24},{9,1},{17,25},{10,2},{18,26},{11,3},{19,27},{12,4},{... | collective-permute-start | bytes 9830408 | tf_op jit(solution)/shard_map/ppermute | solution.py:222
  484.3 70.4 %collective-permute-start.26 = (bf16[2,320,1280]{2,1,0:T(8,128)(2,1)}, bf16[2,320,1280]{2,1,0:T(8,128)(2,1)}, u32[]{:S(2)}, u32[]{:S(2)}) collective-permute-start(bf16[2,320,1280]{2,1,0:T(8,128)(2,1)} %get-tuple-element.223), channel_id=1, source_target_pairs={{0,1},{1,0},{2,3},{3,2},{4,5},{5,4},{6,7},{7,6},{8,9},{9,8},{10,11... | collective-permute-start | bytes 4915208 | tf_op jit(solution)/shard_map/ppermute | solution.py:187
  484.3 74.7 %collective-permute-start.27 = (bf16[2,320,1280]{2,1,0:T(8,128)(2,1)}, bf16[2,320,1280]{2,1,0:T(8,128)(2,1)}, u32[]{:S(2)}, u32[]{:S(2)}) collective-permute-start(bf16[2,320,1280]{2,1,0:T(8,128)(2,1)} %get-tuple-element.221), channel_id=1, source_target_pairs={{0,1},{1,0},{2,3},{3,2},{4,5},{5,4},{6,7},{7,6},{8,9},{9,8},{10,11... | collective-permute-start | bytes 4915208 | tf_op jit(solution)/shard_map/ppermute | solution.py:187
  484.8 95.1 %collective-permute-start.28 = (bf16[1280,1280]{1,0:T(8,128)(2,1)}, bf16[1280,1280]{1,0:T(8,128)(2,1)}, u32[]{:S(2)}, u32[]{:S(2)}) collective-permute-start(bf16[1280,1280]{1,0:T(8,128)(2,1)} %bitcast.53), channel_id=1, source_target_pairs={{8,16},{16,8},{9,17},{17,9},{10,18},{18,10},{11,19},{19,11},{12,20... | collective-permute-start | bytes 9830408 | tf_op jit(solution)/shard_map/ppermute | solution.py:222
  491.1 88.9 %collective-permute-start.29 = (bf16[2,640,1280]{2,1,0:T(8,128)(2,1)}, bf16[2,640,1280]{2,1,0:T(8,128)(2,1)S(1)}, u32[]{:S(2)}, u32[]{:S(2)}) collective-permute-start(bf16[2,640,1280]{2,1,0:T(8,128)(2,1)} %slice_bitcast_fusion), channel_id=1, source_target_pairs={{0,8},{24,16},{1,9},{25,17},{2,10},{26,18},{3,11},{27,19},{4,12},{... | collective-permute-start | bytes 9830408 | tf_op jit(solution)/shard_map/ppermute | solution.py:222
  554.7 15.7 %collective-permute-start.25 = (bf16[2,320,1280]{2,1,0:T(8,128)(2,1)}, bf16[2,320,1280]{2,1,0:T(8,128)(2,1)}, u32[]{:S(2)}, u32[]{:S(2)}) collective-permute-start(bf16[2,320,1280]{2,1,0:T(8,128)(2,1)} %send_product.25), channel_id=1, source_target_pairs={{0,1},{1,0},{2,3},{3,2},{4,5},{5,4},{6,7},{7,6},{8,9},{9,8},{10,11... | collective-permute-start | bytes 4915208 | tf_op jit(solution)/shard_map/ppermute | solution.py:187
  554.7 22.7 %collective-permute-start.24 = (bf16[1,320,1280]{2,1,0:T(8,128)(2,1)}, bf16[1,320,1280]{2,1,0:T(8,128)(2,1)}, u32[]{:S(2)}, u32[]{:S(2)}) collective-permute-start(bf16[1,320,1280]{2,1,0:T(8,128)(2,1)} %get-tuple-element.219), channel_id=1, source_target_pairs={{0,2},{2,0},{1,3},{3,1},{4,6},{6,4},{5,7},{7,5},{8,10},{10,8},{9,1... | collective-permute-start | bytes 2457608 | tf_op jit(solution)/shard_map/ppermute | solution.py:195
  559.0 20.9 %collective-permute-start.31 = (bf16[2,160,1280]{2,1,0:T(8,128)(2,1)}, bf16[2,160,1280]{2,1,0:T(8,128)(2,1)}, u32[]{:S(2)}, u32[]{:S(2)}) collective-permute-start(bf16[2,160,1280]{2,1,0:T(8,128)(2,1)} %get-tuple-element.235), channel_id=1, source_target_pairs={{0,4},{4,0},{1,5},{5,1},{2,6},{6,2},{3,7},{7,3},{8,12},{12,8},{9,1... | collective-permute-start | bytes 2457608 | tf_op jit(solution)/shard_map/ppermute | solution.py:226
  589.9 75.4 %collective-permute-start.37 = (bf16[1280,1280]{1,0:T(8,128)(2,1)}, bf16[1280,1280]{1,0:T(8,128)(2,1)S(1)}, u32[]{:S(2)}, u32[]{:S(2)}) collective-permute-start(bf16[1280,1280]{1,0:T(8,128)(2,1)} %bitcast.49), channel_id=1, source_target_pairs={{8,16},{16,8},{9,17},{17,9},{10,18},{18,10},{11,19},{19,11},{12,20... | collective-permute-start | bytes 9830408 | tf_op jit(solution)/shard_map/ppermute | solution.py:222
  592.5 73.4 %collective-permute-start.38 = (bf16[1280,1280]{1,0:T(8,128)(2,1)}, bf16[1280,1280]{1,0:T(8,128)(2,1)}, u32[]{:S(2)}, u32[]{:S(2)}) collective-permute-start(bf16[1280,1280]{1,0:T(8,128)(2,1)} %bitcast.54), channel_id=1, source_target_pairs={{0,8},{8,0},{16,24},{24,16},{1,9},{9,1},{17,25},{25,17},{2,10},{10... | collective-permute-start | bytes 9830408 | tf_op jit(solution)/shard_map/ppermute | solution.py:222
  600.0 13.3 %collective-permute-start.33 = (bf16[2,320,1280]{2,1,0:T(8,128)(2,1)}, bf16[2,320,1280]{2,1,0:T(8,128)(2,1)}, u32[]{:S(2)}, u32[]{:S(2)}) collective-permute-start(bf16[2,320,1280]{2,1,0:T(8,128)(2,1)} %send_product.27), channel_id=1, source_target_pairs={{0,1},{1,0},{2,3},{3,2},{4,5},{5,4},{6,7},{7,6},{8,9},{9,8},{10,11... | collective-permute-start | bytes 4915208 | tf_op jit(solution)/shard_map/ppermute | solution.py:187
  600.3 38.9 %collective-permute-start.32 = (bf16[2,320,1280]{2,1,0:T(8,128)(2,1)}, bf16[2,320,1280]{2,1,0:T(8,128)(2,1)}, u32[]{:S(2)}, u32[]{:S(2)}) collective-permute-start(bf16[2,320,1280]{2,1,0:T(8,128)(2,1)} %get-tuple-element.236), channel_id=1, source_target_pairs={{0,2},{2,0},{1,3},{3,1},{4,6},{6,4},{5,7},{7,5},{8,10},{10,8},{9,1... | collective-permute-start | bytes 4915208 | tf_op jit(solution)/shard_map/ppermute | solution.py:195
  600.9 55.2 %collective-permute-start.36 = (bf16[1,320,1280]{2,1,0:T(8,128)(2,1)}, bf16[1,320,1280]{2,1,0:T(8,128)(2,1)S(1)}, u32[]{:S(2)}, u32[]{:S(2)}) collective-permute-start(bf16[1,320,1280]{2,1,0:T(8,128)(2,1)} %get-tuple-element.248), channel_id=1, source_target_pairs={{0,2},{2,0},{1,3},{3,1},{4,6},{6,4},{5,7},{7,5},{8,10},{10,8},{9,1... | collective-permute-start | bytes 2457608 | tf_op jit(solution)/shard_map/ppermute | solution.py:195
  677.3 90.5 %collective-permute-start.45 = (bf16[1280,1280]{1,0:T(8,128)(2,1)}, bf16[1280,1280]{1,0:T(8,128)(2,1)}, u32[]{:S(2)}, u32[]{:S(2)}) collective-permute-start(bf16[1280,1280]{1,0:T(8,128)(2,1)} %collective-permute-done.38.refs_1_), channel_id=1, source_target_pairs={{8,16},{16,8},{9,17},{17,9},{10,18},{18,10},{11,19},{19,11},{12,20... | collective-permute-start | bytes 9830408 | tf_op jit(solution)/shard_map/ppermute | solution.py:222
  679.7 88.1 %collective-permute-start.46 = (bf16[1280,1280]{1,0:T(8,128)(2,1)S(1)}, bf16[1280,1280]{1,0:T(8,128)(2,1)}, u32[]{:S(2)}, u32[]{:S(2)}) collective-permute-start(bf16[1280,1280]{1,0:T(8,128)(2,1)S(1)} %bitcast.50), channel_id=1, source_target_pairs={{0,8},{8,0},{16,24},{24,16},{1,9},{9,1},{17,25},{25,17},{2,10},{10... | collective-permute-start | bytes 9830408 | tf_op jit(solution)/shard_map/ppermute | solution.py:222
  686.1 17.0 %collective-permute-start.40 = (bf16[2,320,1280]{2,1,0:T(8,128)(2,1)}, bf16[2,320,1280]{2,1,0:T(8,128)(2,1)}, u32[]{:S(2)}, u32[]{:S(2)}) collective-permute-start(bf16[2,320,1280]{2,1,0:T(8,128)(2,1)} %send_product.29), channel_id=1, source_target_pairs={{0,1},{1,0},{2,3},{3,2},{4,5},{5,4},{6,7},{7,6},{8,9},{9,8},{10,11... | collective-permute-start | bytes 4915208 | tf_op jit(solution)/shard_map/ppermute | solution.py:187
  686.1 47.4 %collective-permute-start.44 = (bf16[2,320,1280]{2,1,0:T(8,128)(2,1)}, bf16[2,320,1280]{2,1,0:T(8,128)(2,1)}, u32[]{:S(2)}, u32[]{:S(2)}) collective-permute-start(bf16[2,320,1280]{2,1,0:T(8,128)(2,1)} %get-tuple-element.266), channel_id=1, source_target_pairs={{0,2},{2,0},{1,3},{3,1},{4,6},{6,4},{5,7},{7,5},{8,10},{10,8},{9,1... | collective-permute-start | bytes 4915208 | tf_op jit(solution)/shard_map/ppermute | solution.py:195
  689.5 61.2 %collective-permute-start.43 = (bf16[1,320,1280]{2,1,0:T(8,128)(2,1)}, bf16[1,320,1280]{2,1,0:T(8,128)(2,1)}, u32[]{:S(2)}, u32[]{:S(2)}) collective-permute-start(bf16[1,320,1280]{2,1,0:T(8,128)(2,1)} %get-tuple-element.264), channel_id=1, source_target_pairs={{0,2},{2,0},{1,3},{3,1},{4,6},{6,4},{5,7},{7,5},{8,10},{10,8},{9,1... | collective-permute-start | bytes 2457608 | tf_op jit(solution)/shard_map/ppermute | solution.py:195
  703.1 64.7 %collective-permute-start.39 = (bf16[2,160,1280]{2,1,0:T(8,128)(2,1)}, bf16[2,160,1280]{2,1,0:T(8,128)(2,1)}, u32[]{:S(2)}, u32[]{:S(2)}) collective-permute-start(bf16[2,160,1280]{2,1,0:T(8,128)(2,1)} %bitcast.90), channel_id=1, source_target_pairs={{8,0},{16,24},{9,1},{17,25},{10,2},{18,26},{11,3},{19,27},{12,4},{... | collective-permute-start | bytes 2457608 | tf_op jit(solution)/shard_map/ppermute | solution.py:222
  733.6 34.2 %collective-permute-start.47 = (bf16[2,160,1280]{2,1,0:T(8,128)(2,1)}, bf16[2,160,1280]{2,1,0:T(8,128)(2,1)}, u32[]{:S(2)}, u32[]{:S(2)}) collective-permute-start(bf16[2,160,1280]{2,1,0:T(8,128)(2,1)} %bitcast.92), channel_id=1, source_target_pairs={{0,4},{4,0},{1,5},{5,1},{2,6},{6,2},{3,7},{7,3},{8,12},{12,8},{9,1... | collective-permute-start | bytes 2457608 | tf_op jit(solution)/shard_map/ppermute | solution.py:226
  777.3 14.3 %collective-permute-start.51 = (bf16[2,320,1280]{2,1,0:T(8,128)(2,1)}, bf16[2,320,1280]{2,1,0:T(8,128)(2,1)}, u32[]{:S(2)}, u32[]{:S(2)}) collective-permute-start(bf16[2,320,1280]{2,1,0:T(8,128)(2,1)} %get-tuple-element.278), channel_id=1, source_target_pairs={{0,1},{1,0},{2,3},{3,2},{4,5},{5,4},{6,7},{7,6},{8,9},{9,8},{10,11... | collective-permute-start | bytes 4915208 | tf_op jit(solution)/shard_map/ppermute | solution.py:187
  777.3 42.4 %collective-permute-start.49 = (bf16[2,320,1280]{2,1,0:T(8,128)(2,1)}, bf16[2,320,1280]{2,1,0:T(8,128)(2,1)}, u32[]{:S(2)}, u32[]{:S(2)}) collective-permute-start(bf16[2,320,1280]{2,1,0:T(8,128)(2,1)} %get-tuple-element.274), channel_id=1, source_target_pairs={{0,2},{2,0},{1,3},{3,1},{4,6},{6,4},{5,7},{7,5},{8,10},{10,8},{9,1... | collective-permute-start | bytes 4915208 | tf_op jit(solution)/shard_map/ppermute | solution.py:195
  777.9 18.6 %collective-permute-start.52 = (bf16[2,320,1280]{2,1,0:T(8,128)(2,1)}, bf16[2,320,1280]{2,1,0:T(8,128)(2,1)}, u32[]{:S(2)}, u32[]{:S(2)}) collective-permute-start(bf16[2,320,1280]{2,1,0:T(8,128)(2,1)} %get-tuple-element.276), channel_id=1, source_target_pairs={{0,1},{1,0},{2,3},{3,2},{4,5},{5,4},{6,7},{7,6},{8,9},{9,8},{10,11... | collective-permute-start | bytes 4915208 | tf_op jit(solution)/shard_map/ppermute | solution.py:187
  784.5 26.6 %collective-permute-start.50 = (bf16[2,320,1280]{2,1,0:T(8,128)(2,1)}, bf16[2,320,1280]{2,1,0:T(8,128)(2,1)}, u32[]{:S(2)}, u32[]{:S(2)}) collective-permute-start(bf16[2,320,1280]{2,1,0:T(8,128)(2,1)} %send_product.31), channel_id=1, source_target_pairs={{0,1},{1,0},{2,3},{3,2},{4,5},{5,4},{6,7},{7,6},{8,9},{9,8},{10,11... | collective-permute-start | bytes 4915208 | tf_op jit(solution)/shard_map/ppermute | solution.py:187
  786.1 47.3 %collective-permute-start.48 = (bf16[1,320,1280]{2,1,0:T(8,128)(2,1)}, bf16[1,320,1280]{2,1,0:T(8,128)(2,1)}, u32[]{:S(2)}, u32[]{:S(2)}) collective-permute-start(bf16[1,320,1280]{2,1,0:T(8,128)(2,1)} %get-tuple-element.272), channel_id=1, source_target_pairs={{0,2},{2,0},{1,3},{3,1},{4,6},{6,4},{5,7},{7,5},{8,10},{10,8},{9,1... | collective-permute-start | bytes 2457608 | tf_op jit(solution)/shard_map/ppermute | solution.py:195
  791.7 44.0 %collective-permute-start.53 = (bf16[1280,640]{1,0:T(8,128)(2,1)}, bf16[1280,640]{1,0:T(8,128)(2,1)S(1)}, u32[]{:S(2)}, u32[]{:S(2)}) collective-permute-start(bf16[1280,640]{1,0:T(8,128)(2,1)} %get-tuple-element.287), channel_id=1, source_target_pairs={{8,16},{16,8},{9,17},{17,9},{10,18},{18,10},{11,19},{19,11},{12,20... | collective-permute-start | bytes 4915208 | tf_op jit(solution)/shard_map/ppermute | solution.py:222
  796.4 39.3 %collective-permute-start.54 = (bf16[2,160,1280]{2,1,0:T(8,128)(2,1)}, bf16[2,160,1280]{2,1,0:T(8,128)(2,1)}, u32[]{:S(2)}, u32[]{:S(2)}) collective-permute-start(bf16[2,160,1280]{2,1,0:T(8,128)(2,1)} %bitcast.13), channel_id=1, source_target_pairs={{8,0},{16,24},{9,1},{17,25},{10,2},{18,26},{11,3},{19,27},{12,4},{... | collective-permute-start | bytes 2457608 | tf_op jit(solution)/shard_map/ppermute | solution.py:222
  811.1 24.6 %collective-permute-start.55 = (bf16[2,160,1280]{2,1,0:T(8,128)(2,1)}, bf16[2,160,1280]{2,1,0:T(8,128)(2,1)S(1)}, u32[]{:S(2)}, u32[]{:S(2)}) collective-permute-start(bf16[2,160,1280]{2,1,0:T(8,128)(2,1)} %get-tuple-element.289), channel_id=1, source_target_pairs={{0,4},{4,0},{1,5},{5,1},{2,6},{6,2},{3,7},{7,3},{8,12},{12,8},{9,1... | collective-permute-start | bytes 2457608 | tf_op jit(solution)/shard_map/ppermute | solution.py:226
  835.7 39.1 %collective-permute-start.56 = (bf16[2,320,1280]{2,1,0:T(8,128)(2,1)}, bf16[2,320,1280]{2,1,0:T(8,128)(2,1)}, u32[]{:S(2)}, u32[]{:S(2)}) collective-permute-start(bf16[2,320,1280]{2,1,0:T(8,128)(2,1)} %get-tuple-element.290), channel_id=1, source_target_pairs={{0,2},{2,0},{1,3},{3,1},{4,6},{6,4},{5,7},{7,5},{8,10},{10,8},{9,1... | collective-permute-start | bytes 4915208 | tf_op jit(solution)/shard_map/ppermute | solution.py:195
  848.0 43.1 %collective-permute-start.59 = (bf16[1,320,1280]{2,1,0:T(8,128)(2,1)}, bf16[1,320,1280]{2,1,0:T(8,128)(2,1)}, u32[]{:S(2)}, u32[]{:S(2)}) collective-permute-start(bf16[1,320,1280]{2,1,0:T(8,128)(2,1)} %get-tuple-element.299), channel_id=1, source_target_pairs={{0,2},{2,0},{1,3},{3,1},{4,6},{6,4},{5,7},{7,5},{8,10},{10,8},{9,1... | collective-permute-start | bytes 2457608 | tf_op jit(solution)/shard_map/ppermute | solution.py:195
  849.4 45.2 %collective-permute-start.60 = (bf16[1280,640]{1,0:T(8,128)(2,1)}, bf16[1280,640]{1,0:T(8,128)(2,1)S(1)}, u32[]{:S(2)}, u32[]{:S(2)}) collective-permute-start(bf16[1280,640]{1,0:T(8,128)(2,1)} %get-tuple-element.301), channel_id=1, source_target_pairs={{8,16},{16,8},{9,17},{17,9},{10,18},{18,10},{11,19},{19,11},{12,20... | collective-permute-start | bytes 4915208 | tf_op jit(solution)/shard_map/ppermute | solution.py:222
  854.2 39.2 %collective-permute-start.61 = (bf16[2,160,1280]{2,1,0:T(8,128)(2,1)}, bf16[2,160,1280]{2,1,0:T(8,128)(2,1)}, u32[]{:S(2)}, u32[]{:S(2)}) collective-permute-start(bf16[2,160,1280]{2,1,0:T(8,128)(2,1)} %bitcast.15), channel_id=1, source_target_pairs={{8,0},{16,24},{9,1},{17,25},{10,2},{18,26},{11,3},{19,27},{12,4},{... | collective-permute-start | bytes 2457608 | tf_op jit(solution)/shard_map/ppermute | solution.py:222
  857.0 36.3 %collective-permute-start.62 = (bf16[2,160,1280]{2,1,0:T(8,128)(2,1)}, bf16[2,160,1280]{2,1,0:T(8,128)(2,1)S(1)}, u32[]{:S(2)}, u32[]{:S(2)}) collective-permute-start(bf16[2,160,1280]{2,1,0:T(8,128)(2,1)} %get-tuple-element.303), channel_id=1, source_target_pairs={{0,4},{4,0},{1,5},{5,1},{2,6},{6,2},{3,7},{7,3},{8,12},{12,8},{9,1... | collective-permute-start | bytes 2457608 | tf_op jit(solution)/shard_map/ppermute | solution.py:226
  874.8 19.7 %collective-permute-start.63 = (bf16[2,160,1280]{2,1,0:T(8,128)(2,1)}, bf16[2,160,1280]{2,1,0:T(8,128)(2,1)}, u32[]{:S(2)}, u32[]{:S(2)}) collective-permute-start(bf16[2,160,1280]{2,1,0:T(8,128)(2,1)} %bitcast.18), channel_id=1, source_target_pairs={{0,4},{4,0},{1,5},{5,1},{2,6},{6,2},{3,7},{7,3},{8,12},{12,8},{9,1... | collective-permute-start | bytes 2457608 | tf_op jit(solution)/shard_map/ppermute | solution.py:226
  904.2 32.7 %collective-permute-start.70 = (bf16[2,160,1280]{2,1,0:T(8,128)(2,1)S(1)}, bf16[2,160,1280]{2,1,0:T(8,128)(2,1)}, u32[]{:S(2)}, u32[]{:S(2)}) collective-permute-start(bf16[2,160,1280]{2,1,0:T(8,128)(2,1)S(1)} %bitcast.73), channel_id=1, source_target_pairs={{4,0},{5,1},{6,2},{7,3},{12,8},{13,9},{14,10},{15,11},{20,16},{21,... | collective-permute-start | bytes 2457608 | tf_op jit(solution)/shard_map/ppermute | solution.py:256
  908.6 28.3 %collective-permute-start.71 = (bf16[2,160,1280]{2,1,0:T(8,128)(2,1)}, bf16[2,160,1280]{2,1,0:T(8,128)(2,1)}, u32[]{:S(2)}, u32[]{:S(2)}) collective-permute-start(bf16[2,160,1280]{2,1,0:T(8,128)(2,1)} %bitcast.19), channel_id=1, source_target_pairs={{8,4},{16,28},{9,5},{17,29},{10,6},{18,30},{11,7},{19,31}} | collective-permute-start | bytes 2457608 | tf_op jit(solution)/shard_map/ppermute | solution.py:250
  910.4 20.8 %collective-permute-start.67 = (bf16[2,320,640]{2,1,0:T(8,128)(2,1)}, bf16[2,320,640]{2,1,0:T(8,128)(2,1)}, u32[]{:S(2)}, u32[]{:S(2)}) collective-permute-start(bf16[2,320,640]{2,1,0:T(8,128)(2,1)} %get-tuple-element.315), channel_id=1, source_target_pairs={{0,2},{2,0},{1,3},{3,1},{4,6},{6,4},{5,7},{7,5},{8,10},{10,8},{9,1... | collective-permute-start | bytes 2457608 | tf_op jit(solution)/shard_map/ppermute | solution.py:195
  913.1 23.8 %collective-permute-start.64 = (bf16[2,160,1280]{2,1,0:T(8,128)(2,1)}, bf16[2,160,1280]{2,1,0:T(8,128)(2,1)}, u32[]{:S(2)}, u32[]{:S(2)}) collective-permute-start(bf16[2,160,1280]{2,1,0:T(8,128)(2,1)} %broadcast_select_fusion.14), channel_id=1, source_target_pairs={{8,12},{16,20},{12,4},{20,28},{9,13},{17,21},{13,5},{21,29},{10,14... | collective-permute-start | bytes 2457608 | tf_op jit(solution)/shard_map/ppermute | solution.py:249
  917.5 26.4 %collective-permute-start.69 = (bf16[2,160,1280]{2,1,0:T(8,128)(2,1)S(1)}, bf16[2,160,1280]{2,1,0:T(8,128)(2,1)}, u32[]{:S(2)}, u32[]{:S(2)}) collective-permute-start(bf16[2,160,1280]{2,1,0:T(8,128)(2,1)S(1)} %bitcast.79), channel_id=1, source_target_pairs={{4,0},{5,1},{6,2},{7,3},{12,8},{13,9},{14,10},{15,11},{20,16},{21,... | collective-permute-start | bytes 2457608 | tf_op jit(solution)/shard_map/ppermute | solution.py:256
  931.2 29.9 %collective-permute-start.68 = (bf16[2,160,1280]{2,1,0:T(8,128)(2,1)}, bf16[2,160,1280]{2,1,0:T(8,128)(2,1)}, u32[]{:S(2)}, u32[]{:S(2)}) collective-permute-start(bf16[2,160,1280]{2,1,0:T(8,128)(2,1)} %get-tuple-element.317), channel_id=1, source_target_pairs={{0,4},{4,0},{1,5},{5,1},{2,6},{6,2},{3,7},{7,3},{8,12},{12,8},{9,1... | collective-permute-start | bytes 2457608 | tf_op jit(solution)/shard_map/ppermute | solution.py:226
  961.1 22.3 %collective-permute-start.72 = (bf16[2,320,640]{2,1,0:T(8,128)(2,1)}, bf16[2,320,640]{2,1,0:T(8,128)(2,1)S(1)}, u32[]{:S(2)}, u32[]{:S(2)}) collective-permute-start(bf16[2,320,640]{2,1,0:T(8,128)(2,1)} %get-tuple-element.320), channel_id=1, source_target_pairs={{0,2},{2,0},{1,3},{3,1},{4,6},{6,4},{5,7},{7,5},{8,10},{10,8},{9,1... | collective-permute-start | bytes 2457608 | tf_op jit(solution)/shard_map/ppermute | solution.py:195
  961.7 19.5 %collective-permute-start.74 = (bf16[2,160,640]{2,1,0:T(8,128)(2,1)S(1)}, bf16[2,160,640]{2,1,0:T(8,128)(2,1)}, u32[]{:S(2)}, u32[]{:S(2)}) collective-permute-start(bf16[2,160,640]{2,1,0:T(8,128)(2,1)S(1)} %bitcast.86), channel_id=1, source_target_pairs={{8,4},{16,28},{9,5},{17,29},{10,6},{18,30},{11,7},{19,31}} | collective-permute-start | bytes 1228808 | tf_op jit(solution)/shard_map/ppermute | solution.py:250
  963.9 17.3 %collective-permute-start.73 = (bf16[2,160,640]{2,1,0:T(8,128)(2,1)}, bf16[2,160,640]{2,1,0:T(8,128)(2,1)}, u32[]{:S(2)}, u32[]{:S(2)}) collective-permute-start(bf16[2,160,640]{2,1,0:T(8,128)(2,1)} %broadcast_select_fusion.20), channel_id=1, source_target_pairs={{8,12},{16,20},{12,4},{20,28},{9,13},{17,21},{13,5},{21,29},{10,14... | collective-permute-start | bytes 1228808 | tf_op jit(solution)/shard_map/ppermute | solution.py:249
  984.4 13.6 %collective-permute-start.75 = (bf16[2,160,640]{2,1,0:T(8,128)(2,1)S(1)}, bf16[2,160,640]{2,1,0:T(8,128)(2,1)S(1)}, u32[]{:S(2)}, u32[]{:S(2)}) collective-permute-start(bf16[2,160,640]{2,1,0:T(8,128)(2,1)S(1)} %broadcast_select_fusion.19), channel_id=1, source_target_pairs={{8,12},{16,20},{12,4},{20,28},{9,13},{17,21},{13,5},{21,29},{10,14... | collective-permute-start | bytes 1228808 | tf_op jit(solution)/shard_map/ppermute | solution.py:249
  (59 other events, 502.1 us)
Sparse Core Ops, SparseCore 0:
  9.6 192.1 all-gather.1
  679.9 51.8 reduce-scatter.1

commit v3 on v0

v3 whole, which is shorter than its diff:
```python
import jax
import jax.numpy as jnp
from jax import lax
from jax.experimental import pallas as pl
from jax.experimental.pallas import tpu as pltpu
from jax.sharding import PartitionSpec as P

F32, BF16 = jnp.float32, jnp.bfloat16

END_TO_MID = [(0, 1), (3, 2)]
MID_TO_MID = [(1, 2), (2, 1)]
MID_TO_END = [(1, 0), (2, 3)]
RELATIVE = (0, 2, 1, 3)
OTHER_CORE = [(0, 1), (1, 0), (2, 3), (3, 2)]
OTHER_Y = [(0, 2), (2, 0), (1, 3), (3, 1)]
OTHER_OCC = [(0, 1), (1, 0)]
NEIGHBOUR = [(0, 1), (1, 0), (2, 3), (3, 2)]
ROOM = 60 << 20
CHEAP = pl.CostEstimate(flops=1 << 20, bytes_accessed=1 << 16, transcendentals=0)


def after(value, *earlier):
    return lax.optimization_barrier((value, *earlier))[0]


def dot_rows(lhs, rhs):
    return jnp.dot(lhs.reshape(-1, lhs.shape[-1]), rhs, preferred_element_type=F32)


def operands(products, first):
    specs, arrays, places = [], [], {}
    for place, (irrep, lhs, _) in enumerate(products):
        rows, depth = lhs.shape[-2] // 4, lhs.shape[-1]

        def quarter(p, r, where, place=place):
            return where[first + jnp.where(p == place, r, jnp.where(p < place, 0, 1))]
        if lhs.ndim == 4:
            specs.append(pl.BlockSpec(
                (1, 2, rows, depth), lambda p, r, where, g=irrep, q=quarter: (g, 0, q(p, r, where), 0)))
        else:
            specs.append(pl.BlockSpec((2, rows, depth), lambda p, r, where, q=quarter: (0, q(p, r, where), 0)))
        arrays.append(lhs)
    for _, _, rhs in products:
        if id(rhs) not in places:
            places[id(rhs)] = len(arrays)
            specs.append(pl.BlockSpec(rhs.shape, lambda p, r, where: (0, 0)))
            arrays.append(rhs)
    return specs, arrays, [places[id(rhs)] for _, _, rhs in products]


def run_products(refs, columns_at, use):
    for place, at in enumerate(columns_at):
        @pl.when(pl.program_id(0) == place)
        def _():
            use(dot_rows(refs[place][...], refs[at][...]))


def send_products(where, products):
    specs, arrays, columns_at = operands(products, 2)
    count, rows, columns = len(products), products[0][1].shape[-2] // 2, products[0][2].shape[1]

    def kernel(where_ref, *refs):
        def use(value):
            refs[-1][0, 0] = value.astype(BF16)
        run_products(refs, columns_at, use)

    return pl.pallas_call(
        kernel,
        out_shape=jax.ShapeDtypeStruct((count, 2, rows, columns), BF16),
        grid_spec=pltpu.PrefetchScalarGridSpec(
            num_scalar_prefetch=1,
            grid=(count, 2),
            in_specs=specs,
            out_specs=pl.BlockSpec((1, 1, rows, columns), lambda p, r, where: (p, r, 0, 0)),
        ),
        compiler_params=pltpu.CompilerParams(vmem_limit_bytes=ROOM),
        cost_estimate=CHEAP,
        name="send_products",
    )(where, *arrays)


def keep_products(where, products, arrived):
    specs, arrays, columns_at = operands(products, 0)
    count, rows, columns = len(products), products[0][1].shape[-2] // 2, products[0][2].shape[1]

    def kernel(where_ref, *refs):
        arrived_ref, away, own = refs[-3:]
        quarter = pl.program_id(1)

        def use(value):
            total = (value + arrived_ref[0, 0].astype(F32)).astype(BF16)

            @pl.when(quarter == 0)
            def _():
                own[0] = total

            @pl.when(quarter == 1)
            def _():
                away[0] = total
        run_products(refs, columns_at, use)

    return pl.pallas_call(
        kernel,
        out_shape=(jax.ShapeDtypeStruct((count, rows, columns), BF16),) * 2,
        grid_spec=pltpu.PrefetchScalarGridSpec(
            num_scalar_prefetch=1,
            grid=(count, 2),
            in_specs=specs + [pl.BlockSpec((1, 1, rows, columns), lambda p, r, where: (p, r, 0, 0))],
            out_specs=(pl.BlockSpec((1, rows, columns), lambda p, r, where: (p, 0, 0)),) * 2,
        ),
        compiler_params=pltpu.CompilerParams(vmem_limit_bytes=ROOM),
        cost_estimate=CHEAP,
        name="keep_products",
    )(where, *arrays, arrived)


def place(base, parity, kept, arrived, out, shape):
    count = len(kept)
    rows, columns = shape[2], shape[4]
    block = rows // 2

    def kernel(base_ref, *refs):
        out_ref, wide = refs[-2:]
        first = base_ref[1] == 0
        for index in range(count):
            mine, theirs = refs[index][0].astype(F32), refs[count + index][0].astype(F32)
            wide[:, index, :] = jnp.where(first, mine, theirs)
            wide[:, count + index, :] = jnp.where(first, theirs, mine)
        out_ref[0, 0] = wide[...].astype(BF16)

    pieces = kept + arrived
    specs = [
        pl.BlockSpec((1, block, columns), lambda a, i, base, j=j, step=array.shape[0] - 2: (
            a + step * (1 - base[1]), i, j))
        for array, j in pieces]
    extra = [] if out is None else [out]
    return pl.pallas_call(
        kernel,
        out_shape=jax.ShapeDtypeStruct(shape, BF16),
        grid_spec=pltpu.PrefetchScalarGridSpec(
            num_scalar_prefetch=1,
            grid=(2, rows // block),
            in_specs=specs + [pl.BlockSpec(memory_space=pl.ANY)] * len(extra),
            out_specs=pl.BlockSpec(
                (1, 1, block, 2 * count, columns),
                lambda a, i, base: (base[0] + (a + parity) % 2, a, i, 0, 0)),
            scratch_shapes=[pltpu.VMEM((block, 2 * count, columns), F32)],
        ),
        input_output_aliases={1 + 2 * count: 0} if extra else {},
        compiler_params=pltpu.CompilerParams(vmem_limit_bytes=ROOM),
        cost_estimate=CHEAP,
        name="place",
    )(base, *[array for array, _ in pieces], *extra)


class Order:
    def __init__(self):
        self.before, self.edge = [], []

    def follow(self, value):
        return after(value, *self.before) if self.before else value

    def step(self, value):
        self.before = [value]
        return value

    def phase(self, *values):
        self.before = self.before + list(values)
        self.edge = self.before

    def open(self, value):
        return after(value, *self.edge) if self.edge else value


class Batch:
    def __init__(self, order, where, *products):
        self.order, self.where, self.products = order, where, products

    def send(self):
        followed = {id(rhs): rhs for _, _, rhs in self.products}
        followed = {key: self.order.follow(rhs) for key, rhs in followed.items()}
        self.products = [(irrep, lhs, followed[id(rhs)]) for irrep, lhs, rhs in self.products]
        part = self.order.step(send_products(self.where, self.products))
        self.arrived = lax.ppermute(part, "ka", OTHER_CORE)

    def keep(self):
        arrived = self.order.follow(self.arrived)
        self.away, self.own = keep_products(self.where, self.products, arrived)
        self.order.step(self.away)

    def swap(self):
        self.other = lax.ppermute(self.order.open(self.away), "ka", OTHER_Y)

    def finish(self):
        other = self.order.follow(self.other)
        total = self.order.step((self.own.astype(F32) + other.astype(F32)).astype(BF16))
        count, rows, columns = total.shape
        return [total[p].reshape(2, rows // 2, columns) for p in range(count)]


def line_local(ladder_amplitudes, ladder_integrals, cycle_amplitudes, cycle_integrals):
    vir, occ, ka = (lax.axis_index(name) for name in ("vir", "occ", "ka"))
    irreps, rows_here, group, depth = cycle_amplitudes.shape
    quarter = group // 4
    columns = cycle_integrals.shape[3]
    at_end = (vir == 0) | (vir == 3)
    where = jnp.bitwise_xor(ka, jnp.array(RELATIVE, jnp.int32))
    order = Order()

    def columns_of(g):
        return order.open(cycle_integrals)[g].reshape(depth, 2 * columns)

    def batch(*products):
        return Batch(order, where, *products)

    def move(value, route):
        return lax.ppermute(order.open(value), "vir", route)

    def cross(near, far):
        near, far = order.open(near), order.open(far)
        away = jnp.where(occ == 0, far, near)
        return jnp.where(occ == 0, near, far), lax.ppermute(away, "occ", OTHER_OCC)

    def home(mine, back):
        return jnp.where(at_end, order.open(back), order.open(mine))

    low = jnp.where((occ == 0) | at_end, 0, 2).astype(jnp.int32)
    shape = (8 // 2, rows_here, quarter, 2 * irreps, columns)

    def put(half, j, crossed, out):
        base = jnp.stack([low if half == 0 else 2 - low, occ.astype(jnp.int32)])
        kept = [(pair[0], jj) for pair, jj in crossed]
        arrived = [(pair[1], jj) for pair, jj in crossed]
        return order.step(place(base, j, kept, arrived, out, shape))

    def rows_of(g):
        return order.open(cycle_amplitudes)[g]

    def straight(near, near_in, rows, one=slice(None)):
        own_rows, foreign = (order.open(value) for value in rows)
        first = lax.ppermute(jnp.where(occ == 0, own_rows, foreign), ("vir", "occ"), [(2, 3), (4, 5), (3, 1), (5, 7)])
        second = lax.ppermute(foreign, ("vir", "occ"), [(2, 1), (4, 7)])
        kept = jnp.where(occ == 0, near[..., one], jnp.where(at_end, first, own_rows))
        arrived = jnp.where(occ == 0, near_in[..., one], jnp.where(at_end, second, first))
        return kept, arrived

    def over(near):
        return lax.ppermute(order.open(near), "occ", [(1, 0)])

    ca = cycle_amplitudes
    b0 = columns_of(0)
    order.phase(b0)
    own0 = move(b0, MID_TO_MID)
    a0 = move(rows_of(0), END_TO_MID)
    b3, b1 = columns_of(3), columns_of(1)
    one = batch((3, ca, b3), (1, ca, b1))
    one.send()
    one.keep()

    order.phase(own0, a0)
    own3 = move(b3, MID_TO_MID)
    swap3 = move(b3, NEIGHBOUR)
    one.swap()
    two = batch((0, ca, own0), (0, a0, own0))
    two.send()
    two.keep()
    s3, s1 = one.finish()

    order.phase(own3, swap3)
    relay3 = move(swap3, MID_TO_MID)
    b0_in = move(b0, END_TO_MID)
    on3 = move(own3, MID_TO_END)
    two.swap()
    b2 = columns_of(2)
    three = batch((3, ca, swap3), (0, ca, b0), (0, a0, b0))
    three.send()
    three.keep()
    f0 = two.finish()

    order.phase(relay3, b0_in, on3)
    relay0 = move(b0_in, MID_TO_MID)
    a1 = move(rows_of(1), END_TO_MID)
    on_relay3 = move(relay3, MID_TO_END)
    three.swap()
    four = batch((2, ca, b2), (0, ca, b0_in), (3, ca, jnp.where(at_end, order.open(on3), own3)))
    four.send()
    four.keep()
    n3, *s0 = three.finish()

    order.phase(relay0, a1, on_relay3)
    own1 = move(b1, MID_TO_MID)
    a2 = move(rows_of(2), END_TO_MID)
    f0_back = move(f0[1], MID_TO_END)
    s0_back = move(s0[1], MID_TO_END)
    four.swap()
    five = batch((0, ca, relay0), (0, a0, relay0), (3, ca, jnp.where(at_end, order.open(on_relay3), relay3)))
    five.send()
    five.keep()
    s2, n0, f3 = four.finish()

    order.phase(own1, a2, f0_back, s0_back)
    own2 = move(b2, MID_TO_MID)
    swap1 = move(b1, NEIGHBOUR)
    x0a = cross(s0[0], home(f0[0], f0_back))
    five.swap()
    six = batch((1, ca, own1), (1, a1, own1))
    six.send()
    six.keep()
    *g0, g3 = five.finish()

    order.phase(own2, swap1, x0a[1])
    relay1 = move(swap1, MID_TO_MID)
    swap2 = move(b2, NEIGHBOUR)
    gathered = lax.all_gather(order.open(ladder_amplitudes), "vir", axis=0, tiled=True)
    x3a = cross(s3, f3)
    six.swap()
    seven = batch((2, ca, own2), (2, a2, own2), (1, ca, swap1))
    seven.send()
    seven.keep()
    f1 = six.finish()

    order.phase(relay1, swap2, x3a[1])
    relay2 = [move(swap2[:, :columns], MID_TO_MID)]
    g0_back = move(g0[1], MID_TO_END)
    f1_back = move(f1[1], MID_TO_END)
    x3b = cross(n3, g3)
    seven.swap()
    eight = batch((1, ca, relay1), (1, a1, relay1), (2, ca, swap2))
    eight.send()
    eight.keep()
    *f2, n1 = seven.finish()

    order.phase(relay2[0], g0_back, f1_back, x3b[1])
    relay2.append(move(swap2[:, columns:], MID_TO_MID))
    f2_back = move(f2[1], MID_TO_END)
    x0b = cross(home(n0, s0_back), home(g0[0], g0_back))
    x1a = cross(s1, home(f1[0], f1_back))
    near1_in = over(n1)
    eight.swap()
    nine = batch((2, ca, relay2[0]), (2, a2, relay2[0]))
    nine.send()
    nine.keep()
    *g1, n2 = eight.finish()

    order.phase(relay2[1], f2_back, x0b[1], x1a[1], near1_in, gathered)
    near2_in = over(n2)
    x2a = cross(s2, home(f2[0], f2_back))
    nine.swap()
    ten = batch((2, ca, relay2[1]), (2, a2, relay2[1]))
    ten.send()
    ten.keep()
    ten.swap()
    x1b = straight(n1, near1_in, g1)
    x2b = [straight(n2, near2_in, nine.finish(), slice(0, columns))]
    partial_ladder = order.step(jnp.dot(
        order.follow(gathered), ladder_integrals, preferred_element_type=F32,
    ).astype(BF16))
    ladder_residual = lax.psum_scatter(partial_ladder, ("occ", "ka"), scatter_dimension=0, tiled=True)
    x2b.append(straight(n2, near2_in, ten.finish(), slice(columns, 2 * columns)))
    out = None
    for j in range(2):
        out = put(0, j, [(x0a, j), (x1a, j), (x2a, j), (x3a, j)], out)
    for j in range(2):
        out = put(1, j, [(x0b, j), (x1b, j), (x2b[j], 0), (x3b, j)], out)
    return ladder_residual, out


def regroup(blocks):
    local_rows = blocks.shape[1]
    first_irrep = lax.axis_index("vir") * local_rows
    pieces = []
    for local_index in range(local_rows):
        permuted = jnp.bitwise_xor(first_irrep + local_index, jnp.arange(8, dtype=jnp.int32))
        pieces.append(jnp.take(blocks[:, local_index], permuted, axis=2))
    stacked = jnp.stack(pieces, axis=1)
    return jnp.transpose(stacked, (3, 1, 2, 0, 4))


def any_local(ladder_amplitudes, ladder_integrals, cycle_amplitudes, cycle_integrals):
    partial_ladder = jnp.dot(
        lax.all_gather(ladder_amplitudes, "vir", axis=0, tiled=True),
        ladder_integrals,
        preferred_element_type=F32,
    )
    summed_ladder = lax.psum_scatter(
        partial_ladder.astype(BF16), ("occ", "ka"), scatter_dimension=0, tiled=True
    )
    partial_cycle = jnp.einsum(
        "gaxk,gkny->gaxny",
        cycle_amplitudes,
        lax.all_gather(cycle_integrals, "vir", axis=2, tiled=True),
        preferred_element_type=F32,
    )
    summed_cycle = lax.psum_scatter(
        partial_cycle.astype(BF16), "ka", scatter_dimension=2, tiled=True
    )
    arranged = regroup(summed_cycle)
    cycle_residual = lax.all_to_all(arranged, "occ", split_axis=0, concat_axis=3, tiled=True)
    return (summed_ladder, cycle_residual)


def solution(mesh):
    line = (mesh.shape["vir"], mesh.shape["occ"], mesh.shape["ka"]) == (4, 2, 4)
    placed = (
        P("vir", ("occ", "ka")),
        P(("occ", "ka"), "vir"),
        P("occ", "vir", None, "ka"),
        P("occ", "ka", "vir", None),
    )
    return jax.shard_map(
        line_local if line else any_local,
        mesh=mesh,
        in_specs=placed,
        out_specs=(P(("occ", "ka"), "vir"), P("occ", "vir", "ka", None, None)),
        check_vma=False,
    )
```

time: 1590 us -> 1070 us (0.67)
  waiting for transfers between devices: 1350 us -> 538 us
  Pallas kernels: 0 us -> 265 us
  starting transfers between devices: 9.29 us -> 102 us
  matrix products: 99.2 us -> 22.3 us
  other arithmetic: 8.37 us -> 61.6 us
  local copies, waits for them, and re-layouts: 98.6 us -> 51.3 us
    all_gather x2 -> x1, waiting for transfers between devices: 944 us -> 0.02 us  [line_local(): lax.all_gather(order.open(ladder_amplitudes), 'vir', axis=0, tiled=True)]
    ppermute x0 -> x57, waiting for transfers between devices: none -> 538 us  [the longest x23 293 us: move(): return lax.ppermute(order.open(value), 'vir', route)]
    reduce_scatter x2 -> x1, waiting for transfers between devices: 357 us -> 0.01 us  [line_local(): lax.psum_scatter(partial_ladder, ('occ', 'ka'), scatter_dimension=0, tile...]
    pallas_call x0 -> x24, Pallas kernels: none -> 265 us  [the longest x10 126 us: keep_products(): pl.pallas_call(kernel, out_shape=(jax.ShapeDtypeStruct((count, rows, colu...]
    ppermute x0 -> x57, starting transfers between devices: none -> 102 us  [the longest x23 63 us: move(): return lax.ppermute(order.open(value), 'vir', route)]
    dot_general x2 -> x1, matrix products: 99.2 us -> 22.3 us  [line_local(): jnp.dot(order.follow(gathered), ladder_integrals, preferred_element_type=...]
    all_to_all x2 -> x0, local copies, waits for them, and re-layouts: 56.2 us -> none  [local(): lax.all_to_all(arranged, 'occ', split_axis=0, concat_axis=3, tiled=True)]
    all_to_all x1 -> x0, waiting for transfers between devices: 52.5 us -> none  [local(): lax.all_to_all(arranged, 'occ', split_axis=0, concat_axis=3, tiled=True)]
  transfers between devices with their start and end apart: 5 -> 59, of which waited for: 4 -> 30; matrix products, arithmetic and copies ran while one was open for 6% -> 10% of each run, Pallas kernels for 0% -> 17%
where the time goes in v3:
time: 1070 us; the launch traced here: 1050 us
  waiting for transfers between devices  538 us (50%)
  Pallas kernels  265 us (25%)
  starting transfers between devices  102 us (10%)
  other arithmetic  61.6 us (6%)
  local copies, waits for them, and re-layouts  51.3 us (5%)
  matrix products  22.3 us (2%)
  between operations  14.9 us (1%)
    ppermute x23, waiting for transfers between devices, move(): return lax.ppermute(order.open(value), 'vir', route)  293 us
    ppermute x10, waiting for transfers between devices, swap(): self.other = lax.ppermute(self.order.open(self.away), 'ka', OTHER_Y)  224 us
    pallas_call x10, Pallas kernels, keep_products(): pl.pallas_call(kernel, out_shape=(jax.ShapeDtypeStruct((count, rows, colu...  126 us
    pallas_call x10, Pallas kernels, send_products(): pl.pallas_call(kernel, out_shape=jax.ShapeDtypeStruct((count, 2, rows, co...  111 us
    ppermute x23, starting transfers between devices, move(): return lax.ppermute(order.open(value), 'vir', route)  63 us
    convert_element_type x10, other arithmetic, finish(): (self.own.astype(F32) + other.astype(F32)).astype(BF16)  32.7 us
    pallas_call x4, Pallas kernels, place(): pl.pallas_call(kernel, out_shape=jax.ShapeDtypeStruct(shape, BF16), grid_...  27.5 us
    dot_general x1, matrix products, line_local(): jnp.dot(order.follow(gathered), ladder_integrals, preferred_element_type=...  22.3 us
  transfers between devices with their start and end apart: 59, of which 30 were waited for; matrix products, arithmetic and copies ran while one was open for 10% of the time, Pallas kernels for 17%

profile of v3, /device:TPU:10, one launch (start us, length us, event | category | flops | bytes accessed | tf_op | source)
XLA Modules:
  0.0 1054.9 jit_solution(16128484136222414380)
XLA Ops:
  11.5 6.9 fusion
  23.7 10.3 send_products.10
  34.0 3.8 slice_bitcast_fusion.2
  42.6 11.6 %keep_products.10 = (bf16[2,320,1280]{2,1,0:T(8,128)(2,1)}, bf16[2,320,1280]{2,1,0:T(8,128)(2,1)}) custom-call(s32[4]{0:T(128)} %broadcast_xor_fusion.where_ref, bf16[4,2,640,1280]{3,2,1,0:T(8,128)(2,1)} %refs_0_.39, bf16[4,2,640,1280]{3,2,1,0:T(8,128)(2,1)} %refs_0_.39, bf16[1280,1280]{1,0:T(8,128)(2,1)} %bitcast.53, bf16[1280,1280]{1,0:T(8,128)(2,1)} %bitcast.49, ...), custom_call_target="tpu_custom_call" | custom-call | flops 1048576 | bytes 65536 | tf_op jit(solution)/shard_map/keep_products/pallas_call | solution.py:102
  54.2 59.0 %collective-permute-done.refs_1_.refs_2_ = bf16[2,640,1280]{2,1,0:T(8,128)(2,1)S(1)} collective-permute-done((bf16[2,640,1280]{2,1,0:T(8,128)(2,1)}, bf16[2,640,1280]{2,1,0:T(8,128)(2,1)S(1)}, u32[]{:S(2)}, u32[]{:S(2)}) %collective-permute-start) | collective-permute-done | bytes 3276832 | tf_op jit(solution)/shard_map/ppermute | solution.py:217
  115.0 9.3 send_products.11
  124.3 3.7 collective-permute-start.5
  130.5 10.6 %keep_products.11 = (bf16[2,320,1280]{2,1,0:T(8,128)(2,1)}, bf16[2,320,1280]{2,1,0:T(8,128)(2,1)}) custom-call(s32[4]{0:T(128)} %broadcast_xor_fusion.where_ref, bf16[4,2,640,1280]{3,2,1,0:T(8,128)(2,1)} %refs_0_.39, bf16[2,640,1280]{2,1,0:T(8,128)(2,1)} %copy-done.1, bf16[1280,1280]{1,0:T(8,128)(2,1)} %collective-permute-done.2.refs_2_, ...), custom_call_target="tpu_custom_call" | custom-call | flops 1048576 | bytes 65536 | tf_op jit(solution)/shard_map/keep_products/pallas_call | solution.py:102
  141.1 25.3 %collective-permute-done.3 = bf16[2,320,1280]{2,1,0:T(8,128)(2,1)} collective-permute-done((bf16[2,320,1280]{2,1,0:T(8,128)(2,1)}, bf16[2,320,1280]{2,1,0:T(8,128)(2,1)}, u32[]{:S(2)}, u32[]{:S(2)}) %collective-permute-start.3) | collective-permute-done | bytes 1638432 | tf_op jit(solution)/shard_map/ppermute | solution.py:192
  169.9 29.9 %collective-permute-done.5 = bf16[1280,1280]{1,0:T(8,128)(2,1)} collective-permute-done((bf16[1280,1280]{1,0:T(8,128)(2,1)}, bf16[1280,1280]{1,0:T(8,128)(2,1)}, u32[]{:S(2)}, u32[]{:S(2)}) %collective-permute-start.5) | collective-permute-done | bytes 3276832 | tf_op jit(solution)/shard_map/ppermute | solution.py:217
  203.0 13.3 %send_products.12 = bf16[3,2,320,1280]{3,2,1,0:T(8,128)(2,1)} custom-call(s32[4]{0:T(128)} %broadcast_xor_fusion.where_ref, bf16[4,2,640,1280]{3,2,1,0:T(8,128)(2,1)} %refs_0_.39, bf16[4,2,640,1280]{3,2,1,0:T(8,128)(2,1)} %refs_0_.39, bf16[2,640,1280]{2,1,0:T(8,128)(2,1)} %copy-done.1, bf16[1280,1280]{1,0:T(8,128)(2,1)} %copy-done.5, ...), custom_call_target="tpu_custom_call" | custom-call | flops 1048576 | bytes 65536 | tf_op jit(solution)/shard_map/send_products/pallas_call | solution.py:67
  219.9 6.7 collective-permute-start.11
  232.5 15.2 %keep_products.12 = (bf16[3,320,1280]{2,1,0:T(8,128)(2,1)}, bf16[3,320,1280]{2,1,0:T(8,128)(2,1)}) custom-call(s32[4]{0:T(128)} %broadcast_xor_fusion.where_ref, bf16[4,2,640,1280]{3,2,1,0:T(8,128)(2,1)} %refs_0_.39, bf16[4,2,640,1280]{3,2,1,0:T(8,128)(2,1)} %refs_0_.39, bf16[2,640,1280]{2,1,0:T(8,128)(2,1)} %copy-done.1, bf16[1280,1280]{1,0:T(8,128)(2,1)} %copy-done.5, ...), custom_call_target="tpu_custom_call" | custom-call | flops 1048576 | bytes 65536 | tf_op jit(solution)/shard_map/keep_products/pallas_call | solution.py:102
  247.7 17.0 %collective-permute-done.8 = bf16[2,320,1280]{2,1,0:T(8,128)(2,1)} collective-permute-done((bf16[2,320,1280]{2,1,0:T(8,128)(2,1)}, bf16[2,320,1280]{2,1,0:T(8,128)(2,1)}, u32[]{:S(2)}, u32[]{:S(2)}) %collective-permute-start.8) | collective-permute-done | bytes 1638432 | tf_op jit(solution)/shard_map/ppermute | solution.py:192
  268.1 23.5 %collective-permute-done.7.refs_4_ = bf16[1280,1280]{1,0:T(8,128)(2,1)S(1)} collective-permute-done((bf16[1280,1280]{1,0:T(8,128)(2,1)}, bf16[1280,1280]{1,0:T(8,128)(2,1)S(1)}, u32[]{:S(2)}, u32[]{:S(2)}) %collective-permute-start.7) | collective-permute-done | bytes 3276832 | tf_op jit(solution)/shard_map/ppermute | solution.py:217
  295.6 3.9 broadcast_select_fusion.1.refs_5_
  299.5 14.2 %send_products.13 = bf16[3,2,320,1280]{3,2,1,0:T(8,128)(2,1)} custom-call(s32[4]{0:T(128)} %broadcast_xor_fusion.where_ref, bf16[4,2,640,1280]{3,2,1,0:T(8,128)(2,1)} %refs_0_.39, bf16[4,2,640,1280]{3,2,1,0:T(8,128)(2,1)} %refs_0_.39, bf16[4,2,640,1280]{3,2,1,0:T(8,128)(2,1)} %refs_0_.39, bf16[1280,1280]{1,0:T(8,128)(2,1)} %bitcast.56, ...), custom_call_target="tpu_custom_call" | custom-call | flops 1048576 | bytes 65536 | tf_op jit(solution)/shard_map/send_products/pallas_call | solution.py:67
  316.1 3.8 slice_bitcast_fusion.1
  321.2 6.9 collective-permute-start.16
  329.7 16.2 %keep_products.13 = (bf16[3,320,1280]{2,1,0:T(8,128)(2,1)}, bf16[3,320,1280]{2,1,0:T(8,128)(2,1)}) custom-call(s32[4]{0:T(128)} %broadcast_xor_fusion.where_ref, bf16[4,2,640,1280]{3,2,1,0:T(8,128)(2,1)} %refs_0_.39, bf16[4,2,640,1280]{3,2,1,0:T(8,128)(2,1)} %refs_0_.39, bf16[4,2,640,1280]{3,2,1,0:T(8,128)(2,1)} %refs_0_.39, bf16[1280,1280]{1,0:T(8,128)(2,1)} %bitcast.57, ...), custom_call_target="tpu_custom_call" | custom-call | flops 1048576 | bytes 65536 | tf_op jit(solution)/shard_map/keep_products/pallas_call | solution.py:102
  345.9 37.9 %collective-permute-done.13 = bf16[3,320,1280]{2,1,0:T(8,128)(2,1)} collective-permute-done((bf16[3,320,1280]{2,1,0:T(8,128)(2,1)}, bf16[3,320,1280]{2,1,0:T(8,128)(2,1)}, u32[]{:S(2)}, u32[]{:S(2)}) %collective-permute-start.13) | collective-permute-done | bytes 2457632 | tf_op jit(solution)/shard_map/ppermute | solution.py:192
  383.8 4.5 add_convert_fusion.4
  389.3 6.1 collective-permute-done.15.refs_1_
  396.9 3.9 broadcast_select_fusion.refs_4_
  400.8 13.3 %send_products.14 = bf16[3,2,320,1280]{3,2,1,0:T(8,128)(2,1)} custom-call(s32[4]{0:T(128)} %broadcast_xor_fusion.where_ref, bf16[4,2,640,1280]{3,2,1,0:T(8,128)(2,1)} %refs_0_.39, bf16[2,640,1280]{2,1,0:T(8,128)(2,1)} %copy-done.1, bf16[4,2,640,1280]{3,2,1,0:T(8,128)(2,1)} %refs_0_.39, bf16[1280,1280]{1,0:T(8,128)(2,1)} %collective-permute-done.12.refs_3_, ...), custom_call_target="tpu_custom_call" | custom-call | flops 1048576 | bytes 65536 | tf_op jit(solution)/shard_map/send_products/pallas_call | solution.py:67
  417.4 3.9 slice_bitcast_fusion
  425.6 5.7 collective-permute-start.21
  435.0 15.2 %keep_products.14 = (bf16[3,320,1280]{2,1,0:T(8,128)(2,1)}, bf16[3,320,1280]{2,1,0:T(8,128)(2,1)}) custom-call(s32[4]{0:T(128)} %broadcast_xor_fusion.where_ref, bf16[4,2,640,1280]{3,2,1,0:T(8,128)(2,1)} %refs_0_.39, bf16[2,640,1280]{2,1,0:T(8,128)(2,1)} %copy-done.1, bf16[4,2,640,1280]{3,2,1,0:T(8,128)(2,1)} %refs_0_.39, ...), custom_call_target="tpu_custom_call" | custom-call | flops 1048576 | bytes 65536 | tf_op jit(solution)/shard_map/keep_products/pallas_call | solution.py:102
  450.2 28.2 %collective-permute-done.18 = bf16[3,320,1280]{2,1,0:T(8,128)(2,1)} collective-permute-done((bf16[3,320,1280]{2,1,0:T(8,128)(2,1)}, bf16[3,320,1280]{2,1,0:T(8,128)(2,1)}, u32[]{:S(2)}, u32[]{:S(2)}) %collective-permute-start.18) | collective-permute-done | bytes 2457632 | tf_op jit(solution)/shard_map/ppermute | solution.py:192
  478.4 4.4 add_convert_fusion.3
  482.8 6.8 collective-permute-done.19.refs_2_
  489.7 6.7 collective-permute-done.20.refs_1_
  496.4 9.7 send_products.15
  513.6 10.8 %keep_products.15 = (bf16[2,320,1280]{2,1,0:T(8,128)(2,1)}, bf16[2,320,1280]{2,1,0:T(8,128)(2,1)}) custom-call(s32[4]{0:T(128)} %broadcast_xor_fusion.where_ref, bf16[4,2,640,1280]{3,2,1,0:T(8,128)(2,1)} %refs_0_.39, bf16[2,640,1280]{2,1,0:T(8,128)(2,1)} %copy-done.2, bf16[1280,1280]{1,0:T(8,128)(2,1)} %collective-permute-done.19.refs_2_, ...), custom_call_target="tpu_custom_call" | custom-call | flops 1048576 | bytes 65536 | tf_op jit(solution)/shard_map/keep_products/pallas_call | solution.py:102
  524.4 40.5 %collective-permute-done.23 = bf16[3,320,1280]{2,1,0:T(8,128)(2,1)} collective-permute-done((bf16[3,320,1280]{2,1,0:T(8,128)(2,1)}, bf16[3,320,1280]{2,1,0:T(8,128)(2,1)}, u32[]{:S(2)}, u32[]{:S(2)}) %collective-permute-start.23) | collective-permute-done | bytes 2457632 | tf_op jit(solution)/shard_map/ppermute | solution.py:192
  564.9 3.7 add_convert_fusion.2
  568.6 13.1 %collective-permute-done.25.refs_3_ = bf16[1280,1280]{1,0:T(8,128)(2,1)} collective-permute-done((bf16[1280,1280]{1,0:T(8,128)(2,1)}, bf16[1280,1280]{1,0:T(8,128)(2,1)}, u32[]{:S(2)}, u32[]{:S(2)}) %collective-permute-start.25) | collective-permute-done | bytes 3276832 | tf_op jit(solution)/shard_map/ppermute | solution.py:217
  582.3 13.3 %send_products.16 = bf16[3,2,320,1280]{3,2,1,0:T(8,128)(2,1)} custom-call(s32[4]{0:T(128)} %broadcast_xor_fusion.where_ref, bf16[4,2,640,1280]{3,2,1,0:T(8,128)(2,1)} %refs_0_.39, bf16[2,640,1280]{2,1,0:T(8,128)(2,1)} %copy-done, bf16[4,2,640,1280]{3,2,1,0:T(8,128)(2,1)} %refs_0_.39, bf16[1280,1280]{1,0:T(8,128)(2,1)} %collective-permute-done.25.refs_3_, ...), custom_call_target="tpu_custom_call" | custom-call | flops 1048576 | bytes 65536 | tf_op jit(solution)/shard_map/send_products/pallas_call | solution.py:67
  596.0 3.6 collective-permute-start.31
  606.8 15.5 %keep_products.16 = (bf16[3,320,1280]{2,1,0:T(8,128)(2,1)}, bf16[3,320,1280]{2,1,0:T(8,128)(2,1)}) custom-call(s32[4]{0:T(128)} %broadcast_xor_fusion.where_ref, bf16[4,2,640,1280]{3,2,1,0:T(8,128)(2,1)} %refs_0_.39, bf16[2,640,1280]{2,1,0:T(8,128)(2,1)} %copy-done, bf16[4,2,640,1280]{3,2,1,0:T(8,128)(2,1)} %refs_0_.39, ...), custom_call_target="tpu_custom_call" | custom-call | flops 1048576 | bytes 65536 | tf_op jit(solution)/shard_map/keep_products/pallas_call | solution.py:102
  622.2 15.1 %collective-permute-done.29 = bf16[2,320,1280]{2,1,0:T(8,128)(2,1)} collective-permute-done((bf16[2,320,1280]{2,1,0:T(8,128)(2,1)}, bf16[2,320,1280]{2,1,0:T(8,128)(2,1)}, u32[]{:S(2)}, u32[]{:S(2)}) %collective-permute-start.29) | collective-permute-done | bytes 1638432 | tf_op jit(solution)/shard_map/ppermute | solution.py:192
  640.9 126.4 %collective-permute-done.28.refs_4_ = bf16[1280,1280]{1,0:T(8,128)(2,1)} collective-permute-done((bf16[1280,1280]{1,0:T(8,128)(2,1)S(1)}, bf16[1280,1280]{1,0:T(8,128)(2,1)}, u32[]{:S(2)}, u32[]{:S(2)}) %collective-permute-start.28) | collective-permute-done | bytes 3276832 | tf_op jit(solution)/shard_map/ppermute | solution.py:217
  767.3 11.8 %collective-permute-done.31.refs_3_ = bf16[1280,1280]{1,0:T(8,128)(2,1)} collective-permute-done((bf16[1280,1280]{1,0:T(8,128)(2,1)}, bf16[1280,1280]{1,0:T(8,128)(2,1)}, u32[]{:S(2)}, u32[]{:S(2)}) %collective-permute-start.31) | collective-permute-done | bytes 3276832 | tf_op jit(solution)/shard_map/ppermute | solution.py:217
  779.1 13.3 %send_products.17 = bf16[3,2,320,1280]{3,2,1,0:T(8,128)(2,1)} custom-call(s32[4]{0:T(128)} %broadcast_xor_fusion.where_ref, bf16[4,2,640,1280]{3,2,1,0:T(8,128)(2,1)} %refs_0_.39, bf16[2,640,1280]{2,1,0:T(8,128)(2,1)} %copy-done.2, bf16[4,2,640,1280]{3,2,1,0:T(8,128)(2,1)} %refs_0_.39, bf16[1280,1280]{1,0:T(8,128)(2,1)} %collective-permute-done.31.refs_3_, ...), custom_call_target="tpu_custom_call" | custom-call | flops 1048576 | bytes 65536 | tf_op jit(solution)/shard_map/send_products/pallas_call | solution.py:67
  796.9 4.0 fusion.1
  801.0 4.2 collective-permute-start.33
  811.7 15.2 %keep_products.17 = (bf16[3,320,1280]{2,1,0:T(8,128)(2,1)}, bf16[3,320,1280]{2,1,0:T(8,128)(2,1)}) custom-call(s32[4]{0:T(128)} %broadcast_xor_fusion.where_ref, bf16[4,2,640,1280]{3,2,1,0:T(8,128)(2,1)} %refs_0_.39, bf16[2,640,1280]{2,1,0:T(8,128)(2,1)} %copy-done.2, bf16[4,2,640,1280]{3,2,1,0:T(8,128)(2,1)} %refs_0_.39, ...), custom_call_target="tpu_custom_call" | custom-call | flops 1048576 | bytes 65536 | tf_op jit(solution)/shard_map/keep_products/pallas_call | solution.py:102
  826.9 21.5 %collective-permute-done.34 = bf16[3,320,1280]{2,1,0:T(8,128)(2,1)} collective-permute-done((bf16[3,320,1280]{2,1,0:T(8,128)(2,1)}, bf16[3,320,1280]{2,1,0:T(8,128)(2,1)}, u32[]{:S(2)}, u32[]{:S(2)}) %collective-permute-start.34) | collective-permute-done | bytes 2457632 | tf_op jit(solution)/shard_map/ppermute | solution.py:192
  854.7 7.4 send_products.18
  862.1 4.2 collective-permute-start.41
  873.6 33.3 %collective-permute-done.40 = bf16[3,320,1280]{2,1,0:T(8,128)(2,1)} collective-permute-done((bf16[3,320,1280]{2,1,0:T(8,128)(2,1)}, bf16[3,320,1280]{2,1,0:T(8,128)(2,1)}, u32[]{:S(2)}, u32[]{:S(2)}) %collective-permute-start.40) | collective-permute-done | bytes 2457632 | tf_op jit(solution)/shard_map/ppermute | solution.py:192
  910.4 7.9 keep_products.18
  921.3 4.7 collective-permute-done.45
  926.1 7.2 send_products.19
  942.5 7.9 keep_products.19
  950.4 5.2 collective-permute-done.46
  957.8 22.3 %convolution_convert_fusion = bf16[512,2048]{1,0:T(8,128)(2,1)} fusion(bf16[512,6656]{1,0:T(8,128)(2,1)} %all-gather.2.cloned.1.call-done, bf16[6656,2048]{1,0:T(8,128)(2,1)} %param.6), kind=kOutput, calls=%fused_computation.13 | convolution fusion | flops 13959692288 | bytes 36175872 | tf_op jit(solution)/shard_map/dot_general | solution.py:355
  988.7 5.1 collective-permute-start.52
  993.8 6.8 place.4.refs_8_
  1000.6 7.0 place.5.refs_8_
  1019.3 4.2 collective-permute-done.54
  1023.5 8.1 collective-permute-done.50
  1034.1 6.8 place.6.refs_8_
  1041.0 6.8 place.7
  (182 shorter events, 145.5 us)
Async XLA Ops:
  7.2 914.1 %all-gather.2.cloned.1.call-start = ((), (), s32[]{:S(2)}) async-start(), calls=%async_computation.1 | async-start | bytes 8519680 | tf_op jit(solution)/shard_map/all_gather | solution.py:314
  34.0 8.6 collective-permute-start.1
  37.8 75.4 %collective-permute-start = (bf16[2,640,1280]{2,1,0:T(8,128)(2,1)}, bf16[2,640,1280]{2,1,0:T(8,128)(2,1)S(1)}, u32[]{:S(2)}, u32[]{:S(2)}) collective-permute-start(bf16[2,640,1280]{2,1,0:T(8,128)(2,1)} %slice_bitcast_fusion.2), channel_id=1, source_target_pairs={{0,8},{24,16},{1,9},{25,17},{2,10},{26,18},{3,11},{27,19},{4,12},{... | collective-permute-start | bytes 9830408 | tf_op jit(solution)/shard_map/ppermute | solution.py:217
  39.1 75.5 %collective-permute-start.2 = (bf16[1280,1280]{1,0:T(8,128)(2,1)}, bf16[1280,1280]{1,0:T(8,128)(2,1)}, u32[]{:S(2)}, u32[]{:S(2)}) collective-permute-start(bf16[1280,1280]{1,0:T(8,128)(2,1)} %bitcast.33.refs_4_), channel_id=1, source_target_pairs={{8,16},{16,8},{9,17},{17,9},{10,18},{18,10},{11,19},{19,11},{12,20... | collective-permute-start | bytes 9830408 | tf_op jit(solution)/shard_map/ppermute | solution.py:217
  124.3 6.2 collective-permute-start.4
  124.3 75.5 %collective-permute-start.5 = (bf16[1280,1280]{1,0:T(8,128)(2,1)}, bf16[1280,1280]{1,0:T(8,128)(2,1)}, u32[]{:S(2)}, u32[]{:S(2)}) collective-permute-start(bf16[1280,1280]{1,0:T(8,128)(2,1)} %bitcast.54), channel_id=1, source_target_pairs={{8,16},{16,8},{9,17},{17,9},{10,18},{18,10},{11,19},{19,11},{12,20... | collective-permute-start | bytes 9830408 | tf_op jit(solution)/shard_map/ppermute | solution.py:217
  128.0 73.3 %collective-permute-start.6 = (bf16[1280,1280]{1,0:T(8,128)(2,1)}, bf16[1280,1280]{1,0:T(8,128)(2,1)S(1)}, u32[]{:S(2)}, u32[]{:S(2)}) collective-permute-start(bf16[1280,1280]{1,0:T(8,128)(2,1)} %bitcast.55), channel_id=1, source_target_pairs={{0,8},{8,0},{16,24},{24,16},{1,9},{9,1},{17,25},{25,17},{2,10},{10... | collective-permute-start | bytes 9830408 | tf_op jit(solution)/shard_map/ppermute | solution.py:217
  128.1 38.3 %collective-permute-start.3 = (bf16[2,320,1280]{2,1,0:T(8,128)(2,1)}, bf16[2,320,1280]{2,1,0:T(8,128)(2,1)}, u32[]{:S(2)}, u32[]{:S(2)}) collective-permute-start(bf16[2,320,1280]{2,1,0:T(8,128)(2,1)} %get-tuple-element.135), channel_id=1, source_target_pairs={{0,2},{2,0},{1,3},{3,1},{4,6},{6,4},{5,7},{7,5},{8,10},{10,8},{9,1... | collective-permute-start | bytes 4915208 | tf_op jit(solution)/shard_map/ppermute | solution.py:192
  216.3 16.2 %collective-permute-start.9 = (bf16[3,2,320,1280]{3,2,1,0:T(8,128)(2,1)}, bf16[3,2,320,1280]{3,2,1,0:T(8,128)(2,1)}, u32[]{:S(2)}, u32[]{:S(2)}) collective-permute-start(bf16[3,2,320,1280]{3,2,1,0:T(8,128)(2,1)} %send_products.12), channel_id=1, source_target_pairs={{0,1},{1,0},{2,3},{3,2},{4,5},{5,4},{6,7},{7,6},{8,9},{9,8},{10,11... | collective-permute-start | bytes 14745608 | tf_op jit(solution)/shard_map/ppermute | solution.py:184
  216.3 75.4 %collective-permute-start.7 = (bf16[1280,1280]{1,0:T(8,128)(2,1)}, bf16[1280,1280]{1,0:T(8,128)(2,1)S(1)}, u32[]{:S(2)}, u32[]{:S(2)}) collective-permute-start(bf16[1280,1280]{1,0:T(8,128)(2,1)} %bitcast.33.refs_4_), channel_id=1, source_target_pairs={{0,8},{24,16},{1,9},{25,17},{2,10},{26,18},{3,11},{27,19},{4,12},{... | collective-permute-start | bytes 9830408 | tf_op jit(solution)/shard_map/ppermute | solution.py:217
  217.5 75.5 %collective-permute-start.10 = (bf16[1280,1280]{1,0:T(8,128)(2,1)}, bf16[1280,1280]{1,0:T(8,128)(2,1)}, u32[]{:S(2)}, u32[]{:S(2)}) collective-permute-start(bf16[1280,1280]{1,0:T(8,128)(2,1)} %copy-done.5), channel_id=1, source_target_pairs={{8,16},{16,8},{9,17},{17,9},{10,18},{18,10},{11,19},{19,11},{12,20... | collective-permute-start | bytes 9830408 | tf_op jit(solution)/shard_map/ppermute | solution.py:217
  219.9 75.7 %collective-permute-start.11 = (bf16[1280,1280]{1,0:T(8,128)(2,1)}, bf16[1280,1280]{1,0:T(8,128)(2,1)}, u32[]{:S(2)}, u32[]{:S(2)}) collective-permute-start(bf16[1280,1280]{1,0:T(8,128)(2,1)} %collective-permute-done.5), channel_id=1, source_target_pairs={{8,0},{16,24},{9,1},{17,25},{10,2},{18,26},{11,3},{19,27},{12,4},{... | collective-permute-start | bytes 9830408 | tf_op jit(solution)/shard_map/ppermute | solution.py:217
  226.6 38.0 %collective-permute-start.8 = (bf16[2,320,1280]{2,1,0:T(8,128)(2,1)}, bf16[2,320,1280]{2,1,0:T(8,128)(2,1)}, u32[]{:S(2)}, u32[]{:S(2)}) collective-permute-start(bf16[2,320,1280]{2,1,0:T(8,128)(2,1)} %get-tuple-element.143), channel_id=1, source_target_pairs={{0,2},{2,0},{1,3},{3,1},{4,6},{6,4},{5,7},{7,5},{8,10},{10,8},{9,1... | collective-permute-start | bytes 4915208 | tf_op jit(solution)/shard_map/ppermute | solution.py:192
  313.8 15.9 %collective-permute-start.14 = (bf16[3,2,320,1280]{3,2,1,0:T(8,128)(2,1)}, bf16[3,2,320,1280]{3,2,1,0:T(8,128)(2,1)}, u32[]{:S(2)}, u32[]{:S(2)}) collective-permute-start(bf16[3,2,320,1280]{3,2,1,0:T(8,128)(2,1)} %send_products.13), channel_id=1, source_target_pairs={{0,1},{1,0},{2,3},{3,2},{4,5},{5,4},{6,7},{7,6},{8,9},{9,8},{10,11... | collective-permute-start | bytes 14745608 | tf_op jit(solution)/shard_map/ppermute | solution.py:184
  313.8 75.5 %collective-permute-start.12 = (bf16[1280,1280]{1,0:T(8,128)(2,1)}, bf16[1280,1280]{1,0:T(8,128)(2,1)}, u32[]{:S(2)}, u32[]{:S(2)}) collective-permute-start(bf16[1280,1280]{1,0:T(8,128)(2,1)} %copy-done.4), channel_id=1, source_target_pairs={{8,16},{16,8},{9,17},{17,9},{10,18},{18,10},{11,19},{19,11},{12,20... | collective-permute-start | bytes 9830408 | tf_op jit(solution)/shard_map/ppermute | solution.py:217
  319.9 75.5 %collective-permute-start.15 = (bf16[2,640,1280]{2,1,0:T(8,128)(2,1)}, bf16[2,640,1280]{2,1,0:T(8,128)(2,1)S(1)}, u32[]{:S(2)}, u32[]{:S(2)}) collective-permute-start(bf16[2,640,1280]{2,1,0:T(8,128)(2,1)} %slice_bitcast_fusion.1), channel_id=1, source_target_pairs={{0,8},{24,16},{1,9},{25,17},{2,10},{26,18},{3,11},{27,19},{4,12},{... | collective-permute-start | bytes 9830408 | tf_op jit(solution)/shard_map/ppermute | solution.py:217
  321.2 75.7 %collective-permute-start.16 = (bf16[1280,1280]{1,0:T(8,128)(2,1)}, bf16[1280,1280]{1,0:T(8,128)(2,1)}, u32[]{:S(2)}, u32[]{:S(2)}) collective-permute-start(bf16[1280,1280]{1,0:T(8,128)(2,1)} %collective-permute-done.10), channel_id=1, source_target_pairs={{8,0},{16,24},{9,1},{17,25},{10,2},{18,26},{11,3},{19,27},{12,4},{... | collective-permute-start | bytes 9830408 | tf_op jit(solution)/shard_map/ppermute | solution.py:217
  328.1 55.7 %collective-permute-start.13 = (bf16[3,320,1280]{2,1,0:T(8,128)(2,1)}, bf16[3,320,1280]{2,1,0:T(8,128)(2,1)}, u32[]{:S(2)}, u32[]{:S(2)}) collective-permute-start(bf16[3,320,1280]{2,1,0:T(8,128)(2,1)} %get-tuple-element.151), channel_id=1, source_target_pairs={{0,2},{2,0},{1,3},{3,1},{4,6},{6,4},{5,7},{7,5},{8,10},{10,8},{9,1... | collective-permute-start | bytes 7372808 | tf_op jit(solution)/shard_map/ppermute | solution.py:192
  414.1 18.5 %collective-permute-start.17 = (bf16[3,2,320,1280]{3,2,1,0:T(8,128)(2,1)}, bf16[3,2,320,1280]{3,2,1,0:T(8,128)(2,1)}, u32[]{:S(2)}, u32[]{:S(2)}) collective-permute-start(bf16[3,2,320,1280]{3,2,1,0:T(8,128)(2,1)} %send_products.14), channel_id=1, source_target_pairs={{0,1},{1,0},{2,3},{3,2},{4,5},{5,4},{6,7},{7,6},{8,9},{9,8},{10,11... | collective-permute-start | bytes 14745608 | tf_op jit(solution)/shard_map/ppermute | solution.py:184
  414.1 75.5 %collective-permute-start.19 = (bf16[1280,1280]{1,0:T(8,128)(2,1)}, bf16[1280,1280]{1,0:T(8,128)(2,1)}, u32[]{:S(2)}, u32[]{:S(2)}) collective-permute-start(bf16[1280,1280]{1,0:T(8,128)(2,1)} %bitcast.50), channel_id=1, source_target_pairs={{8,16},{16,8},{9,17},{17,9},{10,18},{18,10},{11,19},{19,11},{12,20... | collective-permute-start | bytes 9830408 | tf_op jit(solution)/shard_map/ppermute | solution.py:217
  421.3 75.1 %collective-permute-start.20 = (bf16[2,640,1280]{2,1,0:T(8,128)(2,1)}, bf16[2,640,1280]{2,1,0:T(8,128)(2,1)S(1)}, u32[]{:S(2)}, u32[]{:S(2)}) collective-permute-start(bf16[2,640,1280]{2,1,0:T(8,128)(2,1)} %slice_bitcast_fusion), channel_id=1, source_target_pairs={{0,8},{24,16},{1,9},{25,17},{2,10},{26,18},{3,11},{27,19},{4,12},{... | collective-permute-start | bytes 9830408 | tf_op jit(solution)/shard_map/ppermute | solution.py:217
  422.7 55.7 %collective-permute-start.18 = (bf16[3,320,1280]{2,1,0:T(8,128)(2,1)}, bf16[3,320,1280]{2,1,0:T(8,128)(2,1)}, u32[]{:S(2)}, u32[]{:S(2)}) collective-permute-start(bf16[3,320,1280]{2,1,0:T(8,128)(2,1)} %get-tuple-element.169), channel_id=1, source_target_pairs={{0,2},{2,0},{1,3},{3,1},{4,6},{6,4},{5,7},{7,5},{8,10},{10,8},{9,1... | collective-permute-start | bytes 7372808 | tf_op jit(solution)/shard_map/ppermute | solution.py:192
  425.6 57.3 %collective-permute-start.21 = (bf16[2,160,1280]{2,1,0:T(8,128)(2,1)}, bf16[2,160,1280]{2,1,0:T(8,128)(2,1)}, u32[]{:S(2)}, u32[]{:S(2)}) collective-permute-start(bf16[2,160,1280]{2,1,0:T(8,128)(2,1)} %bitcast.3), channel_id=1, source_target_pairs={{8,0},{16,24},{9,1},{17,25},{10,2},{18,26},{11,3},{19,27},{12,4},{... | collective-permute-start | bytes 2457608 | tf_op jit(solution)/shard_map/ppermute | solution.py:217
  432.6 50.2 %collective-permute-start.22 = (bf16[2,160,1280]{2,1,0:T(8,128)(2,1)}, bf16[2,160,1280]{2,1,0:T(8,128)(2,1)}, u32[]{:S(2)}, u32[]{:S(2)}) collective-permute-start(bf16[2,160,1280]{2,1,0:T(8,128)(2,1)} %bitcast.4), channel_id=1, source_target_pairs={{8,0},{16,24},{9,1},{17,25},{10,2},{18,26},{11,3},{19,27},{12,4},{... | collective-permute-start | bytes 2457608 | tf_op jit(solution)/shard_map/ppermute | solution.py:217
  506.1 7.5 collective-permute-start.24
  506.1 75.5 %collective-permute-start.25 = (bf16[1280,1280]{1,0:T(8,128)(2,1)}, bf16[1280,1280]{1,0:T(8,128)(2,1)}, u32[]{:S(2)}, u32[]{:S(2)}) collective-permute-start(bf16[1280,1280]{1,0:T(8,128)(2,1)} %bitcast.58), channel_id=1, source_target_pairs={{8,16},{16,8},{9,17},{17,9},{10,18},{18,10},{11,19},{19,11},{12,20... | collective-permute-start | bytes 9830408 | tf_op jit(solution)/shard_map/ppermute | solution.py:217
  508.9 73.4 %collective-permute-start.26 = (bf16[1280,1280]{1,0:T(8,128)(2,1)}, bf16[1280,1280]{1,0:T(8,128)(2,1)}, u32[]{:S(2)}, u32[]{:S(2)}) collective-permute-start(bf16[1280,1280]{1,0:T(8,128)(2,1)} %bitcast.51), channel_id=1, source_target_pairs={{0,8},{8,0},{16,24},{24,16},{1,9},{9,1},{17,25},{25,17},{2,10},{10... | collective-permute-start | bytes 9830408 | tf_op jit(solution)/shard_map/ppermute | solution.py:217
  509.0 55.9 %collective-permute-start.23 = (bf16[3,320,1280]{2,1,0:T(8,128)(2,1)}, bf16[3,320,1280]{2,1,0:T(8,128)(2,1)}, u32[]{:S(2)}, u32[]{:S(2)}) collective-permute-start(bf16[3,320,1280]{2,1,0:T(8,128)(2,1)} %get-tuple-element.176), channel_id=1, source_target_pairs={{0,2},{2,0},{1,3},{3,1},{4,6},{6,4},{5,7},{7,5},{8,10},{10,8},{9,1... | collective-permute-start | bytes 7372808 | tf_op jit(solution)/shard_map/ppermute | solution.py:192
  513.1 51.8 %copy-start.18 = (bf16[3,320,1280]{2,1,0:T(8,128)(2,1)S(1)}, bf16[3,320,1280]{2,1,0:T(8,128)(2,1)}, u32[]{:S(2)}) copy-start(bf16[3,320,1280]{2,1,0:T(8,128)(2,1)} %get-tuple-element.166) | copy-start | bytes 7372804
  513.1 55.5 %collective-permute-start.27 = (bf16[2,160,1280]{2,1,0:T(8,128)(2,1)}, bf16[2,160,1280]{2,1,0:T(8,128)(2,1)}, u32[]{:S(2)}, u32[]{:S(2)}) collective-permute-start(bf16[2,160,1280]{2,1,0:T(8,128)(2,1)} %get-tuple-element.276), channel_id=1, source_target_pairs={{0,4},{4,0},{1,5},{5,1},{2,6},{6,2},{3,7},{7,3},{8,12},{12,8},{9,1... | collective-permute-start | bytes 2457608 | tf_op jit(solution)/shard_map/ppermute | solution.py:222
  568.6 27.1 %copy-start.3 = (bf16[160,8,2,640]{3,1,2,0:T(8,128)(2,1)S(1)}, bf16[160,8,2,640]{3,1,2,0:T(8,128)(2,1)}, u32[]{:S(2)}) copy-start(bf16[160,8,2,640]{3,1,2,0:T(8,128)(2,1)} %copy.13) | copy-start | bytes 9830404
  595.6 11.2 %collective-permute-start.30 = (bf16[3,2,320,1280]{3,2,1,0:T(8,128)(2,1)}, bf16[3,2,320,1280]{3,2,1,0:T(8,128)(2,1)}, u32[]{:S(2)}, u32[]{:S(2)}) collective-permute-start(bf16[3,2,320,1280]{3,2,1,0:T(8,128)(2,1)} %send_products.16), channel_id=1, source_target_pairs={{0,1},{1,0},{2,3},{3,2},{4,5},{5,4},{6,7},{7,6},{8,9},{9,8},{10,11... | collective-permute-start | bytes 14745608 | tf_op jit(solution)/shard_map/ppermute | solution.py:184
  595.6 171.6 %collective-permute-start.28 = (bf16[1280,1280]{1,0:T(8,128)(2,1)S(1)}, bf16[1280,1280]{1,0:T(8,128)(2,1)}, u32[]{:S(2)}, u32[]{:S(2)}) collective-permute-start(bf16[1280,1280]{1,0:T(8,128)(2,1)S(1)} %bitcast.59), channel_id=1, source_target_pairs={{0,8},{8,0},{16,24},{24,16},{1,9},{9,1},{17,25},{25,17},{2,10},{10... | collective-permute-start | bytes 9830408 | tf_op jit(solution)/shard_map/ppermute | solution.py:217
  596.0 183.1 %collective-permute-start.31 = (bf16[1280,1280]{1,0:T(8,128)(2,1)}, bf16[1280,1280]{1,0:T(8,128)(2,1)}, u32[]{:S(2)}, u32[]{:S(2)}) collective-permute-start(bf16[1280,1280]{1,0:T(8,128)(2,1)} %collective-permute-done.26.refs_4_), channel_id=1, source_target_pairs={{8,16},{16,8},{9,17},{17,9},{10,18},{18,10},{11,19},{19,11},{12,20... | collective-permute-start | bytes 9830408 | tf_op jit(solution)/shard_map/ppermute | solution.py:217
  599.6 37.8 %collective-permute-start.29 = (bf16[2,320,1280]{2,1,0:T(8,128)(2,1)}, bf16[2,320,1280]{2,1,0:T(8,128)(2,1)}, u32[]{:S(2)}, u32[]{:S(2)}) collective-permute-start(bf16[2,320,1280]{2,1,0:T(8,128)(2,1)} %get-tuple-element.190), channel_id=1, source_target_pairs={{0,2},{2,0},{1,3},{3,1},{4,6},{6,4},{5,7},{7,5},{8,10},{10,8},{9,1... | collective-permute-start | bytes 4915208 | tf_op jit(solution)/shard_map/ppermute | solution.py:192
  606.2 34.7 %collective-permute-start.32 = (bf16[2,160,1280]{2,1,0:T(8,128)(2,1)}, bf16[2,160,1280]{2,1,0:T(8,128)(2,1)}, u32[]{:S(2)}, u32[]{:S(2)}) collective-permute-start(bf16[2,160,1280]{2,1,0:T(8,128)(2,1)} %get-tuple-element.272), channel_id=1, source_target_pairs={{0,4},{4,0},{1,5},{5,1},{2,6},{6,2},{3,7},{7,3},{8,12},{12,8},{9,1... | collective-permute-start | bytes 2457608 | tf_op jit(solution)/shard_map/ppermute | solution.py:222
  606.7 441.1 %reduce-scatter.2.cloned.1.call-start = ((), (), s32[]{:S(2)}) async-start(), calls=%async_computation.2 | async-start | bytes 2359296 | tf_op jit(solution)/shard_map/reduce_scatter | solution.py:358
  792.4 18.8 %collective-permute-start.35 = (bf16[3,2,320,1280]{3,2,1,0:T(8,128)(2,1)}, bf16[3,2,320,1280]{3,2,1,0:T(8,128)(2,1)}, u32[]{:S(2)}, u32[]{:S(2)}) collective-permute-start(bf16[3,2,320,1280]{3,2,1,0:T(8,128)(2,1)} %send_products.17), channel_id=1, source_target_pairs={{0,1},{1,0},{2,3},{3,2},{4,5},{5,4},{6,7},{7,6},{8,9},{9,8},{10,11... | collective-permute-start | bytes 14745608 | tf_op jit(solution)/shard_map/ppermute | solution.py:184
  792.4 56.1 %collective-permute-start.34 = (bf16[3,320,1280]{2,1,0:T(8,128)(2,1)}, bf16[3,320,1280]{2,1,0:T(8,128)(2,1)}, u32[]{:S(2)}, u32[]{:S(2)}) collective-permute-start(bf16[3,320,1280]{2,1,0:T(8,128)(2,1)} %get-tuple-element.200), channel_id=1, source_target_pairs={{0,2},{2,0},{1,3},{3,1},{4,6},{6,4},{5,7},{7,5},{8,10},{10,8},{9,1... | collective-permute-start | bytes 7372808 | tf_op jit(solution)/shard_map/ppermute | solution.py:192
  801.0 50.5 %collective-permute-start.33 = (bf16[1280,640]{1,0:T(8,128)(2,1)}, bf16[1280,640]{1,0:T(8,128)(2,1)S(1)}, u32[]{:S(2)}, u32[]{:S(2)}) collective-permute-start(bf16[1280,640]{1,0:T(8,128)(2,1)} %get-tuple-element.198), channel_id=1, source_target_pairs={{8,16},{16,8},{9,17},{17,9},{10,18},{18,10},{11,19},{19,11},{12,20... | collective-permute-start | bytes 4915208 | tf_op jit(solution)/shard_map/ppermute | solution.py:217
  806.2 45.2 %collective-permute-start.36 = (bf16[2,160,1280]{2,1,0:T(8,128)(2,1)}, bf16[2,160,1280]{2,1,0:T(8,128)(2,1)}, u32[]{:S(2)}, u32[]{:S(2)}) collective-permute-start(bf16[2,160,1280]{2,1,0:T(8,128)(2,1)} %bitcast.9), channel_id=1, source_target_pairs={{8,0},{16,24},{9,1},{17,25},{10,2},{18,26},{11,3},{19,27},{12,4},{... | collective-permute-start | bytes 2457608 | tf_op jit(solution)/shard_map/ppermute | solution.py:217
  808.4 43.0 %collective-permute-start.37 = (bf16[2,160,1280]{2,1,0:T(8,128)(2,1)}, bf16[2,160,1280]{2,1,0:T(8,128)(2,1)S(1)}, u32[]{:S(2)}, u32[]{:S(2)}) collective-permute-start(bf16[2,160,1280]{2,1,0:T(8,128)(2,1)} %bitcast.10), channel_id=1, source_target_pairs={{8,0},{16,24},{9,1},{17,25},{10,2},{18,26},{11,3},{19,27},{12,4},{... | collective-permute-start | bytes 2457608 | tf_op jit(solution)/shard_map/ppermute | solution.py:217
  811.2 40.3 %collective-permute-start.38 = (bf16[2,160,1280]{2,1,0:T(8,128)(2,1)}, bf16[2,160,1280]{2,1,0:T(8,128)(2,1)S(1)}, u32[]{:S(2)}, u32[]{:S(2)}) collective-permute-start(bf16[2,160,1280]{2,1,0:T(8,128)(2,1)} %get-tuple-element.278), channel_id=1, source_target_pairs={{0,4},{4,0},{1,5},{5,1},{2,6},{6,2},{3,7},{7,3},{8,12},{12,8},{9,1... | collective-permute-start | bytes 2457608 | tf_op jit(solution)/shard_map/ppermute | solution.py:222
  851.5 55.4 %collective-permute-start.40 = (bf16[3,320,1280]{2,1,0:T(8,128)(2,1)}, bf16[3,320,1280]{2,1,0:T(8,128)(2,1)}, u32[]{:S(2)}, u32[]{:S(2)}) collective-permute-start(bf16[3,320,1280]{2,1,0:T(8,128)(2,1)} %get-tuple-element.215), channel_id=1, source_target_pairs={{0,2},{2,0},{1,3},{3,1},{4,6},{6,4},{5,7},{7,5},{8,10},{10,8},{9,1... | collective-permute-start | bytes 7372808 | tf_op jit(solution)/shard_map/ppermute | solution.py:192
  854.7 13.9 %copy-start.13 = (bf16[1,320,1280]{2,1,0:T(8,128)(2,1)S(1)}, bf16[1,320,1280]{2,1,0:T(8,128)(2,1)}, u32[]{:S(2)}) copy-start(bf16[1,320,1280]{2,1,0:T(8,128)(2,1)} %get-tuple-element.258) | copy-start | bytes 2457604
  862.0 10.0 collective-permute-start.39
  862.1 64.0 %collective-permute-start.41 = (bf16[1280,640]{1,0:T(8,128)(2,1)}, bf16[1280,640]{1,0:T(8,128)(2,1)}, u32[]{:S(2)}, u32[]{:S(2)}) collective-permute-start(bf16[1280,640]{1,0:T(8,128)(2,1)} %get-tuple-element.217), channel_id=1, source_target_pairs={{8,16},{16,8},{9,17},{17,9},{10,18},{18,10},{11,19},{19,11},{12,20... | collective-permute-start | bytes 4915208 | tf_op jit(solution)/shard_map/ppermute | solution.py:217
  866.3 55.0 %collective-permute-start.42 = (bf16[2,160,1280]{2,1,0:T(8,128)(2,1)}, bf16[2,160,1280]{2,1,0:T(8,128)(2,1)}, u32[]{:S(2)}, u32[]{:S(2)}) collective-permute-start(bf16[2,160,1280]{2,1,0:T(8,128)(2,1)} %bitcast.86), channel_id=1, source_target_pairs={{8,0},{16,24},{9,1},{17,25},{10,2},{18,26},{11,3},{19,27},{12,4},{... | collective-permute-start | bytes 2457608 | tf_op jit(solution)/shard_map/ppermute | solution.py:217
  870.3 51.0 %collective-permute-start.43 = (bf16[2,160,1280]{2,1,0:T(8,128)(2,1)}, bf16[2,160,1280]{2,1,0:T(8,128)(2,1)S(1)}, u32[]{:S(2)}, u32[]{:S(2)}) collective-permute-start(bf16[2,160,1280]{2,1,0:T(8,128)(2,1)} %get-tuple-element.280), channel_id=1, source_target_pairs={{0,4},{4,0},{1,5},{5,1},{2,6},{6,2},{3,7},{7,3},{8,12},{12,8},{9,1... | collective-permute-start | bytes 2457608 | tf_op jit(solution)/shard_map/ppermute | solution.py:222
  872.0 38.3 %copy-start.19 = (bf16[2,2,320,640]{3,2,1,0:T(8,128)(2,1)}, bf16[2,2,320,640]{3,2,1,0:T(8,128)(2,1)S(1)}, u32[]{:S(2)}) copy-start(bf16[2,2,320,640]{3,2,1,0:T(8,128)(2,1)S(1)} %collective-permute-done.39.refs_3_) | copy-start | bytes 4915204
  872.0 49.3 %collective-permute-start.44 = (bf16[2,160,1280]{2,1,0:T(8,128)(2,1)}, bf16[2,160,1280]{2,1,0:T(8,128)(2,1)}, u32[]{:S(2)}, u32[]{:S(2)}) collective-permute-start(bf16[2,160,1280]{2,1,0:T(8,128)(2,1)} %get-tuple-element.274), channel_id=1, source_target_pairs={{0,4},{4,0},{1,5},{5,1},{2,6},{6,2},{3,7},{7,3},{8,12},{12,8},{9,1... | collective-permute-start | bytes 2457608 | tf_op jit(solution)/shard_map/ppermute | solution.py:222
  906.9 19.2 %collective-permute-start.45 = (bf16[2,160,1280]{2,1,0:T(8,128)(2,1)}, bf16[2,160,1280]{2,1,0:T(8,128)(2,1)}, u32[]{:S(2)}, u32[]{:S(2)}) collective-permute-start(bf16[2,160,1280]{2,1,0:T(8,128)(2,1)} %bitcast.18), channel_id=1, source_target_pairs={{4,0},{5,1},{6,2},{7,3},{12,8},{13,9},{14,10},{15,11},{20,16},{21,... | collective-permute-start | bytes 2457608 | tf_op jit(solution)/shard_map/ppermute | solution.py:248
  933.3 9.1 collective-permute-start.47
  934.6 21.0 %collective-permute-start.46 = (bf16[2,320,640]{2,1,0:T(8,128)(2,1)}, bf16[2,320,640]{2,1,0:T(8,128)(2,1)}, u32[]{:S(2)}, u32[]{:S(2)}) collective-permute-start(bf16[2,320,640]{2,1,0:T(8,128)(2,1)} %get-tuple-element.230), channel_id=1, source_target_pairs={{0,2},{2,0},{1,3},{3,1},{4,6},{6,4},{5,7},{7,5},{8,10},{10,8},{9,1... | collective-permute-start | bytes 2457608 | tf_op jit(solution)/shard_map/ppermute | solution.py:192
  940.0 15.6 %copy-start.22 = (bf16[2,320,640]{2,1,0:T(8,128)(2,1)S(1)}, bf16[2,320,640]{2,1,0:T(8,128)(2,1)}, u32[]{:S(2)}) copy-start(bf16[2,320,640]{2,1,0:T(8,128)(2,1)} %get-tuple-element.212) | copy-start | bytes 2457604
  940.0 53.8 %collective-permute-start.56 = (bf16[2,160,1280]{2,1,0:T(8,128)(2,1)}, bf16[2,160,1280]{2,1,0:T(8,128)(2,1)}, u32[]{:S(2)}, u32[]{:S(2)}) collective-permute-start(bf16[2,160,1280]{2,1,0:T(8,128)(2,1)} %get-tuple-element.269), channel_id=1, source_target_pairs={{0,4},{4,0},{1,5},{5,1},{2,6},{6,2},{3,7},{7,3},{8,12},{12,8},{9,1... | collective-permute-start | bytes 2457608 | tf_op jit(solution)/shard_map/ppermute | solution.py:222
  981.5 30.5 %collective-permute-start.51 = (bf16[2,160,1280]{2,1,0:T(8,128)(2,1)}, bf16[2,160,1280]{2,1,0:T(8,128)(2,1)}, u32[]{:S(2)}, u32[]{:S(2)}) collective-permute-start(bf16[2,160,1280]{2,1,0:T(8,128)(2,1)} %bitcast.22), channel_id=1, source_target_pairs={{8,4},{16,28},{9,5},{17,29},{10,6},{18,30},{11,7},{19,31}} | collective-permute-start | bytes 2457608 | tf_op jit(solution)/shard_map/ppermute | solution.py:242
  983.1 25.5 %collective-permute-start.49 = (bf16[2,320,640]{2,1,0:T(8,128)(2,1)}, bf16[2,320,640]{2,1,0:T(8,128)(2,1)}, u32[]{:S(2)}, u32[]{:S(2)}) collective-permute-start(bf16[2,320,640]{2,1,0:T(8,128)(2,1)} %get-tuple-element.239), channel_id=1, source_target_pairs={{0,2},{2,0},{1,3},{3,1},{4,6},{6,4},{5,7},{7,5},{8,10},{10,8},{9,1... | collective-permute-start | bytes 2457608 | tf_op jit(solution)/shard_map/ppermute | solution.py:192
  986.8 28.1 %collective-permute-start.48 = (bf16[2,160,1280]{2,1,0:T(8,128)(2,1)}, bf16[2,160,1280]{2,1,0:T(8,128)(2,1)}, u32[]{:S(2)}, u32[]{:S(2)}) collective-permute-start(bf16[2,160,1280]{2,1,0:T(8,128)(2,1)} %broadcast_select_fusion.13), channel_id=1, source_target_pairs={{8,12},{16,20},{12,4},{20,28},{9,13},{17,21},{13,5},{21,29},{10,14... | collective-permute-start | bytes 2457608 | tf_op jit(solution)/shard_map/ppermute | solution.py:241
  988.7 30.6 %collective-permute-start.52 = (bf16[2,160,1280]{2,1,0:T(8,128)(2,1)}, bf16[2,160,1280]{2,1,0:T(8,128)(2,1)S(1)}, u32[]{:S(2)}, u32[]{:S(2)}) collective-permute-start(bf16[2,160,1280]{2,1,0:T(8,128)(2,1)} %bitcast.23), channel_id=1, source_target_pairs={{4,0},{5,1},{6,2},{7,3},{12,8},{13,9},{14,10},{15,11},{20,16},{21,... | collective-permute-start | bytes 2457608 | tf_op jit(solution)/shard_map/ppermute | solution.py:248
  1007.7 15.8 %collective-permute-start.55 = (bf16[2,160,640]{2,1,0:T(8,128)(2,1)S(1)}, bf16[2,160,640]{2,1,0:T(8,128)(2,1)S(1)}, u32[]{:S(2)}, u32[]{:S(2)}) collective-permute-start(bf16[2,160,640]{2,1,0:T(8,128)(2,1)S(1)} %bitcast.82), channel_id=1, source_target_pairs={{8,4},{16,28},{9,5},{17,29},{10,6},{18,30},{11,7},{19,31}} | collective-permute-start | bytes 1228808 | tf_op jit(solution)/shard_map/ppermute | solution.py:242
  1008.6 14.9 %collective-permute-start.54 = (bf16[2,160,640]{2,1,0:T(8,128)(2,1)S(1)}, bf16[2,160,640]{2,1,0:T(8,128)(2,1)S(1)}, u32[]{:S(2)}, u32[]{:S(2)}) collective-permute-start(bf16[2,160,640]{2,1,0:T(8,128)(2,1)S(1)} %broadcast_select_fusion.20), channel_id=1, source_target_pairs={{8,12},{16,20},{12,4},{20,28},{9,13},{17,21},{13,5},{21,29},{10,14... | collective-permute-start | bytes 1228808 | tf_op jit(solution)/shard_map/ppermute | solution.py:241
  1012.1 19.6 %collective-permute-start.53 = (bf16[2,160,640]{2,1,0:T(8,128)(2,1)S(1)}, bf16[2,160,640]{2,1,0:T(8,128)(2,1)S(1)}, u32[]{:S(2)}, u32[]{:S(2)}) collective-permute-start(bf16[2,160,640]{2,1,0:T(8,128)(2,1)S(1)} %bitcast.85), channel_id=1, source_target_pairs={{8,4},{16,28},{9,5},{17,29},{10,6},{18,30},{11,7},{19,31}} | collective-permute-start | bytes 1228808 | tf_op jit(solution)/shard_map/ppermute | solution.py:242
  1014.8 16.8 %collective-permute-start.50 = (bf16[2,160,640]{2,1,0:T(8,128)(2,1)S(1)}, bf16[2,160,640]{2,1,0:T(8,128)(2,1)S(1)}, u32[]{:S(2)}, u32[]{:S(2)}) collective-permute-start(bf16[2,160,640]{2,1,0:T(8,128)(2,1)S(1)} %broadcast_select_fusion.21), channel_id=1, source_target_pairs={{8,12},{16,20},{12,4},{20,28},{9,13},{17,21},{13,5},{21,29},{10,14... | collective-permute-start | bytes 1228808 | tf_op jit(solution)/shard_map/ppermute | solution.py:241
  (21 other events, 123.7 us)
Sparse Core Ops, SparseCore 0:
  606.9 172.4 all-gather.1
  980.3 60.4 reduce-scatter.1

commit v4 on v3

--- a/solution.py
+++ b/solution.py
@@ -61,42 +61,10 @@
 
     def kernel(where_ref, *refs):
         def use(value):
-            refs[-1][0, 0] = value.astype(BF16)
-        run_products(refs, columns_at, use)
-
-    return pl.pallas_call(
-        kernel,
-        out_shape=jax.ShapeDtypeStruct((count, 2, rows, columns), BF16),
-        grid_spec=pltpu.PrefetchScalarGridSpec(
-            num_scalar_prefetch=1,
-            grid=(count, 2),
-            in_specs=specs,
-            out_specs=pl.BlockSpec((1, 1, rows, columns), lambda p, r, where: (p, r, 0, 0)),
-        ),
-        compiler_params=pltpu.CompilerParams(vmem_limit_bytes=ROOM),
-        cost_estimate=CHEAP,
-        name="send_products",
-    )(where, *arrays)
-
-
-def keep_products(where, products, arrived):
-    specs, arrays, columns_at = operands(products, 0)
-    count, rows, columns = len(products), products[0][1].shape[-2] // 2, products[0][2].shape[1]
-
-    def kernel(where_ref, *refs):
-        arrived_ref, away, own = refs[-3:]
-        quarter = pl.program_id(1)
-
-        def use(value):
-            total = (value + arrived_ref[0, 0].astype(F32)).astype(BF16)
-
-            @pl.when(quarter == 0)
-            def _():
-                own[0] = total
-
-            @pl.when(quarter == 1)
-            def _():
-                away[0] = total
+            for quarter, out in enumerate(refs[-2:]):
+                @pl.when(pl.program_id(1) == quarter)
+                def _():
+                    out[0] = value.astype(BF16)
         run_products(refs, columns_at, use)
 
     return pl.pallas_call(
@@ -105,13 +73,40 @@
         grid_spec=pltpu.PrefetchScalarGridSpec(
             num_scalar_prefetch=1,
             grid=(count, 2),
-            in_specs=specs + [pl.BlockSpec((1, 1, rows, columns), lambda p, r, where: (p, r, 0, 0))],
+            in_specs=specs,
+            out_specs=(pl.BlockSpec((1, rows, columns), lambda p, r, where: (p, 0, 0)),) * 2,
+        ),
+        compiler_params=pltpu.CompilerParams(vmem_limit_bytes=ROOM),
+        cost_estimate=CHEAP,
+        name="send_products",
+    )(where, *arrays)
+
+
+def keep_products(where, products, arrived):
+    specs, arrays, columns_at = operands(products, 0)
+    count, rows, columns = len(products), products[0][1].shape[-2] // 2, products[0][2].shape[1]
+
+    def kernel(where_ref, *refs):
+        def use(value):
+            for quarter, (arrived_ref, out) in enumerate(zip(refs[-4:-2], refs[-2:])):
+                @pl.when(pl.program_id(1) == quarter)
+                def _():
+                    out[0] = (value + arrived_ref[0].astype(F32)).astype(BF16)
+        run_products(refs, columns_at, use)
+
+    return pl.pallas_call(
+        kernel,
+        out_shape=(jax.ShapeDtypeStruct((count, rows, columns), BF16),) * 2,
+        grid_spec=pltpu.PrefetchScalarGridSpec(
+            num_scalar_prefetch=1,
+            grid=(count, 2),
+            in_specs=specs + [pl.BlockSpec((1, rows, columns), lambda p, r, where: (p, 0, 0))] * 2,
             out_specs=(pl.BlockSpec((1, rows, columns), lambda p, r, where: (p, 0, 0)),) * 2,
         ),
         compiler_params=pltpu.CompilerParams(vmem_limit_bytes=ROOM),
         cost_estimate=CHEAP,
         name="keep_products",
-    )(where, *arrays, arrived)
+    )(where, *arrays, *arrived)
 
 
 def place(base, parity, kept, arrived, out, shape):
@@ -180,12 +175,13 @@
         followed = {id(rhs): rhs for _, _, rhs in self.products}
         followed = {key: self.order.follow(rhs) for key, rhs in followed.items()}
         self.products = [(irrep, lhs, followed[id(rhs)]) for irrep, lhs, rhs in self.products]
-        part = self.order.step(send_products(self.where, self.products))
-        self.arrived = lax.ppermute(part, "ka", OTHER_CORE)
+        parts = send_products(self.where, self.products)
+        self.order.step(parts[1])
+        self.arrived = [lax.ppermute(part, "ka", OTHER_CORE) for part in parts]
 
     def keep(self):
-        arrived = self.order.follow(self.arrived)
-        self.away, self.own = keep_products(self.where, self.products, arrived)
+        arrived = [self.order.follow(part) for part in self.arrived]
+        self.own, self.away = keep_products(self.where, self.products, arrived)
         self.order.step(self.away)
 
     def swap(self):
@@ -209,6 +205,9 @@
 
     def columns_of(g):
         return order.open(cycle_integrals)[g].reshape(depth, 2 * columns)
+
+    def exchange(inwards, outwards):
+        return move(jnp.where(at_end, order.open(inwards), order.open(outwards)), NEIGHBOUR)
 
     def batch(*products):
         return Batch(order, where, *products)
@@ -268,8 +267,7 @@
 
     order.phase(own3, swap3)
     relay3 = move(swap3, MID_TO_MID)
-    b0_in = move(b0, END_TO_MID)
-    on3 = move(own3, MID_TO_END)
+    both3 = exchange(b0, own3)
     two.swap()
     b2 = columns_of(2)
     three = batch((3, ca, swap3), (0, ca, b0), (0, a0, b0))
@@ -277,28 +275,29 @@
     three.keep()
     f0 = two.finish()
 
-    order.phase(relay3, b0_in, on3)
-    relay0 = move(b0_in, MID_TO_MID)
-    a1 = move(rows_of(1), END_TO_MID)
-    on_relay3 = move(relay3, MID_TO_END)
+    order.phase(relay3, both3)
+    relay0 = move(both3, MID_TO_MID)
+    both4 = exchange(rows_of(1).reshape(b0.shape), relay3)
     three.swap()
-    four = batch((2, ca, b2), (0, ca, b0_in), (3, ca, jnp.where(at_end, order.open(on3), own3)))
+    four = batch((2, ca, b2), (0, ca, both3), (3, ca, jnp.where(at_end, order.open(both3), own3)))
     four.send()
     four.keep()
     n3, *s0 = three.finish()
-
-    order.phase(relay0, a1, on_relay3)
+    rows2 = rows_of(2)
+
+    order.phase(relay0, both4, rows2)
+    a1 = both4.reshape(a0.shape)
     own1 = move(b1, MID_TO_MID)
-    a2 = move(rows_of(2), END_TO_MID)
-    f0_back = move(f0[1], MID_TO_END)
-    s0_back = move(s0[1], MID_TO_END)
+    a2 = move(rows2, END_TO_MID)
+    backs = move(jnp.stack([f0[1], s0[1]]), MID_TO_END)
     four.swap()
-    five = batch((0, ca, relay0), (0, a0, relay0), (3, ca, jnp.where(at_end, order.open(on_relay3), relay3)))
+    five = batch((0, ca, relay0), (0, a0, relay0), (3, ca, jnp.where(at_end, order.open(both4), relay3)))
     five.send()
     five.keep()
     s2, n0, f3 = four.finish()
 
-    order.phase(own1, a2, f0_back, s0_back)
+    order.phase(own1, a2, backs)
+    f0_back, s0_back = backs[0], backs[1]
     own2 = move(b2, MID_TO_MID)
     swap1 = move(b1, NEIGHBOUR)
     x0a = cross(s0[0], home(f0[0], f0_back))
@@ -311,7 +310,6 @@
     order.phase(own2, swap1, x0a[1])
     relay1 = move(swap1, MID_TO_MID)
     swap2 = move(b2, NEIGHBOUR)
-    gathered = lax.all_gather(order.open(ladder_amplitudes), "vir", axis=0, tiled=True)
     x3a = cross(s3, f3)
     six.swap()
     seven = batch((2, ca, own2), (2, a2, own2), (1, ca, swap1))
@@ -320,6 +318,7 @@
     f1 = six.finish()
 
     order.phase(relay1, swap2, x3a[1])
+    gathered = lax.all_gather(order.open(ladder_amplitudes), "vir", axis=0, tiled=True)
     relay2 = [move(swap2[:, :columns], MID_TO_MID)]
     g0_back = move(g0[1], MID_TO_END)
     f1_back = move(f1[1], MID_TO_END)
@@ -343,6 +342,10 @@
     *g1, n2 = eight.finish()
 
     order.phase(relay2[1], f2_back, x0b[1], x1a[1], near1_in, gathered)
+    partial_ladder = order.step(jnp.dot(
+        order.follow(gathered), ladder_integrals, preferred_element_type=F32,
+    ).astype(BF16))
+    ladder_residual = lax.psum_scatter(partial_ladder, ("occ", "ka"), scatter_dimension=0, tiled=True)
     near2_in = over(n2)
     x2a = cross(s2, home(f2[0], f2_back))
     nine.swap()
@@ -352,10 +355,6 @@
     ten.swap()
     x1b = straight(n1, near1_in, g1)
     x2b = [straight(n2, near2_in, nine.finish(), slice(0, columns))]
-    partial_ladder = order.step(jnp.dot(
-        order.follow(gathered), ladder_integrals, preferred_element_type=F32,
-    ).astype(BF16))
-    ladder_residual = lax.psum_scatter(partial_ladder, ("occ", "ka"), scatter_dimension=0, tiled=True)
     x2b.append(straight(n2, near2_in, ten.finish(), slice(columns, 2 * columns)))
     out = None
     for j in range(2):

time: 1070 us -> 958 us (0.90)
  waiting for transfers between devices: 538 us -> 422 us
  starting transfers between devices: 102 us -> 88.7 us
    ppermute x23 -> x20, waiting for transfers between devices: 293 us -> 190 us  [move(): return lax.ppermute(order.open(value), 'vir', route)]
    ppermute x10, waiting for transfers between devices: 224 us -> 180 us  [swap(): self.other = lax.ppermute(self.order.open(self.away), 'ka', OTHER_Y)]
    ppermute x10 -> x20, waiting for transfers between devices: 0.85 us -> 22.4 us  [send(): self.arrived = [lax.ppermute(part, 'ka', OTHER_CORE) for part in parts]]
    ppermute x23 -> x20, starting transfers between devices: 63 us -> 44.9 us  [move(): return lax.ppermute(order.open(value), 'vir', route)]
  transfers between devices with their start and end apart: 59 -> 66, of which waited for: 30 -> 38; matrix products, arithmetic and copies ran while one was open for 10% -> 10% of each run, Pallas kernels for 17% -> 27%
where the time goes in v4:
time: 958 us; the launch traced here: 944 us
  waiting for transfers between devices  422 us (44%)
  Pallas kernels  274 us (29%)
  starting transfers between devices  88.7 us (9%)
  other arithmetic  68.6 us (7%)
  local copies, waits for them, and re-layouts  53.6 us (6%)
  matrix products  22.8 us (2%)
  between operations  14.7 us (2%)
    ppermute x20, waiting for transfers between devices, move(): return lax.ppermute(order.open(value), 'vir', route)  190 us
    ppermute x10, waiting for transfers between devices, swap(): self.other = lax.ppermute(self.order.open(self.away), 'ka', OTHER_Y)  180 us
    pallas_call x10, Pallas kernels, keep_products(): pl.pallas_call(kernel, out_shape=(jax.ShapeDtypeStruct((count, rows, colu...  127 us
    pallas_call x10, Pallas kernels, send_products(): pl.pallas_call(kernel, out_shape=(jax.ShapeDtypeStruct((count, rows, colu...  120 us
    ppermute x20, starting transfers between devices, move(): return lax.ppermute(order.open(value), 'vir', route)  44.9 us
    convert_element_type x10, other arithmetic, finish(): (self.own.astype(F32) + other.astype(F32)).astype(BF16)  31.7 us
    pallas_call x4, Pallas kernels, place(): pl.pallas_call(kernel, out_shape=jax.ShapeDtypeStruct(shape, BF16), grid_...  27.4 us
    dot_general x1, matrix products, line_local(): jnp.dot(order.follow(gathered), ladder_integrals, preferred_element_type=...  22.8 us
  transfers between devices with their start and end apart: 66, of which 38 were waited for; matrix products, arithmetic and copies ran while one was open for 10% of the time, Pallas kernels for 27%

profile of v4, /device:TPU:10, one launch (start us, length us, event | category | flops | bytes accessed | tf_op | source)
XLA Modules:
  0.0 944.4 jit_solution(7147777137372392330)
XLA Ops:
  11.4 3.9 slice_bitcast_fusion.1
  20.0 6.9 fusion
  32.2 11.1 %send_products.10 = (bf16[2,320,1280]{2,1,0:T(8,128)(2,1)}, bf16[2,320,1280]{2,1,0:T(8,128)(2,1)}) custom-call(s32[4]{0:T(128)} %broadcast_xor_fusion.where_ref, bf16[4,2,640,1280]{3,2,1,0:T(8,128)(2,1)} %refs_0_.39, bf16[4,2,640,1280]{3,2,1,0:T(8,128)(2,1)} %refs_0_.39, bf16[1280,1280]{1,0:T(8,128)(2,1)} %bitcast.56, bf16[1280,1280]{1,0:T(8,128)(2,1)} %bitcast.42.refs_3_), custom_call_target="tpu_custom_call" | custom-call | flops 1048576 | bytes 65536 | tf_op jit(solution)/shard_map/send_products/pallas_call | solution.py:70
  49.5 11.7 %keep_products.10 = (bf16[2,320,1280]{2,1,0:T(8,128)(2,1)}, bf16[2,320,1280]{2,1,0:T(8,128)(2,1)}) custom-call(s32[4]{0:T(128)} %broadcast_xor_fusion.where_ref, bf16[4,2,640,1280]{3,2,1,0:T(8,128)(2,1)} %refs_0_.39, bf16[4,2,640,1280]{3,2,1,0:T(8,128)(2,1)} %refs_0_.39, bf16[1280,1280]{1,0:T(8,128)(2,1)} %bitcast.57, bf16[1280,1280]{1,0:T(8,128)(2,1)} %bitcast.42.refs_3_, ...), custom_call_target="tpu_custom_call" | custom-call | flops 1048576 | bytes 65536 | tf_op jit(solution)/shard_map/keep_products/pallas_call | solution.py:97
  61.2 28.8 %collective-permute-done.refs_1_.refs_2_ = bf16[2,640,1280]{2,1,0:T(8,128)(2,1)S(1)} collective-permute-done((bf16[2,640,1280]{2,1,0:T(8,128)(2,1)}, bf16[2,640,1280]{2,1,0:T(8,128)(2,1)S(1)}, u32[]{:S(2)}, u32[]{:S(2)}) %collective-permute-start) | collective-permute-done | bytes 3276832 | tf_op jit(solution)/shard_map/ppermute | solution.py:216
  91.4 3.7 collective-permute-start.7
  95.2 10.1 %send_products.11 = (bf16[2,320,1280]{2,1,0:T(8,128)(2,1)}, bf16[2,320,1280]{2,1,0:T(8,128)(2,1)}) custom-call(s32[4]{0:T(128)} %broadcast_xor_fusion.where_ref, bf16[4,2,640,1280]{3,2,1,0:T(8,128)(2,1)} %refs_0_.39, bf16[2,640,1280]{2,1,0:T(8,128)(2,1)} %copy-done, bf16[1280,1280]{1,0:T(8,128)(2,1)} %collective-permute-done.1.refs_2_), custom_call_target="tpu_custom_call" | custom-call | flops 1048576 | bytes 65536 | tf_op jit(solution)/shard_map/send_products/pallas_call | solution.py:70
  112.5 10.8 %keep_products.11 = (bf16[2,320,1280]{2,1,0:T(8,128)(2,1)}, bf16[2,320,1280]{2,1,0:T(8,128)(2,1)}) custom-call(s32[4]{0:T(128)} %broadcast_xor_fusion.where_ref, bf16[4,2,640,1280]{3,2,1,0:T(8,128)(2,1)} %refs_0_.39, bf16[2,640,1280]{2,1,0:T(8,128)(2,1)} %copy-done, bf16[1280,1280]{1,0:T(8,128)(2,1)} %collective-permute-done.1.refs_2_, ...), custom_call_target="tpu_custom_call" | custom-call | flops 1048576 | bytes 65536 | tf_op jit(solution)/shard_map/keep_products/pallas_call | solution.py:97
  123.3 20.5 %collective-permute-done.6 = bf16[2,320,1280]{2,1,0:T(8,128)(2,1)} collective-permute-done((bf16[2,320,1280]{2,1,0:T(8,128)(2,1)}, bf16[2,320,1280]{2,1,0:T(8,128)(2,1)}, u32[]{:S(2)}, u32[]{:S(2)}) %collective-permute-start.6) | collective-permute-done | bytes 1638432 | tf_op jit(solution)/shard_map/ppermute | solution.py:188
  147.3 18.0 %collective-permute-done.7 = bf16[1280,1280]{1,0:T(8,128)(2,1)} collective-permute-done((bf16[1280,1280]{1,0:T(8,128)(2,1)}, bf16[1280,1280]{1,0:T(8,128)(2,1)}, u32[]{:S(2)}, u32[]{:S(2)}) %collective-permute-start.7) | collective-permute-done | bytes 3276832 | tf_op jit(solution)/shard_map/ppermute | solution.py:216
  169.6 4.0 broadcast_select_fusion.3
  173.8 14.4 %send_products.12 = (bf16[3,320,1280]{2,1,0:T(8,128)(2,1)}, bf16[3,320,1280]{2,1,0:T(8,128)(2,1)}) custom-call(s32[4]{0:T(128)} %broadcast_xor_fusion.where_ref, bf16[4,2,640,1280]{3,2,1,0:T(8,128)(2,1)} %refs_0_.39, bf16[4,2,640,1280]{3,2,1,0:T(8,128)(2,1)} %refs_0_.39, bf16[2,640,1280]{2,1,0:T(8,128)(2,1)} %copy-done, ...), custom_call_target="tpu_custom_call" | custom-call | flops 1048576 | bytes 65536 | tf_op jit(solution)/shard_map/send_products/pallas_call | solution.py:70
  193.3 3.5 collective-permute-done.11.refs_6_
  196.8 15.2 %keep_products.12 = (bf16[3,320,1280]{2,1,0:T(8,128)(2,1)}, bf16[3,320,1280]{2,1,0:T(8,128)(2,1)}) custom-call(s32[4]{0:T(128)} %broadcast_xor_fusion.where_ref, bf16[4,2,640,1280]{3,2,1,0:T(8,128)(2,1)} %refs_0_.39, bf16[4,2,640,1280]{3,2,1,0:T(8,128)(2,1)} %refs_0_.39, bf16[2,640,1280]{2,1,0:T(8,128)(2,1)} %copy-done, ...), custom_call_target="tpu_custom_call" | custom-call | flops 1048576 | bytes 65536 | tf_op jit(solution)/shard_map/keep_products/pallas_call | solution.py:97
  212.0 14.9 %collective-permute-done.9 = bf16[2,320,1280]{2,1,0:T(8,128)(2,1)} collective-permute-done((bf16[2,320,1280]{2,1,0:T(8,128)(2,1)}, bf16[2,320,1280]{2,1,0:T(8,128)(2,1)}, u32[]{:S(2)}, u32[]{:S(2)}) %collective-permute-start.9) | collective-permute-done | bytes 1638432 | tf_op jit(solution)/shard_map/ppermute | solution.py:188
  230.4 9.4 collective-permute-done.12
  239.7 4.3 collective-permute-done.13.refs_4_
  244.1 6.2 slice_bitcast_fusion
  250.3 4.0 broadcast_select_fusion.2
  254.3 3.9 collective-permute-start.18
  258.3 4.0 broadcast_select_fusion.1.refs_5_
  262.3 15.4 %send_products.13 = (bf16[3,320,1280]{2,1,0:T(8,128)(2,1)}, bf16[3,320,1280]{2,1,0:T(8,128)(2,1)}) custom-call(s32[4]{0:T(128)} %broadcast_xor_fusion.where_ref, bf16[4,2,640,1280]{3,2,1,0:T(8,128)(2,1)} %refs_0_.39, bf16[4,2,640,1280]{3,2,1,0:T(8,128)(2,1)} %refs_0_.39, bf16[4,2,640,1280]{3,2,1,0:T(8,128)(2,1)} %refs_0_.39, ...), custom_call_target="tpu_custom_call" | custom-call | flops 1048576 | bytes 65536 | tf_op jit(solution)/shard_map/send_products/pallas_call | solution.py:70
  282.7 3.5 collective-permute-done.17.refs_7_
  286.2 16.1 %keep_products.13 = (bf16[3,320,1280]{2,1,0:T(8,128)(2,1)}, bf16[3,320,1280]{2,1,0:T(8,128)(2,1)}) custom-call(s32[4]{0:T(128)} %broadcast_xor_fusion.where_ref, bf16[4,2,640,1280]{3,2,1,0:T(8,128)(2,1)} %refs_0_.39, bf16[4,2,640,1280]{3,2,1,0:T(8,128)(2,1)} %refs_0_.39, bf16[4,2,640,1280]{3,2,1,0:T(8,128)(2,1)} %refs_0_.39, ...), custom_call_target="tpu_custom_call" | custom-call | flops 1048576 | bytes 65536 | tf_op jit(solution)/shard_map/keep_products/pallas_call | solution.py:97
  302.3 31.5 %collective-permute-done.15 = bf16[3,320,1280]{2,1,0:T(8,128)(2,1)} collective-permute-done((bf16[3,320,1280]{2,1,0:T(8,128)(2,1)}, bf16[3,320,1280]{2,1,0:T(8,128)(2,1)}, u32[]{:S(2)}, u32[]{:S(2)}) %collective-permute-start.15) | collective-permute-done | bytes 2457632 | tf_op jit(solution)/shard_map/ppermute | solution.py:188
  333.8 4.4 add_convert_fusion.4
  338.3 5.1 broadcast_select_fusion.refs_4_
  343.4 14.4 %send_products.14 = (bf16[3,320,1280]{2,1,0:T(8,128)(2,1)}, bf16[3,320,1280]{2,1,0:T(8,128)(2,1)}) custom-call(s32[4]{0:T(128)} %broadcast_xor_fusion.where_ref, bf16[4,2,640,1280]{3,2,1,0:T(8,128)(2,1)} %refs_0_.39, bf16[2,640,1280]{2,1,0:T(8,128)(2,1)} %copy-done, bf16[4,2,640,1280]{3,2,1,0:T(8,128)(2,1)} %refs_0_.39, ...), custom_call_target="tpu_custom_call" | custom-call | flops 1048576 | bytes 65536 | tf_op jit(solution)/shard_map/send_products/pallas_call | solution.py:70
  368.6 5.9 collective-permute-start.24
  374.5 15.2 %keep_products.14 = (bf16[3,320,1280]{2,1,0:T(8,128)(2,1)}, bf16[3,320,1280]{2,1,0:T(8,128)(2,1)}) custom-call(s32[4]{0:T(128)} %broadcast_xor_fusion.where_ref, bf16[4,2,640,1280]{3,2,1,0:T(8,128)(2,1)} %refs_0_.39, bf16[2,640,1280]{2,1,0:T(8,128)(2,1)} %copy-done, bf16[4,2,640,1280]{3,2,1,0:T(8,128)(2,1)} %refs_0_.39, ...), custom_call_target="tpu_custom_call" | custom-call | flops 1048576 | bytes 65536 | tf_op jit(solution)/shard_map/keep_products/pallas_call | solution.py:97
  389.7 28.3 %collective-permute-done.20 = bf16[3,320,1280]{2,1,0:T(8,128)(2,1)} collective-permute-done((bf16[3,320,1280]{2,1,0:T(8,128)(2,1)}, bf16[3,320,1280]{2,1,0:T(8,128)(2,1)}, u32[]{:S(2)}, u32[]{:S(2)}) %collective-permute-start.20) | collective-permute-done | bytes 2457632 | tf_op jit(solution)/shard_map/ppermute | solution.py:188
  418.0 4.4 add_convert_fusion.3
  422.4 11.0 %collective-permute-done.19.refs_2_ = bf16[1280,1280]{1,0:T(8,128)(2,1)} collective-permute-done((bf16[1280,1280]{1,0:T(8,128)(2,1)}, bf16[1280,1280]{1,0:T(8,128)(2,1)}, u32[]{:S(2)}, u32[]{:S(2)}) %collective-permute-start.19) | collective-permute-done | bytes 3276832 | tf_op jit(solution)/shard_map/ppermute | solution.py:216
  440.5 10.1 %send_products.15 = (bf16[2,320,1280]{2,1,0:T(8,128)(2,1)}, bf16[2,320,1280]{2,1,0:T(8,128)(2,1)}) custom-call(s32[4]{0:T(128)} %broadcast_xor_fusion.where_ref, bf16[4,2,640,1280]{3,2,1,0:T(8,128)(2,1)} %refs_0_.39, bf16[2,640,1280]{2,1,0:T(8,128)(2,1)} %bitcast.52, bf16[1280,1280]{1,0:T(8,128)(2,1)} %collective-permute-done.19.refs_2_), custom_call_target="tpu_custom_call" | custom-call | flops 1048576 | bytes 65536 | tf_op jit(solution)/shard_map/send_products/pallas_call | solution.py:70
  457.5 11.0 %keep_products.15 = (bf16[2,320,1280]{2,1,0:T(8,128)(2,1)}, bf16[2,320,1280]{2,1,0:T(8,128)(2,1)}) custom-call(s32[4]{0:T(128)} %broadcast_xor_fusion.where_ref, bf16[4,2,640,1280]{3,2,1,0:T(8,128)(2,1)} %refs_0_.39, bf16[2,640,1280]{2,1,0:T(8,128)(2,1)} %bitcast.53, bf16[1280,1280]{1,0:T(8,128)(2,1)} %collective-permute-done.19.refs_2_, ...), custom_call_target="tpu_custom_call" | custom-call | flops 1048576 | bytes 65536 | tf_op jit(solution)/shard_map/keep_products/pallas_call | solution.py:97
  468.5 25.0 %collective-permute-done.27 = bf16[3,320,1280]{2,1,0:T(8,128)(2,1)} collective-permute-done((bf16[3,320,1280]{2,1,0:T(8,128)(2,1)}, bf16[3,320,1280]{2,1,0:T(8,128)(2,1)}, u32[]{:S(2)}, u32[]{:S(2)}) %collective-permute-start.27) | collective-permute-done | bytes 2457632 | tf_op jit(solution)/shard_map/ppermute | solution.py:188
  493.5 3.7 add_convert_fusion.2
  497.2 12.4 %collective-permute-done.28.refs_3_ = bf16[1280,1280]{1,0:T(8,128)(2,1)} collective-permute-done((bf16[1280,1280]{1,0:T(8,128)(2,1)}, bf16[1280,1280]{1,0:T(8,128)(2,1)}, u32[]{:S(2)}, u32[]{:S(2)}) %collective-permute-start.28) | collective-permute-done | bytes 3276832 | tf_op jit(solution)/shard_map/ppermute | solution.py:216
  513.5 14.5 %send_products.16 = (bf16[3,320,1280]{2,1,0:T(8,128)(2,1)}, bf16[3,320,1280]{2,1,0:T(8,128)(2,1)}) custom-call(s32[4]{0:T(128)} %broadcast_xor_fusion.where_ref, bf16[4,2,640,1280]{3,2,1,0:T(8,128)(2,1)} %refs_0_.39, bf16[2,640,1280]{2,1,0:T(8,128)(2,1)} %copy-done.1, bf16[4,2,640,1280]{3,2,1,0:T(8,128)(2,1)} %refs_0_.39, ...), custom_call_target="tpu_custom_call" | custom-call | flops 1048576 | bytes 65536 | tf_op jit(solution)/shard_map/send_products/pallas_call | solution.py:70
  536.6 15.1 %keep_products.16 = (bf16[3,320,1280]{2,1,0:T(8,128)(2,1)}, bf16[3,320,1280]{2,1,0:T(8,128)(2,1)}) custom-call(s32[4]{0:T(128)} %broadcast_xor_fusion.where_ref, bf16[4,2,640,1280]{3,2,1,0:T(8,128)(2,1)} %refs_0_.39, bf16[2,640,1280]{2,1,0:T(8,128)(2,1)} %copy-done.1, bf16[4,2,640,1280]{3,2,1,0:T(8,128)(2,1)} %refs_0_.39, ...), custom_call_target="tpu_custom_call" | custom-call | flops 1048576 | bytes 65536 | tf_op jit(solution)/shard_map/keep_products/pallas_call | solution.py:97
  551.7 15.2 %collective-permute-done.31 = bf16[2,320,1280]{2,1,0:T(8,128)(2,1)} collective-permute-done((bf16[2,320,1280]{2,1,0:T(8,128)(2,1)}, bf16[2,320,1280]{2,1,0:T(8,128)(2,1)}, u32[]{:S(2)}, u32[]{:S(2)}) %collective-permute-start.31) | collective-permute-done | bytes 1638432 | tf_op jit(solution)/shard_map/ppermute | solution.py:188
  570.4 13.6 %collective-permute-done.34.refs_3_ = bf16[1280,1280]{1,0:T(8,128)(2,1)} collective-permute-done((bf16[1280,1280]{1,0:T(8,128)(2,1)}, bf16[1280,1280]{1,0:T(8,128)(2,1)}, u32[]{:S(2)}, u32[]{:S(2)}) %collective-permute-start.34) | collective-permute-done | bytes 3276832 | tf_op jit(solution)/shard_map/ppermute | solution.py:216
  584.0 17.6 %collective-permute-done.35.refs_4_ = bf16[1280,1280]{1,0:T(8,128)(2,1)S(1)} collective-permute-done((bf16[1280,1280]{1,0:T(8,128)(2,1)}, bf16[1280,1280]{1,0:T(8,128)(2,1)S(1)}, u32[]{:S(2)}, u32[]{:S(2)}) %collective-permute-start.35) | collective-permute-done | bytes 3276832 | tf_op jit(solution)/shard_map/ppermute | solution.py:216
  603.3 14.5 %send_products.17 = (bf16[3,320,1280]{2,1,0:T(8,128)(2,1)}, bf16[3,320,1280]{2,1,0:T(8,128)(2,1)}) custom-call(s32[4]{0:T(128)} %broadcast_xor_fusion.where_ref, bf16[4,2,640,1280]{3,2,1,0:T(8,128)(2,1)} %refs_0_.39, bf16[2,640,1280]{2,1,0:T(8,128)(2,1)} %bitcast.54, bf16[4,2,640,1280]{3,2,1,0:T(8,128)(2,1)} %refs_0_.39, ...), custom_call_target="tpu_custom_call" | custom-call | flops 1048576 | bytes 65536 | tf_op jit(solution)/shard_map/send_products/pallas_call | solution.py:70
  625.5 4.0 collective-permute-start.40
  638.4 15.2 %keep_products.17 = (bf16[3,320,1280]{2,1,0:T(8,128)(2,1)}, bf16[3,320,1280]{2,1,0:T(8,128)(2,1)}) custom-call(s32[4]{0:T(128)} %broadcast_xor_fusion.where_ref, bf16[4,2,640,1280]{3,2,1,0:T(8,128)(2,1)} %refs_0_.39, bf16[2,640,1280]{2,1,0:T(8,128)(2,1)} %bitcast.55, bf16[4,2,640,1280]{3,2,1,0:T(8,128)(2,1)} %refs_0_.39, ...), custom_call_target="tpu_custom_call" | custom-call | flops 1048576 | bytes 65536 | tf_op jit(solution)/shard_map/keep_products/pallas_call | solution.py:97
  653.7 20.9 %collective-permute-done.39 = bf16[3,320,1280]{2,1,0:T(8,128)(2,1)} collective-permute-done((bf16[3,320,1280]{2,1,0:T(8,128)(2,1)}, bf16[3,320,1280]{2,1,0:T(8,128)(2,1)}, u32[]{:S(2)}, u32[]{:S(2)}) %collective-permute-start.39) | collective-permute-done | bytes 2457632 | tf_op jit(solution)/shard_map/ppermute | solution.py:188
  680.1 47.9 %collective-permute-done.42 = bf16[2,160,1280]{2,1,0:T(8,128)(2,1)S(1)} collective-permute-done((bf16[2,160,1280]{2,1,0:T(8,128)(2,1)}, bf16[2,160,1280]{2,1,0:T(8,128)(2,1)S(1)}, u32[]{:S(2)}, u32[]{:S(2)}) %collective-permute-start.42) | collective-permute-done | bytes 819232 | tf_op jit(solution)/shard_map/ppermute | solution.py:216
  728.0 18.7 %collective-permute-done.40.refs_2_ = bf16[1280,640]{1,0:T(8,128)(2,1)S(1)} collective-permute-done((bf16[1280,640]{1,0:T(8,128)(2,1)}, bf16[1280,640]{1,0:T(8,128)(2,1)S(1)}, u32[]{:S(2)}, u32[]{:S(2)}) %collective-permute-start.40) | collective-permute-done | bytes 1638432 | tf_op jit(solution)/shard_map/ppermute | solution.py:216
  748.9 7.6 send_products.18
  769.3 8.1 keep_products.18
  777.4 23.8 %collective-permute-done.44 = bf16[3,320,1280]{2,1,0:T(8,128)(2,1)} collective-permute-done((bf16[3,320,1280]{2,1,0:T(8,128)(2,1)}, bf16[3,320,1280]{2,1,0:T(8,128)(2,1)}, u32[]{:S(2)}, u32[]{:S(2)}) %collective-permute-start.44) | collective-permute-done | bytes 2457632 | tf_op jit(solution)/shard_map/ppermute | solution.py:188
  809.1 11.6 %collective-permute-done.51 = bf16[2,160,1280]{2,1,0:T(8,128)(2,1)} collective-permute-done((bf16[2,160,1280]{2,1,0:T(8,128)(2,1)}, bf16[2,160,1280]{2,1,0:T(8,128)(2,1)}, u32[]{:S(2)}, u32[]{:S(2)}) %collective-permute-start.51) | collective-permute-done | bytes 819232 | tf_op jit(solution)/shard_map/ppermute | solution.py:247
  820.7 22.8 %convolution_convert_fusion = bf16[512,2048]{1,0:T(8,128)(2,1)} fusion(bf16[512,6656]{1,0:T(8,128)(2,1)} %all-gather.2.cloned.1.call-done, bf16[6656,2048]{1,0:T(8,128)(2,1)} %param.6), kind=kOutput, calls=%fused_computation.14 | convolution fusion | flops 13959692288 | bytes 36175872 | tf_op jit(solution)/shard_map/dot_general | solution.py:345
  846.2 7.7 send_products.19
  859.6 8.1 keep_products.19
  871.8 5.7 collective-permute-start.59
  879.8 4.7 collective-permute-done.63.refs_6_
  886.0 6.8 place.4.refs_8_
  892.8 7.0 place.5.refs_8_
  908.5 5.6 collective-permute-done.61
  914.1 7.2 collective-permute-done.57
  923.8 6.8 place.6.refs_8_
  930.6 6.8 place.7
  (223 shorter events, 165.3 us)
Async XLA Ops:
  7.2 813.5 %all-gather.2.cloned.1.call-start = ((), (), s32[]{:S(2)}) async-start(), calls=%async_computation.1 | async-start | bytes 8519680 | tf_op jit(solution)/shard_map/all_gather | solution.py:321
  15.2 74.7 %collective-permute-start = (bf16[2,640,1280]{2,1,0:T(8,128)(2,1)}, bf16[2,640,1280]{2,1,0:T(8,128)(2,1)S(1)}, u32[]{:S(2)}, u32[]{:S(2)}) collective-permute-start(bf16[2,640,1280]{2,1,0:T(8,128)(2,1)} %slice_bitcast_fusion.1), channel_id=1, source_target_pairs={{0,8},{24,16},{1,9},{25,17},{2,10},{26,18},{3,11},{27,19},{4,12},{... | collective-permute-start | bytes 9830408 | tf_op jit(solution)/shard_map/ppermute | solution.py:216
  16.5 74.9 %collective-permute-start.1 = (bf16[1280,1280]{1,0:T(8,128)(2,1)}, bf16[1280,1280]{1,0:T(8,128)(2,1)}, u32[]{:S(2)}, u32[]{:S(2)}) collective-permute-start(bf16[1280,1280]{1,0:T(8,128)(2,1)} %bitcast.36.refs_4_), channel_id=1, source_target_pairs={{8,16},{16,8},{9,17},{17,9},{10,18},{18,10},{11,19},{19,11},{12,20... | collective-permute-start | bytes 9830408 | tf_op jit(solution)/shard_map/ppermute | solution.py:216
  43.3 6.2 collective-permute-start.3
  91.4 74.0 %collective-permute-start.7 = (bf16[1280,1280]{1,0:T(8,128)(2,1)}, bf16[1280,1280]{1,0:T(8,128)(2,1)}, u32[]{:S(2)}, u32[]{:S(2)}) collective-permute-start(bf16[1280,1280]{1,0:T(8,128)(2,1)} %bitcast.58), channel_id=1, source_target_pairs={{8,16},{16,8},{9,17},{17,9},{10,18},{18,10},{11,19},{19,11},{12,20... | collective-permute-start | bytes 9830408 | tf_op jit(solution)/shard_map/ppermute | solution.py:216
  95.1 71.9 %collective-permute-start.8 = (bf16[1280,1280]{1,0:T(8,128)(2,1)}, bf16[1280,1280]{1,0:T(8,128)(2,1)}, u32[]{:S(2)}, u32[]{:S(2)}) collective-permute-start(bf16[1280,1280]{1,0:T(8,128)(2,1)} %bitcast.59), channel_id=1, source_target_pairs={{0,8},{8,0},{16,24},{24,16},{1,9},{9,1},{17,25},{25,17},{2,10},{10... | collective-permute-start | bytes 9830408 | tf_op jit(solution)/shard_map/ppermute | solution.py:216
  105.3 6.1 collective-permute-start.5
  105.8 38.0 %collective-permute-start.6 = (bf16[2,320,1280]{2,1,0:T(8,128)(2,1)}, bf16[2,320,1280]{2,1,0:T(8,128)(2,1)}, u32[]{:S(2)}, u32[]{:S(2)}) collective-permute-start(bf16[2,320,1280]{2,1,0:T(8,128)(2,1)} %get-tuple-element.174), channel_id=1, source_target_pairs={{0,2},{2,0},{1,3},{3,1},{4,6},{6,4},{5,7},{7,5},{8,10},{10,8},{9,1... | collective-permute-start | bytes 4915208 | tf_op jit(solution)/shard_map/ppermute | solution.py:188
  167.0 72.8 %collective-permute-start.12 = (bf16[1280,1280]{1,0:T(8,128)(2,1)}, bf16[1280,1280]{1,0:T(8,128)(2,1)}, u32[]{:S(2)}, u32[]{:S(2)}) collective-permute-start(bf16[1280,1280]{1,0:T(8,128)(2,1)} %collective-permute-done.8.refs_3_), channel_id=1, source_target_pairs={{8,16},{16,8},{9,17},{17,9},{10,18},{18,10},{11,19},{19,11},{12,20... | collective-permute-start | bytes 9830408 | tf_op jit(solution)/shard_map/ppermute | solution.py:216
  173.6 70.5 %collective-permute-start.13 = (bf16[1280,1280]{1,0:T(8,128)(2,1)}, bf16[1280,1280]{1,0:T(8,128)(2,1)S(1)}, u32[]{:S(2)}, u32[]{:S(2)}) collective-permute-start(bf16[1280,1280]{1,0:T(8,128)(2,1)} %broadcast_select_fusion.3), channel_id=1, source_target_pairs={{0,8},{8,0},{16,24},{24,16},{1,9},{9,1},{17,25},{25,17},{2,10},{10... | collective-permute-start | bytes 9830408 | tf_op jit(solution)/shard_map/ppermute | solution.py:216
  188.3 5.0 collective-permute-start.10
  188.3 8.5 collective-permute-start.11
  188.8 38.1 %collective-permute-start.9 = (bf16[2,320,1280]{2,1,0:T(8,128)(2,1)}, bf16[2,320,1280]{2,1,0:T(8,128)(2,1)}, u32[]{:S(2)}, u32[]{:S(2)}) collective-permute-start(bf16[2,320,1280]{2,1,0:T(8,128)(2,1)} %get-tuple-element.177), channel_id=1, source_target_pairs={{0,2},{2,0},{1,3},{3,1},{4,6},{6,4},{5,7},{7,5},{8,10},{10,8},{9,1... | collective-permute-start | bytes 4915208 | tf_op jit(solution)/shard_map/ppermute | solution.py:188
  254.3 83.9 %collective-permute-start.14 = (bf16[1280,1280]{1,0:T(8,128)(2,1)}, bf16[1280,1280]{1,0:T(8,128)(2,1)S(1)}, u32[]{:S(2)}, u32[]{:S(2)}) collective-permute-start(bf16[1280,1280]{1,0:T(8,128)(2,1)} %broadcast_select_fusion.2), channel_id=1, source_target_pairs={{0,8},{8,0},{16,24},{24,16},{1,9},{9,1},{17,25},{25,17},{2,10},{10... | collective-permute-start | bytes 9830408 | tf_op jit(solution)/shard_map/ppermute | solution.py:216
  254.3 83.9 %collective-permute-start.18 = (bf16[1280,1280]{1,0:T(8,128)(2,1)}, bf16[1280,1280]{1,0:T(8,128)(2,1)}, u32[]{:S(2)}, u32[]{:S(2)}) collective-permute-start(bf16[1280,1280]{1,0:T(8,128)(2,1)} %copy-done.5), channel_id=1, source_target_pairs={{8,16},{16,8},{9,17},{17,9},{10,18},{18,10},{11,19},{19,11},{12,20... | collective-permute-start | bytes 9830408 | tf_op jit(solution)/shard_map/ppermute | solution.py:216
  277.7 5.0 collective-permute-start.16
  277.7 8.5 collective-permute-start.17
  278.2 55.6 %collective-permute-start.15 = (bf16[3,320,1280]{2,1,0:T(8,128)(2,1)}, bf16[3,320,1280]{2,1,0:T(8,128)(2,1)}, u32[]{:S(2)}, u32[]{:S(2)}) collective-permute-start(bf16[3,320,1280]{2,1,0:T(8,128)(2,1)} %get-tuple-element.193), channel_id=1, source_target_pairs={{0,2},{2,0},{1,3},{3,1},{4,6},{6,4},{5,7},{7,5},{8,10},{10,8},{9,1... | collective-permute-start | bytes 7372808 | tf_op jit(solution)/shard_map/ppermute | solution.py:188
  357.8 10.7 %collective-permute-start.21 = (bf16[3,320,1280]{2,1,0:T(8,128)(2,1)}, bf16[3,320,1280]{2,1,0:T(8,128)(2,1)}, u32[]{:S(2)}, u32[]{:S(2)}) collective-permute-start(bf16[3,320,1280]{2,1,0:T(8,128)(2,1)} %get-tuple-element.210), channel_id=1, source_target_pairs={{0,1},{1,0},{2,3},{3,2},{4,5},{5,4},{6,7},{7,6},{8,9},{9,8},{10,11... | collective-permute-start | bytes 7372808 | tf_op jit(solution)/shard_map/ppermute | solution.py:180
  357.8 75.5 %collective-permute-start.19 = (bf16[1280,1280]{1,0:T(8,128)(2,1)}, bf16[1280,1280]{1,0:T(8,128)(2,1)}, u32[]{:S(2)}, u32[]{:S(2)}) collective-permute-start(bf16[1280,1280]{1,0:T(8,128)(2,1)} %bitcast.42.refs_3_), channel_id=1, source_target_pairs={{8,16},{16,8},{9,17},{17,9},{10,18},{18,10},{11,19},{19,11},{12,20... | collective-permute-start | bytes 9830408 | tf_op jit(solution)/shard_map/ppermute | solution.py:216
  360.4 75.0 %collective-permute-start.23 = (bf16[2,640,1280]{2,1,0:T(8,128)(2,1)}, bf16[2,640,1280]{2,1,0:T(8,128)(2,1)S(1)}, u32[]{:S(2)}, u32[]{:S(2)}) collective-permute-start(bf16[2,640,1280]{2,1,0:T(8,128)(2,1)} %get-tuple-element.216), channel_id=1, source_target_pairs={{0,8},{24,16},{1,9},{25,17},{2,10},{26,18},{3,11},{27,19},{4,12},{... | collective-permute-start | bytes 9830408 | tf_op jit(solution)/shard_map/ppermute | solution.py:216
  361.8 12.6 %collective-permute-start.22 = (bf16[3,320,1280]{2,1,0:T(8,128)(2,1)}, bf16[3,320,1280]{2,1,0:T(8,128)(2,1)}, u32[]{:S(2)}, u32[]{:S(2)}) collective-permute-start(bf16[3,320,1280]{2,1,0:T(8,128)(2,1)} %get-tuple-element.211), channel_id=1, source_target_pairs={{0,1},{1,0},{2,3},{3,2},{4,5},{5,4},{6,7},{7,6},{8,9},{9,8},{10,11... | collective-permute-start | bytes 7372808 | tf_op jit(solution)/shard_map/ppermute | solution.py:180
  362.0 56.0 %collective-permute-start.20 = (bf16[3,320,1280]{2,1,0:T(8,128)(2,1)}, bf16[3,320,1280]{2,1,0:T(8,128)(2,1)}, u32[]{:S(2)}, u32[]{:S(2)}) collective-permute-start(bf16[3,320,1280]{2,1,0:T(8,128)(2,1)} %get-tuple-element.206), channel_id=1, source_target_pairs={{0,2},{2,0},{1,3},{3,1},{4,6},{6,4},{5,7},{7,5},{8,10},{10,8},{9,1... | collective-permute-start | bytes 7372808 | tf_op jit(solution)/shard_map/ppermute | solution.py:188
  368.6 53.8 %collective-permute-start.24 = (bf16[2,2,160,1280]{3,2,1,0:T(8,128)(2,1)}, bf16[2,2,160,1280]{3,2,1,0:T(8,128)(2,1)}, u32[]{:S(2)}, u32[]{:S(2)}) collective-permute-start(bf16[2,2,160,1280]{3,2,1,0:T(8,128)(2,1)} %pad_maximum_fusion), channel_id=1, source_target_pairs={{8,0},{16,24},{9,1},{17,25},{10,2},{18,26},{11,3},{19,27},{12,4},{... | collective-permute-start | bytes 4915208 | tf_op jit(solution)/shard_map/ppermute | solution.py:216
  435.3 74.2 %collective-permute-start.28 = (bf16[1280,1280]{1,0:T(8,128)(2,1)}, bf16[1280,1280]{1,0:T(8,128)(2,1)}, u32[]{:S(2)}, u32[]{:S(2)}) collective-permute-start(bf16[1280,1280]{1,0:T(8,128)(2,1)} %bitcast.45.refs_3_), channel_id=1, source_target_pairs={{8,16},{16,8},{9,17},{17,9},{10,18},{18,10},{11,19},{19,11},{12,20... | collective-permute-start | bytes 9830408 | tf_op jit(solution)/shard_map/ppermute | solution.py:216
  438.8 72.1 %collective-permute-start.29 = (bf16[1280,1280]{1,0:T(8,128)(2,1)}, bf16[1280,1280]{1,0:T(8,128)(2,1)}, u32[]{:S(2)}, u32[]{:S(2)}) collective-permute-start(bf16[1280,1280]{1,0:T(8,128)(2,1)} %bitcast.42.refs_3_), channel_id=1, source_target_pairs={{0,8},{8,0},{16,24},{24,16},{1,9},{9,1},{17,25},{25,17},{2,10},{10... | collective-permute-start | bytes 9830408 | tf_op jit(solution)/shard_map/ppermute | solution.py:216
  438.9 54.6 %collective-permute-start.27 = (bf16[3,320,1280]{2,1,0:T(8,128)(2,1)}, bf16[3,320,1280]{2,1,0:T(8,128)(2,1)}, u32[]{:S(2)}, u32[]{:S(2)}) collective-permute-start(bf16[3,320,1280]{2,1,0:T(8,128)(2,1)} %get-tuple-element.226), channel_id=1, source_target_pairs={{0,2},{2,0},{1,3},{3,1},{4,6},{6,4},{5,7},{7,5},{8,10},{10,8},{9,1... | collective-permute-start | bytes 7372808 | tf_op jit(solution)/shard_map/ppermute | solution.py:188
  450.6 5.2 collective-permute-start.25
  450.7 6.8 collective-permute-start.26
  457.0 40.2 %collective-permute-start.30 = (bf16[2,160,1280]{2,1,0:T(8,128)(2,1)S(1)}, bf16[2,160,1280]{2,1,0:T(8,128)(2,1)S(1)}, u32[]{:S(2)}, u32[]{:S(2)}) collective-permute-start(bf16[2,160,1280]{2,1,0:T(8,128)(2,1)S(1)} %get-tuple-element.336), channel_id=1, source_target_pairs={{0,4},{4,0},{1,5},{5,1},{2,6},{6,2},{3,7},{7,3},{8,12},{12,8},{9,1... | collective-permute-start | bytes 2457608 | tf_op jit(solution)/shard_map/ppermute | solution.py:221
  511.0 73.0 %collective-permute-start.34 = (bf16[1280,1280]{1,0:T(8,128)(2,1)}, bf16[1280,1280]{1,0:T(8,128)(2,1)}, u32[]{:S(2)}, u32[]{:S(2)}) collective-permute-start(bf16[1280,1280]{1,0:T(8,128)(2,1)} %collective-permute-done.29.refs_4_), channel_id=1, source_target_pairs={{8,16},{16,8},{9,17},{17,9},{10,18},{18,10},{11,19},{19,11},{12,20... | collective-permute-start | bytes 9830408 | tf_op jit(solution)/shard_map/ppermute | solution.py:216
  528.0 7.2 collective-permute-start.32
  528.1 73.5 %collective-permute-start.35 = (bf16[1280,1280]{1,0:T(8,128)(2,1)}, bf16[1280,1280]{1,0:T(8,128)(2,1)S(1)}, u32[]{:S(2)}, u32[]{:S(2)}) collective-permute-start(bf16[1280,1280]{1,0:T(8,128)(2,1)} %bitcast.45.refs_3_), channel_id=1, source_target_pairs={{0,8},{8,0},{16,24},{24,16},{1,9},{9,1},{17,25},{25,17},{2,10},{10... | collective-permute-start | bytes 9830408 | tf_op jit(solution)/shard_map/ppermute | solution.py:216
  528.4 8.2 collective-permute-start.33
  528.6 38.4 %collective-permute-start.31 = (bf16[2,320,1280]{2,1,0:T(8,128)(2,1)}, bf16[2,320,1280]{2,1,0:T(8,128)(2,1)}, u32[]{:S(2)}, u32[]{:S(2)}) collective-permute-start(bf16[2,320,1280]{2,1,0:T(8,128)(2,1)} %get-tuple-element.234), channel_id=1, source_target_pairs={{0,2},{2,0},{1,3},{3,1},{4,6},{6,4},{5,7},{7,5},{8,10},{10,8},{9,1... | collective-permute-start | bytes 4915208 | tf_op jit(solution)/shard_map/ppermute | solution.py:188
  535.2 35.3 %collective-permute-start.36 = (bf16[2,160,1280]{2,1,0:T(8,128)(2,1)}, bf16[2,160,1280]{2,1,0:T(8,128)(2,1)}, u32[]{:S(2)}, u32[]{:S(2)}) collective-permute-start(bf16[2,160,1280]{2,1,0:T(8,128)(2,1)} %get-tuple-element.332), channel_id=1, source_target_pairs={{0,4},{4,0},{1,5},{5,1},{2,6},{6,2},{3,7},{7,3},{8,12},{12,8},{9,1... | collective-permute-start | bytes 2457608 | tf_op jit(solution)/shard_map/ppermute | solution.py:221
  601.6 335.8 %reduce-scatter.2.cloned.1.call-start = ((), (), s32[]{:S(2)}) async-start(), calls=%async_computation.2 | async-start | bytes 2359296 | tf_op jit(solution)/shard_map/reduce_scatter | solution.py:348
  617.8 16.6 %collective-permute-start.37 = (bf16[3,320,1280]{2,1,0:T(8,128)(2,1)}, bf16[3,320,1280]{2,1,0:T(8,128)(2,1)S(1)}, u32[]{:S(2)}, u32[]{:S(2)}) collective-permute-start(bf16[3,320,1280]{2,1,0:T(8,128)(2,1)} %get-tuple-element.249), channel_id=1, source_target_pairs={{0,1},{1,0},{2,3},{3,2},{4,5},{5,4},{6,7},{7,6},{8,9},{9,8},{10,11... | collective-permute-start | bytes 7372808 | tf_op jit(solution)/shard_map/ppermute | solution.py:180
  617.8 17.9 %collective-permute-start.38 = (bf16[3,320,1280]{2,1,0:T(8,128)(2,1)}, bf16[3,320,1280]{2,1,0:T(8,128)(2,1)S(1)}, u32[]{:S(2)}, u32[]{:S(2)}) collective-permute-start(bf16[3,320,1280]{2,1,0:T(8,128)(2,1)} %get-tuple-element.250), channel_id=1, source_target_pairs={{0,1},{1,0},{2,3},{3,2},{4,5},{5,4},{6,7},{7,6},{8,9},{9,8},{10,11... | collective-permute-start | bytes 7372808 | tf_op jit(solution)/shard_map/ppermute | solution.py:180
  618.9 55.6 %collective-permute-start.39 = (bf16[3,320,1280]{2,1,0:T(8,128)(2,1)}, bf16[3,320,1280]{2,1,0:T(8,128)(2,1)}, u32[]{:S(2)}, u32[]{:S(2)}) collective-permute-start(bf16[3,320,1280]{2,1,0:T(8,128)(2,1)} %get-tuple-element.256), channel_id=1, source_target_pairs={{0,2},{2,0},{1,3},{3,1},{4,6},{6,4},{5,7},{7,5},{8,10},{10,8},{9,1... | collective-permute-start | bytes 7372808 | tf_op jit(solution)/shard_map/ppermute | solution.py:188
  625.5 121.2 %collective-permute-start.40 = (bf16[1280,640]{1,0:T(8,128)(2,1)}, bf16[1280,640]{1,0:T(8,128)(2,1)S(1)}, u32[]{:S(2)}, u32[]{:S(2)}) collective-permute-start(bf16[1280,640]{1,0:T(8,128)(2,1)} %get-tuple-element.258), channel_id=1, source_target_pairs={{8,16},{16,8},{9,17},{17,9},{10,18},{18,10},{11,19},{19,11},{12,20... | collective-permute-start | bytes 4915208 | tf_op jit(solution)/shard_map/ppermute | solution.py:216
  630.8 49.3 %collective-permute-start.41 = (bf16[2,160,1280]{2,1,0:T(8,128)(2,1)}, bf16[2,160,1280]{2,1,0:T(8,128)(2,1)}, u32[]{:S(2)}, u32[]{:S(2)}) collective-permute-start(bf16[2,160,1280]{2,1,0:T(8,128)(2,1)} %bitcast.11), channel_id=1, source_target_pairs={{8,0},{16,24},{9,1},{17,25},{10,2},{18,26},{11,3},{19,27},{12,4},{... | collective-permute-start | bytes 2457608 | tf_op jit(solution)/shard_map/ppermute | solution.py:216
  634.4 93.6 %collective-permute-start.42 = (bf16[2,160,1280]{2,1,0:T(8,128)(2,1)}, bf16[2,160,1280]{2,1,0:T(8,128)(2,1)S(1)}, u32[]{:S(2)}, u32[]{:S(2)}) collective-permute-start(bf16[2,160,1280]{2,1,0:T(8,128)(2,1)} %bitcast.12), channel_id=1, source_target_pairs={{8,0},{16,24},{9,1},{17,25},{10,2},{18,26},{11,3},{19,27},{12,4},{... | collective-permute-start | bytes 2457608 | tf_op jit(solution)/shard_map/ppermute | solution.py:216
  637.3 90.7 %collective-permute-start.43 = (bf16[2,160,1280]{2,1,0:T(8,128)(2,1)}, bf16[2,160,1280]{2,1,0:T(8,128)(2,1)S(1)}, u32[]{:S(2)}, u32[]{:S(2)}) collective-permute-start(bf16[2,160,1280]{2,1,0:T(8,128)(2,1)} %get-tuple-element.338), channel_id=1, source_target_pairs={{0,4},{4,0},{1,5},{5,1},{2,6},{6,2},{3,7},{7,3},{8,12},{12,8},{9,1... | collective-permute-start | bytes 2457608 | tf_op jit(solution)/shard_map/ppermute | solution.py:221
  746.7 54.5 %collective-permute-start.44 = (bf16[3,320,1280]{2,1,0:T(8,128)(2,1)}, bf16[3,320,1280]{2,1,0:T(8,128)(2,1)}, u32[]{:S(2)}, u32[]{:S(2)}) collective-permute-start(bf16[3,320,1280]{2,1,0:T(8,128)(2,1)} %get-tuple-element.263), channel_id=1, source_target_pairs={{0,2},{2,0},{1,3},{3,1},{4,6},{6,4},{5,7},{7,5},{8,10},{10,8},{9,1... | collective-permute-start | bytes 7372808 | tf_op jit(solution)/shard_map/ppermute | solution.py:188
  756.5 10.7 %collective-permute-start.45 = (bf16[2,320,640]{2,1,0:T(8,128)(2,1)}, bf16[2,320,640]{2,1,0:T(8,128)(2,1)S(1)}, u32[]{:S(2)}, u32[]{:S(2)}) collective-permute-start(bf16[2,320,640]{2,1,0:T(8,128)(2,1)} %get-tuple-element.265), channel_id=1, source_target_pairs={{0,1},{1,0},{2,3},{3,2},{4,5},{5,4},{6,7},{7,6},{8,9},{9,8},{10,11... | collective-permute-start | bytes 2457608 | tf_op jit(solution)/shard_map/ppermute | solution.py:180
  756.5 11.3 %collective-permute-start.46 = (bf16[2,320,640]{2,1,0:T(8,128)(2,1)}, bf16[2,320,640]{2,1,0:T(8,128)(2,1)}, u32[]{:S(2)}, u32[]{:S(2)}) collective-permute-start(bf16[2,320,640]{2,1,0:T(8,128)(2,1)} %get-tuple-element.266), channel_id=1, source_target_pairs={{0,1},{1,0},{2,3},{3,2},{4,5},{5,4},{6,7},{7,6},{8,9},{9,8},{10,11... | collective-permute-start | bytes 2457608 | tf_op jit(solution)/shard_map/ppermute | solution.py:180
  757.0 63.6 %collective-permute-start.47 = (bf16[1280,640]{1,0:T(8,128)(2,1)}, bf16[1280,640]{1,0:T(8,128)(2,1)S(1)}, u32[]{:S(2)}, u32[]{:S(2)}) collective-permute-start(bf16[1280,640]{1,0:T(8,128)(2,1)} %get-tuple-element.271), channel_id=1, source_target_pairs={{8,16},{16,8},{9,17},{17,9},{10,18},{18,10},{11,19},{19,11},{12,20... | collective-permute-start | bytes 4915208 | tf_op jit(solution)/shard_map/ppermute | solution.py:216
  760.5 48.6 %collective-permute-start.48 = (bf16[2,160,1280]{2,1,0:T(8,128)(2,1)}, bf16[2,160,1280]{2,1,0:T(8,128)(2,1)}, u32[]{:S(2)}, u32[]{:S(2)}) collective-permute-start(bf16[2,160,1280]{2,1,0:T(8,128)(2,1)} %bitcast.93), channel_id=1, source_target_pairs={{8,0},{16,24},{9,1},{17,25},{10,2},{18,26},{11,3},{19,27},{12,4},{... | collective-permute-start | bytes 2457608 | tf_op jit(solution)/shard_map/ppermute | solution.py:216
  767.3 41.8 %collective-permute-start.49 = (bf16[2,160,1280]{2,1,0:T(8,128)(2,1)}, bf16[2,160,1280]{2,1,0:T(8,128)(2,1)S(1)}, u32[]{:S(2)}, u32[]{:S(2)}) collective-permute-start(bf16[2,160,1280]{2,1,0:T(8,128)(2,1)} %get-tuple-element.340), channel_id=1, source_target_pairs={{0,4},{4,0},{1,5},{5,1},{2,6},{6,2},{3,7},{7,3},{8,12},{12,8},{9,1... | collective-permute-start | bytes 2457608 | tf_op jit(solution)/shard_map/ppermute | solution.py:221
  767.8 41.3 %collective-permute-start.50 = (bf16[2,160,1280]{2,1,0:T(8,128)(2,1)}, bf16[2,160,1280]{2,1,0:T(8,128)(2,1)}, u32[]{:S(2)}, u32[]{:S(2)}) collective-permute-start(bf16[2,160,1280]{2,1,0:T(8,128)(2,1)} %get-tuple-element.334), channel_id=1, source_target_pairs={{0,4},{4,0},{1,5},{5,1},{2,6},{6,2},{3,7},{7,3},{8,12},{12,8},{9,1... | collective-permute-start | bytes 2457608 | tf_op jit(solution)/shard_map/ppermute | solution.py:221
  801.2 19.5 %collective-permute-start.51 = (bf16[2,160,1280]{2,1,0:T(8,128)(2,1)}, bf16[2,160,1280]{2,1,0:T(8,128)(2,1)}, u32[]{:S(2)}, u32[]{:S(2)}) collective-permute-start(bf16[2,160,1280]{2,1,0:T(8,128)(2,1)} %bitcast.21), channel_id=1, source_target_pairs={{4,0},{5,1},{6,2},{7,3},{12,8},{13,9},{14,10},{15,11},{20,16},{21,... | collective-permute-start | bytes 2457608 | tf_op jit(solution)/shard_map/ppermute | solution.py:247
  843.5 59.6 %collective-permute-start.58 = (bf16[2,160,1280]{2,1,0:T(8,128)(2,1)}, bf16[2,160,1280]{2,1,0:T(8,128)(2,1)}, u32[]{:S(2)}, u32[]{:S(2)}) collective-permute-start(bf16[2,160,1280]{2,1,0:T(8,128)(2,1)} %bitcast.82), channel_id=1, source_target_pairs={{8,4},{16,28},{9,5},{17,29},{10,6},{18,30},{11,7},{19,31}} | collective-permute-start | bytes 2457608 | tf_op jit(solution)/shard_map/ppermute | solution.py:241
  845.3 26.5 %collective-permute-start.56 = (bf16[2,320,640]{2,1,0:T(8,128)(2,1)}, bf16[2,320,640]{2,1,0:T(8,128)(2,1)}, u32[]{:S(2)}, u32[]{:S(2)}) collective-permute-start(bf16[2,320,640]{2,1,0:T(8,128)(2,1)} %get-tuple-element.296), channel_id=1, source_target_pairs={{0,2},{2,0},{1,3},{3,1},{4,6},{6,4},{5,7},{7,5},{8,10},{10,8},{9,1... | collective-permute-start | bytes 2457608 | tf_op jit(solution)/shard_map/ppermute | solution.py:188
  853.9 5.7 collective-permute-start.53
  853.9 5.7 collective-permute-start.54
  856.4 28.2 %collective-permute-start.63 = (bf16[2,160,1280]{2,1,0:T(8,128)(2,1)}, bf16[2,160,1280]{2,1,0:T(8,128)(2,1)S(1)}, u32[]{:S(2)}, u32[]{:S(2)}) collective-permute-start(bf16[2,160,1280]{2,1,0:T(8,128)(2,1)} %get-tuple-element.329), channel_id=1, source_target_pairs={{0,4},{4,0},{1,5},{5,1},{2,6},{6,2},{3,7},{7,3},{8,12},{12,8},{9,1... | collective-permute-start | bytes 2457608 | tf_op jit(solution)/shard_map/ppermute | solution.py:221
  867.7 32.0 %collective-permute-start.55 = (bf16[2,320,640]{2,1,0:T(8,128)(2,1)}, bf16[2,320,640]{2,1,0:T(8,128)(2,1)}, u32[]{:S(2)}, u32[]{:S(2)}) collective-permute-start(bf16[2,320,640]{2,1,0:T(8,128)(2,1)} %get-tuple-element.294), channel_id=1, source_target_pairs={{0,2},{2,0},{1,3},{3,1},{4,6},{6,4},{5,7},{7,5},{8,10},{10,8},{9,1... | collective-permute-start | bytes 2457608 | tf_op jit(solution)/shard_map/ppermute | solution.py:188
  869.9 34.2 %collective-permute-start.52 = (bf16[2,160,1280]{2,1,0:T(8,128)(2,1)}, bf16[2,160,1280]{2,1,0:T(8,128)(2,1)}, u32[]{:S(2)}, u32[]{:S(2)}) collective-permute-start(bf16[2,160,1280]{2,1,0:T(8,128)(2,1)} %broadcast_select_fusion.15), channel_id=1, source_target_pairs={{8,12},{16,20},{12,4},{20,28},{9,13},{17,21},{13,5},{21,29},{10,14... | collective-permute-start | bytes 2457608 | tf_op jit(solution)/shard_map/ppermute | solution.py:240
  871.8 36.7 %collective-permute-start.59 = (bf16[2,160,1280]{2,1,0:T(8,128)(2,1)S(1)}, bf16[2,160,1280]{2,1,0:T(8,128)(2,1)}, u32[]{:S(2)}, u32[]{:S(2)}) collective-permute-start(bf16[2,160,1280]{2,1,0:T(8,128)(2,1)S(1)} %bitcast.71), channel_id=1, source_target_pairs={{4,0},{5,1},{6,2},{7,3},{12,8},{13,9},{14,10},{15,11},{20,16},{21,... | collective-permute-start | bytes 2457608 | tf_op jit(solution)/shard_map/ppermute | solution.py:247
  884.5 29.6 %collective-permute-start.62 = (bf16[2,160,640]{2,1,0:T(8,128)(2,1)S(1)}, bf16[2,160,640]{2,1,0:T(8,128)(2,1)}, u32[]{:S(2)}, u32[]{:S(2)}) collective-permute-start(bf16[2,160,640]{2,1,0:T(8,128)(2,1)S(1)} %bitcast.90), channel_id=1, source_target_pairs={{8,4},{16,28},{9,5},{17,29},{10,6},{18,30},{11,7},{19,31}} | collective-permute-start | bytes 1228808 | tf_op jit(solution)/shard_map/ppermute | solution.py:241
  899.8 14.4 %collective-permute-start.61 = (bf16[2,160,640]{2,1,0:T(8,128)(2,1)S(1)}, bf16[2,160,640]{2,1,0:T(8,128)(2,1)S(1)}, u32[]{:S(2)}, u32[]{:S(2)}) collective-permute-start(bf16[2,160,640]{2,1,0:T(8,128)(2,1)S(1)} %copy-done.34), channel_id=1, source_target_pairs={{8,12},{16,20},{12,4},{20,28},{9,13},{17,21},{13,5},{21,29},{10,14... | collective-permute-start | bytes 1228808 | tf_op jit(solution)/shard_map/ppermute | solution.py:240
  903.2 18.1 %collective-permute-start.60 = (bf16[2,160,640]{2,1,0:T(8,128)(2,1)S(1)}, bf16[2,160,640]{2,1,0:T(8,128)(2,1)S(1)}, u32[]{:S(2)}, u32[]{:S(2)}) collective-permute-start(bf16[2,160,640]{2,1,0:T(8,128)(2,1)S(1)} %bitcast.92), channel_id=1, source_target_pairs={{8,4},{16,28},{9,5},{17,29},{10,6},{18,30},{11,7},{19,31}} | collective-permute-start | bytes 1228808 | tf_op jit(solution)/shard_map/ppermute | solution.py:241
  904.1 17.2 %collective-permute-start.57 = (bf16[2,160,640]{2,1,0:T(8,128)(2,1)S(1)}, bf16[2,160,640]{2,1,0:T(8,128)(2,1)S(1)}, u32[]{:S(2)}, u32[]{:S(2)}) collective-permute-start(bf16[2,160,640]{2,1,0:T(8,128)(2,1)S(1)} %broadcast_select_fusion.23), channel_id=1, source_target_pairs={{8,12},{16,20},{12,4},{20,28},{9,13},{17,21},{13,5},{21,29},{10,14... | collective-permute-start | bytes 1228808 | tf_op jit(solution)/shard_map/ppermute | solution.py:240
  (40 other events, 321.3 us)
Sparse Core Ops, SparseCore 0:
  601.8 154.7 all-gather.1
  843.7 49.5 reduce-scatter.1

commit v5 on v4

--- a/solution.py
+++ b/solution.py
@@ -125,9 +125,8 @@
 
     pieces = kept + arrived
     specs = [
-        pl.BlockSpec((1, block, columns), lambda a, i, base, j=j, step=array.shape[0] - 2: (
-            a + step * (1 - base[1]), i, j))
-        for array, j in pieces]
+        pl.BlockSpec((1, block, columns), lambda a, i, base, j=j, first=first: (first + a, i, j))
+        for _, first, j in pieces]
     extra = [] if out is None else [out]
     return pl.pallas_call(
         kernel,
@@ -145,7 +144,7 @@
         compiler_params=pltpu.CompilerParams(vmem_limit_bytes=ROOM),
         cost_estimate=CHEAP,
         name="place",
-    )(base, *[array for array, _ in pieces], *extra)
+    )(base, *[array for array, _, _ in pieces], *extra)
 
 
 class Order:
@@ -188,8 +187,7 @@
         self.other = lax.ppermute(self.order.open(self.away), "ka", OTHER_Y)
 
     def finish(self):
-        other = self.order.follow(self.other)
-        total = self.order.step((self.own.astype(F32) + other.astype(F32)).astype(BF16))
+        total = (self.own.astype(F32) + self.order.open(self.other).astype(F32)).astype(BF16)
         count, rows, columns = total.shape
         return [total[p].reshape(2, rows // 2, columns) for p in range(count)]
 
@@ -215,10 +213,10 @@
     def move(value, route):
         return lax.ppermute(order.open(value), "vir", route)
 
-    def cross(near, far):
-        near, far = order.open(near), order.open(far)
-        away = jnp.where(occ == 0, far, near)
-        return jnp.where(occ == 0, near, far), lax.ppermute(away, "occ", OTHER_OCC)
+    def cross(*pairs):
+        pairs = [(order.open(near), order.open(far)) for near, far in pairs]
+        away = jnp.concatenate([jnp.where(occ == 0, far, near) for near, far in pairs])
+        return [jnp.where(occ == 0, near, far) for near, far in pairs], lax.ppermute(away, "occ", OTHER_OCC)
 
     def home(mine, back):
         return jnp.where(at_end, order.open(back), order.open(mine))
@@ -228,8 +226,8 @@
 
     def put(half, j, crossed, out):
         base = jnp.stack([low if half == 0 else 2 - low, occ.astype(jnp.int32)])
-        kept = [(pair[0], jj) for pair, jj in crossed]
-        arrived = [(pair[1], jj) for pair, jj in crossed]
+        kept = [(pair[0][index], 0, jj) for pair, index, jj in crossed]
+        arrived = [(pair[1], 2 * index, jj) for pair, index, jj in crossed]
         return order.step(place(base, j, kept, arrived, out, shape))
 
     def rows_of(g):
@@ -241,7 +239,7 @@
         second = lax.ppermute(foreign, ("vir", "occ"), [(2, 1), (4, 7)])
         kept = jnp.where(occ == 0, near[..., one], jnp.where(at_end, first, own_rows))
         arrived = jnp.where(occ == 0, near_in[..., one], jnp.where(at_end, second, first))
-        return kept, arrived
+        return [kept], arrived
 
     def over(near):
         return lax.ppermute(order.open(near), "occ", [(1, 0)])
@@ -263,9 +261,10 @@
     two = batch((0, ca, own0), (0, a0, own0))
     two.send()
     two.keep()
+    rows1 = rows_of(1)
+
+    order.phase(own3, swap3, rows1, one.other)
     s3, s1 = one.finish()
-
-    order.phase(own3, swap3)
     relay3 = move(swap3, MID_TO_MID)
     both3 = exchange(b0, own3)
     two.swap()
@@ -273,94 +272,91 @@
     three = batch((3, ca, swap3), (0, ca, b0), (0, a0, b0))
     three.send()
     three.keep()
+    rows2 = rows_of(2)
+
+    order.phase(relay3, both3, rows2, b2, two.other)
     f0 = two.finish()
-
-    order.phase(relay3, both3)
     relay0 = move(both3, MID_TO_MID)
-    both4 = exchange(rows_of(1).reshape(b0.shape), relay3)
+    both4 = exchange(rows1.reshape(b0.shape), relay3)
     three.swap()
     four = batch((2, ca, b2), (0, ca, both3), (3, ca, jnp.where(at_end, order.open(both3), own3)))
     four.send()
     four.keep()
+
+    order.phase(relay0, both4, three.other)
     n3, *s0 = three.finish()
-    rows2 = rows_of(2)
-
-    order.phase(relay0, both4, rows2)
     a1 = both4.reshape(a0.shape)
     own1 = move(b1, MID_TO_MID)
-    a2 = move(rows2, END_TO_MID)
-    backs = move(jnp.stack([f0[1], s0[1]]), MID_TO_END)
+    both5 = exchange(rows2.reshape(b0.shape), jnp.concatenate([f0[1], s0[1]] * 2).reshape(b0.shape))
     four.swap()
     five = batch((0, ca, relay0), (0, a0, relay0), (3, ca, jnp.where(at_end, order.open(both4), relay3)))
     five.send()
     five.keep()
+
+    order.phase(own1, both5, four.other)
     s2, n0, f3 = four.finish()
-
-    order.phase(own1, a2, backs)
-    f0_back, s0_back = backs[0], backs[1]
+    a2 = both5.reshape(a0.shape)
+    backs = both5.reshape(8, quarter, 2 * columns)
+    f0_back, s0_back = backs[0:2], backs[2:4]
     own2 = move(b2, MID_TO_MID)
     swap1 = move(b1, NEIGHBOUR)
-    x0a = cross(s0[0], home(f0[0], f0_back))
+    x03a = cross((s0[0], home(f0[0], f0_back)), (s3, f3))
     five.swap()
     six = batch((1, ca, own1), (1, a1, own1))
     six.send()
     six.keep()
+
+    order.phase(own2, swap1, x03a[1], five.other)
     *g0, g3 = five.finish()
-
-    order.phase(own2, swap1, x0a[1])
     relay1 = move(swap1, MID_TO_MID)
     swap2 = move(b2, NEIGHBOUR)
-    x3a = cross(s3, f3)
     six.swap()
     seven = batch((2, ca, own2), (2, a2, own2), (1, ca, swap1))
     seven.send()
     seven.keep()
+
+    order.phase(relay1, swap2, six.other)
     f1 = six.finish()
-
-    order.phase(relay1, swap2, x3a[1])
-    gathered = lax.all_gather(order.open(ladder_amplitudes), "vir", axis=0, tiled=True)
     relay2 = [move(swap2[:, :columns], MID_TO_MID)]
-    g0_back = move(g0[1], MID_TO_END)
-    f1_back = move(f1[1], MID_TO_END)
-    x3b = cross(n3, g3)
+    backs = move(jnp.concatenate([g0[1], f1[1]]), MID_TO_END)
     seven.swap()
     eight = batch((1, ca, relay1), (1, a1, relay1), (2, ca, swap2))
     eight.send()
     eight.keep()
+
+    order.phase(relay2[0], backs, seven.other)
     *f2, n1 = seven.finish()
-
-    order.phase(relay2[0], g0_back, f1_back, x3b[1])
     relay2.append(move(swap2[:, columns:], MID_TO_MID))
+    gathered = lax.all_gather(order.open(ladder_amplitudes), "vir", axis=0, tiled=True)
+    g0_back, f1_back = backs[0:2], backs[2:4]
     f2_back = move(f2[1], MID_TO_END)
-    x0b = cross(home(n0, s0_back), home(g0[0], g0_back))
-    x1a = cross(s1, home(f1[0], f1_back))
-    near1_in = over(n1)
+    x01 = cross((home(n0, s0_back), home(g0[0], g0_back)), (s1, home(f1[0], f1_back)), (n3, g3))
     eight.swap()
     nine = batch((2, ca, relay2[0]), (2, a2, relay2[0]))
     nine.send()
     nine.keep()
+
+    order.phase(relay2[1], f2_back, x01[1], eight.other)
     *g1, n2 = eight.finish()
-
-    order.phase(relay2[1], f2_back, x0b[1], x1a[1], near1_in, gathered)
-    partial_ladder = order.step(jnp.dot(
-        order.follow(gathered), ladder_integrals, preferred_element_type=F32,
-    ).astype(BF16))
-    ladder_residual = lax.psum_scatter(partial_ladder, ("occ", "ka"), scatter_dimension=0, tiled=True)
-    near2_in = over(n2)
-    x2a = cross(s2, home(f2[0], f2_back))
     nine.swap()
     ten = batch((2, ca, relay2[1]), (2, a2, relay2[1]))
     ten.send()
     ten.keep()
     ten.swap()
+    x2a = cross((s2, home(f2[0], f2_back)))
+    near1_in, near2_in = over(n1), over(n2)
     x1b = straight(n1, near1_in, g1)
     x2b = [straight(n2, near2_in, nine.finish(), slice(0, columns))]
-    x2b.append(straight(n2, near2_in, ten.finish(), slice(columns, 2 * columns)))
     out = None
     for j in range(2):
-        out = put(0, j, [(x0a, j), (x1a, j), (x2a, j), (x3a, j)], out)
+        out = put(0, j, [(x03a, 0, j), (x01, 1, j), (x2a, 0, j), (x03a, 1, j)], out)
+    x2b.append(straight(n2, near2_in, ten.finish(), slice(columns, 2 * columns)))
+    partial_ladder = order.step(jnp.dot(
+        order.follow(gathered), ladder_integrals, preferred_element_type=F32,
+    ).astype(BF16))
+    ladder_residual = lax.psum_scatter(partial_ladder, ("occ", "ka"), scatter_dimension=0, tiled=True)
     for j in range(2):
-        out = put(1, j, [(x0b, j), (x1b, j), (x2b[j], 0), (x3b, j)], out)
+        out = put(1, j, [(x01, 0, j), (x1b, 0, j), (x2b[j], 0, 0), (x01, 2, j)], out)
     return ladder_residual, out
 
 

time: 958 us -> 957 us (level)
  waiting for transfers between devices: 422 us -> 438 us
    ppermute x10, waiting for transfers between devices: 180 us -> 125 us  [swap(): self.other = lax.ppermute(self.order.open(self.away), 'ka', OTHER_Y)]
    ppermute x20 -> x18, waiting for transfers between devices: 190 us -> 230 us  [move(): return lax.ppermute(order.open(value), 'vir', route)]
    ppermute x6 -> x3, waiting for transfers between devices: 4.73 us -> 27.2 us  [cross(): lax.ppermute(away, 'occ', OTHER_OCC)]
    ppermute x2, waiting for transfers between devices: 11.6 us -> 23.4 us  [over(): return lax.ppermute(order.open(near), 'occ', [(1, 0)])]
    ppermute x20 -> x18, starting transfers between devices: 44.9 us -> 46.1 us  [move(): return lax.ppermute(order.open(value), 'vir', route)]
  transfers between devices with their start and end apart: 66 -> 61, of which waited for: 38 -> 30; matrix products, arithmetic and copies ran while one was open for 10% -> 10% of each run, Pallas kernels for 27% -> 28%
where the time goes in v5:
time: 957 us; the launch traced here: 947 us
  waiting for transfers between devices  438 us (46%)
  Pallas kernels  275 us (29%)
  starting transfers between devices  80 us (8%)
  other arithmetic  63.5 us (7%)
  local copies, waits for them, and re-layouts  54.4 us (6%)
  matrix products  22.2 us (2%)
  between operations  14.8 us (2%)
    ppermute x18, waiting for transfers between devices, move(): return lax.ppermute(order.open(value), 'vir', route)  230 us
    pallas_call x10, Pallas kernels, keep_products(): pl.pallas_call(kernel, out_shape=(jax.ShapeDtypeStruct((count, rows, colu...  126 us
    ppermute x10, waiting for transfers between devices, swap(): self.other = lax.ppermute(self.order.open(self.away), 'ka', OTHER_Y)  125 us
    pallas_call x10, Pallas kernels, send_products(): pl.pallas_call(kernel, out_shape=(jax.ShapeDtypeStruct((count, rows, colu...  121 us
    ppermute x18, starting transfers between devices, move(): return lax.ppermute(order.open(value), 'vir', route)  46.1 us
    convert_element_type x10, other arithmetic, finish(): (self.own.astype(F32) + self.order.open(self.other).astype(F32)).astype(B...  27.4 us
    pallas_call x4, Pallas kernels, place(): pl.pallas_call(kernel, out_shape=jax.ShapeDtypeStruct(shape, BF16), grid_...  27.2 us
    ppermute x3, waiting for transfers between devices, cross(): lax.ppermute(away, 'occ', OTHER_OCC)  27.2 us
  transfers between devices with their start and end apart: 61, of which 30 were waited for; matrix products, arithmetic and copies ran while one was open for 10% of the time, Pallas kernels for 28%

profile of v5, /device:TPU:10, one launch (start us, length us, event | category | flops | bytes accessed | tf_op | source)
XLA Modules:
  0.0 947.2 jit_solution(9244428380312303685)
XLA Ops:
  11.5 3.8 slice_bitcast_fusion
  16.6 3.5 collective-permute-start.2
  20.1 6.9 fusion.1
  32.2 11.1 %send_products.10 = (bf16[2,320,1280]{2,1,0:T(8,128)(2,1)}, bf16[2,320,1280]{2,1,0:T(8,128)(2,1)}) custom-call(s32[4]{0:T(128)} %broadcast_xor_fusion.where_ref, bf16[4,2,640,1280]{3,2,1,0:T(8,128)(2,1)} %refs_0_.39, bf16[4,2,640,1280]{3,2,1,0:T(8,128)(2,1)} %refs_0_.39, bf16[1280,1280]{1,0:T(8,128)(2,1)} %bitcast.65, bf16[1280,1280]{1,0:T(8,128)(2,1)} %bitcast.46.refs_3_), custom_call_target="tpu_custom_call" | custom-call | flops 1048576 | bytes 65536 | tf_op jit(solution)/shard_map/send_products/pallas_call | solution.py:70
  43.8 3.3 collective-permute-done.refs_4_
  49.5 11.7 %keep_products.10 = (bf16[2,320,1280]{2,1,0:T(8,128)(2,1)}, bf16[2,320,1280]{2,1,0:T(8,128)(2,1)}) custom-call(s32[4]{0:T(128)} %broadcast_xor_fusion.where_ref, bf16[4,2,640,1280]{3,2,1,0:T(8,128)(2,1)} %refs_0_.39, bf16[4,2,640,1280]{3,2,1,0:T(8,128)(2,1)} %refs_0_.39, bf16[1280,1280]{1,0:T(8,128)(2,1)} %bitcast.66, bf16[1280,1280]{1,0:T(8,128)(2,1)} %bitcast.46.refs_3_, ...), custom_call_target="tpu_custom_call" | custom-call | flops 1048576 | bytes 65536 | tf_op jit(solution)/shard_map/keep_products/pallas_call | solution.py:97
  61.2 28.8 %collective-permute-done.3.refs_1_.refs_2_ = bf16[2,640,1280]{2,1,0:T(8,128)(2,1)S(1)} collective-permute-done((bf16[2,640,1280]{2,1,0:T(8,128)(2,1)}, bf16[2,640,1280]{2,1,0:T(8,128)(2,1)S(1)}, u32[]{:S(2)}, u32[]{:S(2)}) %collective-permute-start.3) | collective-permute-done | bytes 3276832 | tf_op jit(solution)/shard_map/ppermute | solution.py:214
  91.4 3.6 collective-permute-start.7
  95.2 10.1 %send_products.11 = (bf16[2,320,1280]{2,1,0:T(8,128)(2,1)}, bf16[2,320,1280]{2,1,0:T(8,128)(2,1)}) custom-call(s32[4]{0:T(128)} %broadcast_xor_fusion.where_ref, bf16[4,2,640,1280]{3,2,1,0:T(8,128)(2,1)} %refs_0_.39, bf16[2,640,1280]{2,1,0:T(8,128)(2,1)} %copy-done.1, bf16[1280,1280]{1,0:T(8,128)(2,1)} %collective-permute-done.2.refs_2_), custom_call_target="tpu_custom_call" | custom-call | flops 1048576 | bytes 65536 | tf_op jit(solution)/shard_map/send_products/pallas_call | solution.py:70
  107.3 3.9 slice_bitcast_fusion.2
  113.6 10.8 %keep_products.11 = (bf16[2,320,1280]{2,1,0:T(8,128)(2,1)}, bf16[2,320,1280]{2,1,0:T(8,128)(2,1)}) custom-call(s32[4]{0:T(128)} %broadcast_xor_fusion.where_ref, bf16[4,2,640,1280]{3,2,1,0:T(8,128)(2,1)} %refs_0_.39, bf16[2,640,1280]{2,1,0:T(8,128)(2,1)} %copy-done.1, bf16[1280,1280]{1,0:T(8,128)(2,1)} %collective-permute-done.2.refs_2_, ...), custom_call_target="tpu_custom_call" | custom-call | flops 1048576 | bytes 65536 | tf_op jit(solution)/shard_map/keep_products/pallas_call | solution.py:97
  124.4 19.4 %collective-permute-done.8 = bf16[2,320,1280]{2,1,0:T(8,128)(2,1)} collective-permute-done((bf16[2,320,1280]{2,1,0:T(8,128)(2,1)}, bf16[2,320,1280]{2,1,0:T(8,128)(2,1)}, u32[]{:S(2)}, u32[]{:S(2)}) %collective-permute-start.8) | collective-permute-done | bytes 1638432 | tf_op jit(solution)/shard_map/ppermute | solution.py:187
  143.8 21.6 %collective-permute-done.7 = bf16[1280,1280]{1,0:T(8,128)(2,1)} collective-permute-done((bf16[1280,1280]{1,0:T(8,128)(2,1)}, bf16[1280,1280]{1,0:T(8,128)(2,1)}, u32[]{:S(2)}, u32[]{:S(2)}) %collective-permute-start.7) | collective-permute-done | bytes 3276832 | tf_op jit(solution)/shard_map/ppermute | solution.py:214
  167.0 4.0 broadcast_select_fusion.4
  173.9 14.4 %send_products.12 = (bf16[3,320,1280]{2,1,0:T(8,128)(2,1)}, bf16[3,320,1280]{2,1,0:T(8,128)(2,1)}) custom-call(s32[4]{0:T(128)} %broadcast_xor_fusion.where_ref, bf16[4,2,640,1280]{3,2,1,0:T(8,128)(2,1)} %refs_0_.39, bf16[4,2,640,1280]{3,2,1,0:T(8,128)(2,1)} %refs_0_.39, bf16[2,640,1280]{2,1,0:T(8,128)(2,1)} %copy-done.1, ...), custom_call_target="tpu_custom_call" | custom-call | flops 1048576 | bytes 65536 | tf_op jit(solution)/shard_map/send_products/pallas_call | solution.py:70
  192.7 3.8 fusion
  196.8 15.2 %keep_products.12 = (bf16[3,320,1280]{2,1,0:T(8,128)(2,1)}, bf16[3,320,1280]{2,1,0:T(8,128)(2,1)}) custom-call(s32[4]{0:T(128)} %broadcast_xor_fusion.where_ref, bf16[4,2,640,1280]{3,2,1,0:T(8,128)(2,1)} %refs_0_.39, bf16[4,2,640,1280]{3,2,1,0:T(8,128)(2,1)} %refs_0_.39, bf16[2,640,1280]{2,1,0:T(8,128)(2,1)} %copy-done.1, ...), custom_call_target="tpu_custom_call" | custom-call | flops 1048576 | bytes 65536 | tf_op jit(solution)/shard_map/keep_products/pallas_call | solution.py:97
  212.0 14.9 %collective-permute-done.13 = bf16[2,320,1280]{2,1,0:T(8,128)(2,1)} collective-permute-done((bf16[2,320,1280]{2,1,0:T(8,128)(2,1)}, bf16[2,320,1280]{2,1,0:T(8,128)(2,1)}, u32[]{:S(2)}, u32[]{:S(2)}) %collective-permute-start.13) | collective-permute-done | bytes 1638432 | tf_op jit(solution)/shard_map/ppermute | solution.py:187
  226.9 14.9 %collective-permute-done.12.refs_4_ = bf16[1280,1280]{1,0:T(8,128)(2,1)S(1)} collective-permute-done((bf16[1280,1280]{1,0:T(8,128)(2,1)}, bf16[1280,1280]{1,0:T(8,128)(2,1)S(1)}, u32[]{:S(2)}, u32[]{:S(2)}) %collective-permute-start.12) | collective-permute-done | bytes 3276832 | tf_op jit(solution)/shard_map/ppermute | solution.py:214
  244.1 4.0 broadcast_select_fusion.3
  250.8 4.1 broadcast_select_fusion.2.refs_5_
  254.9 15.4 %send_products.13 = (bf16[3,320,1280]{2,1,0:T(8,128)(2,1)}, bf16[3,320,1280]{2,1,0:T(8,128)(2,1)}) custom-call(s32[4]{0:T(128)} %broadcast_xor_fusion.where_ref, bf16[4,2,640,1280]{3,2,1,0:T(8,128)(2,1)} %refs_0_.39, bf16[4,2,640,1280]{3,2,1,0:T(8,128)(2,1)} %refs_0_.39, bf16[4,2,640,1280]{3,2,1,0:T(8,128)(2,1)} %refs_0_.39, bf16[1280,1280]{1,0:T(8,128)(2,1)} %bitcast.69, ...), custom_call_target="tpu_custom_call" | custom-call | flops 1048576 | bytes 65536 | tf_op jit(solution)/shard_map/send_products/pallas_call | solution.py:70
  275.7 3.2 collective-permute-done.17.refs_7_
  278.9 16.2 %keep_products.13 = (bf16[3,320,1280]{2,1,0:T(8,128)(2,1)}, bf16[3,320,1280]{2,1,0:T(8,128)(2,1)}) custom-call(s32[4]{0:T(128)} %broadcast_xor_fusion.where_ref, bf16[4,2,640,1280]{3,2,1,0:T(8,128)(2,1)} %refs_0_.39, bf16[4,2,640,1280]{3,2,1,0:T(8,128)(2,1)} %refs_0_.39, bf16[4,2,640,1280]{3,2,1,0:T(8,128)(2,1)} %refs_0_.39, bf16[1280,1280]{1,0:T(8,128)(2,1)} %bitcast.70, ...), custom_call_target="tpu_custom_call" | custom-call | flops 1048576 | bytes 65536 | tf_op jit(solution)/shard_map/keep_products/pallas_call | solution.py:97
  295.0 31.5 %collective-permute-done.18 = bf16[3,320,1280]{2,1,0:T(8,128)(2,1)} collective-permute-done((bf16[3,320,1280]{2,1,0:T(8,128)(2,1)}, bf16[3,320,1280]{2,1,0:T(8,128)(2,1)}, u32[]{:S(2)}, u32[]{:S(2)}) %collective-permute-start.18) | collective-permute-done | bytes 2457632 | tf_op jit(solution)/shard_map/ppermute | solution.py:187
  326.5 4.2 add_convert_fusion.4
  334.0 5.8 broadcast_select_fusion
  339.8 13.5 %collective-permute-start.21 = (bf16[1280,1280]{1,0:T(8,128)(2,1)}, bf16[1280,1280]{1,0:T(8,128)(2,1)}, u32[]{:S(2)}, u32[]{:S(2)}) collective-permute-start(bf16[1280,1280]{1,0:T(8,128)(2,1)} %bitcast.46.refs_3_), channel_id=1, source_target_pairs={{8,16},{16,8},{9,17},{17,9},{10,18},{18,10},{11,19},{19,11},{12,20... | collective-permute-start | bytes 9830408 | tf_op jit(solution)/shard_map/ppermute | solution.py:214
  353.2 14.5 %send_products.14 = (bf16[3,320,1280]{2,1,0:T(8,128)(2,1)}, bf16[3,320,1280]{2,1,0:T(8,128)(2,1)}) custom-call(s32[4]{0:T(128)} %broadcast_xor_fusion.where_ref, bf16[4,2,640,1280]{3,2,1,0:T(8,128)(2,1)} %refs_0_.39, bf16[2,640,1280]{2,1,0:T(8,128)(2,1)} %copy-done.1, bf16[4,2,640,1280]{3,2,1,0:T(8,128)(2,1)} %refs_0_.39, ...), custom_call_target="tpu_custom_call" | custom-call | flops 1048576 | bytes 65536 | tf_op jit(solution)/shard_map/send_products/pallas_call | solution.py:70
  376.2 15.2 %keep_products.14 = (bf16[3,320,1280]{2,1,0:T(8,128)(2,1)}, bf16[3,320,1280]{2,1,0:T(8,128)(2,1)}) custom-call(s32[4]{0:T(128)} %broadcast_xor_fusion.where_ref, bf16[4,2,640,1280]{3,2,1,0:T(8,128)(2,1)} %refs_0_.39, bf16[2,640,1280]{2,1,0:T(8,128)(2,1)} %copy-done.1, bf16[4,2,640,1280]{3,2,1,0:T(8,128)(2,1)} %refs_0_.39, ...), custom_call_target="tpu_custom_call" | custom-call | flops 1048576 | bytes 65536 | tf_op jit(solution)/shard_map/keep_products/pallas_call | solution.py:97
  391.4 32.4 %collective-permute-done.23 = bf16[3,320,1280]{2,1,0:T(8,128)(2,1)} collective-permute-done((bf16[3,320,1280]{2,1,0:T(8,128)(2,1)}, bf16[3,320,1280]{2,1,0:T(8,128)(2,1)}, u32[]{:S(2)}, u32[]{:S(2)}) %collective-permute-start.23) | collective-permute-done | bytes 2457632 | tf_op jit(solution)/shard_map/ppermute | solution.py:187
  423.9 4.2 add_convert_fusion.3
  430.8 10.6 %send_products.15 = (bf16[2,320,1280]{2,1,0:T(8,128)(2,1)}, bf16[2,320,1280]{2,1,0:T(8,128)(2,1)}) custom-call(s32[4]{0:T(128)} %broadcast_xor_fusion.where_ref, bf16[4,2,640,1280]{3,2,1,0:T(8,128)(2,1)} %refs_0_.39, bf16[2,640,1280]{2,1,0:T(8,128)(2,1)} %bitcast.61, bf16[1280,1280]{1,0:T(8,128)(2,1)} %collective-permute-done.21.refs_2_), custom_call_target="tpu_custom_call" | custom-call | flops 1048576 | bytes 65536 | tf_op jit(solution)/shard_map/send_products/pallas_call | solution.py:70
  442.1 3.5 collective-permute-start.27
  451.2 10.8 %keep_products.15 = (bf16[2,320,1280]{2,1,0:T(8,128)(2,1)}, bf16[2,320,1280]{2,1,0:T(8,128)(2,1)}) custom-call(s32[4]{0:T(128)} %broadcast_xor_fusion.where_ref, bf16[4,2,640,1280]{3,2,1,0:T(8,128)(2,1)} %refs_0_.39, bf16[2,640,1280]{2,1,0:T(8,128)(2,1)} %bitcast.62, bf16[1280,1280]{1,0:T(8,128)(2,1)} %collective-permute-done.21.refs_2_, ...), custom_call_target="tpu_custom_call" | custom-call | flops 1048576 | bytes 65536 | tf_op jit(solution)/shard_map/keep_products/pallas_call | solution.py:97
  462.0 27.2 %collective-permute-done.28.refs_4_.refs_7_ = bf16[4,160,1280]{2,1,0:T(8,128)(2,1)} collective-permute-done((bf16[4,160,1280]{2,1,0:T(8,128)(2,1)}, bf16[4,160,1280]{2,1,0:T(8,128)(2,1)}, u32[]{:S(2)}, u32[]{:S(2)}) %collective-permute-start.28) | collective-permute-done | bytes 1638432 | tf_op jit(solution)/shard_map/ppermute | solution.py:219
  489.2 12.0 %collective-permute-done.29 = bf16[3,320,1280]{2,1,0:T(8,128)(2,1)} collective-permute-done((bf16[3,320,1280]{2,1,0:T(8,128)(2,1)}, bf16[3,320,1280]{2,1,0:T(8,128)(2,1)}, u32[]{:S(2)}, u32[]{:S(2)}) %collective-permute-start.29) | collective-permute-done | bytes 2457632 | tf_op jit(solution)/shard_map/ppermute | solution.py:187
  501.2 13.9 %collective-permute-done.24.refs_4_ = bf16[1280,1280]{1,0:T(8,128)(2,1)} collective-permute-done((bf16[1280,1280]{1,0:T(8,128)(2,1)}, bf16[1280,1280]{1,0:T(8,128)(2,1)}, u32[]{:S(2)}, u32[]{:S(2)}) %collective-permute-start.24) | collective-permute-done | bytes 3276832 | tf_op jit(solution)/shard_map/ppermute | solution.py:214
  517.1 3.5 collective-permute-start.30
  520.6 14.9 %send_products.16 = (bf16[3,320,1280]{2,1,0:T(8,128)(2,1)}, bf16[3,320,1280]{2,1,0:T(8,128)(2,1)}) custom-call(s32[4]{0:T(128)} %broadcast_xor_fusion.where_ref, bf16[4,2,640,1280]{3,2,1,0:T(8,128)(2,1)} %refs_0_.39, bf16[2,640,1280]{2,1,0:T(8,128)(2,1)} %bitcast.55, bf16[4,2,640,1280]{3,2,1,0:T(8,128)(2,1)} %refs_0_.39, ...), custom_call_target="tpu_custom_call" | custom-call | flops 1048576 | bytes 65536 | tf_op jit(solution)/shard_map/send_products/pallas_call | solution.py:70
  544.1 15.2 %keep_products.16 = (bf16[3,320,1280]{2,1,0:T(8,128)(2,1)}, bf16[3,320,1280]{2,1,0:T(8,128)(2,1)}) custom-call(s32[4]{0:T(128)} %broadcast_xor_fusion.where_ref, bf16[4,2,640,1280]{3,2,1,0:T(8,128)(2,1)} %refs_0_.39, bf16[2,640,1280]{2,1,0:T(8,128)(2,1)} %bitcast.56, bf16[4,2,640,1280]{3,2,1,0:T(8,128)(2,1)} %refs_0_.39, ...), custom_call_target="tpu_custom_call" | custom-call | flops 1048576 | bytes 65536 | tf_op jit(solution)/shard_map/keep_products/pallas_call | solution.py:97
  559.3 14.8 %collective-permute-done.34 = bf16[2,320,1280]{2,1,0:T(8,128)(2,1)} collective-permute-done((bf16[2,320,1280]{2,1,0:T(8,128)(2,1)}, bf16[2,320,1280]{2,1,0:T(8,128)(2,1)}, u32[]{:S(2)}, u32[]{:S(2)}) %collective-permute-start.34) | collective-permute-done | bytes 1638432 | tf_op jit(solution)/shard_map/ppermute | solution.py:187
  574.1 17.3 %collective-permute-done.30.refs_3_ = bf16[1280,1280]{1,0:T(8,128)(2,1)} collective-permute-done((bf16[1280,1280]{1,0:T(8,128)(2,1)}, bf16[1280,1280]{1,0:T(8,128)(2,1)}, u32[]{:S(2)}, u32[]{:S(2)}) %collective-permute-start.30) | collective-permute-done | bytes 3276832 | tf_op jit(solution)/shard_map/ppermute | solution.py:214
  597.5 14.4 %send_products.17 = (bf16[3,320,1280]{2,1,0:T(8,128)(2,1)}, bf16[3,320,1280]{2,1,0:T(8,128)(2,1)}) custom-call(s32[4]{0:T(128)} %broadcast_xor_fusion.where_ref, bf16[4,2,640,1280]{3,2,1,0:T(8,128)(2,1)} %refs_0_.39, bf16[2,640,1280]{2,1,0:T(8,128)(2,1)} %bitcast.63, bf16[4,2,640,1280]{3,2,1,0:T(8,128)(2,1)} %refs_0_.39, ...), custom_call_target="tpu_custom_call" | custom-call | flops 1048576 | bytes 65536 | tf_op jit(solution)/shard_map/send_products/pallas_call | solution.py:70
  612.6 3.9 fusion.3
  620.8 15.2 %keep_products.17 = (bf16[3,320,1280]{2,1,0:T(8,128)(2,1)}, bf16[3,320,1280]{2,1,0:T(8,128)(2,1)}) custom-call(s32[4]{0:T(128)} %broadcast_xor_fusion.where_ref, bf16[4,2,640,1280]{3,2,1,0:T(8,128)(2,1)} %refs_0_.39, bf16[2,640,1280]{2,1,0:T(8,128)(2,1)} %bitcast.64, bf16[4,2,640,1280]{3,2,1,0:T(8,128)(2,1)} %refs_0_.39, ...), custom_call_target="tpu_custom_call" | custom-call | flops 1048576 | bytes 65536 | tf_op jit(solution)/shard_map/keep_products/pallas_call | solution.py:97
  636.0 20.4 %collective-permute-done.37.refs_2_ = bf16[1280,640]{1,0:T(8,128)(2,1)} collective-permute-done((bf16[1280,640]{1,0:T(8,128)(2,1)}, bf16[1280,640]{1,0:T(8,128)(2,1)}, u32[]{:S(2)}, u32[]{:S(2)}) %collective-permute-start.37) | collective-permute-done | bytes 1638432 | tf_op jit(solution)/shard_map/ppermute | solution.py:214
  667.3 7.9 send_products.18
  678.2 3.0 add_convert_fusion.1
  682.6 4.0 collective-permute-start.43
  687.8 8.1 keep_products.18
  695.9 37.4 %collective-permute-done.43 = bf16[2,160,1280]{2,1,0:T(8,128)(2,1)} collective-permute-done((bf16[2,160,1280]{2,1,0:T(8,128)(2,1)}, bf16[2,160,1280]{2,1,0:T(8,128)(2,1)}, u32[]{:S(2)}, u32[]{:S(2)}) %collective-permute-start.43) | collective-permute-done | bytes 819232 | tf_op jit(solution)/shard_map/ppermute | solution.py:214
  733.3 67.1 %collective-permute-done.42.refs_2_ = bf16[1280,640]{1,0:T(8,128)(2,1)} collective-permute-done((bf16[1280,640]{1,0:T(8,128)(2,1)}, bf16[1280,640]{1,0:T(8,128)(2,1)}, u32[]{:S(2)}, u32[]{:S(2)}) %collective-permute-start.42) | collective-permute-done | bytes 1638432 | tf_op jit(solution)/shard_map/ppermute | solution.py:214
  804.2 7.7 send_products.19
  819.7 8.1 keep_products.19
  829.3 6.8 place.4.refs_8_
  836.1 6.8 place.5.refs_8_
  842.9 22.2 %convolution_convert_fusion = bf16[512,2048]{1,0:T(8,128)(2,1)} fusion(bf16[512,6656]{1,0:T(8,128)(2,1)} %all-gather.2.cloned.1.call-done, bf16[6656,2048]{1,0:T(8,128)(2,1)} %param.6), kind=kOutput, calls=%fused_computation.15 | convolution fusion | flops 13959692288 | bytes 36175872 | tf_op jit(solution)/shard_map/dot_general | solution.py:354
  868.3 4.0 collective-permute-start.54
  877.8 11.2 %collective-permute-done.47 = bf16[2,160,1280]{2,1,0:T(8,128)(2,1)S(1)} collective-permute-done((bf16[2,160,1280]{2,1,0:T(8,128)(2,1)S(1)}, bf16[2,160,1280]{2,1,0:T(8,128)(2,1)S(1)}, u32[]{:S(2)}, u32[]{:S(2)}) %collective-permute-start.47) | collective-permute-done | bytes 819232 | tf_op jit(solution)/shard_map/ppermute | solution.py:238
  891.6 23.4 %collective-permute-done.52 = bf16[2,160,1280]{2,1,0:T(8,128)(2,1)S(1)} collective-permute-done((bf16[2,160,1280]{2,1,0:T(8,128)(2,1)S(1)}, bf16[2,160,1280]{2,1,0:T(8,128)(2,1)S(1)}, u32[]{:S(2)}, u32[]{:S(2)}) %collective-permute-start.52) | collective-permute-done | bytes 819232 | tf_op jit(solution)/shard_map/ppermute | solution.py:245
  918.4 6.8 collective-permute-done.51
  926.6 6.8 place.6.refs_8_
  933.4 6.8 place.7
  (197 shorter events, 126.9 us)
Async XLA Ops:
  7.2 835.7 %all-gather.2.cloned.1.call-start = ((), (), s32[]{:S(2)}) async-start(), calls=%async_computation.1 | async-start | bytes 8519680 | tf_op jit(solution)/shard_map/all_gather | solution.py:330
  15.3 74.7 %collective-permute-start.3 = (bf16[2,640,1280]{2,1,0:T(8,128)(2,1)}, bf16[2,640,1280]{2,1,0:T(8,128)(2,1)S(1)}, u32[]{:S(2)}, u32[]{:S(2)}) collective-permute-start(bf16[2,640,1280]{2,1,0:T(8,128)(2,1)} %slice_bitcast_fusion), channel_id=1, source_target_pairs={{0,8},{24,16},{1,9},{25,17},{2,10},{26,18},{3,11},{27,19},{4,12},{... | collective-permute-start | bytes 9830408 | tf_op jit(solution)/shard_map/ppermute | solution.py:214
  16.6 74.9 %collective-permute-start.2 = (bf16[1280,1280]{1,0:T(8,128)(2,1)}, bf16[1280,1280]{1,0:T(8,128)(2,1)}, u32[]{:S(2)}, u32[]{:S(2)}) collective-permute-start(bf16[1280,1280]{1,0:T(8,128)(2,1)} %bitcast.40.refs_4_), channel_id=1, source_target_pairs={{8,16},{16,8},{9,17},{17,9},{10,18},{18,10},{11,19},{19,11},{12,20... | collective-permute-start | bytes 9830408 | tf_op jit(solution)/shard_map/ppermute | solution.py:214
  43.3 3.8 collective-permute-start
  43.3 6.2 collective-permute-start.1
  91.4 74.0 %collective-permute-start.7 = (bf16[1280,1280]{1,0:T(8,128)(2,1)}, bf16[1280,1280]{1,0:T(8,128)(2,1)}, u32[]{:S(2)}, u32[]{:S(2)}) collective-permute-start(bf16[1280,1280]{1,0:T(8,128)(2,1)} %bitcast.67), channel_id=1, source_target_pairs={{8,16},{16,8},{9,17},{17,9},{10,18},{18,10},{11,19},{19,11},{12,20... | collective-permute-start | bytes 9830408 | tf_op jit(solution)/shard_map/ppermute | solution.py:214
  95.1 71.9 %collective-permute-start.4 = (bf16[1280,1280]{1,0:T(8,128)(2,1)}, bf16[1280,1280]{1,0:T(8,128)(2,1)}, u32[]{:S(2)}, u32[]{:S(2)}) collective-permute-start(bf16[1280,1280]{1,0:T(8,128)(2,1)} %bitcast.68), channel_id=1, source_target_pairs={{0,8},{8,0},{16,24},{24,16},{1,9},{9,1},{17,25},{25,17},{2,10},{10... | collective-permute-start | bytes 9830408 | tf_op jit(solution)/shard_map/ppermute | solution.py:214
  105.3 6.0 collective-permute-start.5
  105.3 6.1 collective-permute-start.6
  105.8 38.0 %collective-permute-start.8 = (bf16[2,320,1280]{2,1,0:T(8,128)(2,1)}, bf16[2,320,1280]{2,1,0:T(8,128)(2,1)}, u32[]{:S(2)}, u32[]{:S(2)}) collective-permute-start(bf16[2,320,1280]{2,1,0:T(8,128)(2,1)} %get-tuple-element.175), channel_id=1, source_target_pairs={{0,2},{2,0},{1,3},{3,1},{4,6},{6,4},{5,7},{7,5},{8,10},{10,8},{9,1... | collective-permute-start | bytes 4915208 | tf_op jit(solution)/shard_map/ppermute | solution.py:187
  171.0 70.8 %collective-permute-start.12 = (bf16[1280,1280]{1,0:T(8,128)(2,1)}, bf16[1280,1280]{1,0:T(8,128)(2,1)S(1)}, u32[]{:S(2)}, u32[]{:S(2)}) collective-permute-start(bf16[1280,1280]{1,0:T(8,128)(2,1)} %broadcast_select_fusion.4), channel_id=1, source_target_pairs={{0,8},{8,0},{16,24},{24,16},{1,9},{9,1},{17,25},{25,17},{2,10},{10... | collective-permute-start | bytes 9830408 | tf_op jit(solution)/shard_map/ppermute | solution.py:214
  171.3 72.8 %collective-permute-start.11 = (bf16[1280,1280]{1,0:T(8,128)(2,1)}, bf16[1280,1280]{1,0:T(8,128)(2,1)}, u32[]{:S(2)}, u32[]{:S(2)}) collective-permute-start(bf16[1280,1280]{1,0:T(8,128)(2,1)} %collective-permute-done.4.refs_3_), channel_id=1, source_target_pairs={{8,16},{16,8},{9,17},{17,9},{10,18},{18,10},{11,19},{19,11},{12,20... | collective-permute-start | bytes 9830408 | tf_op jit(solution)/shard_map/ppermute | solution.py:214
  188.3 8.3 collective-permute-start.9
  188.3 8.5 collective-permute-start.10
  188.8 38.1 %collective-permute-start.13 = (bf16[2,320,1280]{2,1,0:T(8,128)(2,1)}, bf16[2,320,1280]{2,1,0:T(8,128)(2,1)}, u32[]{:S(2)}, u32[]{:S(2)}) collective-permute-start(bf16[2,320,1280]{2,1,0:T(8,128)(2,1)} %get-tuple-element.187), channel_id=1, source_target_pairs={{0,2},{2,0},{1,3},{3,1},{4,6},{6,4},{5,7},{7,5},{8,10},{10,8},{9,1... | collective-permute-start | bytes 4915208 | tf_op jit(solution)/shard_map/ppermute | solution.py:187
  248.1 78.4 %collective-permute-start.14 = (bf16[1280,1280]{1,0:T(8,128)(2,1)}, bf16[1280,1280]{1,0:T(8,128)(2,1)S(1)}, u32[]{:S(2)}, u32[]{:S(2)}) collective-permute-start(bf16[1280,1280]{1,0:T(8,128)(2,1)} %broadcast_select_fusion.3), channel_id=1, source_target_pairs={{0,8},{8,0},{16,24},{24,16},{1,9},{9,1},{17,25},{25,17},{2,10},{10... | collective-permute-start | bytes 9830408 | tf_op jit(solution)/shard_map/ppermute | solution.py:214
  248.1 78.4 %collective-permute-start.15 = (bf16[1280,1280]{1,0:T(8,128)(2,1)}, bf16[1280,1280]{1,0:T(8,128)(2,1)}, u32[]{:S(2)}, u32[]{:S(2)}) collective-permute-start(bf16[1280,1280]{1,0:T(8,128)(2,1)} %copy-done.5), channel_id=1, source_target_pairs={{8,16},{16,8},{9,17},{17,9},{10,18},{18,10},{11,19},{19,11},{12,20... | collective-permute-start | bytes 9830408 | tf_op jit(solution)/shard_map/ppermute | solution.py:214
  270.3 5.4 collective-permute-start.16
  270.3 8.5 collective-permute-start.17
  270.8 55.6 %collective-permute-start.18 = (bf16[3,320,1280]{2,1,0:T(8,128)(2,1)}, bf16[3,320,1280]{2,1,0:T(8,128)(2,1)}, u32[]{:S(2)}, u32[]{:S(2)}) collective-permute-start(bf16[3,320,1280]{2,1,0:T(8,128)(2,1)} %get-tuple-element.199), channel_id=1, source_target_pairs={{0,2},{2,0},{1,3},{3,1},{4,6},{6,4},{5,7},{7,5},{8,10},{10,8},{9,1... | collective-permute-start | bytes 7372808 | tf_op jit(solution)/shard_map/ppermute | solution.py:187
  339.7 84.1 %collective-permute-start.22 = (bf16[1280,1280]{1,0:T(8,128)(2,1)}, bf16[1280,1280]{1,0:T(8,128)(2,1)S(1)}, u32[]{:S(2)}, u32[]{:S(2)}) collective-permute-start(bf16[1280,1280]{1,0:T(8,128)(2,1)} %get-tuple-element.215), channel_id=1, source_target_pairs={{0,8},{8,0},{16,24},{24,16},{1,9},{9,1},{17,25},{25,17},{2,10},{10... | collective-permute-start | bytes 9830408 | tf_op jit(solution)/shard_map/ppermute | solution.py:214
  339.8 84.1 %collective-permute-start.21 = (bf16[1280,1280]{1,0:T(8,128)(2,1)}, bf16[1280,1280]{1,0:T(8,128)(2,1)}, u32[]{:S(2)}, u32[]{:S(2)}) collective-permute-start(bf16[1280,1280]{1,0:T(8,128)(2,1)} %bitcast.46.refs_3_), channel_id=1, source_target_pairs={{8,16},{16,8},{9,17},{17,9},{10,18},{18,10},{11,19},{19,11},{12,20... | collective-permute-start | bytes 9830408 | tf_op jit(solution)/shard_map/ppermute | solution.py:214
  367.7 5.7 collective-permute-start.19
  367.7 8.5 collective-permute-start.20
  368.2 55.6 %collective-permute-start.23 = (bf16[3,320,1280]{2,1,0:T(8,128)(2,1)}, bf16[3,320,1280]{2,1,0:T(8,128)(2,1)}, u32[]{:S(2)}, u32[]{:S(2)}) collective-permute-start(bf16[3,320,1280]{2,1,0:T(8,128)(2,1)} %get-tuple-element.216), channel_id=1, source_target_pairs={{0,2},{2,0},{1,3},{3,1},{4,6},{6,4},{5,7},{7,5},{8,10},{10,8},{9,1... | collective-permute-start | bytes 7372808 | tf_op jit(solution)/shard_map/ppermute | solution.py:187
  430.8 14.8 %copy-start.18 = (bf16[1,320,1280]{2,1,0:T(8,128)(2,1)S(1)}, bf16[1,320,1280]{2,1,0:T(8,128)(2,1)}, u32[]{:S(2)}) copy-start(bf16[1,320,1280]{2,1,0:T(8,128)(2,1)} %get-tuple-element.353) | copy-start | bytes 2457604
  441.3 9.4 collective-permute-start.25
  441.4 73.6 %collective-permute-start.24 = (bf16[1280,1280]{1,0:T(8,128)(2,1)}, bf16[1280,1280]{1,0:T(8,128)(2,1)}, u32[]{:S(2)}, u32[]{:S(2)}) collective-permute-start(bf16[1280,1280]{1,0:T(8,128)(2,1)} %bitcast.46.refs_3_), channel_id=1, source_target_pairs={{0,8},{8,0},{16,24},{24,16},{1,9},{9,1},{17,25},{25,17},{2,10},{10... | collective-permute-start | bytes 9830408 | tf_op jit(solution)/shard_map/ppermute | solution.py:214
  442.1 75.0 %collective-permute-start.27 = (bf16[1280,1280]{1,0:T(8,128)(2,1)S(1)}, bf16[1280,1280]{1,0:T(8,128)(2,1)}, u32[]{:S(2)}, u32[]{:S(2)}) collective-permute-start(bf16[1280,1280]{1,0:T(8,128)(2,1)S(1)} %bitcast.71), channel_id=1, source_target_pairs={{8,16},{16,8},{9,17},{17,9},{10,18},{18,10},{11,19},{19,11},{12,20... | collective-permute-start | bytes 9830408 | tf_op jit(solution)/shard_map/ppermute | solution.py:214
  445.7 55.5 %collective-permute-start.29 = (bf16[3,320,1280]{2,1,0:T(8,128)(2,1)}, bf16[3,320,1280]{2,1,0:T(8,128)(2,1)}, u32[]{:S(2)}, u32[]{:S(2)}) collective-permute-start(bf16[3,320,1280]{2,1,0:T(8,128)(2,1)} %get-tuple-element.235), channel_id=1, source_target_pairs={{0,2},{2,0},{1,3},{3,1},{4,6},{6,4},{5,7},{7,5},{8,10},{10,8},{9,1... | collective-permute-start | bytes 7372808 | tf_op jit(solution)/shard_map/ppermute | solution.py:187
  447.3 4.0 collective-permute-start.26
  450.7 38.5 %collective-permute-start.28 = (bf16[4,160,1280]{2,1,0:T(8,128)(2,1)}, bf16[4,160,1280]{2,1,0:T(8,128)(2,1)}, u32[]{:S(2)}, u32[]{:S(2)}) collective-permute-start(bf16[4,160,1280]{2,1,0:T(8,128)(2,1)} %pad_maximum_fusion.2), channel_id=1, source_target_pairs={{0,4},{4,0},{1,5},{5,1},{2,6},{6,2},{3,7},{7,3},{8,12},{12,8},{9,1... | collective-permute-start | bytes 4915208 | tf_op jit(solution)/shard_map/ppermute | solution.py:219
  517.1 74.3 %collective-permute-start.30 = (bf16[1280,1280]{1,0:T(8,128)(2,1)}, bf16[1280,1280]{1,0:T(8,128)(2,1)}, u32[]{:S(2)}, u32[]{:S(2)}) collective-permute-start(bf16[1280,1280]{1,0:T(8,128)(2,1)} %collective-permute-done.24.refs_4_), channel_id=1, source_target_pairs={{8,16},{16,8},{9,17},{17,9},{10,18},{18,10},{11,19},{19,11},{12,20... | collective-permute-start | bytes 9830408 | tf_op jit(solution)/shard_map/ppermute | solution.py:214
  520.5 72.0 %collective-permute-start.33 = (bf16[1280,1280]{1,0:T(8,128)(2,1)S(1)}, bf16[1280,1280]{1,0:T(8,128)(2,1)}, u32[]{:S(2)}, u32[]{:S(2)}) collective-permute-start(bf16[1280,1280]{1,0:T(8,128)(2,1)S(1)} %bitcast.72), channel_id=1, source_target_pairs={{0,8},{8,0},{16,24},{24,16},{1,9},{9,1},{17,25},{25,17},{2,10},{10... | collective-permute-start | bytes 9830408 | tf_op jit(solution)/shard_map/ppermute | solution.py:214
  535.5 6.4 collective-permute-start.31
  535.5 8.5 collective-permute-start.32
  536.0 38.1 %collective-permute-start.34 = (bf16[2,320,1280]{2,1,0:T(8,128)(2,1)}, bf16[2,320,1280]{2,1,0:T(8,128)(2,1)}, u32[]{:S(2)}, u32[]{:S(2)}) collective-permute-start(bf16[2,320,1280]{2,1,0:T(8,128)(2,1)} %get-tuple-element.244), channel_id=1, source_target_pairs={{0,2},{2,0},{1,3},{3,1},{4,6},{6,4},{5,7},{7,5},{8,10},{10,8},{9,1... | collective-permute-start | bytes 4915208 | tf_op jit(solution)/shard_map/ppermute | solution.py:187
  595.9 16.5 %copy-start.11 = (bf16[1,320,1280]{2,1,0:T(8,128)(2,1)S(1)}, bf16[1,320,1280]{2,1,0:T(8,128)(2,1)}, u32[]{:S(2)}) copy-start(bf16[1,320,1280]{2,1,0:T(8,128)(2,1)} %get-tuple-element.331) | copy-start | bytes 2457604
  595.9 60.5 %collective-permute-start.39 = (bf16[3,320,1280]{2,1,0:T(8,128)(2,1)}, bf16[3,320,1280]{2,1,0:T(8,128)(2,1)}, u32[]{:S(2)}, u32[]{:S(2)}) collective-permute-start(bf16[3,320,1280]{2,1,0:T(8,128)(2,1)} %get-tuple-element.258), channel_id=1, source_target_pairs={{0,2},{2,0},{1,3},{3,1},{4,6},{6,4},{5,7},{7,5},{8,10},{10,8},{9,1... | collective-permute-start | bytes 7372808 | tf_op jit(solution)/shard_map/ppermute | solution.py:187
  611.9 8.9 collective-permute-start.35
  611.9 8.9 collective-permute-start.36
  616.5 40.0 %collective-permute-start.37 = (bf16[1280,640]{1,0:T(8,128)(2,1)}, bf16[1280,640]{1,0:T(8,128)(2,1)}, u32[]{:S(2)}, u32[]{:S(2)}) collective-permute-start(bf16[1280,640]{1,0:T(8,128)(2,1)} %get-tuple-element.252), channel_id=1, source_target_pairs={{8,16},{16,8},{9,17},{17,9},{10,18},{18,10},{11,19},{19,11},{12,20... | collective-permute-start | bytes 4915208 | tf_op jit(solution)/shard_map/ppermute | solution.py:214
  619.0 37.4 %collective-permute-start.38 = (bf16[4,160,1280]{2,1,0:T(8,128)(2,1)S(1)}, bf16[4,160,1280]{2,1,0:T(8,128)(2,1)S(1)}, u32[]{:S(2)}, u32[]{:S(2)}) collective-permute-start(bf16[4,160,1280]{2,1,0:T(8,128)(2,1)S(1)} %pad_maximum_fusion.3), channel_id=1, source_target_pairs={{8,0},{16,24},{9,1},{17,25},{10,2},{18,26},{11,3},{19,27},{12,4},{... | collective-permute-start | bytes 4915208 | tf_op jit(solution)/shard_map/ppermute | solution.py:214
  657.7 282.5 %reduce-scatter.2.cloned.1.call-start = ((), (), s32[]{:S(2)}) async-start(), calls=%async_computation.2 | async-start | bytes 2359296 | tf_op jit(solution)/shard_map/reduce_scatter | solution.py:357
  666.2 134.2 %collective-permute-start.44 = (bf16[6,160,1280]{2,1,0:T(8,128)(2,1)}, bf16[6,160,1280]{2,1,0:T(8,128)(2,1)S(1)}, u32[]{:S(2)}, u32[]{:S(2)}) collective-permute-start(bf16[6,160,1280]{2,1,0:T(8,128)(2,1)} %pad_maximum_fusion.1), channel_id=1, source_target_pairs={{0,4},{4,0},{1,5},{5,1},{2,6},{6,2},{3,7},{7,3},{8,12},{12,8},{9,1... | collective-permute-start | bytes 7372808 | tf_op jit(solution)/shard_map/ppermute | solution.py:219
  666.8 133.7 %collective-permute-start.45 = (bf16[3,320,1280]{2,1,0:T(8,128)(2,1)}, bf16[3,320,1280]{2,1,0:T(8,128)(2,1)}, u32[]{:S(2)}, u32[]{:S(2)}) collective-permute-start(bf16[3,320,1280]{2,1,0:T(8,128)(2,1)} %get-tuple-element.282), channel_id=1, source_target_pairs={{0,2},{2,0},{1,3},{3,1},{4,6},{6,4},{5,7},{7,5},{8,10},{10,8},{9,1... | collective-permute-start | bytes 7372808 | tf_op jit(solution)/shard_map/ppermute | solution.py:187
  675.1 7.5 collective-permute-start.40
  675.1 12.7 %collective-permute-start.41 = (bf16[2,320,640]{2,1,0:T(8,128)(2,1)}, bf16[2,320,640]{2,1,0:T(8,128)(2,1)}, u32[]{:S(2)}, u32[]{:S(2)}) collective-permute-start(bf16[2,320,640]{2,1,0:T(8,128)(2,1)} %get-tuple-element.266), channel_id=1, source_target_pairs={{0,1},{1,0},{2,3},{3,2},{4,5},{5,4},{6,7},{7,6},{8,9},{9,8},{10,11... | collective-permute-start | bytes 2457608 | tf_op jit(solution)/shard_map/ppermute | solution.py:179
  675.6 124.8 %collective-permute-start.42 = (bf16[1280,640]{1,0:T(8,128)(2,1)}, bf16[1280,640]{1,0:T(8,128)(2,1)}, u32[]{:S(2)}, u32[]{:S(2)}) collective-permute-start(bf16[1280,640]{1,0:T(8,128)(2,1)} %get-tuple-element.270), channel_id=1, source_target_pairs={{8,16},{16,8},{9,17},{17,9},{10,18},{18,10},{11,19},{19,11},{12,20... | collective-permute-start | bytes 4915208 | tf_op jit(solution)/shard_map/ppermute | solution.py:214
  682.6 50.7 %collective-permute-start.43 = (bf16[2,160,1280]{2,1,0:T(8,128)(2,1)}, bf16[2,160,1280]{2,1,0:T(8,128)(2,1)}, u32[]{:S(2)}, u32[]{:S(2)}) collective-permute-start(bf16[2,160,1280]{2,1,0:T(8,128)(2,1)} %bitcast.22), channel_id=1, source_target_pairs={{8,0},{16,24},{9,1},{17,25},{10,2},{18,26},{11,3},{19,27},{12,4},{... | collective-permute-start | bytes 2457608 | tf_op jit(solution)/shard_map/ppermute | solution.py:214
  695.9 106.4 %copy-start.8 = (bf16[1,320,1280]{2,1,0:T(8,128)(2,1)S(1)}, bf16[1,320,1280]{2,1,0:T(8,128)(2,1)}, u32[]{:S(2)}) copy-start(bf16[1,320,1280]{2,1,0:T(8,128)(2,1)} %get-tuple-element.327) | copy-start | bytes 2457604
  803.6 24.7 %collective-permute-start.46 = (bf16[2,160,1280]{2,1,0:T(8,128)(2,1)}, bf16[2,160,1280]{2,1,0:T(8,128)(2,1)S(1)}, u32[]{:S(2)}, u32[]{:S(2)}) collective-permute-start(bf16[2,160,1280]{2,1,0:T(8,128)(2,1)} %get-tuple-element.339), channel_id=1, source_target_pairs={{0,4},{4,0},{1,5},{5,1},{2,6},{6,2},{3,7},{7,3},{8,12},{12,8},{9,1... | collective-permute-start | bytes 2457608 | tf_op jit(solution)/shard_map/ppermute | solution.py:219
  811.9 7.9 collective-permute-start.48
  811.9 7.9 collective-permute-start.49
  816.4 74.5 %collective-permute-start.53 = (bf16[2,160,1280]{2,1,0:T(8,128)(2,1)}, bf16[2,160,1280]{2,1,0:T(8,128)(2,1)}, u32[]{:S(2)}, u32[]{:S(2)}) collective-permute-start(bf16[2,160,1280]{2,1,0:T(8,128)(2,1)} %bitcast.32), channel_id=1, source_target_pairs={{8,4},{16,28},{9,5},{17,29},{10,6},{18,30},{11,7},{19,31}} | collective-permute-start | bytes 2457608 | tf_op jit(solution)/shard_map/ppermute | solution.py:239
  818.2 54.1 %collective-permute-start.56 = (bf16[2,320,640]{2,1,0:T(8,128)(2,1)}, bf16[2,320,640]{2,1,0:T(8,128)(2,1)}, u32[]{:S(2)}, u32[]{:S(2)}) collective-permute-start(bf16[2,320,640]{2,1,0:T(8,128)(2,1)} %get-tuple-element.306), channel_id=1, source_target_pairs={{0,2},{2,0},{1,3},{3,1},{4,6},{6,4},{5,7},{7,5},{8,10},{10,8},{9,1... | collective-permute-start | bytes 2457608 | tf_op jit(solution)/shard_map/ppermute | solution.py:187
  827.8 47.8 %collective-permute-start.50 = (bf16[2,320,640]{2,1,0:T(8,128)(2,1)}, bf16[2,320,640]{2,1,0:T(8,128)(2,1)}, u32[]{:S(2)}, u32[]{:S(2)}) collective-permute-start(bf16[2,320,640]{2,1,0:T(8,128)(2,1)} %get-tuple-element.299), channel_id=1, source_target_pairs={{0,2},{2,0},{1,3},{3,1},{4,6},{6,4},{5,7},{7,5},{8,10},{10,8},{9,1... | collective-permute-start | bytes 2457608 | tf_op jit(solution)/shard_map/ppermute | solution.py:187
  866.4 22.7 %collective-permute-start.47 = (bf16[2,160,1280]{2,1,0:T(8,128)(2,1)S(1)}, bf16[2,160,1280]{2,1,0:T(8,128)(2,1)S(1)}, u32[]{:S(2)}, u32[]{:S(2)}) collective-permute-start(bf16[2,160,1280]{2,1,0:T(8,128)(2,1)S(1)} %broadcast_select_fusion.11), channel_id=1, source_target_pairs={{8,12},{16,20},{12,4},{20,28},{9,13},{17,21},{13,5},{21,29},{10,14... | collective-permute-start | bytes 2457608 | tf_op jit(solution)/shard_map/ppermute | solution.py:238
  868.3 50.1 %collective-permute-start.54 = (bf16[2,160,1280]{2,1,0:T(8,128)(2,1)S(1)}, bf16[2,160,1280]{2,1,0:T(8,128)(2,1)S(1)}, u32[]{:S(2)}, u32[]{:S(2)}) collective-permute-start(bf16[2,160,1280]{2,1,0:T(8,128)(2,1)S(1)} %bitcast.88), channel_id=1, source_target_pairs={{4,0},{5,1},{6,2},{7,3},{12,8},{13,9},{14,10},{15,11},{20,16},{21,... | collective-permute-start | bytes 2457608 | tf_op jit(solution)/shard_map/ppermute | solution.py:245
  872.3 42.8 %collective-permute-start.52 = (bf16[2,160,1280]{2,1,0:T(8,128)(2,1)S(1)}, bf16[2,160,1280]{2,1,0:T(8,128)(2,1)S(1)}, u32[]{:S(2)}, u32[]{:S(2)}) collective-permute-start(bf16[2,160,1280]{2,1,0:T(8,128)(2,1)S(1)} %bitcast.86), channel_id=1, source_target_pairs={{4,0},{5,1},{6,2},{7,3},{12,8},{13,9},{14,10},{15,11},{20,16},{21,... | collective-permute-start | bytes 2457608 | tf_op jit(solution)/shard_map/ppermute | solution.py:245
  875.6 42.8 %collective-permute-start.58 = (bf16[2,160,640]{2,1,0:T(8,128)(2,1)S(1)}, bf16[2,160,640]{2,1,0:T(8,128)(2,1)S(1)}, u32[]{:S(2)}, u32[]{:S(2)}) collective-permute-start(bf16[2,160,640]{2,1,0:T(8,128)(2,1)S(1)} %bitcast.109), channel_id=1, source_target_pairs={{8,4},{16,28},{9,5},{17,29},{10,6},{18,30},{11,7},{19,31}} | collective-permute-start | bytes 1228808 | tf_op jit(solution)/shard_map/ppermute | solution.py:239
  889.0 29.4 %collective-permute-start.57 = (bf16[2,160,640]{2,1,0:T(8,128)(2,1)S(1)}, bf16[2,160,640]{2,1,0:T(8,128)(2,1)S(1)}, u32[]{:S(2)}, u32[]{:S(2)}) collective-permute-start(bf16[2,160,640]{2,1,0:T(8,128)(2,1)S(1)} %broadcast_select_fusion.23), channel_id=1, source_target_pairs={{8,12},{16,20},{12,4},{20,28},{9,13},{17,21},{13,5},{21,29},{10,14... | collective-permute-start | bytes 1228808 | tf_op jit(solution)/shard_map/ppermute | solution.py:238
  891.0 34.2 %collective-permute-start.55 = (bf16[2,160,640]{2,1,0:T(8,128)(2,1)S(1)}, bf16[2,160,640]{2,1,0:T(8,128)(2,1)S(1)}, u32[]{:S(2)}, u32[]{:S(2)}) collective-permute-start(bf16[2,160,640]{2,1,0:T(8,128)(2,1)S(1)} %bitcast.111), channel_id=1, source_target_pairs={{8,4},{16,28},{9,5},{17,29},{10,6},{18,30},{11,7},{19,31}} | collective-permute-start | bytes 1228808 | tf_op jit(solution)/shard_map/ppermute | solution.py:239
  915.1 10.1 %collective-permute-start.51 = (bf16[2,160,640]{2,1,0:T(8,128)(2,1)S(1)}, bf16[2,160,640]{2,1,0:T(8,128)(2,1)S(1)}, u32[]{:S(2)}, u32[]{:S(2)}) collective-permute-start(bf16[2,160,640]{2,1,0:T(8,128)(2,1)S(1)} %broadcast_select_fusion.24), channel_id=1, source_target_pairs={{8,12},{16,20},{12,4},{20,28},{9,13},{17,21},{13,5},{21,29},{10,14... | collective-permute-start | bytes 1228808 | tf_op jit(solution)/shard_map/ppermute | solution.py:238
  (24 other events, 77.4 us)
Sparse Core Ops, SparseCore 0:
  657.8 154.7 all-gather.1
  865.2 49.6 reduce-scatter.1

commit v6 on v5

--- a/solution.py
+++ b/solution.py
@@ -245,41 +245,45 @@
         return lax.ppermute(order.open(near), "occ", [(1, 0)])
 
     ca = cycle_amplitudes
+    gathered = lax.all_gather(ladder_amplitudes, "vir", axis=0, tiled=True)
     b0 = columns_of(0)
     order.phase(b0)
     own0 = move(b0, MID_TO_MID)
     a0 = move(rows_of(0), END_TO_MID)
-    b3, b1 = columns_of(3), columns_of(1)
-    one = batch((3, ca, b3), (1, ca, b1))
+    b3, b1, b2 = columns_of(3), columns_of(1), columns_of(2)
+    one = batch((3, ca, b3), (1, ca, b1), (2, ca, b2))
     one.send()
     one.keep()
 
-    order.phase(own0, a0)
+    order.phase(own0, a0, gathered)
     own3 = move(b3, MID_TO_MID)
     swap3 = move(b3, NEIGHBOUR)
     one.swap()
     two = batch((0, ca, own0), (0, a0, own0))
+    partial_ladder = order.step(jnp.dot(
+        order.follow(gathered), ladder_integrals, preferred_element_type=F32,
+    ).astype(BF16))
+    ladder_residual = lax.psum_scatter(partial_ladder, ("occ", "ka"), scatter_dimension=0, tiled=True)
     two.send()
     two.keep()
     rows1 = rows_of(1)
 
     order.phase(own3, swap3, rows1, one.other)
-    s3, s1 = one.finish()
+    s3, s1, s2 = one.finish()
     relay3 = move(swap3, MID_TO_MID)
     both3 = exchange(b0, own3)
     two.swap()
-    b2 = columns_of(2)
     three = batch((3, ca, swap3), (0, ca, b0), (0, a0, b0))
     three.send()
     three.keep()
     rows2 = rows_of(2)
 
-    order.phase(relay3, both3, rows2, b2, two.other)
+    order.phase(relay3, both3, rows2, two.other)
     f0 = two.finish()
     relay0 = move(both3, MID_TO_MID)
     both4 = exchange(rows1.reshape(b0.shape), relay3)
     three.swap()
-    four = batch((2, ca, b2), (0, ca, both3), (3, ca, jnp.where(at_end, order.open(both3), own3)))
+    four = batch((0, ca, both3), (3, ca, jnp.where(at_end, order.open(both3), own3)))
     four.send()
     four.keep()
 
@@ -293,20 +297,19 @@
     five.send()
     five.keep()
 
-    order.phase(own1, both5, four.other)
-    s2, n0, f3 = four.finish()
+    order.phase(own1, both5, four.other, ladder_residual)
+    n0, f3 = four.finish()
     a2 = both5.reshape(a0.shape)
     backs = both5.reshape(8, quarter, 2 * columns)
     f0_back, s0_back = backs[0:2], backs[2:4]
     own2 = move(b2, MID_TO_MID)
     swap1 = move(b1, NEIGHBOUR)
-    x03a = cross((s0[0], home(f0[0], f0_back)), (s3, f3))
     five.swap()
     six = batch((1, ca, own1), (1, a1, own1))
     six.send()
     six.keep()
 
-    order.phase(own2, swap1, x03a[1], five.other)
+    order.phase(own2, swap1, five.other)
     *g0, g3 = five.finish()
     relay1 = move(swap1, MID_TO_MID)
     swap2 = move(b2, NEIGHBOUR)
@@ -319,15 +322,15 @@
     f1 = six.finish()
     relay2 = [move(swap2[:, :columns], MID_TO_MID)]
     backs = move(jnp.concatenate([g0[1], f1[1]]), MID_TO_END)
+    x03a = cross((s0[0], home(f0[0], f0_back)), (s3, f3))
     seven.swap()
     eight = batch((1, ca, relay1), (1, a1, relay1), (2, ca, swap2))
     eight.send()
     eight.keep()
 
-    order.phase(relay2[0], backs, seven.other)
+    order.phase(relay2[0], backs, x03a[1], seven.other)
     *f2, n1 = seven.finish()
     relay2.append(move(swap2[:, columns:], MID_TO_MID))
-    gathered = lax.all_gather(order.open(ladder_amplitudes), "vir", axis=0, tiled=True)
     g0_back, f1_back = backs[0:2], backs[2:4]
     f2_back = move(f2[1], MID_TO_END)
     x01 = cross((home(n0, s0_back), home(g0[0], g0_back)), (s1, home(f1[0], f1_back)), (n3, g3))
@@ -344,17 +347,14 @@
     ten.keep()
     ten.swap()
     x2a = cross((s2, home(f2[0], f2_back)))
-    near1_in, near2_in = over(n1), over(n2)
+    near_in = over(jnp.concatenate([n1, n2]))
+    near1_in, near2_in = near_in[0:2], near_in[2:4]
     x1b = straight(n1, near1_in, g1)
     x2b = [straight(n2, near2_in, nine.finish(), slice(0, columns))]
     out = None
     for j in range(2):
         out = put(0, j, [(x03a, 0, j), (x01, 1, j), (x2a, 0, j), (x03a, 1, j)], out)
     x2b.append(straight(n2, near2_in, ten.finish(), slice(columns, 2 * columns)))
-    partial_ladder = order.step(jnp.dot(
-        order.follow(gathered), ladder_integrals, preferred_element_type=F32,
-    ).astype(BF16))
-    ladder_residual = lax.psum_scatter(partial_ladder, ("occ", "ka"), scatter_dimension=0, tiled=True)
     for j in range(2):
         out = put(1, j, [(x01, 0, j), (x1b, 0, j), (x2b[j], 0, 0), (x01, 2, j)], out)
     return ladder_residual, out

time: 957 us -> 914 us (0.955)
  waiting for transfers between devices: 438 us -> 381 us
    ppermute x10, waiting for transfers between devices: 125 us -> 96 us  [swap(): self.other = lax.ppermute(self.order.open(self.away), 'ka', OTHER_Y)]
    ppermute x2 -> x1, waiting for transfers between devices: 23.4 us -> 8.97 us  [over(): return lax.ppermute(order.open(near), 'occ', [(1, 0)])]
    ppermute x3, waiting for transfers between devices: 17.9 us -> 4.79 us  [straight(): lax.ppermute(jnp.where(occ == 0, own_rows, foreign), ('vir', 'occ'), [(2,...]
  transfers between devices with their start and end apart: 61 -> 60, of which waited for: 30 -> 36; matrix products, arithmetic and copies ran while one was open for 10% -> 13% of each run, Pallas kernels for 28% -> 29%
where the time goes in v6:
time: 914 us; the launch traced here: 899 us
  waiting for transfers between devices  381 us (42%)
  Pallas kernels  274 us (30%)
  starting transfers between devices  73.9 us (8%)
  other arithmetic  71.1 us (8%)
  local copies, waits for them, and re-layouts  61.2 us (7%)
  matrix products  22.2 us (2%)
  between operations  15 us (2%)
    ppermute x18, waiting for transfers between devices, move(): return lax.ppermute(order.open(value), 'vir', route)  227 us
    pallas_call x10, Pallas kernels, keep_products(): pl.pallas_call(kernel, out_shape=(jax.ShapeDtypeStruct((count, rows, colu...  127 us
    pallas_call x10, Pallas kernels, send_products(): pl.pallas_call(kernel, out_shape=(jax.ShapeDtypeStruct((count, rows, colu...  120 us
    ppermute x10, waiting for transfers between devices, swap(): self.other = lax.ppermute(self.order.open(self.away), 'ka', OTHER_Y)  96 us
    ppermute x18, starting transfers between devices, move(): return lax.ppermute(order.open(value), 'vir', route)  39.3 us
    pallas_call x4, Pallas kernels, place(): pl.pallas_call(kernel, out_shape=jax.ShapeDtypeStruct(shape, BF16), grid_...  27.4 us
    convert_element_type x10, other arithmetic, finish(): (self.own.astype(F32) + self.order.open(self.other).astype(F32)).astype(B...  25.5 us
    dot_general x1, matrix products, line_local(): jnp.dot(order.follow(gathered), ladder_integrals, preferred_element_type=...  22.2 us
  transfers between devices with their start and end apart: 60, of which 36 were waited for; matrix products, arithmetic and copies ran while one was open for 13% of the time, Pallas kernels for 29%

profile of v6, /device:TPU:10, one launch (start us, length us, event | category | flops | bytes accessed | tf_op | source)
XLA Modules:
  0.0 898.6 jit_solution(7933498939272293162)
XLA Ops:
  12.2 4.6 slice_bitcast_fusion
  18.2 3.5 collective-permute-start.2
  21.7 8.1 fusion.1
  29.8 4.3 copy.13
  39.9 15.5 %send_products.10 = (bf16[3,320,1280]{2,1,0:T(8,128)(2,1)}, bf16[3,320,1280]{2,1,0:T(8,128)(2,1)}) custom-call(s32[4]{0:T(128)} %broadcast_xor_fusion.where_ref, bf16[4,2,640,1280]{3,2,1,0:T(8,128)(2,1)} %refs_0_.39, bf16[4,2,640,1280]{3,2,1,0:T(8,128)(2,1)} %refs_0_.39, bf16[4,2,640,1280]{3,2,1,0:T(8,128)(2,1)} %refs_0_.39, bf16[1280,1280]{1,0:T(8,128)(2,1)} %bitcast.65, ...), custom_call_target="tpu_custom_call" | custom-call | flops 1048576 | bytes 65536 | tf_op jit(solution)/shard_map/send_products/pallas_call | solution.py:70
  55.9 4.5 collective-permute-done.refs_6_
  60.4 3.5 collective-permute-done.1.refs_7_
  63.9 16.1 %keep_products.10 = (bf16[3,320,1280]{2,1,0:T(8,128)(2,1)}, bf16[3,320,1280]{2,1,0:T(8,128)(2,1)}) custom-call(s32[4]{0:T(128)} %broadcast_xor_fusion.where_ref, bf16[4,2,640,1280]{3,2,1,0:T(8,128)(2,1)} %refs_0_.39, bf16[4,2,640,1280]{3,2,1,0:T(8,128)(2,1)} %refs_0_.39, bf16[4,2,640,1280]{3,2,1,0:T(8,128)(2,1)} %refs_0_.39, bf16[1280,1280]{1,0:T(8,128)(2,1)} %bitcast.66, ...), custom_call_target="tpu_custom_call" | custom-call | flops 1048576 | bytes 65536 | tf_op jit(solution)/shard_map/keep_products/pallas_call | solution.py:97
  80.0 82.3 %collective-permute-done.3.refs_1_.refs_2_ = bf16[2,640,1280]{2,1,0:T(8,128)(2,1)S(1)} collective-permute-done((bf16[2,640,1280]{2,1,0:T(8,128)(2,1)}, bf16[2,640,1280]{2,1,0:T(8,128)(2,1)S(1)}, u32[]{:S(2)}, u32[]{:S(2)}) %collective-permute-start.3) | collective-permute-done | bytes 3276832 | tf_op jit(solution)/shard_map/ppermute | solution.py:214
  162.2 40.3 %collective-permute-done.2.refs_2_ = bf16[1280,1280]{1,0:T(8,128)(2,1)} collective-permute-done((bf16[1280,1280]{1,0:T(8,128)(2,1)}, bf16[1280,1280]{1,0:T(8,128)(2,1)}, u32[]{:S(2)}, u32[]{:S(2)}) %collective-permute-start.2) | collective-permute-done | bytes 3276832 | tf_op jit(solution)/shard_map/ppermute | solution.py:214
  207.2 22.2 %convolution_convert_fusion = bf16[512,2048]{1,0:T(8,128)(2,1)} fusion(bf16[512,6656]{1,0:T(8,128)(2,1)} %all-gather.2.cloned.1.call-done, bf16[6656,2048]{1,0:T(8,128)(2,1)} %param.6), kind=kOutput, calls=%fused_computation.15 | convolution fusion | flops 13959692288 | bytes 36175872 | tf_op jit(solution)/shard_map/dot_general | solution.py:263
  229.5 10.1 %send_products.11 = (bf16[2,320,1280]{2,1,0:T(8,128)(2,1)}, bf16[2,320,1280]{2,1,0:T(8,128)(2,1)}) custom-call(s32[4]{0:T(128)} %broadcast_xor_fusion.where_ref, bf16[4,2,640,1280]{3,2,1,0:T(8,128)(2,1)} %refs_0_.39, bf16[2,640,1280]{2,1,0:T(8,128)(2,1)} %copy-done.2, bf16[1280,1280]{1,0:T(8,128)(2,1)} %collective-permute-done.2.refs_2_), custom_call_target="tpu_custom_call" | custom-call | flops 1048576 | bytes 65536 | tf_op jit(solution)/shard_map/send_products/pallas_call | solution.py:70
  240.1 3.8 fusion
  246.8 10.8 %keep_products.11 = (bf16[2,320,1280]{2,1,0:T(8,128)(2,1)}, bf16[2,320,1280]{2,1,0:T(8,128)(2,1)}) custom-call(s32[4]{0:T(128)} %broadcast_xor_fusion.where_ref, bf16[4,2,640,1280]{3,2,1,0:T(8,128)(2,1)} %refs_0_.39, bf16[2,640,1280]{2,1,0:T(8,128)(2,1)} %copy-done.2, bf16[1280,1280]{1,0:T(8,128)(2,1)} %collective-permute-done.2.refs_2_, ...), custom_call_target="tpu_custom_call" | custom-call | flops 1048576 | bytes 65536 | tf_op jit(solution)/shard_map/keep_products/pallas_call | solution.py:97
  257.5 3.5 collective-permute-done.8
  261.1 14.1 %collective-permute-done.7.refs_3_ = bf16[1280,1280]{1,0:T(8,128)(2,1)} collective-permute-done((bf16[1280,1280]{1,0:T(8,128)(2,1)}, bf16[1280,1280]{1,0:T(8,128)(2,1)}, u32[]{:S(2)}, u32[]{:S(2)}) %collective-permute-start.7) | collective-permute-done | bytes 3276832 | tf_op jit(solution)/shard_map/ppermute | solution.py:214
  277.0 4.0 broadcast_select_fusion.4
  284.5 14.4 %send_products.12 = (bf16[3,320,1280]{2,1,0:T(8,128)(2,1)}, bf16[3,320,1280]{2,1,0:T(8,128)(2,1)}) custom-call(s32[4]{0:T(128)} %broadcast_xor_fusion.where_ref, bf16[4,2,640,1280]{3,2,1,0:T(8,128)(2,1)} %refs_0_.39, bf16[4,2,640,1280]{3,2,1,0:T(8,128)(2,1)} %refs_0_.39, bf16[2,640,1280]{2,1,0:T(8,128)(2,1)} %copy-done.2, ...), custom_call_target="tpu_custom_call" | custom-call | flops 1048576 | bytes 65536 | tf_op jit(solution)/shard_map/send_products/pallas_call | solution.py:70
  300.9 3.9 slice_bitcast_fusion.1
  307.4 15.2 %keep_products.12 = (bf16[3,320,1280]{2,1,0:T(8,128)(2,1)}, bf16[3,320,1280]{2,1,0:T(8,128)(2,1)}) custom-call(s32[4]{0:T(128)} %broadcast_xor_fusion.where_ref, bf16[4,2,640,1280]{3,2,1,0:T(8,128)(2,1)} %refs_0_.39, bf16[4,2,640,1280]{3,2,1,0:T(8,128)(2,1)} %refs_0_.39, bf16[2,640,1280]{2,1,0:T(8,128)(2,1)} %copy-done.2, ...), custom_call_target="tpu_custom_call" | custom-call | flops 1048576 | bytes 65536 | tf_op jit(solution)/shard_map/keep_products/pallas_call | solution.py:97
  322.6 14.9 %collective-permute-done.13 = bf16[2,320,1280]{2,1,0:T(8,128)(2,1)} collective-permute-done((bf16[2,320,1280]{2,1,0:T(8,128)(2,1)}, bf16[2,320,1280]{2,1,0:T(8,128)(2,1)}, u32[]{:S(2)}, u32[]{:S(2)}) %collective-permute-start.13) | collective-permute-done | bytes 1638432 | tf_op jit(solution)/shard_map/ppermute | solution.py:187
  337.5 15.2 %collective-permute-done.9.refs_2_ = bf16[1280,1280]{1,0:T(8,128)(2,1)} collective-permute-done((bf16[1280,1280]{1,0:T(8,128)(2,1)}, bf16[1280,1280]{1,0:T(8,128)(2,1)}, u32[]{:S(2)}, u32[]{:S(2)}) %collective-permute-start.9) | collective-permute-done | bytes 3276832 | tf_op jit(solution)/shard_map/ppermute | solution.py:214
  357.4 3.8 collective-permute-start.16
  362.9 4.0 broadcast_select_fusion.3.refs_3_
  366.9 11.1 %send_products.13 = (bf16[2,320,1280]{2,1,0:T(8,128)(2,1)}, bf16[2,320,1280]{2,1,0:T(8,128)(2,1)}) custom-call(s32[4]{0:T(128)} %broadcast_xor_fusion.where_ref, bf16[4,2,640,1280]{3,2,1,0:T(8,128)(2,1)} %refs_0_.39, bf16[4,2,640,1280]{3,2,1,0:T(8,128)(2,1)} %refs_0_.39, bf16[1280,1280]{1,0:T(8,128)(2,1)} %collective-permute-done.9.refs_2_, ...), custom_call_target="tpu_custom_call" | custom-call | flops 1048576 | bytes 65536 | tf_op jit(solution)/shard_map/send_products/pallas_call | solution.py:70
  384.3 12.3 %keep_products.13 = (bf16[2,320,1280]{2,1,0:T(8,128)(2,1)}, bf16[2,320,1280]{2,1,0:T(8,128)(2,1)}) custom-call(s32[4]{0:T(128)} %broadcast_xor_fusion.where_ref, bf16[4,2,640,1280]{3,2,1,0:T(8,128)(2,1)} %refs_0_.39, bf16[4,2,640,1280]{3,2,1,0:T(8,128)(2,1)} %refs_0_.39, bf16[1280,1280]{1,0:T(8,128)(2,1)} %collective-permute-done.9.refs_2_, ...), custom_call_target="tpu_custom_call" | custom-call | flops 1048576 | bytes 65536 | tf_op jit(solution)/shard_map/keep_products/pallas_call | solution.py:97
  396.5 24.1 %collective-permute-done.18 = bf16[3,320,1280]{2,1,0:T(8,128)(2,1)} collective-permute-done((bf16[3,320,1280]{2,1,0:T(8,128)(2,1)}, bf16[3,320,1280]{2,1,0:T(8,128)(2,1)}, u32[]{:S(2)}, u32[]{:S(2)}) %collective-permute-start.18) | collective-permute-done | bytes 2457632 | tf_op jit(solution)/shard_map/ppermute | solution.py:187
  420.7 10.1 %collective-permute-done.16.refs_3_ = bf16[1280,1280]{1,0:T(8,128)(2,1)} collective-permute-done((bf16[1280,1280]{1,0:T(8,128)(2,1)}, bf16[1280,1280]{1,0:T(8,128)(2,1)}, u32[]{:S(2)}, u32[]{:S(2)}) %collective-permute-start.16) | collective-permute-done | bytes 3276832 | tf_op jit(solution)/shard_map/ppermute | solution.py:214
  432.4 4.2 add_convert_fusion.4
  442.3 3.9 collective-permute-start.22
  448.3 14.5 %send_products.14 = (bf16[3,320,1280]{2,1,0:T(8,128)(2,1)}, bf16[3,320,1280]{2,1,0:T(8,128)(2,1)}) custom-call(s32[4]{0:T(128)} %broadcast_xor_fusion.where_ref, bf16[4,2,640,1280]{3,2,1,0:T(8,128)(2,1)} %refs_0_.39, bf16[2,640,1280]{2,1,0:T(8,128)(2,1)} %copy-done.2, bf16[4,2,640,1280]{3,2,1,0:T(8,128)(2,1)} %refs_0_.39, ...), custom_call_target="tpu_custom_call" | custom-call | flops 1048576 | bytes 65536 | tf_op jit(solution)/shard_map/send_products/pallas_call | solution.py:70
  467.8 3.5 collective-permute-done.21.refs_6_
  471.3 15.2 %keep_products.14 = (bf16[3,320,1280]{2,1,0:T(8,128)(2,1)}, bf16[3,320,1280]{2,1,0:T(8,128)(2,1)}) custom-call(s32[4]{0:T(128)} %broadcast_xor_fusion.where_ref, bf16[4,2,640,1280]{3,2,1,0:T(8,128)(2,1)} %refs_0_.39, bf16[2,640,1280]{2,1,0:T(8,128)(2,1)} %copy-done.2, bf16[4,2,640,1280]{3,2,1,0:T(8,128)(2,1)} %refs_0_.39, ...), custom_call_target="tpu_custom_call" | custom-call | flops 1048576 | bytes 65536 | tf_op jit(solution)/shard_map/keep_products/pallas_call | solution.py:97
  486.6 14.8 %collective-permute-done.23 = bf16[2,320,1280]{2,1,0:T(8,128)(2,1)} collective-permute-done((bf16[2,320,1280]{2,1,0:T(8,128)(2,1)}, bf16[2,320,1280]{2,1,0:T(8,128)(2,1)}, u32[]{:S(2)}, u32[]{:S(2)}) %collective-permute-start.23) | collective-permute-done | bytes 1638432 | tf_op jit(solution)/shard_map/ppermute | solution.py:187
  501.4 10.9 %collective-permute-done.19 = bf16[1280,1280]{1,0:T(8,128)(2,1)S(1)} collective-permute-done((bf16[1280,1280]{1,0:T(8,128)(2,1)}, bf16[1280,1280]{1,0:T(8,128)(2,1)S(1)}, u32[]{:S(2)}, u32[]{:S(2)}) %collective-permute-start.19) | collective-permute-done | bytes 3276832 | tf_op jit(solution)/shard_map/ppermute | solution.py:214
  514.7 4.1 collective-permute-start.27
  520.4 10.1 %send_products.15 = (bf16[2,320,1280]{2,1,0:T(8,128)(2,1)}, bf16[2,320,1280]{2,1,0:T(8,128)(2,1)}) custom-call(s32[4]{0:T(128)} %broadcast_xor_fusion.where_ref, bf16[4,2,640,1280]{3,2,1,0:T(8,128)(2,1)} %refs_0_.39, bf16[2,640,1280]{2,1,0:T(8,128)(2,1)} %bitcast.61, bf16[1280,1280]{1,0:T(8,128)(2,1)} %collective-permute-done.22.refs_2_), custom_call_target="tpu_custom_call" | custom-call | flops 1048576 | bytes 65536 | tf_op jit(solution)/shard_map/send_products/pallas_call | solution.py:70
  531.0 4.4 add_convert_fusion.2
  537.8 10.8 %keep_products.15 = (bf16[2,320,1280]{2,1,0:T(8,128)(2,1)}, bf16[2,320,1280]{2,1,0:T(8,128)(2,1)}) custom-call(s32[4]{0:T(128)} %broadcast_xor_fusion.where_ref, bf16[4,2,640,1280]{3,2,1,0:T(8,128)(2,1)} %refs_0_.39, bf16[2,640,1280]{2,1,0:T(8,128)(2,1)} %bitcast.62, bf16[1280,1280]{1,0:T(8,128)(2,1)} %collective-permute-done.22.refs_2_, ...), custom_call_target="tpu_custom_call" | custom-call | flops 1048576 | bytes 65536 | tf_op jit(solution)/shard_map/keep_products/pallas_call | solution.py:97
  548.6 22.1 %collective-permute-done.28 = bf16[3,320,1280]{2,1,0:T(8,128)(2,1)} collective-permute-done((bf16[3,320,1280]{2,1,0:T(8,128)(2,1)}, bf16[3,320,1280]{2,1,0:T(8,128)(2,1)}, u32[]{:S(2)}, u32[]{:S(2)}) %collective-permute-start.28) | collective-permute-done | bytes 2457632 | tf_op jit(solution)/shard_map/ppermute | solution.py:187
  570.6 13.6 %collective-permute-done.24.refs_4_ = bf16[1280,1280]{1,0:T(8,128)(2,1)} collective-permute-done((bf16[1280,1280]{1,0:T(8,128)(2,1)}, bf16[1280,1280]{1,0:T(8,128)(2,1)}, u32[]{:S(2)}, u32[]{:S(2)}) %collective-permute-start.24) | collective-permute-done | bytes 3276832 | tf_op jit(solution)/shard_map/ppermute | solution.py:214
  586.2 3.8 collective-permute-start.29
  593.0 14.5 %send_products.16 = (bf16[3,320,1280]{2,1,0:T(8,128)(2,1)}, bf16[3,320,1280]{2,1,0:T(8,128)(2,1)}) custom-call(s32[4]{0:T(128)} %broadcast_xor_fusion.where_ref, bf16[4,2,640,1280]{3,2,1,0:T(8,128)(2,1)} %refs_0_.39, bf16[2,640,1280]{2,1,0:T(8,128)(2,1)} %bitcast.55, bf16[4,2,640,1280]{3,2,1,0:T(8,128)(2,1)} %refs_0_.39, ...), custom_call_target="tpu_custom_call" | custom-call | flops 1048576 | bytes 65536 | tf_op jit(solution)/shard_map/send_products/pallas_call | solution.py:70
  618.3 15.1 %keep_products.16 = (bf16[3,320,1280]{2,1,0:T(8,128)(2,1)}, bf16[3,320,1280]{2,1,0:T(8,128)(2,1)}) custom-call(s32[4]{0:T(128)} %broadcast_xor_fusion.where_ref, bf16[4,2,640,1280]{3,2,1,0:T(8,128)(2,1)} %refs_0_.39, bf16[2,640,1280]{2,1,0:T(8,128)(2,1)} %bitcast.56, bf16[4,2,640,1280]{3,2,1,0:T(8,128)(2,1)} %refs_0_.39, ...), custom_call_target="tpu_custom_call" | custom-call | flops 1048576 | bytes 65536 | tf_op jit(solution)/shard_map/keep_products/pallas_call | solution.py:97
  633.5 16.3 %collective-permute-done.33 = bf16[2,320,1280]{2,1,0:T(8,128)(2,1)} collective-permute-done((bf16[2,320,1280]{2,1,0:T(8,128)(2,1)}, bf16[2,320,1280]{2,1,0:T(8,128)(2,1)}, u32[]{:S(2)}, u32[]{:S(2)}) %collective-permute-start.33) | collective-permute-done | bytes 1638432 | tf_op jit(solution)/shard_map/ppermute | solution.py:187
  649.7 6.9 collective-permute-done.29.refs_3_
  668.5 3.9 fusion.2
  676.6 14.4 %send_products.17 = (bf16[3,320,1280]{2,1,0:T(8,128)(2,1)}, bf16[3,320,1280]{2,1,0:T(8,128)(2,1)}) custom-call(s32[4]{0:T(128)} %broadcast_xor_fusion.where_ref, bf16[4,2,640,1280]{3,2,1,0:T(8,128)(2,1)} %refs_0_.39, bf16[2,640,1280]{2,1,0:T(8,128)(2,1)} %bitcast.63, bf16[4,2,640,1280]{3,2,1,0:T(8,128)(2,1)} %refs_0_.39, bf16[1280,1280]{1,0:T(8,128)(2,1)} %copy-done.13, ...), custom_call_target="tpu_custom_call" | custom-call | flops 1048576 | bytes 65536 | tf_op jit(solution)/shard_map/send_products/pallas_call | solution.py:70
  700.7 15.2 %keep_products.17 = (bf16[3,320,1280]{2,1,0:T(8,128)(2,1)}, bf16[3,320,1280]{2,1,0:T(8,128)(2,1)}) custom-call(s32[4]{0:T(128)} %broadcast_xor_fusion.where_ref, bf16[4,2,640,1280]{3,2,1,0:T(8,128)(2,1)} %refs_0_.39, bf16[2,640,1280]{2,1,0:T(8,128)(2,1)} %bitcast.64, bf16[4,2,640,1280]{3,2,1,0:T(8,128)(2,1)} %refs_0_.39, bf16[1280,1280]{1,0:T(8,128)(2,1)} %copy-done.13, ...), custom_call_target="tpu_custom_call" | custom-call | flops 1048576 | bytes 65536 | tf_op jit(solution)/shard_map/keep_products/pallas_call | solution.py:97
  716.0 17.7 %collective-permute-done.38.refs_4_.refs_7_ = bf16[4,160,1280]{2,1,0:T(8,128)(2,1)S(1)} collective-permute-done((bf16[4,160,1280]{2,1,0:T(8,128)(2,1)}, bf16[4,160,1280]{2,1,0:T(8,128)(2,1)S(1)}, u32[]{:S(2)}, u32[]{:S(2)}) %collective-permute-start.38) | collective-permute-done | bytes 1638432 | tf_op jit(solution)/shard_map/ppermute | solution.py:219
  742.9 7.6 send_products.18
  751.0 3.6 collective-permute-start.43
  762.7 8.0 keep_products.18
  770.8 7.5 collective-permute-done.44
  778.3 12.7 %collective-permute-done.43.refs_2_ = bf16[1280,640]{1,0:T(8,128)(2,1)} collective-permute-done((bf16[1280,640]{1,0:T(8,128)(2,1)}, bf16[1280,640]{1,0:T(8,128)(2,1)}, u32[]{:S(2)}, u32[]{:S(2)}) %collective-permute-start.43) | collective-permute-done | bytes 1638432 | tf_op jit(solution)/shard_map/ppermute | solution.py:214
  791.0 3.7 collective-permute-done.45.refs_5_.refs_4_.refs_7_
  803.2 7.6 send_products.19
  819.2 8.1 keep_products.19
  838.8 6.8 place.4.refs_8_
  845.6 7.0 place.5.refs_8_
  858.7 9.0 collective-permute-done.51
  870.5 4.8 collective-permute-done.50
  877.7 6.8 place.6.refs_8_
  884.5 6.8 place.7
  (224 shorter events, 163.4 us)
Async XLA Ops:
  7.2 195.4 %all-gather.2.cloned.1.call-start = ((), (), s32[]{:S(2)}) async-start(), calls=%async_computation.1 | async-start | bytes 8519680 | tf_op jit(solution)/shard_map/all_gather | solution.py:248
  7.9 478.6 %reduce-scatter.2.cloned.1.call-start = ((), (), s32[]{:S(2)}) async-start(), calls=%async_computation.2 | async-start | bytes 2359296 | tf_op jit(solution)/shard_map/reduce_scatter | solution.py:266
  16.8 145.5 %collective-permute-start.3 = (bf16[2,640,1280]{2,1,0:T(8,128)(2,1)}, bf16[2,640,1280]{2,1,0:T(8,128)(2,1)S(1)}, u32[]{:S(2)}, u32[]{:S(2)}) collective-permute-start(bf16[2,640,1280]{2,1,0:T(8,128)(2,1)} %slice_bitcast_fusion), channel_id=1, source_target_pairs={{0,8},{24,16},{1,9},{25,17},{2,10},{26,18},{3,11},{27,19},{4,12},{... | collective-permute-start | bytes 9830408 | tf_op jit(solution)/shard_map/ppermute | solution.py:214
  18.2 184.4 %collective-permute-start.2 = (bf16[1280,1280]{1,0:T(8,128)(2,1)}, bf16[1280,1280]{1,0:T(8,128)(2,1)}, u32[]{:S(2)}, u32[]{:S(2)}) collective-permute-start(bf16[1280,1280]{1,0:T(8,128)(2,1)} %bitcast.40.refs_4_), channel_id=1, source_target_pairs={{8,16},{16,8},{9,17},{17,9},{10,18},{18,10},{11,19},{19,11},{12,20... | collective-permute-start | bytes 9830408 | tf_op jit(solution)/shard_map/ppermute | solution.py:214
  55.3 5.0 collective-permute-start
  55.3 8.5 collective-permute-start.1
  162.2 67.2 %copy-start.2 = (bf16[2,640,1280]{2,1,0:T(8,128)(2,1)}, bf16[2,640,1280]{2,1,0:T(8,128)(2,1)S(1)}, u32[]{:S(2)}) copy-start(bf16[2,640,1280]{2,1,0:T(8,128)(2,1)S(1)} %collective-permute-done.3.refs_1_.refs_2_) | copy-start | bytes 9830404
  202.6 72.6 %collective-permute-start.7 = (bf16[1280,1280]{1,0:T(8,128)(2,1)}, bf16[1280,1280]{1,0:T(8,128)(2,1)}, u32[]{:S(2)}, u32[]{:S(2)}) collective-permute-start(bf16[1280,1280]{1,0:T(8,128)(2,1)} %bitcast.67), channel_id=1, source_target_pairs={{0,8},{8,0},{16,24},{24,16},{1,9},{9,1},{17,25},{25,17},{2,10},{10... | collective-permute-start | bytes 9830408 | tf_op jit(solution)/shard_map/ppermute | solution.py:214
  202.6 74.4 %collective-permute-start.6 = (bf16[1280,1280]{1,0:T(8,128)(2,1)}, bf16[1280,1280]{1,0:T(8,128)(2,1)}, u32[]{:S(2)}, u32[]{:S(2)}) collective-permute-start(bf16[1280,1280]{1,0:T(8,128)(2,1)} %bitcast.68), channel_id=1, source_target_pairs={{8,16},{16,8},{9,17},{17,9},{10,18},{18,10},{11,19},{19,11},{12,20... | collective-permute-start | bytes 9830408 | tf_op jit(solution)/shard_map/ppermute | solution.py:214
  205.7 55.4 %collective-permute-start.8 = (bf16[3,320,1280]{2,1,0:T(8,128)(2,1)}, bf16[3,320,1280]{2,1,0:T(8,128)(2,1)}, u32[]{:S(2)}, u32[]{:S(2)}) collective-permute-start(bf16[3,320,1280]{2,1,0:T(8,128)(2,1)} %get-tuple-element.174), channel_id=1, source_target_pairs={{0,2},{2,0},{1,3},{3,1},{4,6},{6,4},{5,7},{7,5},{8,10},{10,8},{9,1... | collective-permute-start | bytes 7372808 | tf_op jit(solution)/shard_map/ppermute | solution.py:187
  239.5 4.4 collective-permute-start.4
  239.5 6.1 collective-permute-start.5
  281.1 71.6 %collective-permute-start.9 = (bf16[1280,1280]{1,0:T(8,128)(2,1)}, bf16[1280,1280]{1,0:T(8,128)(2,1)}, u32[]{:S(2)}, u32[]{:S(2)}) collective-permute-start(bf16[1280,1280]{1,0:T(8,128)(2,1)} %broadcast_select_fusion.4), channel_id=1, source_target_pairs={{0,8},{8,0},{16,24},{24,16},{1,9},{9,1},{17,25},{25,17},{2,10},{10... | collective-permute-start | bytes 9830408 | tf_op jit(solution)/shard_map/ppermute | solution.py:214
  281.1 73.7 %collective-permute-start.12 = (bf16[1280,1280]{1,0:T(8,128)(2,1)}, bf16[1280,1280]{1,0:T(8,128)(2,1)S(1)}, u32[]{:S(2)}, u32[]{:S(2)}) collective-permute-start(bf16[1280,1280]{1,0:T(8,128)(2,1)} %collective-permute-done.7.refs_3_), channel_id=1, source_target_pairs={{8,16},{16,8},{9,17},{17,9},{10,18},{18,10},{11,19},{19,11},{12,20... | collective-permute-start | bytes 9830408 | tf_op jit(solution)/shard_map/ppermute | solution.py:214
  298.9 5.9 collective-permute-start.10
  298.9 8.5 collective-permute-start.11
  299.4 38.1 %collective-permute-start.13 = (bf16[2,320,1280]{2,1,0:T(8,128)(2,1)}, bf16[2,320,1280]{2,1,0:T(8,128)(2,1)}, u32[]{:S(2)}, u32[]{:S(2)}) collective-permute-start(bf16[2,320,1280]{2,1,0:T(8,128)(2,1)} %get-tuple-element.185), channel_id=1, source_target_pairs={{0,2},{2,0},{1,3},{3,1},{4,6},{6,4},{5,7},{7,5},{8,10},{10,8},{9,1... | collective-permute-start | bytes 4915208 | tf_op jit(solution)/shard_map/ppermute | solution.py:187
  357.4 73.3 %collective-permute-start.16 = (bf16[1280,1280]{1,0:T(8,128)(2,1)}, bf16[1280,1280]{1,0:T(8,128)(2,1)}, u32[]{:S(2)}, u32[]{:S(2)}) collective-permute-start(bf16[1280,1280]{1,0:T(8,128)(2,1)} %collective-permute-done.9.refs_2_), channel_id=1, source_target_pairs={{8,16},{16,8},{9,17},{17,9},{10,18},{18,10},{11,19},{19,11},{12,20... | collective-permute-start | bytes 9830408 | tf_op jit(solution)/shard_map/ppermute | solution.py:214
  361.3 71.1 %collective-permute-start.17 = (bf16[1280,1280]{1,0:T(8,128)(2,1)}, bf16[1280,1280]{1,0:T(8,128)(2,1)S(1)}, u32[]{:S(2)}, u32[]{:S(2)}) collective-permute-start(bf16[1280,1280]{1,0:T(8,128)(2,1)} %broadcast_select_fusion.2), channel_id=1, source_target_pairs={{0,8},{8,0},{16,24},{24,16},{1,9},{9,1},{17,25},{25,17},{2,10},{10... | collective-permute-start | bytes 9830408 | tf_op jit(solution)/shard_map/ppermute | solution.py:214
  361.4 59.3 %collective-permute-start.18 = (bf16[3,320,1280]{2,1,0:T(8,128)(2,1)}, bf16[3,320,1280]{2,1,0:T(8,128)(2,1)}, u32[]{:S(2)}, u32[]{:S(2)}) collective-permute-start(bf16[3,320,1280]{2,1,0:T(8,128)(2,1)} %get-tuple-element.196), channel_id=1, source_target_pairs={{0,2},{2,0},{1,3},{3,1},{4,6},{6,4},{5,7},{7,5},{8,10},{10,8},{9,1... | collective-permute-start | bytes 7372808 | tf_op jit(solution)/shard_map/ppermute | solution.py:187
  378.1 4.1 collective-permute-start.14
  378.1 6.2 collective-permute-start.15
  442.0 70.3 %collective-permute-start.19 = (bf16[1280,1280]{1,0:T(8,128)(2,1)}, bf16[1280,1280]{1,0:T(8,128)(2,1)S(1)}, u32[]{:S(2)}, u32[]{:S(2)}) collective-permute-start(bf16[1280,1280]{1,0:T(8,128)(2,1)} %broadcast_select_fusion.1), channel_id=1, source_target_pairs={{0,8},{8,0},{16,24},{24,16},{1,9},{9,1},{17,25},{25,17},{2,10},{10... | collective-permute-start | bytes 9830408 | tf_op jit(solution)/shard_map/ppermute | solution.py:214
  442.3 72.4 %collective-permute-start.22 = (bf16[1280,1280]{1,0:T(8,128)(2,1)}, bf16[1280,1280]{1,0:T(8,128)(2,1)}, u32[]{:S(2)}, u32[]{:S(2)}) collective-permute-start(bf16[1280,1280]{1,0:T(8,128)(2,1)} %bitcast.46.refs_4_), channel_id=1, source_target_pairs={{8,16},{16,8},{9,17},{17,9},{10,18},{18,10},{11,19},{19,11},{12,20... | collective-permute-start | bytes 9830408 | tf_op jit(solution)/shard_map/ppermute | solution.py:214
  462.8 5.0 collective-permute-start.20
  462.8 8.5 collective-permute-start.21
  463.3 38.1 %collective-permute-start.23 = (bf16[2,320,1280]{2,1,0:T(8,128)(2,1)}, bf16[2,320,1280]{2,1,0:T(8,128)(2,1)}, u32[]{:S(2)}, u32[]{:S(2)}) collective-permute-start(bf16[2,320,1280]{2,1,0:T(8,128)(2,1)} %get-tuple-element.213), channel_id=1, source_target_pairs={{0,2},{2,0},{1,3},{3,1},{4,6},{6,4},{5,7},{7,5},{8,10},{10,8},{9,1... | collective-permute-start | bytes 4915208 | tf_op jit(solution)/shard_map/ppermute | solution.py:187
  514.7 69.5 %collective-permute-start.24 = (bf16[1280,1280]{1,0:T(8,128)(2,1)}, bf16[1280,1280]{1,0:T(8,128)(2,1)}, u32[]{:S(2)}, u32[]{:S(2)}) collective-permute-start(bf16[1280,1280]{1,0:T(8,128)(2,1)} %bitcast.46.refs_4_), channel_id=1, source_target_pairs={{0,8},{8,0},{16,24},{24,16},{1,9},{9,1},{17,25},{25,17},{2,10},{10... | collective-permute-start | bytes 9830408 | tf_op jit(solution)/shard_map/ppermute | solution.py:214
  514.7 71.5 %collective-permute-start.27 = (bf16[1280,1280]{1,0:T(8,128)(2,1)}, bf16[1280,1280]{1,0:T(8,128)(2,1)}, u32[]{:S(2)}, u32[]{:S(2)}) collective-permute-start(bf16[1280,1280]{1,0:T(8,128)(2,1)} %bitcast.49.refs_5_), channel_id=1, source_target_pairs={{8,16},{16,8},{9,17},{17,9},{10,18},{18,10},{11,19},{19,11},{12,20... | collective-permute-start | bytes 9830408 | tf_op jit(solution)/shard_map/ppermute | solution.py:214
  518.8 51.8 %collective-permute-start.28 = (bf16[3,320,1280]{2,1,0:T(8,128)(2,1)}, bf16[3,320,1280]{2,1,0:T(8,128)(2,1)}, u32[]{:S(2)}, u32[]{:S(2)}) collective-permute-start(bf16[3,320,1280]{2,1,0:T(8,128)(2,1)} %get-tuple-element.222), channel_id=1, source_target_pairs={{0,2},{2,0},{1,3},{3,1},{4,6},{6,4},{5,7},{7,5},{8,10},{10,8},{9,1... | collective-permute-start | bytes 7372808 | tf_op jit(solution)/shard_map/ppermute | solution.py:187
  530.5 5.0 collective-permute-start.25
  530.5 6.0 collective-permute-start.26
  586.2 70.4 %collective-permute-start.29 = (bf16[1280,1280]{1,0:T(8,128)(2,1)}, bf16[1280,1280]{1,0:T(8,128)(2,1)S(1)}, u32[]{:S(2)}, u32[]{:S(2)}) collective-permute-start(bf16[1280,1280]{1,0:T(8,128)(2,1)} %collective-permute-done.24.refs_4_), channel_id=1, source_target_pairs={{8,16},{16,8},{9,17},{17,9},{10,18},{18,10},{11,19},{19,11},{12,20... | collective-permute-start | bytes 9830408 | tf_op jit(solution)/shard_map/ppermute | solution.py:214
  590.0 68.4 %collective-permute-start.32 = (bf16[1280,1280]{1,0:T(8,128)(2,1)}, bf16[1280,1280]{1,0:T(8,128)(2,1)}, u32[]{:S(2)}, u32[]{:S(2)}) collective-permute-start(bf16[1280,1280]{1,0:T(8,128)(2,1)} %bitcast.49.refs_5_), channel_id=1, source_target_pairs={{0,8},{8,0},{16,24},{24,16},{1,9},{9,1},{17,25},{25,17},{2,10},{10... | collective-permute-start | bytes 9830408 | tf_op jit(solution)/shard_map/ppermute | solution.py:214
  607.5 10.8 %collective-permute-start.30 = (bf16[3,320,1280]{2,1,0:T(8,128)(2,1)}, bf16[3,320,1280]{2,1,0:T(8,128)(2,1)}, u32[]{:S(2)}, u32[]{:S(2)}) collective-permute-start(bf16[3,320,1280]{2,1,0:T(8,128)(2,1)} %get-tuple-element.225), channel_id=1, source_target_pairs={{0,1},{1,0},{2,3},{3,2},{4,5},{5,4},{6,7},{7,6},{8,9},{9,8},{10,11... | collective-permute-start | bytes 7372808 | tf_op jit(solution)/shard_map/ppermute | solution.py:179
  607.5 10.8 %collective-permute-start.31 = (bf16[3,320,1280]{2,1,0:T(8,128)(2,1)}, bf16[3,320,1280]{2,1,0:T(8,128)(2,1)}, u32[]{:S(2)}, u32[]{:S(2)}) collective-permute-start(bf16[3,320,1280]{2,1,0:T(8,128)(2,1)} %get-tuple-element.226), channel_id=1, source_target_pairs={{0,1},{1,0},{2,3},{3,2},{4,5},{5,4},{6,7},{7,6},{8,9},{9,8},{10,11... | collective-permute-start | bytes 7372808 | tf_op jit(solution)/shard_map/ppermute | solution.py:179
  611.6 38.1 %collective-permute-start.33 = (bf16[2,320,1280]{2,1,0:T(8,128)(2,1)}, bf16[2,320,1280]{2,1,0:T(8,128)(2,1)}, u32[]{:S(2)}, u32[]{:S(2)}) collective-permute-start(bf16[2,320,1280]{2,1,0:T(8,128)(2,1)} %get-tuple-element.231), channel_id=1, source_target_pairs={{0,2},{2,0},{1,3},{3,1},{4,6},{6,4},{5,7},{7,5},{8,10},{10,8},{9,1... | collective-permute-start | bytes 4915208 | tf_op jit(solution)/shard_map/ppermute | solution.py:187
  633.4 27.1 %copy-start.36 = (bf16[2,320,1280]{2,1,0:T(8,128)(2,1)S(1)}, bf16[2,320,1280]{2,1,0:T(8,128)(2,1)}, u32[]{:S(2)}) copy-start(bf16[2,320,1280]{2,1,0:T(8,128)(2,1)} %get-tuple-element.242) | copy-start | bytes 4915204
  665.2 32.3 %collective-permute-start.37 = (bf16[4,160,1280]{2,1,0:T(8,128)(2,1)}, bf16[4,160,1280]{2,1,0:T(8,128)(2,1)}, u32[]{:S(2)}, u32[]{:S(2)}) collective-permute-start(bf16[4,160,1280]{2,1,0:T(8,128)(2,1)} %pad_maximum_fusion.2), channel_id=1, source_target_pairs={{8,0},{16,24},{9,1},{17,25},{10,2},{18,26},{11,3},{19,27},{12,4},{... | collective-permute-start | bytes 4915208 | tf_op jit(solution)/shard_map/ppermute | solution.py:214
  672.5 43.5 %collective-permute-start.36 = (bf16[1280,640]{1,0:T(8,128)(2,1)}, bf16[1280,640]{1,0:T(8,128)(2,1)S(1)}, u32[]{:S(2)}, u32[]{:S(2)}) collective-permute-start(bf16[1280,640]{1,0:T(8,128)(2,1)} %get-tuple-element.239), channel_id=1, source_target_pairs={{8,16},{16,8},{9,17},{17,9},{10,18},{18,10},{11,19},{19,11},{12,20... | collective-permute-start | bytes 4915208 | tf_op jit(solution)/shard_map/ppermute | solution.py:214
  675.0 58.7 %collective-permute-start.39 = (bf16[3,320,1280]{2,1,0:T(8,128)(2,1)}, bf16[3,320,1280]{2,1,0:T(8,128)(2,1)}, u32[]{:S(2)}, u32[]{:S(2)}) collective-permute-start(bf16[3,320,1280]{2,1,0:T(8,128)(2,1)} %get-tuple-element.255), channel_id=1, source_target_pairs={{0,2},{2,0},{1,3},{3,1},{4,6},{6,4},{5,7},{7,5},{8,10},{10,8},{9,1... | collective-permute-start | bytes 7372808 | tf_op jit(solution)/shard_map/ppermute | solution.py:187
  691.0 9.7 %collective-permute-start.34 = (bf16[3,320,1280]{2,1,0:T(8,128)(2,1)}, bf16[3,320,1280]{2,1,0:T(8,128)(2,1)}, u32[]{:S(2)}, u32[]{:S(2)}) collective-permute-start(bf16[3,320,1280]{2,1,0:T(8,128)(2,1)} %get-tuple-element.234), channel_id=1, source_target_pairs={{0,1},{1,0},{2,3},{3,2},{4,5},{5,4},{6,7},{7,6},{8,9},{9,8},{10,11... | collective-permute-start | bytes 7372808 | tf_op jit(solution)/shard_map/ppermute | solution.py:179
  691.0 9.7 %collective-permute-start.35 = (bf16[3,320,1280]{2,1,0:T(8,128)(2,1)}, bf16[3,320,1280]{2,1,0:T(8,128)(2,1)}, u32[]{:S(2)}, u32[]{:S(2)}) collective-permute-start(bf16[3,320,1280]{2,1,0:T(8,128)(2,1)} %get-tuple-element.235), channel_id=1, source_target_pairs={{0,1},{1,0},{2,3},{3,2},{4,5},{5,4},{6,7},{7,6},{8,9},{9,8},{10,11... | collective-permute-start | bytes 7372808 | tf_op jit(solution)/shard_map/ppermute | solution.py:179
  697.5 36.2 %collective-permute-start.38 = (bf16[4,160,1280]{2,1,0:T(8,128)(2,1)}, bf16[4,160,1280]{2,1,0:T(8,128)(2,1)S(1)}, u32[]{:S(2)}, u32[]{:S(2)}) collective-permute-start(bf16[4,160,1280]{2,1,0:T(8,128)(2,1)} %pad_maximum_fusion.3), channel_id=1, source_target_pairs={{0,4},{4,0},{1,5},{5,1},{2,6},{6,2},{3,7},{7,3},{8,12},{12,8},{9,1... | collective-permute-start | bytes 4915208 | tf_op jit(solution)/shard_map/ppermute | solution.py:219
  715.9 19.7 %copy-start.16 = (bf16[1280,640]{1,0:T(8,128)(2,1)}, bf16[1280,640]{1,0:T(8,128)(2,1)S(1)}, u32[]{:S(2)}) copy-start(bf16[1280,640]{1,0:T(8,128)(2,1)S(1)} %collective-permute-done.36.refs_2_) | copy-start | bytes 4915204
  741.8 52.8 %collective-permute-start.45 = (bf16[6,160,1280]{2,1,0:T(8,128)(2,1)}, bf16[6,160,1280]{2,1,0:T(8,128)(2,1)S(1)}, u32[]{:S(2)}, u32[]{:S(2)}) collective-permute-start(bf16[6,160,1280]{2,1,0:T(8,128)(2,1)} %pad_maximum_fusion.1), channel_id=1, source_target_pairs={{0,4},{4,0},{1,5},{5,1},{2,6},{6,2},{3,7},{7,3},{8,12},{12,8},{9,1... | collective-permute-start | bytes 7372808 | tf_op jit(solution)/shard_map/ppermute | solution.py:219
  742.4 52.6 %collective-permute-start.40 = (bf16[3,320,1280]{2,1,0:T(8,128)(2,1)}, bf16[3,320,1280]{2,1,0:T(8,128)(2,1)}, u32[]{:S(2)}, u32[]{:S(2)}) collective-permute-start(bf16[3,320,1280]{2,1,0:T(8,128)(2,1)} %get-tuple-element.265), channel_id=1, source_target_pairs={{0,2},{2,0},{1,3},{3,1},{4,6},{6,4},{5,7},{7,5},{8,10},{10,8},{9,1... | collective-permute-start | bytes 7372808 | tf_op jit(solution)/shard_map/ppermute | solution.py:187
  750.5 8.5 collective-permute-start.41
  750.5 12.2 %collective-permute-start.42 = (bf16[2,320,640]{2,1,0:T(8,128)(2,1)}, bf16[2,320,640]{2,1,0:T(8,128)(2,1)}, u32[]{:S(2)}, u32[]{:S(2)}) collective-permute-start(bf16[2,320,640]{2,1,0:T(8,128)(2,1)} %get-tuple-element.268), channel_id=1, source_target_pairs={{0,1},{1,0},{2,3},{3,2},{4,5},{5,4},{6,7},{7,6},{8,9},{9,8},{10,11... | collective-permute-start | bytes 2457608 | tf_op jit(solution)/shard_map/ppermute | solution.py:179
  751.0 39.9 %collective-permute-start.43 = (bf16[1280,640]{1,0:T(8,128)(2,1)}, bf16[1280,640]{1,0:T(8,128)(2,1)}, u32[]{:S(2)}, u32[]{:S(2)}) collective-permute-start(bf16[1280,640]{1,0:T(8,128)(2,1)} %get-tuple-element.272), channel_id=1, source_target_pairs={{8,16},{16,8},{9,17},{17,9},{10,18},{18,10},{11,19},{19,11},{12,20... | collective-permute-start | bytes 4915208 | tf_op jit(solution)/shard_map/ppermute | solution.py:214
  759.0 19.3 %collective-permute-start.44 = (bf16[2,160,1280]{2,1,0:T(8,128)(2,1)}, bf16[2,160,1280]{2,1,0:T(8,128)(2,1)}, u32[]{:S(2)}, u32[]{:S(2)}) collective-permute-start(bf16[2,160,1280]{2,1,0:T(8,128)(2,1)} %bitcast.23), channel_id=1, source_target_pairs={{8,0},{16,24},{9,1},{17,25},{10,2},{18,26},{11,3},{19,27},{12,4},{... | collective-permute-start | bytes 2457608 | tf_op jit(solution)/shard_map/ppermute | solution.py:214
  770.8 26.8 %copy-start.30 = (bf16[3,320,1280]{2,1,0:T(8,128)(2,1)S(1)}, bf16[3,320,1280]{2,1,0:T(8,128)(2,1)}, u32[]{:S(2)}) copy-start(bf16[3,320,1280]{2,1,0:T(8,128)(2,1)} %get-tuple-element.264) | copy-start | bytes 7372804
  801.5 55.3 %collective-permute-start.52 = (bf16[2,160,1280]{2,1,0:T(8,128)(2,1)}, bf16[2,160,1280]{2,1,0:T(8,128)(2,1)}, u32[]{:S(2)}, u32[]{:S(2)}) collective-permute-start(bf16[2,160,1280]{2,1,0:T(8,128)(2,1)} %bitcast.29), channel_id=1, source_target_pairs={{8,4},{16,28},{9,5},{17,29},{10,6},{18,30},{11,7},{19,31}} | collective-permute-start | bytes 2457608 | tf_op jit(solution)/shard_map/ppermute | solution.py:239
  803.2 28.3 %collective-permute-start.54 = (bf16[2,320,640]{2,1,0:T(8,128)(2,1)}, bf16[2,320,640]{2,1,0:T(8,128)(2,1)}, u32[]{:S(2)}, u32[]{:S(2)}) collective-permute-start(bf16[2,320,640]{2,1,0:T(8,128)(2,1)} %get-tuple-element.296), channel_id=1, source_target_pairs={{0,2},{2,0},{1,3},{3,1},{4,6},{6,4},{5,7},{7,5},{8,10},{10,8},{9,1... | collective-permute-start | bytes 2457608 | tf_op jit(solution)/shard_map/ppermute | solution.py:187
  810.8 5.1 collective-permute-start.47
  810.8 8.4 collective-permute-start.48
  812.7 24.7 %collective-permute-start.57 = (bf16[2,160,1280]{2,1,0:T(8,128)(2,1)}, bf16[2,160,1280]{2,1,0:T(8,128)(2,1)S(1)}, u32[]{:S(2)}, u32[]{:S(2)}) collective-permute-start(bf16[2,160,1280]{2,1,0:T(8,128)(2,1)} %get-tuple-element.330), channel_id=1, source_target_pairs={{0,4},{4,0},{1,5},{5,1},{2,6},{6,2},{3,7},{7,3},{8,12},{12,8},{9,1... | collective-permute-start | bytes 2457608 | tf_op jit(solution)/shard_map/ppermute | solution.py:219
  815.9 51.8 %collective-permute-start.51 = (bf16[4,160,1280]{2,1,0:T(8,128)(2,1)}, bf16[4,160,1280]{2,1,0:T(8,128)(2,1)}, u32[]{:S(2)}, u32[]{:S(2)}) collective-permute-start(bf16[4,160,1280]{2,1,0:T(8,128)(2,1)} %pad_maximum_fusion.4), channel_id=1, source_target_pairs={{4,0},{5,1},{6,2},{7,3},{12,8},{13,9},{14,10},{15,11},{20,16},{21,... | collective-permute-start | bytes 4915208 | tf_op jit(solution)/shard_map/ppermute | solution.py:245
  827.3 25.3 %collective-permute-start.49 = (bf16[2,320,640]{2,1,0:T(8,128)(2,1)}, bf16[2,320,640]{2,1,0:T(8,128)(2,1)}, u32[]{:S(2)}, u32[]{:S(2)}) collective-permute-start(bf16[2,320,640]{2,1,0:T(8,128)(2,1)} %get-tuple-element.290), channel_id=1, source_target_pairs={{0,2},{2,0},{1,3},{3,1},{4,6},{6,4},{5,7},{7,5},{8,10},{10,8},{9,1... | collective-permute-start | bytes 2457608 | tf_op jit(solution)/shard_map/ppermute | solution.py:187
  831.4 24.7 %collective-permute-start.46 = (bf16[2,160,1280]{2,1,0:T(8,128)(2,1)}, bf16[2,160,1280]{2,1,0:T(8,128)(2,1)}, u32[]{:S(2)}, u32[]{:S(2)}) collective-permute-start(bf16[2,160,1280]{2,1,0:T(8,128)(2,1)} %broadcast_select_fusion.16), channel_id=1, source_target_pairs={{8,12},{16,20},{12,4},{20,28},{9,13},{17,21},{13,5},{21,29},{10,14... | collective-permute-start | bytes 2457608 | tf_op jit(solution)/shard_map/ppermute | solution.py:238
  837.4 33.1 %collective-permute-start.56 = (bf16[2,160,640]{2,1,0:T(8,128)(2,1)}, bf16[2,160,640]{2,1,0:T(8,128)(2,1)}, u32[]{:S(2)}, u32[]{:S(2)}) collective-permute-start(bf16[2,160,640]{2,1,0:T(8,128)(2,1)} %bitcast.34), channel_id=1, source_target_pairs={{8,4},{16,28},{9,5},{17,29},{10,6},{18,30},{11,7},{19,31}} | collective-permute-start | bytes 1228808 | tf_op jit(solution)/shard_map/ppermute | solution.py:239
  852.5 17.9 %collective-permute-start.55 = (bf16[2,160,640]{2,1,0:T(8,128)(2,1)}, bf16[2,160,640]{2,1,0:T(8,128)(2,1)S(1)}, u32[]{:S(2)}, u32[]{:S(2)}) collective-permute-start(bf16[2,160,640]{2,1,0:T(8,128)(2,1)} %broadcast_select_fusion.23), channel_id=1, source_target_pairs={{8,12},{16,20},{12,4},{20,28},{9,13},{17,21},{13,5},{21,29},{10,14... | collective-permute-start | bytes 1228808 | tf_op jit(solution)/shard_map/ppermute | solution.py:238
  856.1 19.1 %collective-permute-start.53 = (bf16[2,160,640]{2,1,0:T(8,128)(2,1)S(1)}, bf16[2,160,640]{2,1,0:T(8,128)(2,1)S(1)}, u32[]{:S(2)}, u32[]{:S(2)}) collective-permute-start(bf16[2,160,640]{2,1,0:T(8,128)(2,1)S(1)} %bitcast.105), channel_id=1, source_target_pairs={{8,4},{16,28},{9,5},{17,29},{10,6},{18,30},{11,7},{19,31}} | collective-permute-start | bytes 1228808 | tf_op jit(solution)/shard_map/ppermute | solution.py:239
  856.8 18.4 %collective-permute-start.50 = (bf16[2,160,640]{2,1,0:T(8,128)(2,1)S(1)}, bf16[2,160,640]{2,1,0:T(8,128)(2,1)S(1)}, u32[]{:S(2)}, u32[]{:S(2)}) collective-permute-start(bf16[2,160,640]{2,1,0:T(8,128)(2,1)S(1)} %broadcast_select_fusion.24), channel_id=1, source_target_pairs={{8,12},{16,20},{12,4},{20,28},{9,13},{17,21},{13,5},{21,29},{10,14... | collective-permute-start | bytes 1228808 | tf_op jit(solution)/shard_map/ppermute | solution.py:238
  (37 other events, 227.5 us)
Sparse Core Ops, SparseCore 0:
  9.6 192.0 all-gather.1
  378.7 46.1 reduce-scatter.1

commit v7 on v6

--- a/solution.py
+++ b/solution.py
@@ -245,24 +245,39 @@
         return lax.ppermute(order.open(near), "occ", [(1, 0)])
 
     ca = cycle_amplitudes
-    gathered = lax.all_gather(ladder_amplitudes, "vir", axis=0, tiled=True)
+    ladder_near = move(ladder_amplitudes, NEIGHBOUR)
+    ladder_far = move(ladder_amplitudes, MID_TO_MID)
     b0 = columns_of(0)
-    order.phase(b0)
+
+    order.phase(ladder_near, ladder_far, b0)
+    ladder_last = move(ladder_near, MID_TO_MID)
+    on_far = move(ladder_far, MID_TO_END)
+    b3, b1, b2 = columns_of(3), columns_of(1), columns_of(2)
+
+    order.phase(ladder_last, on_far, b3, b1, b2)
+    on_last = move(ladder_last, MID_TO_END)
     own0 = move(b0, MID_TO_MID)
     a0 = move(rows_of(0), END_TO_MID)
-    b3, b1, b2 = columns_of(3), columns_of(1), columns_of(2)
     one = batch((3, ca, b3), (1, ca, b1), (2, ca, b2))
     one.send()
     one.keep()
 
-    order.phase(own0, a0, gathered)
+    order.phase(own0, a0, on_last)
     own3 = move(b3, MID_TO_MID)
     swap3 = move(b3, NEIGHBOUR)
     one.swap()
     two = batch((0, ca, own0), (0, a0, own0))
+    rows = jnp.concatenate([
+        ladder_amplitudes, ladder_near,
+        jnp.where(at_end, order.open(on_far), ladder_far), jnp.where(at_end, order.open(on_last), ladder_last)])
     partial_ladder = order.step(jnp.dot(
-        order.follow(gathered), ladder_integrals, preferred_element_type=F32,
-    ).astype(BF16))
+        order.follow(rows), ladder_integrals, preferred_element_type=F32).astype(BF16))
+    plane = jnp.arange(4)
+    held = jnp.where(
+        plane // 2 == vir // 2, jnp.where(plane == vir, 0, 1), jnp.where((plane == 1) | (plane == 2), 2, 3))
+    step = ladder_amplitudes.shape[0]
+    partial_ladder = jnp.concatenate([
+        lax.dynamic_slice_in_dim(partial_ladder, held[w] * step, step, 0) for w in range(4)])
     ladder_residual = lax.psum_scatter(partial_ladder, ("occ", "ka"), scatter_dimension=0, tiled=True)
     two.send()
     two.keep()
@@ -287,7 +302,7 @@
     four.send()
     four.keep()
 
-    order.phase(relay0, both4, three.other)
+    order.phase(relay0, both4, three.other, f0[1])
     n3, *s0 = three.finish()
     a1 = both4.reshape(a0.shape)
     own1 = move(b1, MID_TO_MID)

time: 914 us -> 872 us (0.954)
  waiting for transfers between devices: 381 us -> 321 us
  starting transfers between devices: 73.9 us -> 92.1 us
    ppermute x18 -> x23, waiting for transfers between devices: 227 us -> 180 us  [move(): return lax.ppermute(order.open(value), 'vir', route)]
    ppermute x18 -> x23, starting transfers between devices: 39.3 us -> 54.1 us  [move(): return lax.ppermute(order.open(value), 'vir', route)]
    ppermute x10, waiting for transfers between devices: 96 us -> 82.2 us  [swap(): self.other = lax.ppermute(self.order.open(self.away), 'ka', OTHER_Y)]
    reduce_scatter x1, waiting for transfers between devices: 0.01 us -> 12.1 us  [line_local(): lax.psum_scatter(partial_ladder, ('occ', 'ka'), scatter_dimension=0, tile...]
  transfers between devices with their start and end apart: 60 -> 64, of which waited for: 36 -> 40; matrix products, arithmetic and copies ran while one was open for 13% -> 12% of each run, Pallas kernels for 29% -> 30%
where the time goes in v7:
time: 872 us; the launch traced here: 862 us
  waiting for transfers between devices  321 us (37%)
  Pallas kernels  274 us (31%)
  starting transfers between devices  92.1 us (11%)
  other arithmetic  77.3 us (9%)
  local copies, waits for them, and re-layouts  59.8 us (7%)
  matrix products  20.3 us (2%)
  between operations  17.7 us (2%)
    ppermute x23, waiting for transfers between devices, move(): return lax.ppermute(order.open(value), 'vir', route)  180 us
    pallas_call x10, Pallas kernels, keep_products(): pl.pallas_call(kernel, out_shape=(jax.ShapeDtypeStruct((count, rows, colu...  126 us
    pallas_call x10, Pallas kernels, send_products(): pl.pallas_call(kernel, out_shape=(jax.ShapeDtypeStruct((count, rows, colu...  120 us
    ppermute x10, waiting for transfers between devices, swap(): self.other = lax.ppermute(self.order.open(self.away), 'ka', OTHER_Y)  82.2 us
    ppermute x23, starting transfers between devices, move(): return lax.ppermute(order.open(value), 'vir', route)  54.1 us
    pallas_call x4, Pallas kernels, place(): pl.pallas_call(kernel, out_shape=jax.ShapeDtypeStruct(shape, BF16), grid_...  27.4 us
    convert_element_type x10, other arithmetic, finish(): (self.own.astype(F32) + self.order.open(self.other).astype(F32)).astype(B...  25.5 us
    dot_general x1, matrix products, line_local(): jnp.dot(order.follow(rows), ladder_integrals, preferred_element_type=F32)  20.3 us
  transfers between devices with their start and end apart: 64, of which 40 were waited for; matrix products, arithmetic and copies ran while one was open for 12% of the time, Pallas kernels for 30%

profile of v7, /device:TPU:10, one launch (start us, length us, event | category | flops | bytes accessed | tf_op | source)
XLA Modules:
  0.0 861.9 jit_solution(9906942622558975551)
XLA Ops:
  7.7 4.6 collective-permute-start.1
  14.7 31.8 %collective-permute-done = bf16[128,6656]{1,0:T(8,128)(2,1)S(1)} collective-permute-done((bf16[128,6656]{1,0:T(8,128)(2,1)}, bf16[128,6656]{1,0:T(8,128)(2,1)S(1)}, u32[]{:S(2)}, u32[]{:S(2)}) %collective-permute-start) | collective-permute-done | bytes 1703968 | tf_op jit(solution)/shard_map/ppermute | solution.py:214
  50.9 3.6 collective-permute-start.3
  54.5 8.8 %fusion.1 = (bf16[1,1280,2,640]{3,2,1,0:T(2,128)(2,1)S(1)}, bf16[1,1280,2,640]{3,2,1,0:T(2,128)(2,1)S(1)}, bf16[1,1280,2,640]{3,2,1,0:T(2,128)(2,1)S(1)}) fusion(bf16[4,1280,2,640]{3,2,1,0:T(2,128)(2,1)} %param.8), kind=kLoop, calls=%fused_computation.69 | loop fusion | bytes 19660800 | tf_op jit(solution)/shard_map/slice | solution.py:205
  70.4 16.2 %collective-permute-done.2 = bf16[128,6656]{1,0:T(8,128)(2,1)S(1)} collective-permute-done((bf16[128,6656]{1,0:T(8,128)(2,1)S(1)}, bf16[128,6656]{1,0:T(8,128)(2,1)S(1)}, u32[]{:S(2)}, u32[]{:S(2)}) %collective-permute-start.2) | collective-permute-done | bytes 1703968 | tf_op jit(solution)/shard_map/ppermute | solution.py:214
  86.6 4.2 collective-permute-done.3
  90.8 4.5 slice_bitcast_fusion
  100.5 15.4 %send_products.10 = (bf16[3,320,1280]{2,1,0:T(8,128)(2,1)}, bf16[3,320,1280]{2,1,0:T(8,128)(2,1)}) custom-call(s32[4]{0:T(128)} %broadcast_xor_fusion.where_ref, bf16[4,2,640,1280]{3,2,1,0:T(8,128)(2,1)} %refs_0_.39, bf16[4,2,640,1280]{3,2,1,0:T(8,128)(2,1)} %refs_0_.39, bf16[4,2,640,1280]{3,2,1,0:T(8,128)(2,1)} %refs_0_.39, bf16[1280,1280]{1,0:T(8,128)(2,1)} %bitcast.69, ...), custom_call_target="tpu_custom_call" | custom-call | flops 1048576 | bytes 65536 | tf_op jit(solution)/shard_map/send_products/pallas_call | solution.py:70
  116.4 5.5 collective-permute-start.8
  124.4 16.1 %keep_products.10 = (bf16[3,320,1280]{2,1,0:T(8,128)(2,1)}, bf16[3,320,1280]{2,1,0:T(8,128)(2,1)}) custom-call(s32[4]{0:T(128)} %broadcast_xor_fusion.where_ref, bf16[4,2,640,1280]{3,2,1,0:T(8,128)(2,1)} %refs_0_.39, bf16[4,2,640,1280]{3,2,1,0:T(8,128)(2,1)} %refs_0_.39, bf16[4,2,640,1280]{3,2,1,0:T(8,128)(2,1)} %refs_0_.39, bf16[1280,1280]{1,0:T(8,128)(2,1)} %bitcast.70, ...), custom_call_target="tpu_custom_call" | custom-call | flops 1048576 | bytes 65536 | tf_op jit(solution)/shard_map/keep_products/pallas_call | solution.py:97
  140.5 16.7 %collective-permute-done.8 = bf16[128,6656]{1,0:T(8,128)(2,1)} collective-permute-done((bf16[128,6656]{1,0:T(8,128)(2,1)}, bf16[128,6656]{1,0:T(8,128)(2,1)}, u32[]{:S(2)}, u32[]{:S(2)}) %collective-permute-start.8) | collective-permute-done | bytes 1703968 | tf_op jit(solution)/shard_map/ppermute | solution.py:214
  157.2 11.1 %collective-permute-done.7.refs_1_.refs_2_ = bf16[2,640,1280]{2,1,0:T(8,128)(2,1)S(1)} collective-permute-done((bf16[2,640,1280]{2,1,0:T(8,128)(2,1)}, bf16[2,640,1280]{2,1,0:T(8,128)(2,1)S(1)}, u32[]{:S(2)}, u32[]{:S(2)}) %collective-permute-start.7) | collective-permute-done | bytes 3276832 | tf_op jit(solution)/shard_map/ppermute | solution.py:214
  178.8 20.3 %convolution_convert_fusion = bf16[512,2048]{1,0:T(8,128)(2,1)} fusion(bf16[512,6656]{1,0:T(8,128)(2,1)S(1)} %pad_maximum_fusion, bf16[6656,2048]{1,0:T(8,128)(2,1)} %param.6), kind=kOutput, calls=%fused_computation.16 | convolution fusion | flops 13959692288 | bytes 36175872 | tf_op jit(solution)/shard_map/dot_general | solution.py:273
  199.1 10.1 %send_products.11 = (bf16[2,320,1280]{2,1,0:T(8,128)(2,1)}, bf16[2,320,1280]{2,1,0:T(8,128)(2,1)}) custom-call(s32[4]{0:T(128)} %broadcast_xor_fusion.where_ref, bf16[4,2,640,1280]{3,2,1,0:T(8,128)(2,1)} %refs_0_.39, bf16[2,640,1280]{2,1,0:T(8,128)(2,1)} %copy-done.2, bf16[1280,1280]{1,0:T(8,128)(2,1)} %collective-permute-done.6.refs_2_), custom_call_target="tpu_custom_call" | custom-call | flops 1048576 | bytes 65536 | tf_op jit(solution)/shard_map/send_products/pallas_call | solution.py:70
  215.4 10.8 %keep_products.11 = (bf16[2,320,1280]{2,1,0:T(8,128)(2,1)}, bf16[2,320,1280]{2,1,0:T(8,128)(2,1)}) custom-call(s32[4]{0:T(128)} %broadcast_xor_fusion.where_ref, bf16[4,2,640,1280]{3,2,1,0:T(8,128)(2,1)} %refs_0_.39, bf16[2,640,1280]{2,1,0:T(8,128)(2,1)} %copy-done.2, bf16[1280,1280]{1,0:T(8,128)(2,1)} %collective-permute-done.6.refs_2_, ...), custom_call_target="tpu_custom_call" | custom-call | flops 1048576 | bytes 65536 | tf_op jit(solution)/shard_map/keep_products/pallas_call | solution.py:97
  229.4 10.6 %collective-permute-done.12.refs_3_ = bf16[1280,1280]{1,0:T(8,128)(2,1)} collective-permute-done((bf16[1280,1280]{1,0:T(8,128)(2,1)}, bf16[1280,1280]{1,0:T(8,128)(2,1)}, u32[]{:S(2)}, u32[]{:S(2)}) %collective-permute-start.12) | collective-permute-done | bytes 3276832 | tf_op jit(solution)/shard_map/ppermute | solution.py:214
  242.1 4.0 broadcast_select_fusion.4
  249.0 14.4 %send_products.12 = (bf16[3,320,1280]{2,1,0:T(8,128)(2,1)}, bf16[3,320,1280]{2,1,0:T(8,128)(2,1)}) custom-call(s32[4]{0:T(128)} %broadcast_xor_fusion.where_ref, bf16[4,2,640,1280]{3,2,1,0:T(8,128)(2,1)} %refs_0_.39, bf16[4,2,640,1280]{3,2,1,0:T(8,128)(2,1)} %refs_0_.39, bf16[2,640,1280]{2,1,0:T(8,128)(2,1)} %copy-done.2, ...), custom_call_target="tpu_custom_call" | custom-call | flops 1048576 | bytes 65536 | tf_op jit(solution)/shard_map/send_products/pallas_call | solution.py:70
  265.4 3.8 slice_bitcast_fusion.1
  271.9 15.2 %keep_products.12 = (bf16[3,320,1280]{2,1,0:T(8,128)(2,1)}, bf16[3,320,1280]{2,1,0:T(8,128)(2,1)}) custom-call(s32[4]{0:T(128)} %broadcast_xor_fusion.where_ref, bf16[4,2,640,1280]{3,2,1,0:T(8,128)(2,1)} %refs_0_.39, bf16[4,2,640,1280]{3,2,1,0:T(8,128)(2,1)} %refs_0_.39, bf16[2,640,1280]{2,1,0:T(8,128)(2,1)} %copy-done.2, ...), custom_call_target="tpu_custom_call" | custom-call | flops 1048576 | bytes 65536 | tf_op jit(solution)/shard_map/keep_products/pallas_call | solution.py:97
  287.1 14.9 %collective-permute-done.18 = bf16[2,320,1280]{2,1,0:T(8,128)(2,1)} collective-permute-done((bf16[2,320,1280]{2,1,0:T(8,128)(2,1)}, bf16[2,320,1280]{2,1,0:T(8,128)(2,1)}, u32[]{:S(2)}, u32[]{:S(2)}) %collective-permute-start.18) | collective-permute-done | bytes 1638432 | tf_op jit(solution)/shard_map/ppermute | solution.py:187
  302.0 13.4 %collective-permute-done.14.refs_2_ = bf16[1280,1280]{1,0:T(8,128)(2,1)} collective-permute-done((bf16[1280,1280]{1,0:T(8,128)(2,1)}, bf16[1280,1280]{1,0:T(8,128)(2,1)}, u32[]{:S(2)}, u32[]{:S(2)}) %collective-permute-start.14) | collective-permute-done | bytes 3276832 | tf_op jit(solution)/shard_map/ppermute | solution.py:214
  317.3 4.0 broadcast_select_fusion.2
  325.5 4.0 broadcast_select_fusion.3.refs_3_
  329.5 11.1 %send_products.13 = (bf16[2,320,1280]{2,1,0:T(8,128)(2,1)}, bf16[2,320,1280]{2,1,0:T(8,128)(2,1)}) custom-call(s32[4]{0:T(128)} %broadcast_xor_fusion.where_ref, bf16[4,2,640,1280]{3,2,1,0:T(8,128)(2,1)} %refs_0_.39, bf16[4,2,640,1280]{3,2,1,0:T(8,128)(2,1)} %refs_0_.39, bf16[1280,1280]{1,0:T(8,128)(2,1)} %collective-permute-done.14.refs_2_, ...), custom_call_target="tpu_custom_call" | custom-call | flops 1048576 | bytes 65536 | tf_op jit(solution)/shard_map/send_products/pallas_call | solution.py:70
  350.5 11.8 %keep_products.13 = (bf16[2,320,1280]{2,1,0:T(8,128)(2,1)}, bf16[2,320,1280]{2,1,0:T(8,128)(2,1)}) custom-call(s32[4]{0:T(128)} %broadcast_xor_fusion.where_ref, bf16[4,2,640,1280]{3,2,1,0:T(8,128)(2,1)} %refs_0_.39, bf16[4,2,640,1280]{3,2,1,0:T(8,128)(2,1)} %refs_0_.39, bf16[1280,1280]{1,0:T(8,128)(2,1)} %collective-permute-done.14.refs_2_, ...), custom_call_target="tpu_custom_call" | custom-call | flops 1048576 | bytes 65536 | tf_op jit(solution)/shard_map/keep_products/pallas_call | solution.py:97
  362.2 12.2 %collective-permute-done.23 = bf16[3,320,1280]{2,1,0:T(8,128)(2,1)} collective-permute-done((bf16[3,320,1280]{2,1,0:T(8,128)(2,1)}, bf16[3,320,1280]{2,1,0:T(8,128)(2,1)}, u32[]{:S(2)}, u32[]{:S(2)}) %collective-permute-start.23) | collective-permute-done | bytes 2457632 | tf_op jit(solution)/shard_map/ppermute | solution.py:187
  374.4 17.2 %collective-permute-done.21.refs_3_ = bf16[1280,1280]{1,0:T(8,128)(2,1)} collective-permute-done((bf16[1280,1280]{1,0:T(8,128)(2,1)}, bf16[1280,1280]{1,0:T(8,128)(2,1)}, u32[]{:S(2)}, u32[]{:S(2)}) %collective-permute-start.21) | collective-permute-done | bytes 3276832 | tf_op jit(solution)/shard_map/ppermute | solution.py:214
  391.8 4.2 add_convert_fusion.4
  399.3 5.4 broadcast_select_fusion
  404.7 3.9 collective-permute-start.27
  411.3 14.6 %send_products.14 = (bf16[3,320,1280]{2,1,0:T(8,128)(2,1)}, bf16[3,320,1280]{2,1,0:T(8,128)(2,1)}) custom-call(s32[4]{0:T(128)} %broadcast_xor_fusion.where_ref, bf16[4,2,640,1280]{3,2,1,0:T(8,128)(2,1)} %refs_0_.39, bf16[2,640,1280]{2,1,0:T(8,128)(2,1)} %copy-done.2, bf16[4,2,640,1280]{3,2,1,0:T(8,128)(2,1)} %refs_0_.39, ...), custom_call_target="tpu_custom_call" | custom-call | flops 1048576 | bytes 65536 | tf_op jit(solution)/shard_map/send_products/pallas_call | solution.py:70
  434.4 15.2 %keep_products.14 = (bf16[3,320,1280]{2,1,0:T(8,128)(2,1)}, bf16[3,320,1280]{2,1,0:T(8,128)(2,1)}) custom-call(s32[4]{0:T(128)} %broadcast_xor_fusion.where_ref, bf16[4,2,640,1280]{3,2,1,0:T(8,128)(2,1)} %refs_0_.39, bf16[2,640,1280]{2,1,0:T(8,128)(2,1)} %copy-done.2, bf16[4,2,640,1280]{3,2,1,0:T(8,128)(2,1)} %refs_0_.39, ...), custom_call_target="tpu_custom_call" | custom-call | flops 1048576 | bytes 65536 | tf_op jit(solution)/shard_map/keep_products/pallas_call | solution.py:97
  449.6 12.1 %reduce-scatter.2.cloned.1.call-done = bf16[64,2048]{1,0:T(8,128)(2,1)} async-done(((bf16[512,2048]{1,0:T(8,128)(2,1)}), bf16[64,2048]{1,0:T(8,128)(2,1)}) %reduce-scatter.2.cloned.1.call-update) | async-done | bytes 262160 | tf_op jit(solution)/shard_map/reduce_scatter | solution.py:281
  461.7 11.2 %collective-permute-done.28 = bf16[2,320,1280]{2,1,0:T(8,128)(2,1)} collective-permute-done((bf16[2,320,1280]{2,1,0:T(8,128)(2,1)}, bf16[2,320,1280]{2,1,0:T(8,128)(2,1)}, u32[]{:S(2)}, u32[]{:S(2)}) %collective-permute-start.28) | collective-permute-done | bytes 1638432 | tf_op jit(solution)/shard_map/ppermute | solution.py:187
  473.9 4.1 collective-permute-start.32
  479.6 10.1 %send_products.15 = (bf16[2,320,1280]{2,1,0:T(8,128)(2,1)}, bf16[2,320,1280]{2,1,0:T(8,128)(2,1)}) custom-call(s32[4]{0:T(128)} %broadcast_xor_fusion.where_ref, bf16[4,2,640,1280]{3,2,1,0:T(8,128)(2,1)} %refs_0_.39, bf16[2,640,1280]{2,1,0:T(8,128)(2,1)} %bitcast.65, bf16[1280,1280]{1,0:T(8,128)(2,1)} %collective-permute-done.27.refs_2_), custom_call_target="tpu_custom_call" | custom-call | flops 1048576 | bytes 65536 | tf_op jit(solution)/shard_map/send_products/pallas_call | solution.py:70
  490.2 4.5 add_convert_fusion.2
  497.1 10.8 %keep_products.15 = (bf16[2,320,1280]{2,1,0:T(8,128)(2,1)}, bf16[2,320,1280]{2,1,0:T(8,128)(2,1)}) custom-call(s32[4]{0:T(128)} %broadcast_xor_fusion.where_ref, bf16[4,2,640,1280]{3,2,1,0:T(8,128)(2,1)} %refs_0_.39, bf16[2,640,1280]{2,1,0:T(8,128)(2,1)} %bitcast.66, bf16[1280,1280]{1,0:T(8,128)(2,1)} %collective-permute-done.27.refs_2_, ...), custom_call_target="tpu_custom_call" | custom-call | flops 1048576 | bytes 65536 | tf_op jit(solution)/shard_map/keep_products/pallas_call | solution.py:97
  507.9 24.2 %collective-permute-done.33 = bf16[3,320,1280]{2,1,0:T(8,128)(2,1)} collective-permute-done((bf16[3,320,1280]{2,1,0:T(8,128)(2,1)}, bf16[3,320,1280]{2,1,0:T(8,128)(2,1)}, u32[]{:S(2)}, u32[]{:S(2)}) %collective-permute-start.33) | collective-permute-done | bytes 2457632 | tf_op jit(solution)/shard_map/ppermute | solution.py:187
  532.1 13.3 %collective-permute-done.29.refs_4_ = bf16[1280,1280]{1,0:T(8,128)(2,1)} collective-permute-done((bf16[1280,1280]{1,0:T(8,128)(2,1)}, bf16[1280,1280]{1,0:T(8,128)(2,1)}, u32[]{:S(2)}, u32[]{:S(2)}) %collective-permute-start.29) | collective-permute-done | bytes 3276832 | tf_op jit(solution)/shard_map/ppermute | solution.py:214
  547.7 3.8 collective-permute-start.34
  554.5 14.4 %send_products.16 = (bf16[3,320,1280]{2,1,0:T(8,128)(2,1)}, bf16[3,320,1280]{2,1,0:T(8,128)(2,1)}) custom-call(s32[4]{0:T(128)} %broadcast_xor_fusion.where_ref, bf16[4,2,640,1280]{3,2,1,0:T(8,128)(2,1)} %refs_0_.39, bf16[2,640,1280]{2,1,0:T(8,128)(2,1)} %bitcast.59, bf16[4,2,640,1280]{3,2,1,0:T(8,128)(2,1)} %refs_0_.39, ...), custom_call_target="tpu_custom_call" | custom-call | flops 1048576 | bytes 65536 | tf_op jit(solution)/shard_map/send_products/pallas_call | solution.py:70
  579.9 15.2 %keep_products.16 = (bf16[3,320,1280]{2,1,0:T(8,128)(2,1)}, bf16[3,320,1280]{2,1,0:T(8,128)(2,1)}) custom-call(s32[4]{0:T(128)} %broadcast_xor_fusion.where_ref, bf16[4,2,640,1280]{3,2,1,0:T(8,128)(2,1)} %refs_0_.39, bf16[2,640,1280]{2,1,0:T(8,128)(2,1)} %bitcast.60, bf16[4,2,640,1280]{3,2,1,0:T(8,128)(2,1)} %refs_0_.39, ...), custom_call_target="tpu_custom_call" | custom-call | flops 1048576 | bytes 65536 | tf_op jit(solution)/shard_map/keep_products/pallas_call | solution.py:97
  595.1 16.1 %collective-permute-done.38 = bf16[2,320,1280]{2,1,0:T(8,128)(2,1)} collective-permute-done((bf16[2,320,1280]{2,1,0:T(8,128)(2,1)}, bf16[2,320,1280]{2,1,0:T(8,128)(2,1)}, u32[]{:S(2)}, u32[]{:S(2)}) %collective-permute-start.38) | collective-permute-done | bytes 1638432 | tf_op jit(solution)/shard_map/ppermute | solution.py:187
  611.2 9.2 %collective-permute-done.34.refs_3_ = bf16[1280,1280]{1,0:T(8,128)(2,1)S(1)} collective-permute-done((bf16[1280,1280]{1,0:T(8,128)(2,1)}, bf16[1280,1280]{1,0:T(8,128)(2,1)S(1)}, u32[]{:S(2)}, u32[]{:S(2)}) %collective-permute-start.34) | collective-permute-done | bytes 3276832 | tf_op jit(solution)/shard_map/ppermute | solution.py:214
  630.8 3.9 fusion.2
  639.9 14.4 %send_products.17 = (bf16[3,320,1280]{2,1,0:T(8,128)(2,1)}, bf16[3,320,1280]{2,1,0:T(8,128)(2,1)}) custom-call(s32[4]{0:T(128)} %broadcast_xor_fusion.where_ref, bf16[4,2,640,1280]{3,2,1,0:T(8,128)(2,1)} %refs_0_.39, bf16[2,640,1280]{2,1,0:T(8,128)(2,1)} %bitcast.67, bf16[4,2,640,1280]{3,2,1,0:T(8,128)(2,1)} %refs_0_.39, bf16[1280,1280]{1,0:T(8,128)(2,1)} %copy-done.7, ...), custom_call_target="tpu_custom_call" | custom-call | flops 1048576 | bytes 65536 | tf_op jit(solution)/shard_map/send_products/pallas_call | solution.py:70
  658.3 3.8 collective-permute-done.42
  665.3 15.2 %keep_products.17 = (bf16[3,320,1280]{2,1,0:T(8,128)(2,1)}, bf16[3,320,1280]{2,1,0:T(8,128)(2,1)}) custom-call(s32[4]{0:T(128)} %broadcast_xor_fusion.where_ref, bf16[4,2,640,1280]{3,2,1,0:T(8,128)(2,1)} %refs_0_.39, bf16[2,640,1280]{2,1,0:T(8,128)(2,1)} %bitcast.68, bf16[4,2,640,1280]{3,2,1,0:T(8,128)(2,1)} %refs_0_.39, bf16[1280,1280]{1,0:T(8,128)(2,1)} %copy-done.7, ...), custom_call_target="tpu_custom_call" | custom-call | flops 1048576 | bytes 65536 | tf_op jit(solution)/shard_map/keep_products/pallas_call | solution.py:97
  680.5 15.7 %collective-permute-done.43.refs_4_.refs_7_ = bf16[4,160,1280]{2,1,0:T(8,128)(2,1)S(1)} collective-permute-done((bf16[4,160,1280]{2,1,0:T(8,128)(2,1)}, bf16[4,160,1280]{2,1,0:T(8,128)(2,1)S(1)}, u32[]{:S(2)}, u32[]{:S(2)}) %collective-permute-start.43) | collective-permute-done | bytes 1638432 | tf_op jit(solution)/shard_map/ppermute | solution.py:219
  706.3 7.7 send_products.18
  721.7 4.5 collective-permute-start.49
  727.4 8.1 keep_products.18
  735.5 7.6 collective-permute-done.49
  743.1 11.3 %collective-permute-done.48.refs_2_ = bf16[1280,640]{1,0:T(8,128)(2,1)} collective-permute-done((bf16[1280,640]{1,0:T(8,128)(2,1)}, bf16[1280,640]{1,0:T(8,128)(2,1)}, u32[]{:S(2)}, u32[]{:S(2)}) %collective-permute-start.48) | collective-permute-done | bytes 1638432 | tf_op jit(solution)/shard_map/ppermute | solution.py:214
  764.9 7.6 send_products.19
  774.5 5.2 collective-permute-start.62
  784.2 8.1 keep_products.19
  802.3 6.8 place.4.refs_8_
  809.1 7.0 place.5.refs_8_
  822.1 10.7 %collective-permute-done.56 = bf16[4,160,1280]{2,1,0:T(8,128)(2,1)} collective-permute-done((bf16[4,160,1280]{2,1,0:T(8,128)(2,1)}, bf16[4,160,1280]{2,1,0:T(8,128)(2,1)}, u32[]{:S(2)}, u32[]{:S(2)}) %collective-permute-start.56) | collective-permute-done | bytes 1638432 | tf_op jit(solution)/shard_map/ppermute | solution.py:245
  841.0 6.8 place.6.refs_8_
  847.8 6.8 place.7
  (248 shorter events, 184.5 us)
Async XLA Ops:
  7.2 454.6 %reduce-scatter.2.cloned.1.call-start = ((), (), s32[]{:S(2)}) async-start(), calls=%async_computation.1 | async-start | bytes 2359296 | tf_op jit(solution)/shard_map/reduce_scatter | solution.py:281
  7.2 39.2 %collective-permute-start = (bf16[128,6656]{1,0:T(8,128)(2,1)}, bf16[128,6656]{1,0:T(8,128)(2,1)S(1)}, u32[]{:S(2)}, u32[]{:S(2)}) collective-permute-start(bf16[128,6656]{1,0:T(8,128)(2,1)} %param.5), channel_id=1, source_target_pairs={{0,8},{8,0},{16,24},{24,16},{1,9},{9,1},{17,25},{25,17},{2,10},{10... | collective-permute-start | bytes 5111816 | tf_op jit(solution)/shard_map/ppermute | solution.py:214
  7.7 41.7 %collective-permute-start.1 = (bf16[128,6656]{1,0:T(8,128)(2,1)}, bf16[128,6656]{1,0:T(8,128)(2,1)S(1)}, u32[]{:S(2)}, u32[]{:S(2)}) collective-permute-start(bf16[128,6656]{1,0:T(8,128)(2,1)} %param.5), channel_id=1, source_target_pairs={{8,16},{16,8},{9,17},{17,9},{10,18},{18,10},{11,19},{19,11},{12,20... | collective-permute-start | bytes 5111816 | tf_op jit(solution)/shard_map/ppermute | solution.py:214
  49.5 37.1 %collective-permute-start.2 = (bf16[128,6656]{1,0:T(8,128)(2,1)S(1)}, bf16[128,6656]{1,0:T(8,128)(2,1)S(1)}, u32[]{:S(2)}, u32[]{:S(2)}) collective-permute-start(bf16[128,6656]{1,0:T(8,128)(2,1)S(1)} %collective-permute-done.1), channel_id=1, source_target_pairs={{8,0},{16,24},{9,1},{17,25},{10,2},{18,26},{11,3},{19,27},{12,4},{... | collective-permute-start | bytes 5111816 | tf_op jit(solution)/shard_map/ppermute | solution.py:214
  50.9 40.0 %collective-permute-start.3 = (bf16[128,6656]{1,0:T(8,128)(2,1)S(1)}, bf16[128,6656]{1,0:T(8,128)(2,1)S(1)}, u32[]{:S(2)}, u32[]{:S(2)}) collective-permute-start(bf16[128,6656]{1,0:T(8,128)(2,1)S(1)} %collective-permute-done), channel_id=1, source_target_pairs={{8,16},{16,8},{9,17},{17,9},{10,18},{18,10},{11,19},{19,11},{12,20... | collective-permute-start | bytes 5111816 | tf_op jit(solution)/shard_map/ppermute | solution.py:214
  95.4 72.9 %collective-permute-start.7 = (bf16[2,640,1280]{2,1,0:T(8,128)(2,1)}, bf16[2,640,1280]{2,1,0:T(8,128)(2,1)S(1)}, u32[]{:S(2)}, u32[]{:S(2)}) collective-permute-start(bf16[2,640,1280]{2,1,0:T(8,128)(2,1)} %slice_bitcast_fusion), channel_id=1, source_target_pairs={{0,8},{24,16},{1,9},{25,17},{2,10},{26,18},{3,11},{27,19},{4,12},{... | collective-permute-start | bytes 9830408 | tf_op jit(solution)/shard_map/ppermute | solution.py:214
  96.6 73.1 %collective-permute-start.6 = (bf16[1280,1280]{1,0:T(8,128)(2,1)}, bf16[1280,1280]{1,0:T(8,128)(2,1)}, u32[]{:S(2)}, u32[]{:S(2)}) collective-permute-start(bf16[1280,1280]{1,0:T(8,128)(2,1)} %bitcast.44.refs_4_), channel_id=1, source_target_pairs={{8,16},{16,8},{9,17},{17,9},{10,18},{18,10},{11,19},{19,11},{12,20... | collective-permute-start | bytes 9830408 | tf_op jit(solution)/shard_map/ppermute | solution.py:214
  115.9 6.0 collective-permute-start.4
  115.9 8.5 collective-permute-start.5
  116.4 40.8 %collective-permute-start.8 = (bf16[128,6656]{1,0:T(8,128)(2,1)}, bf16[128,6656]{1,0:T(8,128)(2,1)}, u32[]{:S(2)}, u32[]{:S(2)}) collective-permute-start(bf16[128,6656]{1,0:T(8,128)(2,1)} %copy-done.38), channel_id=1, source_target_pairs={{8,0},{16,24},{9,1},{17,25},{10,2},{18,26},{11,3},{19,27},{12,4},{... | collective-permute-start | bytes 5111816 | tf_op jit(solution)/shard_map/ppermute | solution.py:214
  169.7 70.2 %collective-permute-start.12 = (bf16[1280,1280]{1,0:T(8,128)(2,1)}, bf16[1280,1280]{1,0:T(8,128)(2,1)}, u32[]{:S(2)}, u32[]{:S(2)}) collective-permute-start(bf16[1280,1280]{1,0:T(8,128)(2,1)} %bitcast.71), channel_id=1, source_target_pairs={{0,8},{8,0},{16,24},{24,16},{1,9},{9,1},{17,25},{25,17},{2,10},{10... | collective-permute-start | bytes 9830408 | tf_op jit(solution)/shard_map/ppermute | solution.py:214
  169.7 72.4 %collective-permute-start.11 = (bf16[1280,1280]{1,0:T(8,128)(2,1)}, bf16[1280,1280]{1,0:T(8,128)(2,1)}, u32[]{:S(2)}, u32[]{:S(2)}) collective-permute-start(bf16[1280,1280]{1,0:T(8,128)(2,1)} %bitcast.72), channel_id=1, source_target_pairs={{8,16},{16,8},{9,17},{17,9},{10,18},{18,10},{11,19},{19,11},{12,20... | collective-permute-start | bytes 9830408 | tf_op jit(solution)/shard_map/ppermute | solution.py:214
  177.2 52.2 %collective-permute-start.13 = (bf16[3,320,1280]{2,1,0:T(8,128)(2,1)}, bf16[3,320,1280]{2,1,0:T(8,128)(2,1)}, u32[]{:S(2)}, u32[]{:S(2)}) collective-permute-start(bf16[3,320,1280]{2,1,0:T(8,128)(2,1)} %get-tuple-element.184), channel_id=1, source_target_pairs={{0,2},{2,0},{1,3},{3,1},{4,6},{6,4},{5,7},{7,5},{8,10},{10,8},{9,1... | collective-permute-start | bytes 7372808 | tf_op jit(solution)/shard_map/ppermute | solution.py:187
  209.2 3.8 collective-permute-start.9
  209.2 6.2 collective-permute-start.10
  246.1 69.3 %collective-permute-start.14 = (bf16[1280,1280]{1,0:T(8,128)(2,1)}, bf16[1280,1280]{1,0:T(8,128)(2,1)}, u32[]{:S(2)}, u32[]{:S(2)}) collective-permute-start(bf16[1280,1280]{1,0:T(8,128)(2,1)} %broadcast_select_fusion.4), channel_id=1, source_target_pairs={{0,8},{8,0},{16,24},{24,16},{1,9},{9,1},{17,25},{25,17},{2,10},{10... | collective-permute-start | bytes 9830408 | tf_op jit(solution)/shard_map/ppermute | solution.py:214
  246.1 71.2 %collective-permute-start.17 = (bf16[1280,1280]{1,0:T(8,128)(2,1)}, bf16[1280,1280]{1,0:T(8,128)(2,1)}, u32[]{:S(2)}, u32[]{:S(2)}) collective-permute-start(bf16[1280,1280]{1,0:T(8,128)(2,1)} %collective-permute-done.12.refs_3_), channel_id=1, source_target_pairs={{8,16},{16,8},{9,17},{17,9},{10,18},{18,10},{11,19},{19,11},{12,20... | collective-permute-start | bytes 9830408 | tf_op jit(solution)/shard_map/ppermute | solution.py:214
  263.4 5.9 collective-permute-start.15
  263.4 8.5 collective-permute-start.16
  263.9 38.1 %collective-permute-start.18 = (bf16[2,320,1280]{2,1,0:T(8,128)(2,1)}, bf16[2,320,1280]{2,1,0:T(8,128)(2,1)}, u32[]{:S(2)}, u32[]{:S(2)}) collective-permute-start(bf16[2,320,1280]{2,1,0:T(8,128)(2,1)} %get-tuple-element.195), channel_id=1, source_target_pairs={{0,2},{2,0},{1,3},{3,1},{4,6},{6,4},{5,7},{7,5},{8,10},{10,8},{9,1... | collective-permute-start | bytes 4915208 | tf_op jit(solution)/shard_map/ppermute | solution.py:187
  321.3 70.3 %collective-permute-start.21 = (bf16[1280,1280]{1,0:T(8,128)(2,1)}, bf16[1280,1280]{1,0:T(8,128)(2,1)}, u32[]{:S(2)}, u32[]{:S(2)}) collective-permute-start(bf16[1280,1280]{1,0:T(8,128)(2,1)} %collective-permute-done.14.refs_2_), channel_id=1, source_target_pairs={{8,16},{16,8},{9,17},{17,9},{10,18},{18,10},{11,19},{19,11},{12,20... | collective-permute-start | bytes 9830408 | tf_op jit(solution)/shard_map/ppermute | solution.py:214
  323.9 67.9 %collective-permute-start.22 = (bf16[1280,1280]{1,0:T(8,128)(2,1)}, bf16[1280,1280]{1,0:T(8,128)(2,1)S(1)}, u32[]{:S(2)}, u32[]{:S(2)}) collective-permute-start(bf16[1280,1280]{1,0:T(8,128)(2,1)} %broadcast_select_fusion.2), channel_id=1, source_target_pairs={{0,8},{8,0},{16,24},{24,16},{1,9},{9,1},{17,25},{25,17},{2,10},{10... | collective-permute-start | bytes 9830408 | tf_op jit(solution)/shard_map/ppermute | solution.py:214
  324.0 50.5 %collective-permute-start.23 = (bf16[3,320,1280]{2,1,0:T(8,128)(2,1)}, bf16[3,320,1280]{2,1,0:T(8,128)(2,1)}, u32[]{:S(2)}, u32[]{:S(2)}) collective-permute-start(bf16[3,320,1280]{2,1,0:T(8,128)(2,1)} %get-tuple-element.206), channel_id=1, source_target_pairs={{0,2},{2,0},{1,3},{3,1},{4,6},{6,4},{5,7},{7,5},{8,10},{10,8},{9,1... | collective-permute-start | bytes 7372808 | tf_op jit(solution)/shard_map/ppermute | solution.py:187
  340.6 9.8 %collective-permute-start.19 = (bf16[2,320,1280]{2,1,0:T(8,128)(2,1)}, bf16[2,320,1280]{2,1,0:T(8,128)(2,1)}, u32[]{:S(2)}, u32[]{:S(2)}) collective-permute-start(bf16[2,320,1280]{2,1,0:T(8,128)(2,1)} %get-tuple-element.198), channel_id=1, source_target_pairs={{0,1},{1,0},{2,3},{3,2},{4,5},{5,4},{6,7},{7,6},{8,9},{9,8},{10,11... | collective-permute-start | bytes 4915208 | tf_op jit(solution)/shard_map/ppermute | solution.py:179
  340.6 9.8 %collective-permute-start.20 = (bf16[2,320,1280]{2,1,0:T(8,128)(2,1)}, bf16[2,320,1280]{2,1,0:T(8,128)(2,1)}, u32[]{:S(2)}, u32[]{:S(2)}) collective-permute-start(bf16[2,320,1280]{2,1,0:T(8,128)(2,1)} %get-tuple-element.199), channel_id=1, source_target_pairs={{0,1},{1,0},{2,3},{3,2},{4,5},{5,4},{6,7},{7,6},{8,9},{9,8},{10,11... | collective-permute-start | bytes 4915208 | tf_op jit(solution)/shard_map/ppermute | solution.py:179
  404.7 68.3 %collective-permute-start.24 = (bf16[1280,1280]{1,0:T(8,128)(2,1)}, bf16[1280,1280]{1,0:T(8,128)(2,1)S(1)}, u32[]{:S(2)}, u32[]{:S(2)}) collective-permute-start(bf16[1280,1280]{1,0:T(8,128)(2,1)} %get-tuple-element.213), channel_id=1, source_target_pairs={{0,8},{8,0},{16,24},{24,16},{1,9},{9,1},{17,25},{25,17},{2,10},{10... | collective-permute-start | bytes 9830408 | tf_op jit(solution)/shard_map/ppermute | solution.py:214
  404.7 69.2 %collective-permute-start.27 = (bf16[1280,1280]{1,0:T(8,128)(2,1)}, bf16[1280,1280]{1,0:T(8,128)(2,1)}, u32[]{:S(2)}, u32[]{:S(2)}) collective-permute-start(bf16[1280,1280]{1,0:T(8,128)(2,1)} %bitcast.50.refs_4_), channel_id=1, source_target_pairs={{8,16},{16,8},{9,17},{17,9},{10,18},{18,10},{11,19},{19,11},{12,20... | collective-permute-start | bytes 9830408 | tf_op jit(solution)/shard_map/ppermute | solution.py:214
  425.9 5.0 collective-permute-start.25
  425.9 8.5 collective-permute-start.26
  426.4 46.5 %collective-permute-start.28 = (bf16[2,320,1280]{2,1,0:T(8,128)(2,1)}, bf16[2,320,1280]{2,1,0:T(8,128)(2,1)}, u32[]{:S(2)}, u32[]{:S(2)}) collective-permute-start(bf16[2,320,1280]{2,1,0:T(8,128)(2,1)} %get-tuple-element.223), channel_id=1, source_target_pairs={{0,2},{2,0},{1,3},{3,1},{4,6},{6,4},{5,7},{7,5},{8,10},{10,8},{9,1... | collective-permute-start | bytes 4915208 | tf_op jit(solution)/shard_map/ppermute | solution.py:187
  473.9 71.5 %collective-permute-start.29 = (bf16[1280,1280]{1,0:T(8,128)(2,1)}, bf16[1280,1280]{1,0:T(8,128)(2,1)}, u32[]{:S(2)}, u32[]{:S(2)}) collective-permute-start(bf16[1280,1280]{1,0:T(8,128)(2,1)} %bitcast.50.refs_4_), channel_id=1, source_target_pairs={{0,8},{8,0},{16,24},{24,16},{1,9},{9,1},{17,25},{25,17},{2,10},{10... | collective-permute-start | bytes 9830408 | tf_op jit(solution)/shard_map/ppermute | solution.py:214
  473.9 73.8 %collective-permute-start.32 = (bf16[1280,1280]{1,0:T(8,128)(2,1)}, bf16[1280,1280]{1,0:T(8,128)(2,1)}, u32[]{:S(2)}, u32[]{:S(2)}) collective-permute-start(bf16[1280,1280]{1,0:T(8,128)(2,1)} %bitcast.53.refs_5_), channel_id=1, source_target_pairs={{8,16},{16,8},{9,17},{17,9},{10,18},{18,10},{11,19},{19,11},{12,20... | collective-permute-start | bytes 9830408 | tf_op jit(solution)/shard_map/ppermute | solution.py:214
  478.0 54.1 %collective-permute-start.33 = (bf16[3,320,1280]{2,1,0:T(8,128)(2,1)}, bf16[3,320,1280]{2,1,0:T(8,128)(2,1)}, u32[]{:S(2)}, u32[]{:S(2)}) collective-permute-start(bf16[3,320,1280]{2,1,0:T(8,128)(2,1)} %get-tuple-element.232), channel_id=1, source_target_pairs={{0,2},{2,0},{1,3},{3,1},{4,6},{6,4},{5,7},{7,5},{8,10},{10,8},{9,1... | collective-permute-start | bytes 7372808 | tf_op jit(solution)/shard_map/ppermute | solution.py:187
  489.7 5.0 collective-permute-start.30
  489.7 6.0 collective-permute-start.31
  547.7 72.8 %collective-permute-start.34 = (bf16[1280,1280]{1,0:T(8,128)(2,1)}, bf16[1280,1280]{1,0:T(8,128)(2,1)S(1)}, u32[]{:S(2)}, u32[]{:S(2)}) collective-permute-start(bf16[1280,1280]{1,0:T(8,128)(2,1)} %collective-permute-done.29.refs_4_), channel_id=1, source_target_pairs={{8,16},{16,8},{9,17},{17,9},{10,18},{18,10},{11,19},{19,11},{12,20... | collective-permute-start | bytes 9830408 | tf_op jit(solution)/shard_map/ppermute | solution.py:214
  551.5 70.8 %collective-permute-start.37 = (bf16[1280,1280]{1,0:T(8,128)(2,1)}, bf16[1280,1280]{1,0:T(8,128)(2,1)}, u32[]{:S(2)}, u32[]{:S(2)}) collective-permute-start(bf16[1280,1280]{1,0:T(8,128)(2,1)} %bitcast.53.refs_5_), channel_id=1, source_target_pairs={{0,8},{8,0},{16,24},{24,16},{1,9},{9,1},{17,25},{25,17},{2,10},{10... | collective-permute-start | bytes 9830408 | tf_op jit(solution)/shard_map/ppermute | solution.py:214
  568.9 10.9 %collective-permute-start.35 = (bf16[3,320,1280]{2,1,0:T(8,128)(2,1)}, bf16[3,320,1280]{2,1,0:T(8,128)(2,1)}, u32[]{:S(2)}, u32[]{:S(2)}) collective-permute-start(bf16[3,320,1280]{2,1,0:T(8,128)(2,1)} %get-tuple-element.235), channel_id=1, source_target_pairs={{0,1},{1,0},{2,3},{3,2},{4,5},{5,4},{6,7},{7,6},{8,9},{9,8},{10,11... | collective-permute-start | bytes 7372808 | tf_op jit(solution)/shard_map/ppermute | solution.py:179
  568.9 10.9 %collective-permute-start.36 = (bf16[3,320,1280]{2,1,0:T(8,128)(2,1)}, bf16[3,320,1280]{2,1,0:T(8,128)(2,1)}, u32[]{:S(2)}, u32[]{:S(2)}) collective-permute-start(bf16[3,320,1280]{2,1,0:T(8,128)(2,1)} %get-tuple-element.236), channel_id=1, source_target_pairs={{0,1},{1,0},{2,3},{3,2},{4,5},{5,4},{6,7},{7,6},{8,9},{9,8},{10,11... | collective-permute-start | bytes 7372808 | tf_op jit(solution)/shard_map/ppermute | solution.py:179
  573.1 38.1 %collective-permute-start.38 = (bf16[2,320,1280]{2,1,0:T(8,128)(2,1)}, bf16[2,320,1280]{2,1,0:T(8,128)(2,1)}, u32[]{:S(2)}, u32[]{:S(2)}) collective-permute-start(bf16[2,320,1280]{2,1,0:T(8,128)(2,1)} %get-tuple-element.241), channel_id=1, source_target_pairs={{0,2},{2,0},{1,3},{3,1},{4,6},{6,4},{5,7},{7,5},{8,10},{10,8},{9,1... | collective-permute-start | bytes 4915208 | tf_op jit(solution)/shard_map/ppermute | solution.py:187
  627.3 34.8 %collective-permute-start.42 = (bf16[4,160,1280]{2,1,0:T(8,128)(2,1)}, bf16[4,160,1280]{2,1,0:T(8,128)(2,1)}, u32[]{:S(2)}, u32[]{:S(2)}) collective-permute-start(bf16[4,160,1280]{2,1,0:T(8,128)(2,1)} %pad_maximum_fusion.4), channel_id=1, source_target_pairs={{8,0},{16,24},{9,1},{17,25},{10,2},{18,26},{11,3},{19,27},{12,4},{... | collective-permute-start | bytes 4915208 | tf_op jit(solution)/shard_map/ppermute | solution.py:214
  635.7 44.8 %collective-permute-start.41 = (bf16[1280,640]{1,0:T(8,128)(2,1)}, bf16[1280,640]{1,0:T(8,128)(2,1)S(1)}, u32[]{:S(2)}, u32[]{:S(2)}) collective-permute-start(bf16[1280,640]{1,0:T(8,128)(2,1)} %get-tuple-element.249), channel_id=1, source_target_pairs={{8,16},{16,8},{9,17},{17,9},{10,18},{18,10},{11,19},{19,11},{12,20... | collective-permute-start | bytes 4915208 | tf_op jit(solution)/shard_map/ppermute | solution.py:214
  638.2 58.0 %collective-permute-start.44 = (bf16[3,320,1280]{2,1,0:T(8,128)(2,1)}, bf16[3,320,1280]{2,1,0:T(8,128)(2,1)}, u32[]{:S(2)}, u32[]{:S(2)}) collective-permute-start(bf16[3,320,1280]{2,1,0:T(8,128)(2,1)} %get-tuple-element.265), channel_id=1, source_target_pairs={{0,2},{2,0},{1,3},{3,1},{4,6},{6,4},{5,7},{7,5},{8,10},{10,8},{9,1... | collective-permute-start | bytes 7372808 | tf_op jit(solution)/shard_map/ppermute | solution.py:187
  654.3 11.0 %collective-permute-start.39 = (bf16[3,320,1280]{2,1,0:T(8,128)(2,1)}, bf16[3,320,1280]{2,1,0:T(8,128)(2,1)}, u32[]{:S(2)}, u32[]{:S(2)}) collective-permute-start(bf16[3,320,1280]{2,1,0:T(8,128)(2,1)} %get-tuple-element.244), channel_id=1, source_target_pairs={{0,1},{1,0},{2,3},{3,2},{4,5},{5,4},{6,7},{7,6},{8,9},{9,8},{10,11... | collective-permute-start | bytes 7372808 | tf_op jit(solution)/shard_map/ppermute | solution.py:179
  654.4 10.9 %collective-permute-start.40 = (bf16[3,320,1280]{2,1,0:T(8,128)(2,1)}, bf16[3,320,1280]{2,1,0:T(8,128)(2,1)}, u32[]{:S(2)}, u32[]{:S(2)}) collective-permute-start(bf16[3,320,1280]{2,1,0:T(8,128)(2,1)} %get-tuple-element.245), channel_id=1, source_target_pairs={{0,1},{1,0},{2,3},{3,2},{4,5},{5,4},{6,7},{7,6},{8,9},{9,8},{10,11... | collective-permute-start | bytes 7372808 | tf_op jit(solution)/shard_map/ppermute | solution.py:179
  662.1 34.2 %collective-permute-start.43 = (bf16[4,160,1280]{2,1,0:T(8,128)(2,1)}, bf16[4,160,1280]{2,1,0:T(8,128)(2,1)S(1)}, u32[]{:S(2)}, u32[]{:S(2)}) collective-permute-start(bf16[4,160,1280]{2,1,0:T(8,128)(2,1)} %pad_maximum_fusion.5), channel_id=1, source_target_pairs={{0,4},{4,0},{1,5},{5,1},{2,6},{6,2},{3,7},{7,3},{8,12},{12,8},{9,1... | collective-permute-start | bytes 4915208 | tf_op jit(solution)/shard_map/ppermute | solution.py:219
  704.5 50.8 %collective-permute-start.50 = (bf16[6,160,1280]{2,1,0:T(8,128)(2,1)}, bf16[6,160,1280]{2,1,0:T(8,128)(2,1)S(1)}, u32[]{:S(2)}, u32[]{:S(2)}) collective-permute-start(bf16[6,160,1280]{2,1,0:T(8,128)(2,1)} %pad_maximum_fusion.2), channel_id=1, source_target_pairs={{0,4},{4,0},{1,5},{5,1},{2,6},{6,2},{3,7},{7,3},{8,12},{12,8},{9,1... | collective-permute-start | bytes 7372808 | tf_op jit(solution)/shard_map/ppermute | solution.py:219
  705.0 50.6 %collective-permute-start.45 = (bf16[3,320,1280]{2,1,0:T(8,128)(2,1)}, bf16[3,320,1280]{2,1,0:T(8,128)(2,1)}, u32[]{:S(2)}, u32[]{:S(2)}) collective-permute-start(bf16[3,320,1280]{2,1,0:T(8,128)(2,1)} %get-tuple-element.275), channel_id=1, source_target_pairs={{0,2},{2,0},{1,3},{3,1},{4,6},{6,4},{5,7},{7,5},{8,10},{10,8},{9,1... | collective-permute-start | bytes 7372808 | tf_op jit(solution)/shard_map/ppermute | solution.py:187
  714.0 7.7 collective-permute-start.46
  714.0 13.4 %collective-permute-start.47 = (bf16[2,320,640]{2,1,0:T(8,128)(2,1)}, bf16[2,320,640]{2,1,0:T(8,128)(2,1)}, u32[]{:S(2)}, u32[]{:S(2)}) collective-permute-start(bf16[2,320,640]{2,1,0:T(8,128)(2,1)} %get-tuple-element.278), channel_id=1, source_target_pairs={{0,1},{1,0},{2,3},{3,2},{4,5},{5,4},{6,7},{7,6},{8,9},{9,8},{10,11... | collective-permute-start | bytes 2457608 | tf_op jit(solution)/shard_map/ppermute | solution.py:179
  714.5 39.9 %collective-permute-start.48 = (bf16[1280,640]{1,0:T(8,128)(2,1)}, bf16[1280,640]{1,0:T(8,128)(2,1)}, u32[]{:S(2)}, u32[]{:S(2)}) collective-permute-start(bf16[1280,640]{1,0:T(8,128)(2,1)} %get-tuple-element.282), channel_id=1, source_target_pairs={{8,16},{16,8},{9,17},{17,9},{10,18},{18,10},{11,19},{19,11},{12,20... | collective-permute-start | bytes 4915208 | tf_op jit(solution)/shard_map/ppermute | solution.py:214
  721.7 21.3 %collective-permute-start.49 = (bf16[2,160,1280]{2,1,0:T(8,128)(2,1)}, bf16[2,160,1280]{2,1,0:T(8,128)(2,1)}, u32[]{:S(2)}, u32[]{:S(2)}) collective-permute-start(bf16[2,160,1280]{2,1,0:T(8,128)(2,1)} %bitcast.27), channel_id=1, source_target_pairs={{8,0},{16,24},{9,1},{17,25},{10,2},{18,26},{11,3},{19,27},{12,4},{... | collective-permute-start | bytes 2457608 | tf_op jit(solution)/shard_map/ppermute | solution.py:214
  762.2 58.0 %collective-permute-start.57 = (bf16[2,160,1280]{2,1,0:T(8,128)(2,1)}, bf16[2,160,1280]{2,1,0:T(8,128)(2,1)}, u32[]{:S(2)}, u32[]{:S(2)}) collective-permute-start(bf16[2,160,1280]{2,1,0:T(8,128)(2,1)} %bitcast.33), channel_id=1, source_target_pairs={{8,4},{16,28},{9,5},{17,29},{10,6},{18,30},{11,7},{19,31}} | collective-permute-start | bytes 2457608 | tf_op jit(solution)/shard_map/ppermute | solution.py:239
  763.8 31.0 %collective-permute-start.59 = (bf16[2,320,640]{2,1,0:T(8,128)(2,1)}, bf16[2,320,640]{2,1,0:T(8,128)(2,1)}, u32[]{:S(2)}, u32[]{:S(2)}) collective-permute-start(bf16[2,320,640]{2,1,0:T(8,128)(2,1)} %get-tuple-element.306), channel_id=1, source_target_pairs={{0,2},{2,0},{1,3},{3,1},{4,6},{6,4},{5,7},{7,5},{8,10},{10,8},{9,1... | collective-permute-start | bytes 2457608 | tf_op jit(solution)/shard_map/ppermute | solution.py:187
  772.6 8.4 collective-permute-start.52
  772.6 11.6 %collective-permute-start.53 = (bf16[2,320,640]{2,1,0:T(8,128)(2,1)}, bf16[2,320,640]{2,1,0:T(8,128)(2,1)}, u32[]{:S(2)}, u32[]{:S(2)}) collective-permute-start(bf16[2,320,640]{2,1,0:T(8,128)(2,1)} %get-tuple-element.295), channel_id=1, source_target_pairs={{0,1},{1,0},{2,3},{3,2},{4,5},{5,4},{6,7},{7,6},{8,9},{9,8},{10,11... | collective-permute-start | bytes 2457608 | tf_op jit(solution)/shard_map/ppermute | solution.py:179
  774.5 26.4 %collective-permute-start.62 = (bf16[2,160,1280]{2,1,0:T(8,128)(2,1)}, bf16[2,160,1280]{2,1,0:T(8,128)(2,1)S(1)}, u32[]{:S(2)}, u32[]{:S(2)}) collective-permute-start(bf16[2,160,1280]{2,1,0:T(8,128)(2,1)} %get-tuple-element.344), channel_id=1, source_target_pairs={{0,4},{4,0},{1,5},{5,1},{2,6},{6,2},{3,7},{7,3},{8,12},{12,8},{9,1... | collective-permute-start | bytes 2457608 | tf_op jit(solution)/shard_map/ppermute | solution.py:219
  781.0 51.8 %collective-permute-start.56 = (bf16[4,160,1280]{2,1,0:T(8,128)(2,1)}, bf16[4,160,1280]{2,1,0:T(8,128)(2,1)}, u32[]{:S(2)}, u32[]{:S(2)}) collective-permute-start(bf16[4,160,1280]{2,1,0:T(8,128)(2,1)} %pad_maximum_fusion.6), channel_id=1, source_target_pairs={{4,0},{5,1},{6,2},{7,3},{12,8},{13,9},{14,10},{15,11},{20,16},{21,... | collective-permute-start | bytes 4915208 | tf_op jit(solution)/shard_map/ppermute | solution.py:245
  792.3 23.8 %collective-permute-start.54 = (bf16[2,320,640]{2,1,0:T(8,128)(2,1)}, bf16[2,320,640]{2,1,0:T(8,128)(2,1)}, u32[]{:S(2)}, u32[]{:S(2)}) collective-permute-start(bf16[2,320,640]{2,1,0:T(8,128)(2,1)} %get-tuple-element.300), channel_id=1, source_target_pairs={{0,2},{2,0},{1,3},{3,1},{4,6},{6,4},{5,7},{7,5},{8,10},{10,8},{9,1... | collective-permute-start | bytes 2457608 | tf_op jit(solution)/shard_map/ppermute | solution.py:187
  794.9 24.6 %collective-permute-start.51 = (bf16[2,160,1280]{2,1,0:T(8,128)(2,1)}, bf16[2,160,1280]{2,1,0:T(8,128)(2,1)}, u32[]{:S(2)}, u32[]{:S(2)}) collective-permute-start(bf16[2,160,1280]{2,1,0:T(8,128)(2,1)} %broadcast_select_fusion.18), channel_id=1, source_target_pairs={{8,12},{16,20},{12,4},{20,28},{9,13},{17,21},{13,5},{21,29},{10,14... | collective-permute-start | bytes 2457608 | tf_op jit(solution)/shard_map/ppermute | solution.py:238
  800.8 34.7 %collective-permute-start.61 = (bf16[2,160,640]{2,1,0:T(8,128)(2,1)}, bf16[2,160,640]{2,1,0:T(8,128)(2,1)}, u32[]{:S(2)}, u32[]{:S(2)}) collective-permute-start(bf16[2,160,640]{2,1,0:T(8,128)(2,1)} %bitcast.38), channel_id=1, source_target_pairs={{8,4},{16,28},{9,5},{17,29},{10,6},{18,30},{11,7},{19,31}} | collective-permute-start | bytes 1228808 | tf_op jit(solution)/shard_map/ppermute | solution.py:239
  816.0 19.5 %collective-permute-start.60 = (bf16[2,160,640]{2,1,0:T(8,128)(2,1)}, bf16[2,160,640]{2,1,0:T(8,128)(2,1)S(1)}, u32[]{:S(2)}, u32[]{:S(2)}) collective-permute-start(bf16[2,160,640]{2,1,0:T(8,128)(2,1)} %broadcast_select_fusion.25), channel_id=1, source_target_pairs={{8,12},{16,20},{12,4},{20,28},{9,13},{17,21},{13,5},{21,29},{10,14... | collective-permute-start | bytes 1228808 | tf_op jit(solution)/shard_map/ppermute | solution.py:238
  819.5 19.1 %collective-permute-start.58 = (bf16[2,160,640]{2,1,0:T(8,128)(2,1)S(1)}, bf16[2,160,640]{2,1,0:T(8,128)(2,1)S(1)}, u32[]{:S(2)}, u32[]{:S(2)}) collective-permute-start(bf16[2,160,640]{2,1,0:T(8,128)(2,1)S(1)} %bitcast.109), channel_id=1, source_target_pairs={{8,4},{16,28},{9,5},{17,29},{10,6},{18,30},{11,7},{19,31}} | collective-permute-start | bytes 1228808 | tf_op jit(solution)/shard_map/ppermute | solution.py:239
  820.2 18.3 %collective-permute-start.55 = (bf16[2,160,640]{2,1,0:T(8,128)(2,1)S(1)}, bf16[2,160,640]{2,1,0:T(8,128)(2,1)S(1)}, u32[]{:S(2)}, u32[]{:S(2)}) collective-permute-start(bf16[2,160,640]{2,1,0:T(8,128)(2,1)S(1)} %broadcast_select_fusion.26), channel_id=1, source_target_pairs={{8,12},{16,20},{12,4},{20,28},{9,13},{17,21},{13,5},{21,29},{10,14... | collective-permute-start | bytes 1228808 | tf_op jit(solution)/shard_map/ppermute | solution.py:238
  (46 other events, 332.2 us)
Sparse Core Ops, SparseCore 0:
  411.5 50.2 reduce-scatter.1

commit v8 on v7

--- a/solution.py
+++ b/solution.py
@@ -225,7 +225,7 @@
     shape = (8 // 2, rows_here, quarter, 2 * irreps, columns)
 
     def put(half, j, crossed, out):
-        base = jnp.stack([low if half == 0 else 2 - low, occ.astype(jnp.int32)])
+        base = order.follow(jnp.stack([low if half == 0 else 2 - low, occ.astype(jnp.int32)]))
         kept = [(pair[0][index], 0, jj) for pair, index, jj in crossed]
         arrived = [(pair[1], 2 * index, jj) for pair, index, jj in crossed]
         return order.step(place(base, j, kept, arrived, out, shape))
@@ -253,11 +253,12 @@
     ladder_last = move(ladder_near, MID_TO_MID)
     on_far = move(ladder_far, MID_TO_END)
     b3, b1, b2 = columns_of(3), columns_of(1), columns_of(2)
-
-    order.phase(ladder_last, on_far, b3, b1, b2)
+    rows0 = rows_of(0)
+
+    order.phase(ladder_last, on_far, b3, b1, b2, rows0)
     on_last = move(ladder_last, MID_TO_END)
     own0 = move(b0, MID_TO_MID)
-    a0 = move(rows_of(0), END_TO_MID)
+    a0 = move(rows0, END_TO_MID)
     one = batch((3, ca, b3), (1, ca, b1), (2, ca, b2))
     one.send()
     one.keep()
@@ -306,7 +307,7 @@
     n3, *s0 = three.finish()
     a1 = both4.reshape(a0.shape)
     own1 = move(b1, MID_TO_MID)
-    both5 = exchange(rows2.reshape(b0.shape), jnp.concatenate([f0[1], s0[1]] * 2).reshape(b0.shape))
+    both5 = exchange(rows2.reshape(2, 4, quarter, depth), jnp.concatenate([f0[1], s0[1]])).reshape(b0.shape)
     four.swap()
     five = batch((0, ca, relay0), (0, a0, relay0), (3, ca, jnp.where(at_end, order.open(both4), relay3)))
     five.send()
@@ -353,6 +354,7 @@
     nine = batch((2, ca, relay2[0]), (2, a2, relay2[0]))
     nine.send()
     nine.keep()
+    near1_in = over(n1)
 
     order.phase(relay2[1], f2_back, x01[1], eight.other)
     *g1, n2 = eight.finish()
@@ -362,14 +364,15 @@
     ten.keep()
     ten.swap()
     x2a = cross((s2, home(f2[0], f2_back)))
-    near_in = over(jnp.concatenate([n1, n2]))
-    near1_in, near2_in = near_in[0:2], near_in[2:4]
+    near2_in = over(n2)
     x1b = straight(n1, near1_in, g1)
     x2b = [straight(n2, near2_in, nine.finish(), slice(0, columns))]
+    final = ten.finish()
+    order.before = order.before + [final[0]]
+    x2b.append(straight(n2, near2_in, final, slice(columns, 2 * columns)))
     out = None
     for j in range(2):
         out = put(0, j, [(x03a, 0, j), (x01, 1, j), (x2a, 0, j), (x03a, 1, j)], out)
-    x2b.append(straight(n2, near2_in, ten.finish(), slice(columns, 2 * columns)))
     for j in range(2):
         out = put(1, j, [(x01, 0, j), (x1b, 0, j), (x2b[j], 0, 0), (x01, 2, j)], out)
     return ladder_residual, out

time: 872 us -> 871 us (level)
  other arithmetic: 77.3 us -> 68.3 us
    ppermute x10, waiting for transfers between devices: 82.2 us -> 95.8 us  [swap(): self.other = lax.ppermute(self.order.open(self.away), 'ka', OTHER_Y)]
    reduce_scatter x1, waiting for transfers between devices: 12.1 us -> 0.01 us  [line_local(): lax.psum_scatter(partial_ladder, ('occ', 'ka'), scatter_dimension=0, tile...]
    ppermute x1 -> x2, waiting for transfers between devices: 10.7 us -> 0.01 us  [over(): return lax.ppermute(order.open(near), 'occ', [(1, 0)])]
    ppermute x3, waiting for transfers between devices: 16.6 us -> 25.7 us  [cross(): lax.ppermute(away, 'occ', OTHER_OCC)]
  transfers between devices with their start and end apart: 64 -> 65, of which waited for: 40 -> 39; matrix products, arithmetic and copies ran while one was open for 12% -> 14% of each run, Pallas kernels for 30% -> 30%
where the time goes in v8:
time: 871 us; the launch traced here: 858 us
  waiting for transfers between devices  319 us (37%)
  Pallas kernels  274 us (31%)
  starting transfers between devices  98.1 us (11%)
  other arithmetic  68.3 us (8%)
  local copies, waits for them, and re-layouts  60.7 us (7%)
  matrix products  20.3 us (2%)
  between operations  17.8 us (2%)
    ppermute x23, waiting for transfers between devices, move(): return lax.ppermute(order.open(value), 'vir', route)  185 us
    pallas_call x10, Pallas kernels, keep_products(): pl.pallas_call(kernel, out_shape=(jax.ShapeDtypeStruct((count, rows, colu...  127 us
    pallas_call x10, Pallas kernels, send_products(): pl.pallas_call(kernel, out_shape=(jax.ShapeDtypeStruct((count, rows, colu...  120 us
    ppermute x10, waiting for transfers between devices, swap(): self.other = lax.ppermute(self.order.open(self.away), 'ka', OTHER_Y)  95.8 us
    ppermute x23, starting transfers between devices, move(): return lax.ppermute(order.open(value), 'vir', route)  53.3 us
    pallas_call x4, Pallas kernels, place(): pl.pallas_call(kernel, out_shape=jax.ShapeDtypeStruct(shape, BF16), grid_...  27.2 us
    convert_element_type x10, other arithmetic, finish(): (self.own.astype(F32) + self.order.open(self.other).astype(F32)).astype(B...  26.5 us
    ppermute x3, waiting for transfers between devices, cross(): lax.ppermute(away, 'occ', OTHER_OCC)  25.7 us
  transfers between devices with their start and end apart: 65, of which 39 were waited for; matrix products, arithmetic and copies ran while one was open for 14% of the time, Pallas kernels for 30%

profile of v8, /device:TPU:10, one launch (start us, length us, event | category | flops | bytes accessed | tf_op | source)
XLA Modules:
  0.0 857.8 jit_solution(12769752476857936379)
XLA Ops:
  7.7 4.6 collective-permute-start.1
  14.6 31.8 %collective-permute-done = bf16[128,6656]{1,0:T(8,128)(2,1)S(1)} collective-permute-done((bf16[128,6656]{1,0:T(8,128)(2,1)}, bf16[128,6656]{1,0:T(8,128)(2,1)S(1)}, u32[]{:S(2)}, u32[]{:S(2)}) %collective-permute-start) | collective-permute-done | bytes 1703968 | tf_op jit(solution)/shard_map/ppermute | solution.py:214
  54.5 8.8 %fusion.1 = (bf16[1,1280,2,640]{3,2,1,0:T(2,128)(2,1)S(1)}, bf16[1,1280,2,640]{3,2,1,0:T(2,128)(2,1)S(1)}, bf16[1,1280,2,640]{3,2,1,0:T(2,128)(2,1)S(1)}) fusion(bf16[4,1280,2,640]{3,2,1,0:T(2,128)(2,1)} %param.8), kind=kLoop, calls=%fused_computation.68 | loop fusion | bytes 19660800 | tf_op jit(solution)/shard_map/slice | solution.py:205
  70.5 3.9 slice_bitcast_fusion
  74.3 12.3 %collective-permute-done.2 = bf16[128,6656]{1,0:T(8,128)(2,1)S(1)} collective-permute-done((bf16[128,6656]{1,0:T(8,128)(2,1)S(1)}, bf16[128,6656]{1,0:T(8,128)(2,1)S(1)}, u32[]{:S(2)}, u32[]{:S(2)}) %collective-permute-start.2) | collective-permute-done | bytes 1703968 | tf_op jit(solution)/shard_map/ppermute | solution.py:214
  86.6 4.2 collective-permute-done.3
  96.0 15.4 %send_products.10 = (bf16[3,320,1280]{2,1,0:T(8,128)(2,1)}, bf16[3,320,1280]{2,1,0:T(8,128)(2,1)}) custom-call(s32[4]{0:T(128)} %broadcast_xor_fusion.where_ref, bf16[4,2,640,1280]{3,2,1,0:T(8,128)(2,1)} %refs_0_.39, bf16[4,2,640,1280]{3,2,1,0:T(8,128)(2,1)} %refs_0_.39, bf16[4,2,640,1280]{3,2,1,0:T(8,128)(2,1)} %refs_0_.39, bf16[1280,1280]{1,0:T(8,128)(2,1)} %bitcast.69, ...), custom_call_target="tpu_custom_call" | custom-call | flops 1048576 | bytes 65536 | tf_op jit(solution)/shard_map/send_products/pallas_call | solution.py:70
  111.9 6.3 collective-permute-start.8
  119.9 16.1 %keep_products.10 = (bf16[3,320,1280]{2,1,0:T(8,128)(2,1)}, bf16[3,320,1280]{2,1,0:T(8,128)(2,1)}) custom-call(s32[4]{0:T(128)} %broadcast_xor_fusion.where_ref, bf16[4,2,640,1280]{3,2,1,0:T(8,128)(2,1)} %refs_0_.39, bf16[4,2,640,1280]{3,2,1,0:T(8,128)(2,1)} %refs_0_.39, bf16[4,2,640,1280]{3,2,1,0:T(8,128)(2,1)} %refs_0_.39, bf16[1280,1280]{1,0:T(8,128)(2,1)} %bitcast.70, ...), custom_call_target="tpu_custom_call" | custom-call | flops 1048576 | bytes 65536 | tf_op jit(solution)/shard_map/keep_products/pallas_call | solution.py:97
  136.0 17.6 %collective-permute-done.8 = bf16[128,6656]{1,0:T(8,128)(2,1)} collective-permute-done((bf16[128,6656]{1,0:T(8,128)(2,1)}, bf16[128,6656]{1,0:T(8,128)(2,1)}, u32[]{:S(2)}, u32[]{:S(2)}) %collective-permute-start.8) | collective-permute-done | bytes 1703968 | tf_op jit(solution)/shard_map/ppermute | solution.py:214
  153.6 10.3 %collective-permute-done.6.refs_2_ = bf16[1280,1280]{1,0:T(8,128)(2,1)} collective-permute-done((bf16[1280,1280]{1,0:T(8,128)(2,1)}, bf16[1280,1280]{1,0:T(8,128)(2,1)}, u32[]{:S(2)}, u32[]{:S(2)}) %collective-permute-start.6) | collective-permute-done | bytes 3276832 | tf_op jit(solution)/shard_map/ppermute | solution.py:214
  174.5 20.3 %convolution_convert_fusion = bf16[512,2048]{1,0:T(8,128)(2,1)} fusion(bf16[512,6656]{1,0:T(8,128)(2,1)S(1)} %pad_maximum_fusion, bf16[6656,2048]{1,0:T(8,128)(2,1)} %param.6), kind=kOutput, calls=%fused_computation.15 | convolution fusion | flops 13959692288 | bytes 36175872 | tf_op jit(solution)/shard_map/dot_general | solution.py:274
  194.8 10.1 %send_products.11 = (bf16[2,320,1280]{2,1,0:T(8,128)(2,1)}, bf16[2,320,1280]{2,1,0:T(8,128)(2,1)}) custom-call(s32[4]{0:T(128)} %broadcast_xor_fusion.where_ref, bf16[4,2,640,1280]{3,2,1,0:T(8,128)(2,1)} %refs_0_.39, bf16[2,640,1280]{2,1,0:T(8,128)(2,1)} %copy-done.2, bf16[1280,1280]{1,0:T(8,128)(2,1)} %collective-permute-done.6.refs_2_), custom_call_target="tpu_custom_call" | custom-call | flops 1048576 | bytes 65536 | tf_op jit(solution)/shard_map/send_products/pallas_call | solution.py:70
  205.3 3.9 fusion
  212.0 10.8 %keep_products.11 = (bf16[2,320,1280]{2,1,0:T(8,128)(2,1)}, bf16[2,320,1280]{2,1,0:T(8,128)(2,1)}) custom-call(s32[4]{0:T(128)} %broadcast_xor_fusion.where_ref, bf16[4,2,640,1280]{3,2,1,0:T(8,128)(2,1)} %refs_0_.39, bf16[2,640,1280]{2,1,0:T(8,128)(2,1)} %copy-done.2, bf16[1280,1280]{1,0:T(8,128)(2,1)} %collective-permute-done.6.refs_2_, ...), custom_call_target="tpu_custom_call" | custom-call | flops 1048576 | bytes 65536 | tf_op jit(solution)/shard_map/keep_products/pallas_call | solution.py:97
  224.8 12.1 %collective-permute-done.12.refs_3_ = bf16[1280,1280]{1,0:T(8,128)(2,1)} collective-permute-done((bf16[1280,1280]{1,0:T(8,128)(2,1)}, bf16[1280,1280]{1,0:T(8,128)(2,1)}, u32[]{:S(2)}, u32[]{:S(2)}) %collective-permute-start.12) | collective-permute-done | bytes 3276832 | tf_op jit(solution)/shard_map/ppermute | solution.py:214
  238.6 4.0 broadcast_select_fusion.3
  245.8 14.4 %send_products.12 = (bf16[3,320,1280]{2,1,0:T(8,128)(2,1)}, bf16[3,320,1280]{2,1,0:T(8,128)(2,1)}) custom-call(s32[4]{0:T(128)} %broadcast_xor_fusion.where_ref, bf16[4,2,640,1280]{3,2,1,0:T(8,128)(2,1)} %refs_0_.39, bf16[4,2,640,1280]{3,2,1,0:T(8,128)(2,1)} %refs_0_.39, bf16[2,640,1280]{2,1,0:T(8,128)(2,1)} %copy-done.2, ...), custom_call_target="tpu_custom_call" | custom-call | flops 1048576 | bytes 65536 | tf_op jit(solution)/shard_map/send_products/pallas_call | solution.py:70
  265.6 3.8 slice_bitcast_fusion.1
  269.4 15.2 %keep_products.12 = (bf16[3,320,1280]{2,1,0:T(8,128)(2,1)}, bf16[3,320,1280]{2,1,0:T(8,128)(2,1)}) custom-call(s32[4]{0:T(128)} %broadcast_xor_fusion.where_ref, bf16[4,2,640,1280]{3,2,1,0:T(8,128)(2,1)} %refs_0_.39, bf16[4,2,640,1280]{3,2,1,0:T(8,128)(2,1)} %refs_0_.39, bf16[2,640,1280]{2,1,0:T(8,128)(2,1)} %copy-done.2, ...), custom_call_target="tpu_custom_call" | custom-call | flops 1048576 | bytes 65536 | tf_op jit(solution)/shard_map/keep_products/pallas_call | solution.py:97
  284.6 14.2 %collective-permute-done.18 = bf16[2,320,1280]{2,1,0:T(8,128)(2,1)} collective-permute-done((bf16[2,320,1280]{2,1,0:T(8,128)(2,1)}, bf16[2,320,1280]{2,1,0:T(8,128)(2,1)}, u32[]{:S(2)}, u32[]{:S(2)}) %collective-permute-start.18) | collective-permute-done | bytes 1638432 | tf_op jit(solution)/shard_map/ppermute | solution.py:187
  298.8 12.2 %collective-permute-done.14.refs_2_ = bf16[1280,1280]{1,0:T(8,128)(2,1)} collective-permute-done((bf16[1280,1280]{1,0:T(8,128)(2,1)}, bf16[1280,1280]{1,0:T(8,128)(2,1)}, u32[]{:S(2)}, u32[]{:S(2)}) %collective-permute-start.14) | collective-permute-done | bytes 3276832 | tf_op jit(solution)/shard_map/ppermute | solution.py:214
  320.7 4.0 broadcast_select_fusion.2.refs_3_
  324.7 11.1 %send_products.13 = (bf16[2,320,1280]{2,1,0:T(8,128)(2,1)}, bf16[2,320,1280]{2,1,0:T(8,128)(2,1)}) custom-call(s32[4]{0:T(128)} %broadcast_xor_fusion.where_ref, bf16[4,2,640,1280]{3,2,1,0:T(8,128)(2,1)} %refs_0_.39, bf16[4,2,640,1280]{3,2,1,0:T(8,128)(2,1)} %refs_0_.39, bf16[1280,1280]{1,0:T(8,128)(2,1)} %collective-permute-done.14.refs_2_, ...), custom_call_target="tpu_custom_call" | custom-call | flops 1048576 | bytes 65536 | tf_op jit(solution)/shard_map/send_products/pallas_call | solution.py:70
  343.3 12.2 %keep_products.13 = (bf16[2,320,1280]{2,1,0:T(8,128)(2,1)}, bf16[2,320,1280]{2,1,0:T(8,128)(2,1)}) custom-call(s32[4]{0:T(128)} %broadcast_xor_fusion.where_ref, bf16[4,2,640,1280]{3,2,1,0:T(8,128)(2,1)} %refs_0_.39, bf16[4,2,640,1280]{3,2,1,0:T(8,128)(2,1)} %refs_0_.39, bf16[1280,1280]{1,0:T(8,128)(2,1)} %collective-permute-done.14.refs_2_, ...), custom_call_target="tpu_custom_call" | custom-call | flops 1048576 | bytes 65536 | tf_op jit(solution)/shard_map/keep_products/pallas_call | solution.py:97
  355.5 15.8 %collective-permute-done.23 = bf16[3,320,1280]{2,1,0:T(8,128)(2,1)} collective-permute-done((bf16[3,320,1280]{2,1,0:T(8,128)(2,1)}, bf16[3,320,1280]{2,1,0:T(8,128)(2,1)}, u32[]{:S(2)}, u32[]{:S(2)}) %collective-permute-start.23) | collective-permute-done | bytes 2457632 | tf_op jit(solution)/shard_map/ppermute | solution.py:187
  371.3 15.2 %collective-permute-done.21.refs_3_ = bf16[1280,1280]{1,0:T(8,128)(2,1)} collective-permute-done((bf16[1280,1280]{1,0:T(8,128)(2,1)}, bf16[1280,1280]{1,0:T(8,128)(2,1)}, u32[]{:S(2)}, u32[]{:S(2)}) %collective-permute-start.21) | collective-permute-done | bytes 3276832 | tf_op jit(solution)/shard_map/ppermute | solution.py:214
  388.1 4.2 add_convert_fusion.4
  403.6 14.5 %send_products.14 = (bf16[3,320,1280]{2,1,0:T(8,128)(2,1)}, bf16[3,320,1280]{2,1,0:T(8,128)(2,1)}) custom-call(s32[4]{0:T(128)} %broadcast_xor_fusion.where_ref, bf16[4,2,640,1280]{3,2,1,0:T(8,128)(2,1)} %refs_0_.39, bf16[2,640,1280]{2,1,0:T(8,128)(2,1)} %copy-done.2, bf16[4,2,640,1280]{3,2,1,0:T(8,128)(2,1)} %refs_0_.39, ...), custom_call_target="tpu_custom_call" | custom-call | flops 1048576 | bytes 65536 | tf_op jit(solution)/shard_map/send_products/pallas_call | solution.py:70
  419.1 4.0 collective-permute-done.26.refs_5_
  426.6 15.2 %keep_products.14 = (bf16[3,320,1280]{2,1,0:T(8,128)(2,1)}, bf16[3,320,1280]{2,1,0:T(8,128)(2,1)}) custom-call(s32[4]{0:T(128)} %broadcast_xor_fusion.where_ref, bf16[4,2,640,1280]{3,2,1,0:T(8,128)(2,1)} %refs_0_.39, bf16[2,640,1280]{2,1,0:T(8,128)(2,1)} %copy-done.2, bf16[4,2,640,1280]{3,2,1,0:T(8,128)(2,1)} %refs_0_.39, ...), custom_call_target="tpu_custom_call" | custom-call | flops 1048576 | bytes 65536 | tf_op jit(solution)/shard_map/keep_products/pallas_call | solution.py:97
  441.8 14.9 %collective-permute-done.28 = bf16[2,320,1280]{2,1,0:T(8,128)(2,1)} collective-permute-done((bf16[2,320,1280]{2,1,0:T(8,128)(2,1)}, bf16[2,320,1280]{2,1,0:T(8,128)(2,1)}, u32[]{:S(2)}, u32[]{:S(2)}) %collective-permute-start.28) | collective-permute-done | bytes 1638432 | tf_op jit(solution)/shard_map/ppermute | solution.py:187
  456.7 7.4 collective-permute-done.24
  464.1 5.1 collective-permute-done.25.refs_2_
  473.5 10.1 %send_products.15 = (bf16[2,320,1280]{2,1,0:T(8,128)(2,1)}, bf16[2,320,1280]{2,1,0:T(8,128)(2,1)}) custom-call(s32[4]{0:T(128)} %broadcast_xor_fusion.where_ref, bf16[4,2,640,1280]{3,2,1,0:T(8,128)(2,1)} %refs_0_.39, bf16[2,640,1280]{2,1,0:T(8,128)(2,1)} %bitcast.65, bf16[1280,1280]{1,0:T(8,128)(2,1)} %collective-permute-done.25.refs_2_), custom_call_target="tpu_custom_call" | custom-call | flops 1048576 | bytes 65536 | tf_op jit(solution)/shard_map/send_products/pallas_call | solution.py:70
  484.1 4.4 add_convert_fusion.2
  490.9 10.8 %keep_products.15 = (bf16[2,320,1280]{2,1,0:T(8,128)(2,1)}, bf16[2,320,1280]{2,1,0:T(8,128)(2,1)}) custom-call(s32[4]{0:T(128)} %broadcast_xor_fusion.where_ref, bf16[4,2,640,1280]{3,2,1,0:T(8,128)(2,1)} %refs_0_.39, bf16[2,640,1280]{2,1,0:T(8,128)(2,1)} %bitcast.66, bf16[1280,1280]{1,0:T(8,128)(2,1)} %collective-permute-done.25.refs_2_, ...), custom_call_target="tpu_custom_call" | custom-call | flops 1048576 | bytes 65536 | tf_op jit(solution)/shard_map/keep_products/pallas_call | solution.py:97
  501.6 17.1 %collective-permute-done.33 = bf16[3,320,1280]{2,1,0:T(8,128)(2,1)} collective-permute-done((bf16[3,320,1280]{2,1,0:T(8,128)(2,1)}, bf16[3,320,1280]{2,1,0:T(8,128)(2,1)}, u32[]{:S(2)}, u32[]{:S(2)}) %collective-permute-start.33) | collective-permute-done | bytes 2457632 | tf_op jit(solution)/shard_map/ppermute | solution.py:187
  518.8 21.5 %collective-permute-done.31.refs_3_ = bf16[1280,1280]{1,0:T(8,128)(2,1)} collective-permute-done((bf16[1280,1280]{1,0:T(8,128)(2,1)}, bf16[1280,1280]{1,0:T(8,128)(2,1)}, u32[]{:S(2)}, u32[]{:S(2)}) %collective-permute-start.31) | collective-permute-done | bytes 3276832 | tf_op jit(solution)/shard_map/ppermute | solution.py:214
  546.7 14.4 %send_products.16 = (bf16[3,320,1280]{2,1,0:T(8,128)(2,1)}, bf16[3,320,1280]{2,1,0:T(8,128)(2,1)}) custom-call(s32[4]{0:T(128)} %broadcast_xor_fusion.where_ref, bf16[4,2,640,1280]{3,2,1,0:T(8,128)(2,1)} %refs_0_.39, bf16[2,640,1280]{2,1,0:T(8,128)(2,1)} %bitcast.58, bf16[4,2,640,1280]{3,2,1,0:T(8,128)(2,1)} %refs_0_.39, ...), custom_call_target="tpu_custom_call" | custom-call | flops 1048576 | bytes 65536 | tf_op jit(solution)/shard_map/send_products/pallas_call | solution.py:70
  571.6 15.1 %keep_products.16 = (bf16[3,320,1280]{2,1,0:T(8,128)(2,1)}, bf16[3,320,1280]{2,1,0:T(8,128)(2,1)}) custom-call(s32[4]{0:T(128)} %broadcast_xor_fusion.where_ref, bf16[4,2,640,1280]{3,2,1,0:T(8,128)(2,1)} %refs_0_.39, bf16[2,640,1280]{2,1,0:T(8,128)(2,1)} %bitcast.59, bf16[4,2,640,1280]{3,2,1,0:T(8,128)(2,1)} %refs_0_.39, ...), custom_call_target="tpu_custom_call" | custom-call | flops 1048576 | bytes 65536 | tf_op jit(solution)/shard_map/keep_products/pallas_call | solution.py:97
  586.8 17.2 %collective-permute-done.38 = bf16[2,320,1280]{2,1,0:T(8,128)(2,1)} collective-permute-done((bf16[2,320,1280]{2,1,0:T(8,128)(2,1)}, bf16[2,320,1280]{2,1,0:T(8,128)(2,1)}, u32[]{:S(2)}, u32[]{:S(2)}) %collective-permute-start.38) | collective-permute-done | bytes 1638432 | tf_op jit(solution)/shard_map/ppermute | solution.py:187
  616.2 3.9 fusion.3
  625.0 14.5 %send_products.17 = (bf16[3,320,1280]{2,1,0:T(8,128)(2,1)}, bf16[3,320,1280]{2,1,0:T(8,128)(2,1)}) custom-call(s32[4]{0:T(128)} %broadcast_xor_fusion.where_ref, bf16[4,2,640,1280]{3,2,1,0:T(8,128)(2,1)} %refs_0_.39, bf16[2,640,1280]{2,1,0:T(8,128)(2,1)} %bitcast.67, bf16[4,2,640,1280]{3,2,1,0:T(8,128)(2,1)} %refs_0_.39, bf16[1280,1280]{1,0:T(8,128)(2,1)} %copy-done.10, ...), custom_call_target="tpu_custom_call" | custom-call | flops 1048576 | bytes 65536 | tf_op jit(solution)/shard_map/send_products/pallas_call | solution.py:70
  643.4 3.8 collective-permute-done.42
  650.5 15.2 %keep_products.17 = (bf16[3,320,1280]{2,1,0:T(8,128)(2,1)}, bf16[3,320,1280]{2,1,0:T(8,128)(2,1)}) custom-call(s32[4]{0:T(128)} %broadcast_xor_fusion.where_ref, bf16[4,2,640,1280]{3,2,1,0:T(8,128)(2,1)} %refs_0_.39, bf16[2,640,1280]{2,1,0:T(8,128)(2,1)} %bitcast.68, bf16[4,2,640,1280]{3,2,1,0:T(8,128)(2,1)} %refs_0_.39, bf16[1280,1280]{1,0:T(8,128)(2,1)} %copy-done.10, ...), custom_call_target="tpu_custom_call" | custom-call | flops 1048576 | bytes 65536 | tf_op jit(solution)/shard_map/keep_products/pallas_call | solution.py:97
  665.7 15.7 %collective-permute-done.43.refs_4_.refs_7_ = bf16[4,160,1280]{2,1,0:T(8,128)(2,1)S(1)} collective-permute-done((bf16[4,160,1280]{2,1,0:T(8,128)(2,1)}, bf16[4,160,1280]{2,1,0:T(8,128)(2,1)S(1)}, u32[]{:S(2)}, u32[]{:S(2)}) %collective-permute-start.43) | collective-permute-done | bytes 1638432 | tf_op jit(solution)/shard_map/ppermute | solution.py:219
  691.6 7.7 send_products.18
  710.4 4.6 collective-permute-start.58
  715.0 8.0 keep_products.18
  726.5 13.2 %collective-permute-done.45.refs_2_ = bf16[1280,640]{1,0:T(8,128)(2,1)} collective-permute-done((bf16[1280,640]{1,0:T(8,128)(2,1)}, bf16[1280,640]{1,0:T(8,128)(2,1)}, u32[]{:S(2)}, u32[]{:S(2)}) %collective-permute-start.45) | collective-permute-done | bytes 1638432 | tf_op jit(solution)/shard_map/ppermute | solution.py:214
  739.7 4.5 collective-permute-done.49.refs_5_.refs_4_.refs_7_
  744.3 3.9 add_convert_fusion
  749.5 7.8 send_products.19
  763.2 8.1 keep_products.19
  773.1 4.8 collective-permute-start.55
  782.8 13.2 %collective-permute-done.53 = bf16[2,320,640]{2,1,0:T(8,128)(2,1)S(1)} collective-permute-done((bf16[2,320,640]{2,1,0:T(8,128)(2,1)}, bf16[2,320,640]{2,1,0:T(8,128)(2,1)S(1)}, u32[]{:S(2)}, u32[]{:S(2)}) %collective-permute-start.53) | collective-permute-done | bytes 819232 | tf_op jit(solution)/shard_map/ppermute | solution.py:187
  796.0 5.2 collective-permute-start.60
  805.4 4.9 collective-permute-start.57
  810.3 5.4 collective-permute-done.54.refs_6_
  820.5 6.8 place.4.refs_8_
  827.3 6.8 place.5.refs_8_
  836.9 6.8 place.6.refs_8_
  843.7 6.8 place.7
  (248 shorter events, 182.0 us)
Async XLA Ops:
  7.2 434.7 %reduce-scatter.2.cloned.1.call-start = ((), (), s32[]{:S(2)}) async-start(), calls=%async_computation.1 | async-start | bytes 2359296 | tf_op jit(solution)/shard_map/reduce_scatter | solution.py:282
  7.2 39.2 %collective-permute-start = (bf16[128,6656]{1,0:T(8,128)(2,1)}, bf16[128,6656]{1,0:T(8,128)(2,1)S(1)}, u32[]{:S(2)}, u32[]{:S(2)}) collective-permute-start(bf16[128,6656]{1,0:T(8,128)(2,1)} %param.5), channel_id=1, source_target_pairs={{0,8},{8,0},{16,24},{24,16},{1,9},{9,1},{17,25},{25,17},{2,10},{10... | collective-permute-start | bytes 5111816 | tf_op jit(solution)/shard_map/ppermute | solution.py:214
  7.7 41.7 %collective-permute-start.1 = (bf16[128,6656]{1,0:T(8,128)(2,1)}, bf16[128,6656]{1,0:T(8,128)(2,1)S(1)}, u32[]{:S(2)}, u32[]{:S(2)}) collective-permute-start(bf16[128,6656]{1,0:T(8,128)(2,1)} %param.5), channel_id=1, source_target_pairs={{8,16},{16,8},{9,17},{17,9},{10,18},{18,10},{11,19},{19,11},{12,20... | collective-permute-start | bytes 5111816 | tf_op jit(solution)/shard_map/ppermute | solution.py:214
  49.5 37.1 %collective-permute-start.2 = (bf16[128,6656]{1,0:T(8,128)(2,1)S(1)}, bf16[128,6656]{1,0:T(8,128)(2,1)S(1)}, u32[]{:S(2)}, u32[]{:S(2)}) collective-permute-start(bf16[128,6656]{1,0:T(8,128)(2,1)S(1)} %collective-permute-done.1), channel_id=1, source_target_pairs={{8,0},{16,24},{9,1},{17,25},{10,2},{18,26},{11,3},{19,27},{12,4},{... | collective-permute-start | bytes 5111816 | tf_op jit(solution)/shard_map/ppermute | solution.py:214
  50.9 40.0 %collective-permute-start.3 = (bf16[128,6656]{1,0:T(8,128)(2,1)S(1)}, bf16[128,6656]{1,0:T(8,128)(2,1)S(1)}, u32[]{:S(2)}, u32[]{:S(2)}) collective-permute-start(bf16[128,6656]{1,0:T(8,128)(2,1)S(1)} %collective-permute-done), channel_id=1, source_target_pairs={{8,16},{16,8},{9,17},{17,9},{10,18},{18,10},{11,19},{19,11},{12,20... | collective-permute-start | bytes 5111816 | tf_op jit(solution)/shard_map/ppermute | solution.py:214
  90.8 73.1 %collective-permute-start.6 = (bf16[1280,1280]{1,0:T(8,128)(2,1)}, bf16[1280,1280]{1,0:T(8,128)(2,1)}, u32[]{:S(2)}, u32[]{:S(2)}) collective-permute-start(bf16[1280,1280]{1,0:T(8,128)(2,1)} %bitcast.43.refs_4_), channel_id=1, source_target_pairs={{8,16},{16,8},{9,17},{17,9},{10,18},{18,10},{11,19},{19,11},{12,20... | collective-permute-start | bytes 9830408 | tf_op jit(solution)/shard_map/ppermute | solution.py:214
  94.2 72.9 %collective-permute-start.7 = (bf16[2,640,1280]{2,1,0:T(8,128)(2,1)}, bf16[2,640,1280]{2,1,0:T(8,128)(2,1)S(1)}, u32[]{:S(2)}, u32[]{:S(2)}) collective-permute-start(bf16[2,640,1280]{2,1,0:T(8,128)(2,1)} %slice_bitcast_fusion), channel_id=1, source_target_pairs={{0,8},{24,16},{1,9},{25,17},{2,10},{26,18},{3,11},{27,19},{4,12},{... | collective-permute-start | bytes 9830408 | tf_op jit(solution)/shard_map/ppermute | solution.py:214
  111.4 6.9 collective-permute-start.4
  111.4 8.5 collective-permute-start.5
  111.9 41.7 %collective-permute-start.8 = (bf16[128,6656]{1,0:T(8,128)(2,1)}, bf16[128,6656]{1,0:T(8,128)(2,1)}, u32[]{:S(2)}, u32[]{:S(2)}) collective-permute-start(bf16[128,6656]{1,0:T(8,128)(2,1)} %copy-done.34), channel_id=1, source_target_pairs={{8,0},{16,24},{9,1},{17,25},{10,2},{18,26},{11,3},{19,27},{12,4},{... | collective-permute-start | bytes 5111816 | tf_op jit(solution)/shard_map/ppermute | solution.py:214
  167.0 69.8 %collective-permute-start.12 = (bf16[1280,1280]{1,0:T(8,128)(2,1)}, bf16[1280,1280]{1,0:T(8,128)(2,1)}, u32[]{:S(2)}, u32[]{:S(2)}) collective-permute-start(bf16[1280,1280]{1,0:T(8,128)(2,1)} %bitcast.71), channel_id=1, source_target_pairs={{0,8},{8,0},{16,24},{24,16},{1,9},{9,1},{17,25},{25,17},{2,10},{10... | collective-permute-start | bytes 9830408 | tf_op jit(solution)/shard_map/ppermute | solution.py:214
  167.0 71.6 %collective-permute-start.11 = (bf16[1280,1280]{1,0:T(8,128)(2,1)}, bf16[1280,1280]{1,0:T(8,128)(2,1)}, u32[]{:S(2)}, u32[]{:S(2)}) collective-permute-start(bf16[1280,1280]{1,0:T(8,128)(2,1)} %bitcast.72), channel_id=1, source_target_pairs={{8,16},{16,8},{9,17},{17,9},{10,18},{18,10},{11,19},{19,11},{12,20... | collective-permute-start | bytes 9830408 | tf_op jit(solution)/shard_map/ppermute | solution.py:214
  172.9 51.9 %collective-permute-start.13 = (bf16[3,320,1280]{2,1,0:T(8,128)(2,1)}, bf16[3,320,1280]{2,1,0:T(8,128)(2,1)S(1)}, u32[]{:S(2)}, u32[]{:S(2)}) collective-permute-start(bf16[3,320,1280]{2,1,0:T(8,128)(2,1)} %get-tuple-element.189), channel_id=1, source_target_pairs={{0,2},{2,0},{1,3},{3,1},{4,6},{6,4},{5,7},{7,5},{8,10},{10,8},{9,1... | collective-permute-start | bytes 7372808 | tf_op jit(solution)/shard_map/ppermute | solution.py:187
  204.8 6.0 collective-permute-start.9
  204.8 6.2 collective-permute-start.10
  242.6 68.5 %collective-permute-start.14 = (bf16[1280,1280]{1,0:T(8,128)(2,1)}, bf16[1280,1280]{1,0:T(8,128)(2,1)}, u32[]{:S(2)}, u32[]{:S(2)}) collective-permute-start(bf16[1280,1280]{1,0:T(8,128)(2,1)} %broadcast_select_fusion.3), channel_id=1, source_target_pairs={{0,8},{8,0},{16,24},{24,16},{1,9},{9,1},{17,25},{25,17},{2,10},{10... | collective-permute-start | bytes 9830408 | tf_op jit(solution)/shard_map/ppermute | solution.py:214
  242.6 70.2 %collective-permute-start.17 = (bf16[1280,1280]{1,0:T(8,128)(2,1)}, bf16[1280,1280]{1,0:T(8,128)(2,1)S(1)}, u32[]{:S(2)}, u32[]{:S(2)}) collective-permute-start(bf16[1280,1280]{1,0:T(8,128)(2,1)} %collective-permute-done.12.refs_3_), channel_id=1, source_target_pairs={{8,16},{16,8},{9,17},{17,9},{10,18},{18,10},{11,19},{19,11},{12,20... | collective-permute-start | bytes 9830408 | tf_op jit(solution)/shard_map/ppermute | solution.py:214
  260.2 9.2 %collective-permute-start.15 = (bf16[3,320,1280]{2,1,0:T(8,128)(2,1)}, bf16[3,320,1280]{2,1,0:T(8,128)(2,1)}, u32[]{:S(2)}, u32[]{:S(2)}) collective-permute-start(bf16[3,320,1280]{2,1,0:T(8,128)(2,1)} %get-tuple-element.195), channel_id=1, source_target_pairs={{0,1},{1,0},{2,3},{3,2},{4,5},{5,4},{6,7},{7,6},{8,9},{9,8},{10,11... | collective-permute-start | bytes 7372808 | tf_op jit(solution)/shard_map/ppermute | solution.py:179
  260.2 9.2 %collective-permute-start.16 = (bf16[3,320,1280]{2,1,0:T(8,128)(2,1)}, bf16[3,320,1280]{2,1,0:T(8,128)(2,1)}, u32[]{:S(2)}, u32[]{:S(2)}) collective-permute-start(bf16[3,320,1280]{2,1,0:T(8,128)(2,1)} %get-tuple-element.196), channel_id=1, source_target_pairs={{0,1},{1,0},{2,3},{3,2},{4,5},{5,4},{6,7},{7,6},{8,9},{9,8},{10,11... | collective-permute-start | bytes 7372808 | tf_op jit(solution)/shard_map/ppermute | solution.py:179
  260.7 38.1 %collective-permute-start.18 = (bf16[2,320,1280]{2,1,0:T(8,128)(2,1)}, bf16[2,320,1280]{2,1,0:T(8,128)(2,1)}, u32[]{:S(2)}, u32[]{:S(2)}) collective-permute-start(bf16[2,320,1280]{2,1,0:T(8,128)(2,1)} %get-tuple-element.200), channel_id=1, source_target_pairs={{0,2},{2,0},{1,3},{3,1},{4,6},{6,4},{5,7},{7,5},{8,10},{10,8},{9,1... | collective-permute-start | bytes 4915208 | tf_op jit(solution)/shard_map/ppermute | solution.py:187
  315.5 55.7 %collective-permute-start.23 = (bf16[3,320,1280]{2,1,0:T(8,128)(2,1)}, bf16[3,320,1280]{2,1,0:T(8,128)(2,1)}, u32[]{:S(2)}, u32[]{:S(2)}) collective-permute-start(bf16[3,320,1280]{2,1,0:T(8,128)(2,1)} %get-tuple-element.211), channel_id=1, source_target_pairs={{0,2},{2,0},{1,3},{3,1},{4,6},{6,4},{5,7},{7,5},{8,10},{10,8},{9,1... | collective-permute-start | bytes 7372808 | tf_op jit(solution)/shard_map/ppermute | solution.py:187
  317.1 69.4 %collective-permute-start.21 = (bf16[1280,1280]{1,0:T(8,128)(2,1)}, bf16[1280,1280]{1,0:T(8,128)(2,1)}, u32[]{:S(2)}, u32[]{:S(2)}) collective-permute-start(bf16[1280,1280]{1,0:T(8,128)(2,1)} %collective-permute-done.14.refs_2_), channel_id=1, source_target_pairs={{8,16},{16,8},{9,17},{17,9},{10,18},{18,10},{11,19},{19,11},{12,20... | collective-permute-start | bytes 9830408 | tf_op jit(solution)/shard_map/ppermute | solution.py:214
  320.7 67.4 %collective-permute-start.22 = (bf16[1280,1280]{1,0:T(8,128)(2,1)}, bf16[1280,1280]{1,0:T(8,128)(2,1)S(1)}, u32[]{:S(2)}, u32[]{:S(2)}) collective-permute-start(bf16[1280,1280]{1,0:T(8,128)(2,1)} %broadcast_select_fusion.1), channel_id=1, source_target_pairs={{0,8},{8,0},{16,24},{24,16},{1,9},{9,1},{17,25},{25,17},{2,10},{10... | collective-permute-start | bytes 9830408 | tf_op jit(solution)/shard_map/ppermute | solution.py:214
  335.8 7.4 collective-permute-start.19
  335.8 7.4 collective-permute-start.20
  397.6 66.6 %collective-permute-start.24 = (bf16[2,4,160,1280]{3,2,1,0:T(8,128)(2,1)}, bf16[2,4,160,1280]{3,2,1,0:T(8,128)(2,1)S(1)}, u32[]{:S(2)}, u32[]{:S(2)}) collective-permute-start(bf16[2,4,160,1280]{3,2,1,0:T(8,128)(2,1)} %broadcast_select_fusion.4), channel_id=1, source_target_pairs={{0,8},{8,0},{16,24},{24,16},{1,9},{9,1},{17,25},{25,17},{2,10},{10... | collective-permute-start | bytes 9830408 | tf_op jit(solution)/shard_map/ppermute | solution.py:214
  397.9 71.3 %collective-permute-start.25 = (bf16[1280,1280]{1,0:T(8,128)(2,1)}, bf16[1280,1280]{1,0:T(8,128)(2,1)}, u32[]{:S(2)}, u32[]{:S(2)}) collective-permute-start(bf16[1280,1280]{1,0:T(8,128)(2,1)} %bitcast.49.refs_4_), channel_id=1, source_target_pairs={{8,16},{16,8},{9,17},{17,9},{10,18},{18,10},{11,19},{19,11},{12,20... | collective-permute-start | bytes 9830408 | tf_op jit(solution)/shard_map/ppermute | solution.py:214
  418.1 5.0 collective-permute-start.26
  418.1 8.5 collective-permute-start.27
  418.6 38.1 %collective-permute-start.28 = (bf16[2,320,1280]{2,1,0:T(8,128)(2,1)}, bf16[2,320,1280]{2,1,0:T(8,128)(2,1)}, u32[]{:S(2)}, u32[]{:S(2)}) collective-permute-start(bf16[2,320,1280]{2,1,0:T(8,128)(2,1)} %get-tuple-element.228), channel_id=1, source_target_pairs={{0,2},{2,0},{1,3},{3,1},{4,6},{6,4},{5,7},{7,5},{8,10},{10,8},{9,1... | collective-permute-start | bytes 4915208 | tf_op jit(solution)/shard_map/ppermute | solution.py:187
  469.2 71.1 %collective-permute-start.31 = (bf16[1280,1280]{1,0:T(8,128)(2,1)}, bf16[1280,1280]{1,0:T(8,128)(2,1)}, u32[]{:S(2)}, u32[]{:S(2)}) collective-permute-start(bf16[1280,1280]{1,0:T(8,128)(2,1)} %bitcast.52.refs_5_), channel_id=1, source_target_pairs={{8,16},{16,8},{9,17},{17,9},{10,18},{18,10},{11,19},{19,11},{12,20... | collective-permute-start | bytes 9830408 | tf_op jit(solution)/shard_map/ppermute | solution.py:214
  472.9 68.0 %collective-permute-start.32 = (bf16[1280,1280]{1,0:T(8,128)(2,1)}, bf16[1280,1280]{1,0:T(8,128)(2,1)}, u32[]{:S(2)}, u32[]{:S(2)}) collective-permute-start(bf16[1280,1280]{1,0:T(8,128)(2,1)} %bitcast.49.refs_4_), channel_id=1, source_target_pairs={{0,8},{8,0},{16,24},{24,16},{1,9},{9,1},{17,25},{25,17},{2,10},{10... | collective-permute-start | bytes 9830408 | tf_op jit(solution)/shard_map/ppermute | solution.py:214
  472.9 45.8 %collective-permute-start.33 = (bf16[3,320,1280]{2,1,0:T(8,128)(2,1)}, bf16[3,320,1280]{2,1,0:T(8,128)(2,1)}, u32[]{:S(2)}, u32[]{:S(2)}) collective-permute-start(bf16[3,320,1280]{2,1,0:T(8,128)(2,1)} %get-tuple-element.237), channel_id=1, source_target_pairs={{0,2},{2,0},{1,3},{3,1},{4,6},{6,4},{5,7},{7,5},{8,10},{10,8},{9,1... | collective-permute-start | bytes 7372808 | tf_op jit(solution)/shard_map/ppermute | solution.py:187
  483.6 6.0 collective-permute-start.30
  540.9 65.6 %collective-permute-start.34 = (bf16[1280,1280]{1,0:T(8,128)(2,1)}, bf16[1280,1280]{1,0:T(8,128)(2,1)}, u32[]{:S(2)}, u32[]{:S(2)}) collective-permute-start(bf16[1280,1280]{1,0:T(8,128)(2,1)} %bitcast.52.refs_5_), channel_id=1, source_target_pairs={{0,8},{8,0},{16,24},{24,16},{1,9},{9,1},{17,25},{25,17},{2,10},{10... | collective-permute-start | bytes 9830408 | tf_op jit(solution)/shard_map/ppermute | solution.py:214
  541.2 65.8 %collective-permute-start.35 = (bf16[1280,1280]{1,0:T(8,128)(2,1)}, bf16[1280,1280]{1,0:T(8,128)(2,1)S(1)}, u32[]{:S(2)}, u32[]{:S(2)}) collective-permute-start(bf16[1280,1280]{1,0:T(8,128)(2,1)} %collective-permute-done.32.refs_4_), channel_id=1, source_target_pairs={{8,16},{16,8},{9,17},{17,9},{10,18},{18,10},{11,19},{19,11},{12,20... | collective-permute-start | bytes 9830408 | tf_op jit(solution)/shard_map/ppermute | solution.py:214
  561.1 10.5 %collective-permute-start.36 = (bf16[3,320,1280]{2,1,0:T(8,128)(2,1)}, bf16[3,320,1280]{2,1,0:T(8,128)(2,1)}, u32[]{:S(2)}, u32[]{:S(2)}) collective-permute-start(bf16[3,320,1280]{2,1,0:T(8,128)(2,1)} %get-tuple-element.241), channel_id=1, source_target_pairs={{0,1},{1,0},{2,3},{3,2},{4,5},{5,4},{6,7},{7,6},{8,9},{9,8},{10,11... | collective-permute-start | bytes 7372808 | tf_op jit(solution)/shard_map/ppermute | solution.py:179
  561.1 10.5 %collective-permute-start.37 = (bf16[3,320,1280]{2,1,0:T(8,128)(2,1)}, bf16[3,320,1280]{2,1,0:T(8,128)(2,1)}, u32[]{:S(2)}, u32[]{:S(2)}) collective-permute-start(bf16[3,320,1280]{2,1,0:T(8,128)(2,1)} %get-tuple-element.242), channel_id=1, source_target_pairs={{0,1},{1,0},{2,3},{3,2},{4,5},{5,4},{6,7},{7,6},{8,9},{9,8},{10,11... | collective-permute-start | bytes 7372808 | tf_op jit(solution)/shard_map/ppermute | solution.py:179
  565.8 38.1 %collective-permute-start.38 = (bf16[2,320,1280]{2,1,0:T(8,128)(2,1)}, bf16[2,320,1280]{2,1,0:T(8,128)(2,1)}, u32[]{:S(2)}, u32[]{:S(2)}) collective-permute-start(bf16[2,320,1280]{2,1,0:T(8,128)(2,1)} %get-tuple-element.246), channel_id=1, source_target_pairs={{0,2},{2,0},{1,3},{3,1},{4,6},{6,4},{5,7},{7,5},{8,10},{10,8},{9,1... | collective-permute-start | bytes 4915208 | tf_op jit(solution)/shard_map/ppermute | solution.py:187
  613.2 34.0 %collective-permute-start.42 = (bf16[4,160,1280]{2,1,0:T(8,128)(2,1)}, bf16[4,160,1280]{2,1,0:T(8,128)(2,1)}, u32[]{:S(2)}, u32[]{:S(2)}) collective-permute-start(bf16[4,160,1280]{2,1,0:T(8,128)(2,1)} %pad_maximum_fusion.4), channel_id=1, source_target_pairs={{8,0},{16,24},{9,1},{17,25},{10,2},{18,26},{11,3},{19,27},{12,4},{... | collective-permute-start | bytes 4915208 | tf_op jit(solution)/shard_map/ppermute | solution.py:214
  621.1 44.6 %collective-permute-start.41 = (bf16[1280,640]{1,0:T(8,128)(2,1)}, bf16[1280,640]{1,0:T(8,128)(2,1)S(1)}, u32[]{:S(2)}, u32[]{:S(2)}) collective-permute-start(bf16[1280,640]{1,0:T(8,128)(2,1)} %get-tuple-element.254), channel_id=1, source_target_pairs={{8,16},{16,8},{9,17},{17,9},{10,18},{18,10},{11,19},{19,11},{12,20... | collective-permute-start | bytes 4915208 | tf_op jit(solution)/shard_map/ppermute | solution.py:214
  624.4 57.0 %collective-permute-start.44 = (bf16[3,320,1280]{2,1,0:T(8,128)(2,1)}, bf16[3,320,1280]{2,1,0:T(8,128)(2,1)}, u32[]{:S(2)}, u32[]{:S(2)}) collective-permute-start(bf16[3,320,1280]{2,1,0:T(8,128)(2,1)} %get-tuple-element.270), channel_id=1, source_target_pairs={{0,2},{2,0},{1,3},{3,1},{4,6},{6,4},{5,7},{7,5},{8,10},{10,8},{9,1... | collective-permute-start | bytes 7372808 | tf_op jit(solution)/shard_map/ppermute | solution.py:187
  639.5 11.0 %collective-permute-start.39 = (bf16[3,320,1280]{2,1,0:T(8,128)(2,1)}, bf16[3,320,1280]{2,1,0:T(8,128)(2,1)}, u32[]{:S(2)}, u32[]{:S(2)}) collective-permute-start(bf16[3,320,1280]{2,1,0:T(8,128)(2,1)} %get-tuple-element.249), channel_id=1, source_target_pairs={{0,1},{1,0},{2,3},{3,2},{4,5},{5,4},{6,7},{7,6},{8,9},{9,8},{10,11... | collective-permute-start | bytes 7372808 | tf_op jit(solution)/shard_map/ppermute | solution.py:179
  639.6 10.9 %collective-permute-start.40 = (bf16[3,320,1280]{2,1,0:T(8,128)(2,1)}, bf16[3,320,1280]{2,1,0:T(8,128)(2,1)}, u32[]{:S(2)}, u32[]{:S(2)}) collective-permute-start(bf16[3,320,1280]{2,1,0:T(8,128)(2,1)} %get-tuple-element.250), channel_id=1, source_target_pairs={{0,1},{1,0},{2,3},{3,2},{4,5},{5,4},{6,7},{7,6},{8,9},{9,8},{10,11... | collective-permute-start | bytes 7372808 | tf_op jit(solution)/shard_map/ppermute | solution.py:179
  647.2 34.2 %collective-permute-start.43 = (bf16[4,160,1280]{2,1,0:T(8,128)(2,1)}, bf16[4,160,1280]{2,1,0:T(8,128)(2,1)S(1)}, u32[]{:S(2)}, u32[]{:S(2)}) collective-permute-start(bf16[4,160,1280]{2,1,0:T(8,128)(2,1)} %pad_maximum_fusion.5), channel_id=1, source_target_pairs={{0,4},{4,0},{1,5},{5,1},{2,6},{6,2},{3,7},{7,3},{8,12},{12,8},{9,1... | collective-permute-start | bytes 4915208 | tf_op jit(solution)/shard_map/ppermute | solution.py:219
  689.6 54.7 %collective-permute-start.49 = (bf16[6,160,1280]{2,1,0:T(8,128)(2,1)}, bf16[6,160,1280]{2,1,0:T(8,128)(2,1)S(1)}, u32[]{:S(2)}, u32[]{:S(2)}) collective-permute-start(bf16[6,160,1280]{2,1,0:T(8,128)(2,1)} %pad_maximum_fusion.1), channel_id=1, source_target_pairs={{0,4},{4,0},{1,5},{5,1},{2,6},{6,2},{3,7},{7,3},{8,12},{12,8},{9,1... | collective-permute-start | bytes 7372808 | tf_op jit(solution)/shard_map/ppermute | solution.py:219
  690.1 54.1 %collective-permute-start.50 = (bf16[3,320,1280]{2,1,0:T(8,128)(2,1)}, bf16[3,320,1280]{2,1,0:T(8,128)(2,1)}, u32[]{:S(2)}, u32[]{:S(2)}) collective-permute-start(bf16[3,320,1280]{2,1,0:T(8,128)(2,1)} %get-tuple-element.293), channel_id=1, source_target_pairs={{0,2},{2,0},{1,3},{3,1},{4,6},{6,4},{5,7},{7,5},{8,10},{10,8},{9,1... | collective-permute-start | bytes 7372808 | tf_op jit(solution)/shard_map/ppermute | solution.py:187
  699.3 7.7 collective-permute-start.46
  699.3 11.1 %collective-permute-start.47 = (bf16[2,320,640]{2,1,0:T(8,128)(2,1)}, bf16[2,320,640]{2,1,0:T(8,128)(2,1)}, u32[]{:S(2)}, u32[]{:S(2)}) collective-permute-start(bf16[2,320,640]{2,1,0:T(8,128)(2,1)} %get-tuple-element.274), channel_id=1, source_target_pairs={{0,1},{1,0},{2,3},{3,2},{4,5},{5,4},{6,7},{7,6},{8,9},{9,8},{10,11... | collective-permute-start | bytes 2457608 | tf_op jit(solution)/shard_map/ppermute | solution.py:179
  699.8 39.9 %collective-permute-start.45 = (bf16[1280,640]{1,0:T(8,128)(2,1)}, bf16[1280,640]{1,0:T(8,128)(2,1)}, u32[]{:S(2)}, u32[]{:S(2)}) collective-permute-start(bf16[1280,640]{1,0:T(8,128)(2,1)} %get-tuple-element.271), channel_id=1, source_target_pairs={{8,16},{16,8},{9,17},{17,9},{10,18},{18,10},{11,19},{19,11},{12,20... | collective-permute-start | bytes 4915208 | tf_op jit(solution)/shard_map/ppermute | solution.py:214
  706.9 19.6 %collective-permute-start.48 = (bf16[2,160,1280]{2,1,0:T(8,128)(2,1)S(1)}, bf16[2,160,1280]{2,1,0:T(8,128)(2,1)}, u32[]{:S(2)}, u32[]{:S(2)}) collective-permute-start(bf16[2,160,1280]{2,1,0:T(8,128)(2,1)S(1)} %bitcast.105), channel_id=1, source_target_pairs={{8,0},{16,24},{9,1},{17,25},{10,2},{18,26},{11,3},{19,27},{12,4},{... | collective-permute-start | bytes 2457608 | tf_op jit(solution)/shard_map/ppermute | solution.py:214
  710.4 93.6 %collective-permute-start.58 = (bf16[2,160,1280]{2,1,0:T(8,128)(2,1)}, bf16[2,160,1280]{2,1,0:T(8,128)(2,1)}, u32[]{:S(2)}, u32[]{:S(2)}) collective-permute-start(bf16[2,160,1280]{2,1,0:T(8,128)(2,1)} %bitcast.34), channel_id=1, source_target_pairs={{4,0},{5,1},{6,2},{7,3},{12,8},{13,9},{14,10},{15,11},{20,16},{21,... | collective-permute-start | bytes 2457608 | tf_op jit(solution)/shard_map/ppermute | solution.py:245
  757.3 5.0 collective-permute-start.51
  757.3 5.0 collective-permute-start.52
  757.9 21.4 %collective-permute-start.56 = (bf16[2,320,640]{2,1,0:T(8,128)(2,1)}, bf16[2,320,640]{2,1,0:T(8,128)(2,1)S(1)}, u32[]{:S(2)}, u32[]{:S(2)}) collective-permute-start(bf16[2,320,640]{2,1,0:T(8,128)(2,1)} %get-tuple-element.315), channel_id=1, source_target_pairs={{0,2},{2,0},{1,3},{3,1},{4,6},{6,4},{5,7},{7,5},{8,10},{10,8},{9,1... | collective-permute-start | bytes 2457608 | tf_op jit(solution)/shard_map/ppermute | solution.py:187
  760.8 56.4 %collective-permute-start.59 = (bf16[2,160,1280]{2,1,0:T(8,128)(2,1)}, bf16[2,160,1280]{2,1,0:T(8,128)(2,1)}, u32[]{:S(2)}, u32[]{:S(2)}) collective-permute-start(bf16[2,160,1280]{2,1,0:T(8,128)(2,1)} %bitcast.36), channel_id=1, source_target_pairs={{8,4},{16,28},{9,5},{17,29},{10,6},{18,30},{11,7},{19,31}} | collective-permute-start | bytes 2457608 | tf_op jit(solution)/shard_map/ppermute | solution.py:239
  771.3 24.6 %collective-permute-start.53 = (bf16[2,320,640]{2,1,0:T(8,128)(2,1)}, bf16[2,320,640]{2,1,0:T(8,128)(2,1)S(1)}, u32[]{:S(2)}, u32[]{:S(2)}) collective-permute-start(bf16[2,320,640]{2,1,0:T(8,128)(2,1)} %get-tuple-element.301), channel_id=1, source_target_pairs={{0,2},{2,0},{1,3},{3,1},{4,6},{6,4},{5,7},{7,5},{8,10},{10,8},{9,1... | collective-permute-start | bytes 2457608 | tf_op jit(solution)/shard_map/ppermute | solution.py:187
  773.1 32.3 %collective-permute-start.55 = (bf16[2,160,1280]{2,1,0:T(8,128)(2,1)S(1)}, bf16[2,160,1280]{2,1,0:T(8,128)(2,1)S(1)}, u32[]{:S(2)}, u32[]{:S(2)}) collective-permute-start(bf16[2,160,1280]{2,1,0:T(8,128)(2,1)S(1)} %broadcast_select_fusion.13), channel_id=1, source_target_pairs={{8,12},{16,20},{12,4},{20,28},{9,13},{17,21},{13,5},{21,29},{10,14... | collective-permute-start | bytes 2457608 | tf_op jit(solution)/shard_map/ppermute | solution.py:238
  779.3 36.5 %collective-permute-start.54 = (bf16[2,160,1280]{2,1,0:T(8,128)(2,1)}, bf16[2,160,1280]{2,1,0:T(8,128)(2,1)S(1)}, u32[]{:S(2)}, u32[]{:S(2)}) collective-permute-start(bf16[2,160,1280]{2,1,0:T(8,128)(2,1)} %get-tuple-element.358), channel_id=1, source_target_pairs={{0,4},{4,0},{1,5},{5,1},{2,6},{6,2},{3,7},{7,3},{8,12},{12,8},{9,1... | collective-permute-start | bytes 2457608 | tf_op jit(solution)/shard_map/ppermute | solution.py:219
  796.0 38.2 %collective-permute-start.60 = (bf16[2,160,1280]{2,1,0:T(8,128)(2,1)S(1)}, bf16[2,160,1280]{2,1,0:T(8,128)(2,1)}, u32[]{:S(2)}, u32[]{:S(2)}) collective-permute-start(bf16[2,160,1280]{2,1,0:T(8,128)(2,1)S(1)} %bitcast.85), channel_id=1, source_target_pairs={{4,0},{5,1},{6,2},{7,3},{12,8},{13,9},{14,10},{15,11},{20,16},{21,... | collective-permute-start | bytes 2457608 | tf_op jit(solution)/shard_map/ppermute | solution.py:245
  804.0 30.2 %collective-permute-start.61 = (bf16[2,160,640]{2,1,0:T(8,128)(2,1)S(1)}, bf16[2,160,640]{2,1,0:T(8,128)(2,1)}, u32[]{:S(2)}, u32[]{:S(2)}) collective-permute-start(bf16[2,160,640]{2,1,0:T(8,128)(2,1)S(1)} %bitcast.104), channel_id=1, source_target_pairs={{8,4},{16,28},{9,5},{17,29},{10,6},{18,30},{11,7},{19,31}} | collective-permute-start | bytes 1228808 | tf_op jit(solution)/shard_map/ppermute | solution.py:239
  805.4 28.7 %collective-permute-start.57 = (bf16[2,160,640]{2,1,0:T(8,128)(2,1)}, bf16[2,160,640]{2,1,0:T(8,128)(2,1)}, u32[]{:S(2)}, u32[]{:S(2)}) collective-permute-start(bf16[2,160,640]{2,1,0:T(8,128)(2,1)} %broadcast_select_fusion.26), channel_id=1, source_target_pairs={{8,12},{16,20},{12,4},{20,28},{9,13},{17,21},{13,5},{21,29},{10,14... | collective-permute-start | bytes 1228808 | tf_op jit(solution)/shard_map/ppermute | solution.py:238
  815.8 18.4 %collective-permute-start.63 = (bf16[2,160,640]{2,1,0:T(8,128)(2,1)}, bf16[2,160,640]{2,1,0:T(8,128)(2,1)}, u32[]{:S(2)}, u32[]{:S(2)}) collective-permute-start(bf16[2,160,640]{2,1,0:T(8,128)(2,1)} %bitcast.40), channel_id=1, source_target_pairs={{8,4},{16,28},{9,5},{17,29},{10,6},{18,30},{11,7},{19,31}} | collective-permute-start | bytes 1228808 | tf_op jit(solution)/shard_map/ppermute | solution.py:239
  817.2 17.0 %collective-permute-start.62 = (bf16[2,160,640]{2,1,0:T(8,128)(2,1)}, bf16[2,160,640]{2,1,0:T(8,128)(2,1)}, u32[]{:S(2)}, u32[]{:S(2)}) collective-permute-start(bf16[2,160,640]{2,1,0:T(8,128)(2,1)} %broadcast_select_fusion.25), channel_id=1, source_target_pairs={{8,12},{16,20},{12,4},{20,28},{9,13},{17,21},{13,5},{21,29},{10,14... | collective-permute-start | bytes 1228808 | tf_op jit(solution)/shard_map/ppermute | solution.py:238
  (47 other events, 343.0 us)
Sparse Core Ops, SparseCore 0:
  339.8 43.5 reduce-scatter.1
